TPU v7x, 128 devices: a whole 4x4x4 slice. The times are simulated.
128 devices in a mesh: rows: 128 (over x, y, z, core).
Axes of the slice: x: 4, y: 4, z: 4, core: 2. Of those that a mesh axis runs over, the one named last changes fastest.
Arguments:
- vectors: bfloat16 [64, 131072], P(None, 'rows'), may hold values from -6 to 6
- diag_blocks: bfloat16 [512, 256, 256], P('rows')
- near_blocks: bfloat16 [16384, 256, 256], P('rows'), may hold values from -0.0625 to 0.0625
- near_rows: int32 [16384], P('rows'), may hold values from 0 to 511, as said below
- near_cols: int32 [16384], P('rows'), may hold values from 0 to 511, as said below
- far_left: bfloat16 [16384, 32, 256], P('rows'), may hold values from -1 to 1
- far_right: bfloat16 [16384, 32, 256], P('rows'), may hold values from -0.0625 to 0.0625
- far_rows: int32 [16384], P('rows'), may hold values from 0 to 511, as said below
- far_cols: int32 [16384], P('rows'), may hold values from 0 to 511, as said below
- counts: int32 [128, 2], P('rows'), may hold values from 16 to 128, as said below
Outputs:
- first_image: float32 [64, 131072], P(None, 'rows')
- second_image: float32 [64, 131072], P(None, 'rows')
Inputs may be any that keep to these rules, and one draw needn't show every extreme that they name: `near_rows`: slot s belongs to device d = s // 128, and its row cluster lies on d: it is one of d * 4 to d * 4 + 3. `near_cols`: the column cluster of a slot of device d lies on device (d + e) mod 128, with e one of -6 to -1 and 1 to 6; all slots of device d, near and far, whose column clusters lie on one device name the same cluster. `far_rows`: as for near_rows, with device d = s // 128. `far_cols`: as for near_cols, and consistent with it: one cluster per pair of devices. counts[d, 0] is at most 128 and counts[d, 1] at most 128; some device uses all 128 near slots and some device all 128 far slots.
All inputs are finite; a program needn't handle non-finite values.
Results may differ from a plain program's by a relative error of at most 0.0024.
Values may be sent and summed in bfloat16 or wider, within the bound.
No kernel may reach another device: no remote copies, remote signals or barrier semaphores. Data moves between devices by JAX's collectives and lax.ppermute only.
A program may use at most 128 MiB of HBM per device.

v0:
```python
import functools

import jax
import jax.numpy as jnp
from jax import lax
from jax.experimental import pallas as pl
from jax.experimental.pallas import tpu as pltpu
from jax.sharding import PartitionSpec as P

RHS, B, K = 64, 256, 32
CL, SLOTS, CHUNK = 4, 128, 16
CHUNKS = SLOTS // CHUNK
GROUP = B // K
PEERS = 12
DEAD = 12
EXTRA = 8
QUAD = 4
LISTED = SLOTS + PEERS * (QUAD - 1) + 12
VMEM_BYTES = 44 * 2**20
F32, BF16 = jnp.float32, jnp.bfloat16


def dot(x, y):
    return lax.dot_general(x, y, (((1,), (0,)), ((), ())), preferred_element_type=F32)


def dot_t(x, y):
    return lax.dot_general(x, y, (((1,), (1,)), ((), ())), preferred_element_type=F32)


def peer_number(delta, core):
    kappa, other = delta // 2 - 3, delta % 2
    step = kappa * (1 - 2 * core)
    same = int(other != core)
    if step == 0:
        return 11 if same else DEAD
    if step < 0:
        return 2 * (-step - 1) + same
    return 6 + 2 * (step - 1) + same if step < 3 or not same else DEAD


class Stream:
    def __init__(self, plan, near, left, right, near_buf, left_buf, right_buf, near_sem, left_sem, right_sem):
        self.plan = plan
        self.near = (near, near_buf, near_sem)
        self.far = ((left, left_buf, left_sem), (right, right_buf, right_sem))

    @staticmethod
    def copy(triple, chunk):
        source, target, sem = triple
        place = pl.ds(chunk * CHUNK, CHUNK)
        return pltpu.make_async_copy(source.at[place], target.at[place], sem.at[chunk])

    def start(self, near_chunks, far_chunks):
        def far_start(chunk, carry):
            for triple in self.far:
                self.copy(triple, chunk).start()
            return carry

        def near_start(chunk, carry):
            self.copy(self.near, chunk).start()
            return carry

        lax.fori_loop(0, far_chunks, far_start, 0)
        lax.fori_loop(0, near_chunks, near_start, 0)

    def start_planned(self):
        self.start(self.plan[4, 16], self.plan[4, 17])

    def far_loop(self, body):
        def arrived(chunk, carry):
            for triple in self.far:
                self.copy(triple, chunk).wait()
            return carry

        lax.fori_loop(0, self.plan[4, 17], arrived, 0)

        def step(index, carry):
            for part in range(2):
                first = index * 2 + part
                entries = [self.plan[2, first * GROUP + k] for k in range(GROUP)]
                slots = [entry & 255 for entry in entries]
                left = jnp.concatenate([self.far[0][1][slot] for slot in slots], axis=0)
                right = jnp.concatenate([self.far[1][1][slot] for slot in slots], axis=0)
                lane = lax.broadcasted_iota(jnp.int32, (1, B), 1) // K
                rows = jnp.zeros((1, B), jnp.int32)
                for k in range(GROUP):
                    rows = jnp.where(lane == k, entries[k] >> 8, rows)
                rows = jnp.broadcast_to(rows, (RHS, B))
                body(left, right, rows, [self.plan[3, 2 * first + half] for half in (0, 1)])
            return carry

        lax.fori_loop(0, self.plan[4, 18], step, 0)

    def near_loop(self, body):
        def step(chunk, carry):
            self.copy(self.near, chunk).wait()
            for part in range(CHUNK):
                body(chunk * CHUNK + part)
            return carry

        lax.fori_loop(0, self.plan[4, 16], step, 0)


HALF = B // 2


def back_products(stream, own, acc, near_buf):
    plan = stream.plan
    acc[...] = jnp.zeros_like(acc)

    def far(left, right, rows, partners):
        every = dot_t(own[0:CL].reshape(CL * RHS, B), left)
        coef = jnp.zeros((RHS, B), F32)
        for cluster in range(CL):
            coef = jnp.where(rows == cluster, every[cluster * RHS : (cluster + 1) * RHS], coef)
        coef = coef.astype(BF16)
        for half, partner in enumerate(partners):
            part = slice(half * HALF, (half + 1) * HALF)
            acc[partner] += dot(coef[:, part], right[part])

    def near(slot):
        acc[plan[1, slot]] += dot(own[plan[0, slot]], near_buf[slot])

    stream.far_loop(far)
    stream.near_loop(near)


def forward_products(stream, fetched, acc, near_buf):
    plan = stream.plan

    def far(left, right, rows, partners):
        coef = [
            dot_t(fetched[partner], right[half * HALF : (half + 1) * HALF])
            for half, partner in enumerate(partners)
        ]
        coef = jnp.concatenate(coef, axis=1).astype(BF16).astype(F32)
        spread = [jnp.where(rows == cluster, coef, 0.0).astype(BF16) for cluster in range(CL)]
        acc[0:CL] += dot(jnp.concatenate(spread, axis=0), left).reshape(CL, RHS, B)

    def near(slot):
        acc[plan[0, slot]] += dot_t(fetched[plan[1, slot]], near_buf[slot])

    stream.far_loop(far)
    stream.near_loop(near)


def make_plan(me, near_rows, near_cols, far_rows, far_cols, counts, plan, lut, fill, rank):
    core = me % 2
    base = me - core - 6
    for delta in range(16):
        pair = [peer_number(delta, a) if delta < 14 else DEAD for a in (0, 1)]
        lut[delta] = jnp.where(core == 0, pair[0], pair[1])
        plan[4, delta] = 0
        fill[delta] = 0
    near_chunks = (counts[0, 0] + (CHUNK - 1)) // CHUNK
    far_chunks = (counts[0, 1] + (CHUNK - 1)) // CHUNK

    def near_note(index, carry):
        for part in range(8):
            slot = index * 8 + part
            live = slot < counts[0, 0]
            col = near_cols[slot]
            rho = jnp.where(live, lut[((col // CL) - base) & 15], DEAD)
            plan[0, slot] = jnp.where(live, near_rows[slot] & (CL - 1), CL)
            plan[1, slot] = rho
            plan[4, rho] = col & (CL - 1)
        return carry

    def far_note(slot, carry):
        col = far_cols[slot]
        rho = lut[((col // CL) - base) & 15]
        plan[4, rho] = col & (CL - 1)
        before = fill[rho]
        rank[slot] = before + 256 * rho
        fill[rho] = before + 1
        return carry

    def far_place(slot, carry):
        noted = rank[slot]
        plan[2, fill[noted >> 8] + (noted & 255)] = slot + 256 * (far_rows[slot] & (CL - 1))
        return carry

    lax.fori_loop(0, counts[0, 1], far_note, 0)
    quads = 0
    for rho in range(PEERS):
        number = fill[rho]
        first = quads
        fill[rho] = first * QUAD
        wanted = (number + (QUAD - 1)) // QUAD

        def own_quad(index, carry, rho=rho):
            plan[3, index] = rho
            return carry

        quads = first + wanted
        lax.fori_loop(first, quads, own_quad, 0)
        for pad in range(1, QUAD):

            @pl.when(quads * QUAD - pad >= first * QUAD + number)
            def _(pad=pad, quads=quads):
                plan[2, quads * QUAD - pad] = 256 * CL

    fours = (quads + 3) // 4

    def dead_quad(index, carry):
        plan[3, index] = DEAD
        for k in range(QUAD):
            plan[2, index * QUAD + k] = 256 * CL
        return carry

    lax.fori_loop(quads, fours * 4, dead_quad, 0)
    lax.fori_loop(0, counts[0, 1], far_place, 0)
    lax.fori_loop(0, near_chunks * (CHUNK // 8), near_note, 0)
    plan[4, 16] = near_chunks
    plan[4, 17] = far_chunks
    plan[4, 18] = fours


def place_out(rho):
    if rho == 11:
        return 3, 6
    if rho < 6:
        return 3, rho ^ 1
    k, same = divmod(rho - 6, 2)
    return k, 3 * same


def place_in(rho):
    if rho == 11:
        return 4, 6
    if rho < 6:
        return rho // 2, rho % 2
    return 3, rho - 6


MESSAGE = (4, 4, 3)


def back_first(
    me, near_rows, near_cols, far_rows, far_cols, counts, vectors, near, left, right,
    m1, m2, m3, give, plan,
    near_buf, left_buf, right_buf, own, acc, lists, few, lut, fill, rank, near_sem, left_sem, right_sem, list_sem,
):
    copies = [pltpu.make_async_copy(counts, few, list_sem.at[4])]
    for index, source in enumerate((near_rows, near_cols, far_rows, far_cols)):
        copies.append(pltpu.make_async_copy(source, lists[index], list_sem.at[index]))
    for copy in copies:
        copy.start()
    for cluster in range(CL):
        own[cluster] = vectors[:, cluster * B : (cluster + 1) * B]
    own[CL] = jnp.zeros((RHS, B), BF16)
    for copy in copies:
        copy.wait()
    stream = Stream(plan, near, left, right, near_buf, left_buf, right_buf, near_sem, left_sem, right_sem)
    stream.start((few[0, 0] + (CHUNK - 1)) // CHUNK, (few[0, 1] + (CHUNK - 1)) // CHUNK)
    make_plan(me[0], *lists, few, plan, lut, fill, rank)
    back_products(stream, own, acc, near_buf)
    outs = (m1, m2, m3, give)
    for rho in range(PEERS):
        message, index = place_out(rho)
        outs[message][index, 0:RHS] = acc[rho]
        outs[message][index, RHS:] = jnp.full((EXTRA, B), plan[4, rho].astype(F32), F32)


def forward_first(
    plan, vectors, sib, h1, h2, h3, post, diag, near, left, right,
    out,
    near_buf, left_buf, right_buf, fetched, acc, near_sem, left_sem, right_sem, fetch_sem,
):
    stream = Stream(plan, near, left, right, near_buf, left_buf, right_buf, near_sem, left_sem, right_sem)
    halo = (h1, h2, h3)
    copies = []
    for rho in range(PEERS):
        lanes = pl.ds(pl.multiple_of(plan[4, rho] * B, B), B)
        if rho == 11:
            source = sib.at[:, lanes]
        elif rho < 6:
            source = halo[rho // 2].at[rho % 2, :, lanes]
        else:
            k, same = divmod(rho - 6, 2)
            source = post.at[2 * k + (1 - same if k < 2 else 0), :, lanes]
        copies.append(pltpu.make_async_copy(source, fetched.at[rho], fetch_sem.at[rho]))
    for copy in copies:
        copy.start()
    stream.start_planned()
    fetched[DEAD] = jnp.zeros((RHS, B), BF16)
    acc[CL] = jnp.zeros((RHS, B), F32)
    for cluster in range(CL):
        acc[cluster] = dot_t(vectors[:, cluster * B : (cluster + 1) * B], diag[cluster])
    for copy in copies:
        copy.wait()
    forward_products(stream, fetched, acc, near_buf)
    out[...] = acc[0:CL]


def back_second(
    plan, partial, r1, r2, r3, post, got, near, left, right,
    image, rounded, wanted, m1, m2, m3, give,
    near_buf, left_buf, right_buf, own, arrived, acc, near_sem, left_sem, right_sem, arrived_sem,
):
    stream = Stream(plan, near, left, right, near_buf, left_buf, right_buf, near_sem, left_sem, right_sem)
    ins = (r1, r2, r3, post, got)
    copies = []
    for rho in range(PEERS):
        message, index = place_in(rho)
        copies.append(pltpu.make_async_copy(ins[message].at[index], arrived.at[rho], arrived_sem.at[rho]))
    for copy in copies:
        copy.start()
    stream.start_planned()
    own[CL] = jnp.zeros((RHS, B), BF16)
    for copy in copies:
        copy.wait()
    for rho in range(PEERS):
        wanted[rho] = arrived[rho, RHS:]
    for cluster in range(CL):
        total = partial[cluster]
        for rho in range(PEERS):
            mine = arrived[rho, RHS : RHS + 1] == float(cluster)
            total += jnp.where(jnp.broadcast_to(mine, (RHS, B)), arrived[rho, 0:RHS], 0.0)
        image[:, cluster * B : (cluster + 1) * B] = total
        own[cluster] = total.astype(BF16)
        rounded[cluster] = total.astype(BF16)
    back_products(stream, own, acc, near_buf)
    outs = (m1, m2, m3, give)
    for rho in range(PEERS):
        message, index = place_out(rho)
        outs[message][index, 0:RHS] = acc[rho].astype(BF16)
        pick = jnp.broadcast_to(wanted[rho, 0:1], (RHS, B))
        chosen = jnp.zeros((RHS, B), F32)
        for cluster in range(CL):
            chosen = jnp.where(pick == float(cluster), own[cluster].astype(F32), chosen)
        outs[message][index, RHS:] = chosen.astype(BF16)


def forward_second(
    plan, own, wanted, r1, r2, r3, post, got, diag, near, left, right,
    image,
    near_buf, left_buf, right_buf, arrived, fetched, acc, near_sem, left_sem, right_sem, arrived_sem,
):
    stream = Stream(plan, near, left, right, near_buf, left_buf, right_buf, near_sem, left_sem, right_sem)
    ins = (r1, r2, r3, post, got)
    copies = []
    for rho in range(PEERS):
        message, index = place_in(rho)
        source = ins[message].at[index]
        copies.append(pltpu.make_async_copy(source, arrived.at[rho], arrived_sem.at[rho]))
    for copy in copies:
        copy.start()
    stream.start_planned()
    fetched[DEAD] = jnp.zeros((RHS, B), BF16)
    acc[CL] = jnp.zeros((RHS, B), F32)
    for cluster in range(CL):
        acc[cluster] = dot_t(own[cluster], diag[cluster])
    for copy in copies:
        copy.wait()
    for rho in range(PEERS):
        fetched[rho] = arrived[rho, RHS:]
    for cluster in range(CL):
        total = acc[cluster]
        for rho in range(PEERS):
            mine = wanted[rho, 0:1] == float(cluster)
            total += jnp.where(jnp.broadcast_to(mine, (RHS, B)), arrived[rho, 0:RHS].astype(F32), 0.0)
        acc[cluster] = total
    forward_products(stream, fetched, acc, near_buf)
    for cluster in range(CL):
        image[:, cluster * B : (cluster + 1) * B] = acc[cluster]


SMEM = pl.BlockSpec(memory_space=pltpu.SMEM)
VMEM = pl.BlockSpec(memory_space=pltpu.VMEM)
ANY = pl.BlockSpec(memory_space=pl.ANY)
HBM = pl.BlockSpec(memory_space=pltpu.HBM)


def blocks_scratch():
    return [
        pltpu.VMEM((SLOTS, B, B), BF16),
        pltpu.VMEM((SLOTS, K, B), BF16),
        pltpu.VMEM((SLOTS, K, B), BF16),
    ]


def sems(*more):
    return [pltpu.SemaphoreType.DMA((CHUNKS,))] * 3 + [pltpu.SemaphoreType.DMA((n,)) for n in more]


def call(kernel, name, outs, out_specs, in_specs, scratch):
    return pl.pallas_call(
        kernel,
        name=name,
        out_shape=outs,
        in_specs=in_specs,
        out_specs=out_specs,
        scratch_shapes=scratch,
        compiler_params=pltpu.CompilerParams(vmem_limit_bytes=VMEM_BYTES),
        cost_estimate=pl.CostEstimate(flops=2 * 10**9, bytes_accessed=22 * 10**6, transcendentals=0),
    )


def shaped(shape, dtype):
    return jax.ShapeDtypeStruct(shape, dtype)


def message_shapes(rows, dtype):
    return [shaped((n, rows, B), dtype) for n in MESSAGE + (7,)]


def k1(*args):
    return call(
        back_first, "transposed_products",
        message_shapes(RHS + EXTRA, F32) + [shaped((5, LISTED), jnp.int32)],
        [VMEM] * 4 + [SMEM],
        [SMEM] + [HBM] * 5 + [VMEM] + [HBM] * 3,
        blocks_scratch()
        + [
            pltpu.VMEM((CL + 1, RHS, B), BF16),
            pltpu.VMEM((PEERS + 1, RHS, B), F32),
            [pltpu.SMEM((SLOTS,), jnp.int32)] * 4,
            pltpu.SMEM((1, 2), jnp.int32),
            pltpu.SMEM((16,), jnp.int32),
            pltpu.SMEM((16,), jnp.int32),
            pltpu.SMEM((SLOTS,), jnp.int32),
        ]
        + sems(5),
    )(*args)


def k2(*args):
    return call(
        forward_first, "forward_products",
        shaped((CL, RHS, B), F32), VMEM,
        [SMEM] + [VMEM] + [ANY] * 5 + [VMEM] + [HBM] * 3,
        blocks_scratch()
        + [pltpu.VMEM((PEERS + 1, RHS, B), BF16), pltpu.VMEM((CL + 1, RHS, B), F32)]
        + sems(PEERS),
    )(*args)


def k3(*args):
    return call(
        back_second, "image_and_transposed_products",
        [
            shaped((RHS, CL * B), F32),
            shaped((CL, RHS, B), BF16),
            shaped((PEERS, EXTRA, B), F32),
        ]
        + message_shapes(2 * RHS, BF16),
        [VMEM] * 7,
        [SMEM] + [VMEM] + [ANY] * 5 + [HBM] * 3,
        blocks_scratch()
        + [
            pltpu.VMEM((CL + 1, RHS, B), BF16),
            pltpu.VMEM((PEERS, RHS + EXTRA, B), F32),
            pltpu.VMEM((PEERS + 1, RHS, B), F32),
        ]
        + sems(PEERS),
    )(*args)


def k4(*args):
    return call(
        forward_second, "second_image",
        shaped((RHS, CL * B), F32), VMEM,
        [SMEM] + [VMEM] * 2 + [ANY] * 5 + [VMEM] + [HBM] * 3,
        blocks_scratch()
        + [
            pltpu.VMEM((PEERS, 2 * RHS, B), BF16),
            pltpu.VMEM((PEERS + 1, RHS, B), BF16),
            pltpu.VMEM((CL + 1, RHS, B), F32),
        ]
        + sems(PEERS),
    )(*args)


def carriers(size, k):
    pairs = []
    for chip in range(size // 2):
        for core in range(2):
            step = k if core == 0 else -k
            pairs.append((2 * chip + core, (2 * (chip + step) + core) % size))
    return pairs


def per_device(
    vectors, diag_blocks, near_blocks, near_rows, near_cols, far_left, far_right, far_rows, far_cols, counts
):
    size = lax.axis_size("rows")
    me = lax.axis_index("rows").reshape(1)

    def swap(block):
        return lax.ppermute(block, "rows", [(i, i ^ 1) for i in range(size)])

    def carry(block, k):
        return lax.ppermute(block, "rows", carriers(size, k))

    def exchange(m1, m2, m3, give):
        got = swap(give)
        messages = []
        for k, message in enumerate((m1, m2, m3)):
            messages.append(lax.dynamic_update_slice(message, got[2 * k : 2 * k + 2], (1, 0, 0)))
        return [carry(message, k + 1) for k, message in enumerate(messages)] + [got, messages]

    def passed_on(r1, r2, r3):
        return swap(jnp.concatenate([r1[2:4], r2[2:4], r3[2:3]]))

    sib = swap(vectors)
    both = jnp.stack([vectors, sib])
    halo = [carry(both, k) for k in (1, 2, 3)]
    own, both = lax.optimization_barrier((vectors, both))
    m1, m2, m3, give, plan = k1(
        me, near_rows, near_cols, far_rows, far_cols, counts, own, near_blocks, far_left, far_right
    )
    r1, r2, r3, got, messages = exchange(m1, m2, m3, give)
    halo_post = swap(jnp.concatenate([halo[0], halo[1], halo[2][1:]]))
    halo_post, messages = lax.optimization_barrier((halo_post, messages))
    partial = k2(plan, vectors, sib, *halo, halo_post, diag_blocks, near_blocks, far_left, far_right)
    partial, r1, r2, r3 = lax.optimization_barrier((partial, r1, r2, r3))
    post = passed_on(r1, r2, r3)
    first_image, rounded, wanted, m1, m2, m3, give = k3(
        plan, partial, r1, r2, r3, post, got, near_blocks, far_left, far_right
    )
    r1, r2, r3, got, messages = exchange(m1, m2, m3, give)
    post = passed_on(r1, r2, r3)
    second_image = k4(
        plan, rounded, wanted, r1, r2, r3, post, got, diag_blocks, near_blocks, far_left, far_right
    )
    return first_image, second_image


def solution(mesh):
    return jax.shard_map(
        per_device,
        mesh=mesh,
        in_specs=(
            P(None, "rows"),
            P("rows", None, None),
            P("rows", None, None),
            P("rows"),
            P("rows"),
            P("rows", None, None),
            P("rows", None, None),
            P("rows"),
            P("rows"),
            P("rows", None),
        ),
        out_specs=(P(None, "rows"), P(None, "rows")),
        check_vma=False,
    )
```

profile of v0, /device:TPU:1, one launch (start us, length us, event | category | flops | bytes accessed | tf_op | source)
XLA Modules:
  0.0 91.5 jit_solution(18418122652742863407)
XLA Ops:
  0.6 1.5 %collective-permute-start = (bf16[64,1024]{1,0:T(8,128)(2,1)}, bf16[64,1024]{1,0:T(8,128)(2,1)S(1)}, u32[]{:S(2)}, u32[]{:S(2)}) collective-permute-start(bf16[64,1024]{1,0:T(8,128)(2,1)} %vectors.2), channel_id=1, source_target_pairs={{0,1},{1,0},{2,3},{3,2},{4,5},{5,4},{6,7},{7,6},{8,9},{9,8},{10,11... | collective-permute-start | bytes 393224 | tf_op jit(solution)/shard_map/ppermute | solution.py:492
  2.1 1.2 %collective-permute-done.sib = bf16[64,1024]{1,0:T(8,128)(2,1)S(1)} collective-permute-done((bf16[64,1024]{1,0:T(8,128)(2,1)}, bf16[64,1024]{1,0:T(8,128)(2,1)S(1)}, u32[]{:S(2)}, u32[]{:S(2)}) %collective-permute-start) | collective-permute-done | bytes 131104 | tf_op jit(solution)/shard_map/ppermute | solution.py:492
  3.3 0.9 %pad_maximum_fusion.3 = bf16[2,64,1024]{2,1,0:T(8,128)(2,1)S(1)} fusion(bf16[1,64,1024]{2,1,0:T(8,128)(2,1)S(1)} %bitcast.4, bf16[1,64,1024]{2,1,0:T(8,128)(2,1)} %bitcast.3), kind=kLoop, calls=%fused_computation.3 | loop fusion | flops 131072 | bytes 524288 | tf_op jit(solution)/shard_map/stack | solution.py:508
  4.3 6.4 %collective-permute-start.3 = (bf16[2,64,1024]{2,1,0:T(8,128)(2,1)S(1)}, bf16[2,64,1024]{2,1,0:T(8,128)(2,1)S(1)}, u32[]{:S(2)}, u32[]{:S(2)}) collective-permute-start(bf16[2,64,1024]{2,1,0:T(8,128)(2,1)S(1)} %pad_maximum_fusion.3), channel_id=1, source_target_pairs={{0,6},{1,123},{2,8},{3,125},{4,10},{5,127},{6,12},{7,1},{8,14},{9,... | collective-permute-start | bytes 786440 | tf_op jit(solution)/shard_map/ppermute | solution.py:495
  10.7 2.2 %collective-permute-start.1 = (bf16[2,64,1024]{2,1,0:T(8,128)(2,1)S(1)}, bf16[2,64,1024]{2,1,0:T(8,128)(2,1)S(1)}, u32[]{:S(2)}, u32[]{:S(2)}) collective-permute-start(bf16[2,64,1024]{2,1,0:T(8,128)(2,1)S(1)} %pad_maximum_fusion.3), channel_id=1, source_target_pairs={{0,2},{1,127},{2,4},{3,1},{4,6},{5,3},{6,8},{7,5},{8,10},{9,7},{10... | collective-permute-start | bytes 786440 | tf_op jit(solution)/shard_map/ppermute | solution.py:495
  12.9 1.4 %collective-permute-start.2 = (bf16[2,64,1024]{2,1,0:T(8,128)(2,1)S(1)}, bf16[2,64,1024]{2,1,0:T(8,128)(2,1)S(1)}, u32[]{:S(2)}, u32[]{:S(2)}) collective-permute-start(bf16[2,64,1024]{2,1,0:T(8,128)(2,1)S(1)} %pad_maximum_fusion.3), channel_id=1, source_target_pairs={{0,4},{1,125},{2,6},{3,127},{4,8},{5,1},{6,10},{7,3},{8,12},{9,5},... | collective-permute-start | bytes 786440 | tf_op jit(solution)/shard_map/ppermute | solution.py:495
  14.3 1.6 %copy-done = bf16[128,32,256]{2,1,0:T(8,128)(2,1)S(1)} copy-done((bf16[128,32,256]{2,1,0:T(8,128)(2,1)S(1)}, bf16[128,32,256]{2,1,0:T(8,128)(2,1)}, u32[]{:S(2)}) %copy-start) | copy-done | bytes 2097176
  15.9 1.6 %copy-done.2 = bf16[128,32,256]{2,1,0:T(8,128)(2,1)S(1)} copy-done((bf16[128,32,256]{2,1,0:T(8,128)(2,1)S(1)}, bf16[128,32,256]{2,1,0:T(8,128)(2,1)}, u32[]{:S(2)}) %copy-start.2) | copy-done | bytes 2097176
  17.5 0.9 copy-done.5
  18.4 0.7 copy-done.7
  19.0 0.7 copy-done.8
  19.7 0.7 copy-done.9
  20.4 0.7 copy-done.10
  21.0 0.7 copy-done.11
  21.7 7.4 %transposed_products.1 = (f32[4,72,256]{2,1,0:T(8,128)S(1)}, f32[4,72,256]{2,1,0:T(8,128)S(1)}, f32[3,72,256]{2,1,0:T(8,128)S(1)}, f32[7,72,256]{2,1,0:T(8,128)S(1)}, s32[5,176]{1,0:T(8,128)S(1)}) custom-call(s32[1]{0:T(128)} %bitcast.me, s32[128]{0:T(128)S(1)} %copy-done.7, s32[128]{0:T(128)S(1)} %copy-done.8, s32[128]{0:T(128)S(1)} %copy-done.9, ...), custom_call_target="tpu_custom_call" | custom-call | flops 2000000000 | bytes 22000000 | tf_op jit(solution)/shard_map/transposed_products/pallas_call | solution.py:410
  29.1 0.0 copy-start.1
  29.1 0.0 copy-start.6
  29.1 0.1 collective-permute-start.5
  29.2 0.0 collective-permute-done.3.h3
  29.3 0.0 collective-permute-done.1.h1
  29.3 0.0 collective-permute-done.2.h2
  29.3 0.1 pad_maximum_fusion
  29.4 0.6 collective-permute-start.4
  29.9 1.2 %collective-permute-done.5.got = f32[7,72,256]{2,1,0:T(8,128)S(1)} collective-permute-done((f32[7,72,256]{2,1,0:T(8,128)S(1)}, f32[7,72,256]{2,1,0:T(8,128)S(1)}, u32[]{:S(2)}, u32[]{:S(2)}) %collective-permute-start.5) | collective-permute-done | bytes 516128 | tf_op jit(solution)/shard_map/ppermute | solution.py:492
  31.2 5.0 %collective-permute-start.6 = (f32[4,72,256]{2,1,0:T(8,128)S(1)}, f32[4,72,256]{2,1,0:T(8,128)S(1)}, u32[]{:S(2)}, u32[]{:S(2)}) collective-permute-start(f32[4,72,256]{2,1,0:T(8,128)S(1)} %get-tuple-element.40), channel_id=1, source_target_pairs={{0,2},{1,127},{2,4},{3,1},{4,6},{5,3},{6,8},{7,5},{8,10},{9,7},{10... | collective-permute-start | bytes 884744 | tf_op jit(solution)/shard_map/ppermute | solution.py:495
  36.2 1.0 %collective-permute-start.7 = (f32[4,72,256]{2,1,0:T(8,128)S(1)}, f32[4,72,256]{2,1,0:T(8,128)S(1)}, u32[]{:S(2)}, u32[]{:S(2)}) collective-permute-start(f32[4,72,256]{2,1,0:T(8,128)S(1)} %get-tuple-element.39), channel_id=1, source_target_pairs={{0,4},{1,125},{2,6},{3,127},{4,8},{5,1},{6,10},{7,3},{8,12},{9,5},... | collective-permute-start | bytes 884744 | tf_op jit(solution)/shard_map/ppermute | solution.py:495
  37.2 2.4 %collective-permute-start.8 = (f32[3,72,256]{2,1,0:T(8,128)S(1)}, f32[3,72,256]{2,1,0:T(8,128)S(1)}, u32[]{:S(2)}, u32[]{:S(2)}) collective-permute-start(f32[3,72,256]{2,1,0:T(8,128)S(1)} %get-tuple-element.38), channel_id=1, source_target_pairs={{0,6},{1,123},{2,8},{3,125},{4,10},{5,127},{6,12},{7,1},{8,14},{9,... | collective-permute-start | bytes 663560 | tf_op jit(solution)/shard_map/ppermute | solution.py:495
  39.6 0.0 collective-permute-done.4.post
  39.6 0.0 copy-done.3
  39.6 0.0 copy-done.4
  39.6 4.9 %forward_products.1.partial = f32[4,64,256]{2,1,0:T(8,128)S(1)} custom-call(s32[5,176]{1,0:T(8,128)S(1)} %get-tuple-element.21.plan, bf16[64,1024]{1,0:T(8,128)(2,1)S(1)} %copy-done.6, bf16[64,1024]{1,0:T(8,128)(2,1)S(1)} %collective-permute-done.sib, bf16[2,64,1024]{2,1,0:T(8,128)(2,1)S(1)} %collective-permute-done.1.h1, ...), custom_call_target="tpu_custom_call" | custom-call | flops 2000000000 | bytes 22000000 | tf_op jit(solution)/shard_map/forward_products/pallas_call | solution.py:430
  44.5 7.0 %collective-permute-done.8.r3 = f32[3,72,256]{2,1,0:T(8,128)S(1)} collective-permute-done((f32[3,72,256]{2,1,0:T(8,128)S(1)}, f32[3,72,256]{2,1,0:T(8,128)S(1)}, u32[]{:S(2)}, u32[]{:S(2)}) %collective-permute-start.8) | collective-permute-done | bytes 221216 | tf_op jit(solution)/shard_map/ppermute | solution.py:495
  51.5 0.0 collective-permute-done.6.r1
  51.5 0.0 collective-permute-done.7.r2
  51.6 0.1 collective-permute-start.9
  51.7 1.7 %collective-permute-done.9.post = f32[5,72,256]{2,1,0:T(8,128)S(1)} collective-permute-done((f32[5,72,256]{2,1,0:T(8,128)S(1)}, f32[5,72,256]{2,1,0:T(8,128)S(1)}, u32[]{:S(2)}, u32[]{:S(2)}) %collective-permute-start.9) | collective-permute-done | bytes 368672 | tf_op jit(solution)/shard_map/ppermute | solution.py:492
  53.4 7.0 %image_and_transposed_products.1 = (f32[64,1024]{1,0:T(8,128)}, bf16[4,64,256]{2,1,0:T(8,128)(2,1)S(1)}, f32[12,8,256]{2,1,0:T(8,128)S(1)}, bf16[4,128,256]{2,1,...) custom-call(s32[5,176]{1,0:T(8,128)S(1)} %get-tuple-element.21.plan,, ...), custom_call_target="tpu_custom_call" | custom-call | flops 2000000000 | bytes 22000000 | tf_op jit(solution)/shard_map/image_and_transposed_products/pallas_call | solution.py:441
  60.4 1.6 %collective-permute-start.10 = (bf16[7,128,256]{2,1,0:T(8,128)(2,1)S(1)}, bf16[7,128,256]{2,1,0:T(8,128)(2,1)S(1)}, u32[]{:S(2)}, u32[]{:S(2)}) collective-permute-start(bf16[7,128,256]{2,1,0:T(8,128)(2,1)S(1)} %get-tuple-element.35), channel_id=1, source_target_pairs={{0,1},{1,0},{2,3},{3,2},{4,5},{5,4},{6,7},{7,6},{8,9},{9,8},{10,11... | collective-permute-start | bytes 1376264 | tf_op jit(solution)/shard_map/ppermute | solution.py:492
  62.0 1.4 %collective-permute-done.10.got = bf16[7,128,256]{2,1,0:T(8,128)(2,1)S(1)} collective-permute-done((bf16[7,128,256]{2,1,0:T(8,128)(2,1)S(1)}, bf16[7,128,256]{2,1,0:T(8,128)(2,1)S(1)}, u32[]{:S(2)}, u32[]{:S(2)}) %collective-permute-start.10) | collective-permute-done | bytes 458784 | tf_op jit(solution)/shard_map/ppermute | solution.py:492
  63.5 4.6 %collective-permute-start.11 = (bf16[4,128,256]{2,1,0:T(8,128)(2,1)S(1)}, bf16[4,128,256]{2,1,0:T(8,128)(2,1)S(1)}, u32[]{:S(2)}, u32[]{:S(2)}) collective-permute-start(bf16[4,128,256]{2,1,0:T(8,128)(2,1)S(1)} %get-tuple-element.43), channel_id=1, source_target_pairs={{0,2},{1,127},{2,4},{3,1},{4,6},{5,3},{6,8},{7,5},{8,10},{9,7},{10... | collective-permute-start | bytes 786440 | tf_op jit(solution)/shard_map/ppermute | solution.py:495
  68.1 1.1 %collective-permute-start.12 = (bf16[4,128,256]{2,1,0:T(8,128)(2,1)S(1)}, bf16[4,128,256]{2,1,0:T(8,128)(2,1)S(1)}, u32[]{:S(2)}, u32[]{:S(2)}) collective-permute-start(bf16[4,128,256]{2,1,0:T(8,128)(2,1)S(1)} %get-tuple-element.42), channel_id=1, source_target_pairs={{0,4},{1,125},{2,6},{3,127},{4,8},{5,1},{6,10},{7,3},{8,12},{9,5},... | collective-permute-start | bytes 786440 | tf_op jit(solution)/shard_map/ppermute | solution.py:495
  69.2 1.6 %collective-permute-start.13 = (bf16[3,128,256]{2,1,0:T(8,128)(2,1)S(1)}, bf16[3,128,256]{2,1,0:T(8,128)(2,1)S(1)}, u32[]{:S(2)}, u32[]{:S(2)}) collective-permute-start(bf16[3,128,256]{2,1,0:T(8,128)(2,1)S(1)} %get-tuple-element.41), channel_id=1, source_target_pairs={{0,6},{1,123},{2,8},{3,125},{4,10},{5,127},{6,12},{7,1},{8,14},{9,... | collective-permute-start | bytes 589832 | tf_op jit(solution)/shard_map/ppermute | solution.py:495
  70.8 12.0 %collective-permute-done.13.r3 = bf16[3,128,256]{2,1,0:T(8,128)(2,1)S(1)} collective-permute-done((bf16[3,128,256]{2,1,0:T(8,128)(2,1)S(1)}, bf16[3,128,256]{2,1,0:T(8,128)(2,1)S(1)}, u32[]{:S(2)}, u32[]{:S(2)}) %collective-permute-start.13) | collective-permute-done | bytes 196640 | tf_op jit(solution)/shard_map/ppermute | solution.py:495
  82.8 0.0 collective-permute-done.11.r1
  82.8 0.0 collective-permute-done.12.r2
  82.9 0.1 collective-permute-start.14
  83.0 1.6 %collective-permute-done.14.post = bf16[5,128,256]{2,1,0:T(8,128)(2,1)S(1)} collective-permute-done((bf16[5,128,256]{2,1,0:T(8,128)(2,1)S(1)}, bf16[5,128,256]{2,1,0:T(8,128)(2,1)S(1)}, u32[]{:S(2)}, u32[]{:S(2)}) %collective-permute-start.14) | collective-permute-done | bytes 327712 | tf_op jit(solution)/shard_map/ppermute | solution.py:492
  84.6 6.9 %second_image.1 = f32[64,1024]{1,0:T(8,128)} custom-call(s32[5,176]{1,0:T(8,128)S(1)} %get-tuple-element.21.plan, bf16[4,64,256]{2,1,0:T(8,128)(2,1)S(1)} %get-tuple-element.32.own, f32[12,8,256]{2,1,0:T(8,128)S(1)} %get-tuple-element.33.wanted, bf16[4,128,256]{2,1,0:T(8,128)(2,1)S(1)} %collective-permute-done.11.r1, ...), custom_call_target="tpu_custom_call" | custom-call | flops 2000000000 | bytes 22000000 | tf_op jit(solution)/shard_map/second_image/pallas_call | solution.py:462
  (23 shorter events, 0.2 us)
Async XLA Ops:
  0.6 2.7 %collective-permute-start = (bf16[64,1024]{1,0:T(8,128)(2,1)}, bf16[64,1024]{1,0:T(8,128)(2,1)S(1)}, u32[]{:S(2)}, u32[]{:S(2)}) collective-permute-start(bf16[64,1024]{1,0:T(8,128)(2,1)} %vectors.2), channel_id=1, source_target_pairs={{0,1},{1,0},{2,3},{3,2},{4,5},{5,4},{6,7},{7,6},{8,9},{9,8},{10,11... | collective-permute-start | bytes 393224 | tf_op jit(solution)/shard_map/ppermute | solution.py:492
  4.3 25.0 %collective-permute-start.3 = (bf16[2,64,1024]{2,1,0:T(8,128)(2,1)S(1)}, bf16[2,64,1024]{2,1,0:T(8,128)(2,1)S(1)}, u32[]{:S(2)}, u32[]{:S(2)}) collective-permute-start(bf16[2,64,1024]{2,1,0:T(8,128)(2,1)S(1)} %pad_maximum_fusion.3), channel_id=1, source_target_pairs={{0,6},{1,123},{2,8},{3,125},{4,10},{5,127},{6,12},{7,1},{8,14},{9,... | collective-permute-start | bytes 786440 | tf_op jit(solution)/shard_map/ppermute | solution.py:495
  10.7 18.6 %collective-permute-start.1 = (bf16[2,64,1024]{2,1,0:T(8,128)(2,1)S(1)}, bf16[2,64,1024]{2,1,0:T(8,128)(2,1)S(1)}, u32[]{:S(2)}, u32[]{:S(2)}) collective-permute-start(bf16[2,64,1024]{2,1,0:T(8,128)(2,1)S(1)} %pad_maximum_fusion.3), channel_id=1, source_target_pairs={{0,2},{1,127},{2,4},{3,1},{4,6},{5,3},{6,8},{7,5},{8,10},{9,7},{10... | collective-permute-start | bytes 786440 | tf_op jit(solution)/shard_map/ppermute | solution.py:495
  12.9 16.4 %collective-permute-start.2 = (bf16[2,64,1024]{2,1,0:T(8,128)(2,1)S(1)}, bf16[2,64,1024]{2,1,0:T(8,128)(2,1)S(1)}, u32[]{:S(2)}, u32[]{:S(2)}) collective-permute-start(bf16[2,64,1024]{2,1,0:T(8,128)(2,1)S(1)} %pad_maximum_fusion.3), channel_id=1, source_target_pairs={{0,4},{1,125},{2,6},{3,127},{4,8},{5,1},{6,10},{7,3},{8,12},{9,5},... | collective-permute-start | bytes 786440 | tf_op jit(solution)/shard_map/ppermute | solution.py:495
  14.3 1.6 %copy-start = (bf16[128,32,256]{2,1,0:T(8,128)(2,1)S(1)}, bf16[128,32,256]{2,1,0:T(8,128)(2,1)}, u32[]{:S(2)}) copy-start(bf16[128,32,256]{2,1,0:T(8,128)(2,1)} %left.7) | copy-start | bytes 6291460
  15.9 1.6 %copy-start.2 = (bf16[128,32,256]{2,1,0:T(8,128)(2,1)S(1)}, bf16[128,32,256]{2,1,0:T(8,128)(2,1)}, u32[]{:S(2)}) copy-start(bf16[128,32,256]{2,1,0:T(8,128)(2,1)} %right.7) | copy-start | bytes 6291460
  17.5 0.9 copy-start.5
  18.4 0.7 copy-start.7
  19.0 0.7 copy-start.8
  19.7 0.7 copy-start.9
  20.4 0.7 copy-start.10
  21.0 0.7 copy-start.11
  21.7 17.9 %copy-start.3 = (bf16[128,32,256]{2,1,0:T(8,128)(2,1)S(1)}, bf16[128,32,256]{2,1,0:T(8,128)(2,1)}, u32[]{:S(2)}) copy-start(bf16[128,32,256]{2,1,0:T(8,128)(2,1)} %right.7) | copy-start | bytes 6291460
  21.7 17.9 %copy-start.4 = (bf16[4,256,256]{2,1,0:T(8,128)(2,1)S(1)}, bf16[4,256,256]{2,1,0:T(8,128)(2,1)}, u32[]{:S(2)}) copy-start(bf16[4,256,256]{2,1,0:T(8,128)(2,1)} %diag.3) | copy-start | bytes 1572868
  29.1 10.5 %copy-start.1 = (bf16[128,32,256]{2,1,0:T(8,128)(2,1)S(1)}, bf16[128,32,256]{2,1,0:T(8,128)(2,1)}, u32[]{:S(2)}) copy-start(bf16[128,32,256]{2,1,0:T(8,128)(2,1)} %left.7) | copy-start | bytes 6291460
  29.1 10.5 %copy-start.6 = (bf16[64,1024]{1,0:T(8,128)(2,1)S(1)}, bf16[64,1024]{1,0:T(8,128)(2,1)}, u32[]{:S(2)}) copy-start(bf16[64,1024]{1,0:T(8,128)(2,1)} %vectors.2) | copy-start | bytes 393220
  29.1 2.0 %collective-permute-start.5 = (f32[7,72,256]{2,1,0:T(8,128)S(1)}, f32[7,72,256]{2,1,0:T(8,128)S(1)}, u32[]{:S(2)}, u32[]{:S(2)}) collective-permute-start(f32[7,72,256]{2,1,0:T(8,128)S(1)} %get-tuple-element.23), channel_id=1, source_target_pairs={{0,1},{1,0},{2,3},{3,2},{4,5},{5,4},{6,7},{7,6},{8,9},{9,8},{10,11... | collective-permute-start | bytes 1548296 | tf_op jit(solution)/shard_map/ppermute | solution.py:492
  29.4 10.2 %collective-permute-start.4 = (bf16[5,64,1024]{2,1,0:T(8,128)(2,1)S(1)}, bf16[5,64,1024]{2,1,0:T(8,128)(2,1)S(1)}, u32[]{:S(2)}, u32[]{:S(2)}) collective-permute-start(bf16[5,64,1024]{2,1,0:T(8,128)(2,1)S(1)} %pad_maximum_fusion), channel_id=1, source_target_pairs={{0,1},{1,0},{2,3},{3,2},{4,5},{5,4},{6,7},{7,6},{8,9},{9,8},{10,11... | collective-permute-start | bytes 1966088 | tf_op jit(solution)/shard_map/ppermute | solution.py:492
  31.2 20.4 %collective-permute-start.6 = (f32[4,72,256]{2,1,0:T(8,128)S(1)}, f32[4,72,256]{2,1,0:T(8,128)S(1)}, u32[]{:S(2)}, u32[]{:S(2)}) collective-permute-start(f32[4,72,256]{2,1,0:T(8,128)S(1)} %get-tuple-element.40), channel_id=1, source_target_pairs={{0,2},{1,127},{2,4},{3,1},{4,6},{5,3},{6,8},{7,5},{8,10},{9,7},{10... | collective-permute-start | bytes 884744 | tf_op jit(solution)/shard_map/ppermute | solution.py:495
  36.2 15.3 %collective-permute-start.7 = (f32[4,72,256]{2,1,0:T(8,128)S(1)}, f32[4,72,256]{2,1,0:T(8,128)S(1)}, u32[]{:S(2)}, u32[]{:S(2)}) collective-permute-start(f32[4,72,256]{2,1,0:T(8,128)S(1)} %get-tuple-element.39), channel_id=1, source_target_pairs={{0,4},{1,125},{2,6},{3,127},{4,8},{5,1},{6,10},{7,3},{8,12},{9,5},... | collective-permute-start | bytes 884744 | tf_op jit(solution)/shard_map/ppermute | solution.py:495
  37.2 14.4 %collective-permute-start.8 = (f32[3,72,256]{2,1,0:T(8,128)S(1)}, f32[3,72,256]{2,1,0:T(8,128)S(1)}, u32[]{:S(2)}, u32[]{:S(2)}) collective-permute-start(f32[3,72,256]{2,1,0:T(8,128)S(1)} %get-tuple-element.38), channel_id=1, source_target_pairs={{0,6},{1,123},{2,8},{3,125},{4,10},{5,127},{6,12},{7,1},{8,14},{9,... | collective-permute-start | bytes 663560 | tf_op jit(solution)/shard_map/ppermute | solution.py:495
  51.6 1.8 %collective-permute-start.9 = (f32[5,72,256]{2,1,0:T(8,128)S(1)}, f32[5,72,256]{2,1,0:T(8,128)S(1)}, u32[]{:S(2)}, u32[]{:S(2)}) collective-permute-start(f32[5,72,256]{2,1,0:T(8,128)S(1)} %pad_maximum_fusion.1), channel_id=1, source_target_pairs={{0,1},{1,0},{2,3},{3,2},{4,5},{5,4},{6,7},{7,6},{8,9},{9,8},{10,11... | collective-permute-start | bytes 1105928 | tf_op jit(solution)/shard_map/ppermute | solution.py:492
  60.4 3.1 %collective-permute-start.10 = (bf16[7,128,256]{2,1,0:T(8,128)(2,1)S(1)}, bf16[7,128,256]{2,1,0:T(8,128)(2,1)S(1)}, u32[]{:S(2)}, u32[]{:S(2)}) collective-permute-start(bf16[7,128,256]{2,1,0:T(8,128)(2,1)S(1)} %get-tuple-element.35), channel_id=1, source_target_pairs={{0,1},{1,0},{2,3},{3,2},{4,5},{5,4},{6,7},{7,6},{8,9},{9,8},{10,11... | collective-permute-start | bytes 1376264 | tf_op jit(solution)/shard_map/ppermute | solution.py:492
  63.5 19.3 %collective-permute-start.11 = (bf16[4,128,256]{2,1,0:T(8,128)(2,1)S(1)}, bf16[4,128,256]{2,1,0:T(8,128)(2,1)S(1)}, u32[]{:S(2)}, u32[]{:S(2)}) collective-permute-start(bf16[4,128,256]{2,1,0:T(8,128)(2,1)S(1)} %get-tuple-element.43), channel_id=1, source_target_pairs={{0,2},{1,127},{2,4},{3,1},{4,6},{5,3},{6,8},{7,5},{8,10},{9,7},{10... | collective-permute-start | bytes 786440 | tf_op jit(solution)/shard_map/ppermute | solution.py:495
  68.1 14.7 %collective-permute-start.12 = (bf16[4,128,256]{2,1,0:T(8,128)(2,1)S(1)}, bf16[4,128,256]{2,1,0:T(8,128)(2,1)S(1)}, u32[]{:S(2)}, u32[]{:S(2)}) collective-permute-start(bf16[4,128,256]{2,1,0:T(8,128)(2,1)S(1)} %get-tuple-element.42), channel_id=1, source_target_pairs={{0,4},{1,125},{2,6},{3,127},{4,8},{5,1},{6,10},{7,3},{8,12},{9,5},... | collective-permute-start | bytes 786440 | tf_op jit(solution)/shard_map/ppermute | solution.py:495
  69.2 13.6 %collective-permute-start.13 = (bf16[3,128,256]{2,1,0:T(8,128)(2,1)S(1)}, bf16[3,128,256]{2,1,0:T(8,128)(2,1)S(1)}, u32[]{:S(2)}, u32[]{:S(2)}) collective-permute-start(bf16[3,128,256]{2,1,0:T(8,128)(2,1)S(1)} %get-tuple-element.41), channel_id=1, source_target_pairs={{0,6},{1,123},{2,8},{3,125},{4,10},{5,127},{6,12},{7,1},{8,14},{9,... | collective-permute-start | bytes 589832 | tf_op jit(solution)/shard_map/ppermute | solution.py:495
  82.9 1.7 %collective-permute-start.14 = (bf16[5,128,256]{2,1,0:T(8,128)(2,1)S(1)}, bf16[5,128,256]{2,1,0:T(8,128)(2,1)S(1)}, u32[]{:S(2)}, u32[]{:S(2)}) collective-permute-start(bf16[5,128,256]{2,1,0:T(8,128)(2,1)S(1)} %pad_maximum_fusion.2), channel_id=1, source_target_pairs={{0,1},{1,0},{2,3},{3,2},{4,5},{5,4},{6,7},{7,6},{8,9},{9,8},{10,11... | collective-permute-start | bytes 983048 | tf_op jit(solution)/shard_map/ppermute | solution.py:492
where the time goes:
time: 93.4 us; the launch traced here: 91.5 us
  starting transfers between devices  29.7 us (32%)
  Pallas kernels  26.3 us (28%)
  waiting for transfers between devices  26.1 us (28%)
  local copies, waits for them, and re-layouts  7.5 us (8%)
  other arithmetic  1.08 us (1%)
    ppermute x9, starting transfers between devices, carry(): return lax.ppermute(block, 'rows', carriers(size, k))  25.7 us
    ppermute x9, waiting for transfers between devices, carry(): return lax.ppermute(block, 'rows', carriers(size, k))  19 us
    pallas_call x1, Pallas kernels, k1(): call(back_first, 'transposed_products', message_shapes(RHS + EXTRA, F32)...  7.44 us
    unnamed x24, local copies, waits for them, and re-layouts  7.38 us
    ppermute x6, waiting for transfers between devices, swap(): return lax.ppermute(block, 'rows', [(i, i ^ 1) for i in range(size)])  7.11 us
    pallas_call x1, Pallas kernels, k3(): call(back_second, 'image_and_transposed_products', [shaped((RHS, CL * B),...  6.99 us
    pallas_call x1, Pallas kernels, k4(): call(forward_second, 'second_image', shaped((RHS, CL * B), F32), VMEM, [S...  6.94 us
    pallas_call x1, Pallas kernels, k2(): call(forward_first, 'forward_products', shaped((CL, RHS, B), F32), VMEM,...  4.93 us
  transfers between devices with their start and end apart: 15, of which 7 were waited for; matrix products, arithmetic and copies ran while one was open for 0% of the time, Pallas kernels for 14%

commit v1 on v0

v1 whole, which is shorter than its diff:
```python
import functools

import jax
import jax.numpy as jnp
from jax import lax
from jax.experimental import pallas as pl
from jax.experimental.pallas import tpu as pltpu
from jax.sharding import PartitionSpec as P

RHS, B, K = 64, 256, 32
CL, SLOTS, CHUNK = 4, 128, 16
CHUNKS = SLOTS // CHUNK
GROUP = B // K
HALF = B // 2
PEERS = 12
DEAD = 12
EXTRA = 8
QUAD = 4
VMEM_BYTES = 16 * 2**20
F32, BF16 = jnp.float32, jnp.bfloat16


def dot(x, y):
    return lax.dot_general(x, y, (((1,), (0,)), ((), ())), preferred_element_type=F32)


def dot_t(x, y):
    return lax.dot_general(x, y, (((1,), (1,)), ((), ())), preferred_element_type=F32)


def peer_number(delta, core):
    kappa, other = delta // 2 - 3, delta % 2
    step = kappa * (1 - 2 * core)
    same = int(other != core)
    if step == 0:
        return 11 if same else DEAD
    if step < 0:
        return 2 * (-step - 1) + same
    return 6 + 2 * (step - 1) + same if step < 3 or not same else DEAD


PLAN = (24, 2 * SLOTS)
COUNTS, WANTED = 4, 8


class Blocks:
    def __init__(self, plan, near, left, right, sources=None):
        self.plan, self.near, self.left, self.right = plan, near, left, right
        self.sources = sources

    def copy(self, which, chunk):
        source, sem = self.sources[which]
        place = pl.ds(chunk * CHUNK, CHUNK)
        target = (self.near, self.left, self.right)[which]
        return pltpu.make_async_copy(source.at[place], target.at[place], sem.at[chunk])

    def start(self, near_chunks, far_chunks):
        def far_start(chunk, carry):
            self.copy(1, chunk).start()
            self.copy(2, chunk).start()
            return carry

        def near_start(chunk, carry):
            self.copy(0, chunk).start()
            return carry

        lax.fori_loop(0, far_chunks, far_start, 0)
        lax.fori_loop(0, near_chunks, near_start, 0)

    def far_loop(self, body):
        def arrived(chunk, carry):
            self.copy(1, chunk).wait()
            self.copy(2, chunk).wait()
            return carry

        if self.sources is not None:
            lax.fori_loop(0, self.plan[COUNTS, 1], arrived, 0)

        def step(index, carry):
            for part in range(2):
                first = index * 2 + part
                entries = [self.plan[2, first * GROUP + k] for k in range(GROUP)]
                slots = [entry & 255 for entry in entries]
                left = jnp.concatenate([self.left[slot] for slot in slots], axis=0)
                right = jnp.concatenate([self.right[slot] for slot in slots], axis=0)
                lane = lax.broadcasted_iota(jnp.int32, (1, B), 1) // K
                rows = jnp.zeros((1, B), jnp.int32)
                for k in range(GROUP):
                    rows = jnp.where(lane == k, entries[k] >> 8, rows)
                rows = jnp.broadcast_to(rows, (RHS, B))
                body(left, right, rows, [self.plan[3, 2 * first + half] for half in (0, 1)])
            return carry

        lax.fori_loop(0, self.plan[COUNTS, 2], step, 0)

    def near_loop(self, body):
        def step(chunk, carry):
            if self.sources is not None:
                self.copy(0, chunk).wait()
            for part in range(CHUNK):
                body(chunk * CHUNK + part)
            return carry

        lax.fori_loop(0, self.plan[COUNTS, 0], step, 0)


def back_products(blocks, own, acc):
    plan = blocks.plan

    def far(left, right, rows, partners):
        every = dot_t(own[0:CL].reshape(CL * RHS, B), left)
        coef = jnp.zeros((RHS, B), F32)
        for cluster in range(CL):
            coef = jnp.where(rows == cluster, every[cluster * RHS : (cluster + 1) * RHS], coef)
        coef = coef.astype(BF16)
        for half, partner in enumerate(partners):
            part = slice(half * HALF, (half + 1) * HALF)
            acc[partner] += dot(coef[:, part], right[part])

    def near(slot):
        acc[plan[1, slot]] += dot(own[plan[0, slot]], blocks.near[slot])

    blocks.far_loop(far)
    blocks.near_loop(near)


def forward_products(blocks, fetched, acc):
    plan = blocks.plan

    def far(left, right, rows, partners):
        coef = [
            dot_t(fetched[partner], right[half * HALF : (half + 1) * HALF])
            for half, partner in enumerate(partners)
        ]
        coef = jnp.concatenate(coef, axis=1).astype(BF16).astype(F32)
        spread = [jnp.where(rows == cluster, coef, 0.0).astype(BF16) for cluster in range(CL)]
        acc[0:CL] += dot(jnp.concatenate(spread, axis=0), left).reshape(CL, RHS, B)

    def near(slot):
        acc[plan[0, slot]] += dot_t(fetched[plan[1, slot]], blocks.near[slot])

    blocks.far_loop(far)
    blocks.near_loop(near)


def make_plan(me, lists, few, draft):
    core = me % 2
    base = me - core - 6
    lane = lax.broadcasted_iota(jnp.int32, (1, SLOTS), 1)
    row16 = lax.broadcasted_iota(jnp.int32, (16, SLOTS), 0)
    kinds = []
    for kind in (0, 1):
        rows, cols = lists[2 * kind : 2 * kind + 1, :], lists[2 * kind + 1 : 2 * kind + 2, :]
        live = lane < few[0, kind]
        delta = ((cols >> 2) - base) & 15
        partner = jnp.full((1, SLOTS), DEAD, jnp.int32)
        for value in range(14):
            pair = [peer_number(value, a) for a in (0, 1)]
            partner = jnp.where(delta == value, jnp.where(core == 0, pair[0], pair[1]), partner)
        partner = jnp.where(live, partner, DEAD)
        kinds.append((jnp.where(live, rows & (CL - 1), CL), partner, cols & (CL - 1)))
    (near_row, near_rho, near_part), (far_row, far_rho, far_part) = kinds
    wide = lambda x: jnp.broadcast_to(x, (16, SLOTS))
    hot = row16 == wide(far_rho)
    wanted = jnp.maximum(
        jnp.where(row16 == wide(near_rho), wide(near_part).astype(F32), 0.0),
        jnp.where(hot, wide(far_part).astype(F32), 0.0),
    )
    wanted = jnp.max(wanted, axis=1, keepdims=True)
    hot = jnp.where(hot, 1.0, 0.0)
    square = (SLOTS, SLOTS)
    earlier = lax.broadcasted_iota(jnp.int32, square, 0) < lax.broadcasted_iota(jnp.int32, square, 1)
    rank = dot(hot.astype(BF16), jnp.where(earlier, 1.0, 0.0).astype(BF16)).astype(jnp.int32)
    number = wide(jnp.sum(hot, axis=1, keepdims=True)).astype(jnp.int32)
    padded = ((number + (QUAD - 1)) >> 2) << 2
    place = jnp.full((1, SLOTS), -1, jnp.int32)
    quad_rho = jnp.full((1, SLOTS), DEAD, jnp.int32)
    first = jnp.zeros((1, SLOTS), jnp.int32)
    for rho in range(PEERS):
        place = jnp.where(far_rho == rho, rank[rho : rho + 1] + first, place)
        last = first + padded[rho : rho + 1]
        quad_rho = jnp.where((lane * QUAD >= first) & (lane * QUAD < last), rho, quad_rho)
        first = last
    column = jnp.transpose(jnp.broadcast_to(place.astype(F32), square))
    spots = lax.broadcasted_iota(jnp.int32, square, 1).astype(F32)
    hits = jnp.concatenate([jnp.where(column == spots + shift, 1.0, 0.0).astype(BF16) for shift in (0.0, float(SLOTS))], axis=1)
    codes = jnp.where(row16 == 0, wide(lane), jnp.where(row16 == 1, wide(far_row), 1)).astype(F32).astype(BF16)
    found = dot(codes, hits)
    entry = jnp.where(found[2:3] > 0.5, found[0:1] + 256.0 * found[1:2], 256.0 * CL).astype(jnp.int32)
    draft[0:1, 0:SLOTS] = near_row
    draft[1:2, 0:SLOTS] = near_rho
    draft[2:3, :] = entry
    draft[3:4, 0:SLOTS] = quad_rho
    chunks = [(few[0, kind] + (CHUNK - 1)) // CHUNK for kind in (0, 1)]
    numbers = jnp.where(lane == 0, chunks[0], jnp.where(lane == 1, chunks[1], (first + 15) >> 4))
    draft[COUNTS : COUNTS + 1, 0:SLOTS] = numbers
    draft[WANTED : WANTED + 16, 0:SLOTS] = wide(wanted).astype(jnp.int32)


def place_out(rho):
    if rho == 11:
        return 3, 6
    if rho < 6:
        return 3, rho ^ 1
    k, same = divmod(rho - 6, 2)
    return k, 3 * same


def place_in(rho):
    if rho == 11:
        return 4, 6
    if rho < 6:
        return rho // 2, rho % 2
    return 3, rho - 6


MESSAGE = (4, 4, 3)


def back_first(
    me, near_rows, near_cols, far_rows, far_cols, counts, both, near, left, right,
    m1, m2, m3, give, plan, near_held, left_held, right_held,
    own, acc, lists, few, draft, near_sem, left_sem, right_sem, list_sem,
):
    copies = [pltpu.make_async_copy(counts, few, list_sem.at[4])]
    for index, source in enumerate((near_rows, near_cols, far_rows, far_cols)):
        copies.append(pltpu.make_async_copy(source, lists.at[pl.ds(index, 1)], list_sem.at[index]))
    for copy in copies:
        copy.start()
    for cluster in range(CL):
        own[cluster] = both[0, :, cluster * B : (cluster + 1) * B]
    own[CL] = jnp.zeros((RHS, B), BF16)
    draft[...] = jnp.zeros_like(draft)
    copies[0].wait()
    blocks = Blocks(plan, near_held, left_held, right_held, ((near, near_sem), (left, left_sem), (right, right_sem)))
    blocks.start((few[0, 0] + (CHUNK - 1)) // CHUNK, (few[0, 1] + (CHUNK - 1)) // CHUNK)
    for copy in copies[1:]:
        copy.wait()
    make_plan(me[0], lists, few, draft)
    copy = pltpu.make_async_copy(draft, plan, list_sem.at[5])
    copy.start()
    acc[...] = jnp.zeros_like(acc)
    copy.wait()
    back_products(blocks, own, acc)
    outs = (m1, m2, m3, give)
    for rho in range(PEERS):
        message, index = place_out(rho)
        outs[message][index, 0:RHS] = acc[rho]
        outs[message][index, RHS:] = jnp.full((EXTRA, B), plan[WANTED + rho, 0].astype(F32), F32)


def forward_first(
    plan, both, h1, h2, h3, post, diag, near, left, right,
    out,
    fetched, acc, fetch_sem,
):
    halo = (h1, h2, h3)
    copies = []
    for rho in range(PEERS):
        lanes = pl.ds(pl.multiple_of(plan[WANTED + rho, 0] * B, B), B)
        if rho == 11:
            source = both.at[1, :, lanes]
        elif rho < 6:
            source = halo[rho // 2].at[rho % 2, :, lanes]
        else:
            k, same = divmod(rho - 6, 2)
            source = post.at[2 * k + (1 - same if k < 2 else 0), :, lanes]
        copies.append(pltpu.make_async_copy(source, fetched.at[rho], fetch_sem.at[rho]))
    for copy in copies:
        copy.start()
    fetched[DEAD] = jnp.zeros((RHS, B), BF16)
    acc[CL] = jnp.zeros((RHS, B), F32)
    for cluster in range(CL):
        acc[cluster] = dot_t(both[0, :, cluster * B : (cluster + 1) * B], diag[cluster])
    for copy in copies:
        copy.wait()
    forward_products(Blocks(plan, near, left, right), fetched, acc)
    out[...] = acc[0:CL]


def back_second(
    plan, partial, r1, r2, r3, post, got, near, left, right,
    image, rounded, wanted, m1, m2, m3, give,
    own, acc,
):
    ins = (r1, r2, r3, post, got)
    own[CL] = jnp.zeros((RHS, B), BF16)
    acc[...] = jnp.zeros_like(acc)
    places = [place_in(rho) for rho in range(PEERS)]
    for rho, (message, index) in enumerate(places):
        wanted[rho] = ins[message][index, RHS:]
    for cluster in range(CL):
        total = partial[cluster]
        for message, index in places:
            mine = ins[message][index, RHS : RHS + 1] == float(cluster)
            total += jnp.where(jnp.broadcast_to(mine, (RHS, B)), ins[message][index, 0:RHS], 0.0)
        image[:, cluster * B : (cluster + 1) * B] = total
        own[cluster] = total.astype(BF16)
        rounded[cluster] = total.astype(BF16)
    back_products(Blocks(plan, near, left, right), own, acc)
    outs = (m1, m2, m3, give)
    for rho in range(PEERS):
        message, index = place_out(rho)
        outs[message][index, 0:RHS] = acc[rho].astype(BF16)
        pick = jnp.broadcast_to(wanted[rho, 0:1], (RHS, B))
        chosen = jnp.zeros((RHS, B), F32)
        for cluster in range(CL):
            chosen = jnp.where(pick == float(cluster), own[cluster].astype(F32), chosen)
        outs[message][index, RHS:] = chosen.astype(BF16)


def forward_second(
    plan, own, wanted, r1, r2, r3, post, got, diag, near, left, right,
    image,
    fetched, acc,
):
    ins = (r1, r2, r3, post, got)
    fetched[DEAD] = jnp.zeros((RHS, B), BF16)
    acc[CL] = jnp.zeros((RHS, B), F32)
    places = [place_in(rho) for rho in range(PEERS)]
    for rho, (message, index) in enumerate(places):
        fetched[rho] = ins[message][index, RHS:]
    for cluster in range(CL):
        total = dot_t(own[cluster], diag[cluster])
        for rho, (message, index) in enumerate(places):
            mine = wanted[rho, 0:1] == float(cluster)
            total += jnp.where(jnp.broadcast_to(mine, (RHS, B)), ins[message][index, 0:RHS].astype(F32), 0.0)
        acc[cluster] = total
    forward_products(Blocks(plan, near, left, right), fetched, acc)
    for cluster in range(CL):
        image[:, cluster * B : (cluster + 1) * B] = acc[cluster]


SMEM = pl.BlockSpec(memory_space=pltpu.SMEM)
VMEM = pl.BlockSpec(memory_space=pltpu.VMEM)
ANY = pl.BlockSpec(memory_space=pl.ANY)
HBM = pl.BlockSpec(memory_space=pltpu.HBM)


def call(kernel, name, outs, out_specs, in_specs, scratch):
    return pl.pallas_call(
        kernel,
        name=name,
        out_shape=outs,
        in_specs=in_specs,
        out_specs=out_specs,
        scratch_shapes=scratch,
        compiler_params=pltpu.CompilerParams(vmem_limit_bytes=VMEM_BYTES),
        cost_estimate=pl.CostEstimate(flops=2 * 10**9, bytes_accessed=22 * 10**6, transcendentals=0),
    )


def shaped(shape, dtype):
    return jax.ShapeDtypeStruct(shape, dtype)


def message_shapes(rows, dtype):
    return [shaped((n, rows, B), dtype) for n in MESSAGE + (7,)]


def k1(*args):
    held = [pltpu.VMEM(shape, BF16) for shape in ((SLOTS, B, B), (SLOTS, K, B), (SLOTS, K, B))]
    return call(
        back_first, "transposed_products",
        message_shapes(RHS + EXTRA, F32) + [shaped(PLAN, jnp.int32)] + held,
        [VMEM] * 4 + [SMEM] + [VMEM] * 3,
        [SMEM] + [HBM] * 5 + [VMEM] + [HBM] * 3,
        [
            pltpu.VMEM((CL + 1, RHS, B), BF16),
            pltpu.VMEM((PEERS + 1, RHS, B), F32),
            pltpu.VMEM((8, SLOTS), jnp.int32),
            pltpu.SMEM((1, 2), jnp.int32),
            pltpu.VMEM(PLAN, jnp.int32),
        ]
        + [pltpu.SemaphoreType.DMA((n,)) for n in (CHUNKS, CHUNKS, CHUNKS, 6)],
    )(*args)


def k2(*args):
    return call(
        forward_first, "forward_products",
        shaped((CL, RHS, B), F32), VMEM,
        [SMEM] + [VMEM] + [ANY] * 4 + [VMEM] * 4,
        [
            pltpu.VMEM((PEERS + 1, RHS, B), BF16),
            pltpu.VMEM((CL + 1, RHS, B), F32),
            pltpu.SemaphoreType.DMA((PEERS,)),
        ],
    )(*args)


def k3(*args):
    return call(
        back_second, "image_and_transposed_products",
        [
            shaped((RHS, CL * B), F32),
            shaped((CL, RHS, B), BF16),
            shaped((PEERS, EXTRA, B), F32),
        ]
        + message_shapes(2 * RHS, BF16),
        [VMEM] * 7,
        [SMEM] + [VMEM] * 9,
        [pltpu.VMEM((CL + 1, RHS, B), BF16), pltpu.VMEM((PEERS + 1, RHS, B), F32)],
    )(*args)


def k4(*args):
    return call(
        forward_second, "second_image",
        shaped((RHS, CL * B), F32), VMEM,
        [SMEM] + [VMEM] * 11,
        [pltpu.VMEM((PEERS + 1, RHS, B), BF16), pltpu.VMEM((CL + 1, RHS, B), F32)],
    )(*args)


def carriers(size, k):
    pairs = []
    for chip in range(size // 2):
        for core in range(2):
            step = k if core == 0 else -k
            pairs.append((2 * chip + core, (2 * (chip + step) + core) % size))
    return pairs


def per_device(
    vectors, diag_blocks, near_blocks, near_rows, near_cols, far_left, far_right, far_rows, far_cols, counts
):
    size = lax.axis_size("rows")
    me = lax.axis_index("rows").reshape(1)

    def swap(block):
        return lax.ppermute(block, "rows", [(i, i ^ 1) for i in range(size)])

    def carry(block, k):
        return lax.ppermute(block, "rows", carriers(size, k))

    def exchange(m1, m2, m3, give):
        got = swap(give)
        messages = []
        for k, message in enumerate((m1, m2, m3)):
            messages.append(lax.dynamic_update_slice(message, got[2 * k : 2 * k + 2], (1, 0, 0)))
        return [carry(message, k + 1) for k, message in enumerate(messages)] + [got, messages]

    def passed_on(r1, r2, r3):
        return swap(jnp.concatenate([r1[2:4], r2[2:4], r3[2:3]]))

    def in_hbm(x):
        return pltpu.with_memory_space_constraint(x, pltpu.HBM)

    lists = [in_hbm(x.reshape(1, SLOTS)) for x in (near_rows, near_cols, far_rows, far_cols)]
    sib = swap(vectors)
    both = jnp.stack([vectors, sib])
    halo = [carry(both, k) for k in (1, 2, 3)]
    m1, m2, m3, give, plan, *held = k1(
        me, *lists, in_hbm(counts), both, in_hbm(near_blocks), in_hbm(far_left), in_hbm(far_right)
    )
    r1, r2, r3, got, messages = exchange(m1, m2, m3, give)
    halo_post = swap(jnp.concatenate([halo[0], halo[1], halo[2][1:]]))
    halo_post, messages = lax.optimization_barrier((halo_post, messages))
    partial = k2(plan, both, *halo, halo_post, diag_blocks, *held)
    partial, r1, r2, r3 = lax.optimization_barrier((partial, r1, r2, r3))
    post = passed_on(r1, r2, r3)
    first_image, rounded, wanted, m1, m2, m3, give = k3(plan, partial, r1, r2, r3, post, got, *held)
    r1, r2, r3, got, messages = exchange(m1, m2, m3, give)
    post = passed_on(r1, r2, r3)
    second_image = k4(plan, rounded, wanted, r1, r2, r3, post, got, diag_blocks, *held)
    return first_image, second_image


def solution(mesh):
    return jax.shard_map(
        per_device,
        mesh=mesh,
        in_specs=(
            P(None, "rows"),
            P("rows", None, None),
            P("rows", None, None),
            P("rows"),
            P("rows"),
            P("rows", None, None),
            P("rows", None, None),
            P("rows"),
            P("rows"),
            P("rows", None),
        ),
        out_specs=(P(None, "rows"), P(None, "rows")),
        check_vma=False,
    )
```

time: 93.4 us -> 85.1 us (0.911); the launches traced: 91.5 us -> 86.5 us
  local copies, waits for them, and re-layouts: 7.5 us -> 0.13 us
  starting transfers between devices: 29.7 us -> 22.4 us
  Pallas kernels: 26.3 us -> 32.9 us
  waiting for transfers between devices: 26.1 us -> 29.1 us
    unnamed x24 -> x2, local copies, waits for them, and re-layouts: 7.38 us -> 0.01 us
    ppermute x9, starting transfers between devices: 25.7 us -> 19 us  [carry(): return lax.ppermute(block, 'rows', carriers(size, k))]
    ppermute x9, waiting for transfers between devices: 19 us -> 23.2 us  [carry(): return lax.ppermute(block, 'rows', carriers(size, k))]
    pallas_call x1, Pallas kernels: 4.93 us -> 7.83 us  [k2(): call(forward_first, 'forward_products', shaped((CL, RHS, B), F32), VMEM,...]
    pallas_call x1, Pallas kernels: 6.94 us -> 8.58 us  [k4(): call(forward_second, 'second_image', shaped((RHS, CL * B), F32), VMEM, [S...]
    pallas_call x1, Pallas kernels: 7.44 us -> 8.95 us  [k1(): call(back_first, 'transposed_products', message_shapes(RHS + EXTRA, F32)...]
    ppermute x6, waiting for transfers between devices: 7.11 us -> 5.94 us  [swap(): return lax.ppermute(block, 'rows', [(i, i ^ 1) for i in range(size)])]
  transfers between devices with their start and end apart: 15 -> 15, of which waited for: 7 -> 7; matrix products, arithmetic and copies ran while one was open for 0% -> 0% of each run, Pallas kernels for 14% -> 19%
where the time goes in v1:
time: 85.1 us; the launch traced here: 86.5 us
  Pallas kernels  32.9 us (39%)
  waiting for transfers between devices  29.1 us (34%)
  starting transfers between devices  22.4 us (26%)
  other arithmetic  1.08 us (1%)
    ppermute x9, waiting for transfers between devices, carry(): return lax.ppermute(block, 'rows', carriers(size, k))  23.2 us
    ppermute x9, starting transfers between devices, carry(): return lax.ppermute(block, 'rows', carriers(size, k))  19 us
    pallas_call x1, Pallas kernels, k1(): call(back_first, 'transposed_products', message_shapes(RHS + EXTRA, F32)...  8.95 us
    pallas_call x1, Pallas kernels, k4(): call(forward_second, 'second_image', shaped((RHS, CL * B), F32), VMEM, [S...  8.58 us
    pallas_call x1, Pallas kernels, k2(): call(forward_first, 'forward_products', shaped((CL, RHS, B), F32), VMEM,...  7.83 us
    pallas_call x1, Pallas kernels, k3(): call(back_second, 'image_and_transposed_products', [shaped((RHS, CL * B),...  7.56 us
    ppermute x6, waiting for transfers between devices, swap(): return lax.ppermute(block, 'rows', [(i, i ^ 1) for i in range(size)])  5.94 us
    ppermute x6, starting transfers between devices, swap(): return lax.ppermute(block, 'rows', [(i, i ^ 1) for i in range(size)])  3.45 us
  transfers between devices with their start and end apart: 15, of which 7 were waited for; matrix products, arithmetic and copies ran while one was open for 0% of the time, Pallas kernels for 19%

profile of v1, /device:TPU:1, one launch (start us, length us, event | category | flops | bytes accessed | tf_op | source)
XLA Modules:
  0.0 86.5 jit_solution(11244802816782551293)
XLA Ops:
  0.6 1.5 %collective-permute-start = (bf16[64,1024]{1,0:T(8,128)(2,1)}, bf16[64,1024]{1,0:T(8,128)(2,1)S(1)}, u32[]{:S(2)}, u32[]{:S(2)}) collective-permute-start(bf16[64,1024]{1,0:T(8,128)(2,1)} %param.10), channel_id=1, source_target_pairs={{0,1},{1,0},{2,3},{3,2},{4,5},{5,4},{6,7},{7,6},{8,9},{9,8},{10,11... | collective-permute-start | bytes 393224 | tf_op jit(solution)/shard_map/ppermute | solution.py:432
  2.1 1.2 %collective-permute-done = bf16[64,1024]{1,0:T(8,128)(2,1)S(1)} collective-permute-done((bf16[64,1024]{1,0:T(8,128)(2,1)}, bf16[64,1024]{1,0:T(8,128)(2,1)S(1)}, u32[]{:S(2)}, u32[]{:S(2)}) %collective-permute-start) | collective-permute-done | bytes 131104 | tf_op jit(solution)/shard_map/ppermute | solution.py:432
  3.3 0.9 %pad_maximum_fusion.3.both = bf16[2,64,1024]{2,1,0:T(8,128)(2,1)S(1)} fusion(bf16[1,64,1024]{2,1,0:T(8,128)(2,1)S(1)} %bitcast.8, bf16[1,64,1024]{2,1,0:T(8,128)(2,1)} %bitcast.7), kind=kLoop, calls=%fused_computation.3 | loop fusion | flops 131072 | bytes 524288 | tf_op jit(solution)/shard_map/stack | solution.py:452
  4.3 6.4 %collective-permute-start.3 = (bf16[2,64,1024]{2,1,0:T(8,128)(2,1)S(1)}, bf16[2,64,1024]{2,1,0:T(8,128)(2,1)S(1)}, u32[]{:S(2)}, u32[]{:S(2)}) collective-permute-start(bf16[2,64,1024]{2,1,0:T(8,128)(2,1)S(1)} %pad_maximum_fusion.3.both), channel_id=1, source_target_pairs={{0,6},{1,123},{2,8},{3,125},{4,10},{5,127},{6,12},{7,1},{8,14},{9,... | collective-permute-start | bytes 786440 | tf_op jit(solution)/shard_map/ppermute | solution.py:435
  10.7 2.2 %collective-permute-start.1 = (bf16[2,64,1024]{2,1,0:T(8,128)(2,1)S(1)}, bf16[2,64,1024]{2,1,0:T(8,128)(2,1)S(1)}, u32[]{:S(2)}, u32[]{:S(2)}) collective-permute-start(bf16[2,64,1024]{2,1,0:T(8,128)(2,1)S(1)} %pad_maximum_fusion.3.both), channel_id=1, source_target_pairs={{0,2},{1,127},{2,4},{3,1},{4,6},{5,3},{6,8},{7,5},{8,10},{9,7},{10... | collective-permute-start | bytes 786440 | tf_op jit(solution)/shard_map/ppermute | solution.py:435
  12.9 1.4 %collective-permute-start.2 = (bf16[2,64,1024]{2,1,0:T(8,128)(2,1)S(1)}, bf16[2,64,1024]{2,1,0:T(8,128)(2,1)S(1)}, u32[]{:S(2)}, u32[]{:S(2)}) collective-permute-start(bf16[2,64,1024]{2,1,0:T(8,128)(2,1)S(1)} %pad_maximum_fusion.3.both), channel_id=1, source_target_pairs={{0,4},{1,125},{2,6},{3,127},{4,8},{5,1},{6,10},{7,3},{8,12},{9,5},... | collective-permute-start | bytes 786440 | tf_op jit(solution)/shard_map/ppermute | solution.py:435
  14.3 9.0 %transposed_products.1 = (f32[4,72,256]{2,1,0:T(8,128)S(1)}, f32[4,72,256]{2,1,0:T(8,128)S(1)}, f32[3,72,256]{2,1,0:T(8,128)S(1)}, f32[7,72,256]{2,1,0:T(8,128)S...) custom-call(s32[1]{0:T(128)} %bitcast.me, ...), custom_call_target="tpu_custom_call" | custom-call | flops 2000000000 | bytes 22000000 | tf_op jit(solution)/shard_map/transposed_products/pallas_call | solution.py:363
  23.3 0.0 copy-start
  23.3 0.1 collective-permute-start.5
  23.4 0.0 collective-permute-done.3.h3
  23.4 0.0 collective-permute-done.1.h1
  23.4 1.8 %collective-permute-done.2.h2 = bf16[2,64,1024]{2,1,0:T(8,128)(2,1)S(1)} collective-permute-done((bf16[2,64,1024]{2,1,0:T(8,128)(2,1)S(1)}, bf16[2,64,1024]{2,1,0:T(8,128)(2,1)S(1)}, u32[]{:S(2)}, u32[]{:S(2)}) %collective-permute-start.2) | collective-permute-done | bytes 262176 | tf_op jit(solution)/shard_map/ppermute | solution.py:435
  25.2 0.1 pad_maximum_fusion
  25.3 0.1 collective-permute-start.4
  25.4 0.0 collective-permute-done.5.got
  25.5 4.8 %collective-permute-start.6 = (f32[4,72,256]{2,1,0:T(8,128)S(1)}, f32[4,72,256]{2,1,0:T(8,128)S(1)}, u32[]{:S(2)}, u32[]{:S(2)}) collective-permute-start(f32[4,72,256]{2,1,0:T(8,128)S(1)} %get-tuple-element.44), channel_id=1, source_target_pairs={{0,2},{1,127},{2,4},{3,1},{4,6},{5,3},{6,8},{7,5},{8,10},{9,7},{10... | collective-permute-start | bytes 884744 | tf_op jit(solution)/shard_map/ppermute | solution.py:435
  30.3 0.0 collective-permute-start.7
  30.3 0.4 collective-permute-start.8
  30.7 0.0 collective-permute-done.4.post
  30.7 0.0 copy-done
  30.7 7.8 %forward_products.1.partial = f32[4,64,256]{2,1,0:T(8,128)S(1)} custom-call(s32[24,256]{1,0:T(8,128)S(1)} %get-tuple-element.22.plan, bf16[2,64,1024]{2,1,0:T(8,128)(2,1)S(1)} %pad_maximum_fusion.3.both, bf16[2,64,1024]{2,1,0:T(8,128)(2,1)S(1)} %collective-permute-done.1.h1, bf16[2,64,1024]{2,1,0:T(8,128)(2,1)S(1)} %collective-permute-done.2.h2, ...), custom_call_target="tpu_custom_call" | custom-call | flops 2000000000 | bytes 22000000 | tf_op jit(solution)/shard_map/forward_products/pallas_call | solution.py:380
  38.6 7.2 %collective-permute-done.8.r3 = f32[3,72,256]{2,1,0:T(8,128)S(1)} collective-permute-done((f32[3,72,256]{2,1,0:T(8,128)S(1)}, f32[3,72,256]{2,1,0:T(8,128)S(1)}, u32[]{:S(2)}, u32[]{:S(2)}) %collective-permute-start.8) | collective-permute-done | bytes 221216 | tf_op jit(solution)/shard_map/ppermute | solution.py:435
  45.8 0.0 collective-permute-done.6.r1
  45.8 0.0 collective-permute-done.7.r2
  45.9 0.1 collective-permute-start.9
  46.0 1.7 %collective-permute-done.9.post = f32[5,72,256]{2,1,0:T(8,128)S(1)} collective-permute-done((f32[5,72,256]{2,1,0:T(8,128)S(1)}, f32[5,72,256]{2,1,0:T(8,128)S(1)}, u32[]{:S(2)}, u32[]{:S(2)}) %collective-permute-start.9) | collective-permute-done | bytes 368672 | tf_op jit(solution)/shard_map/ppermute | solution.py:432
  47.6 7.6 %image_and_transposed_products.1 = (f32[64,1024]{1,0:T(8,128)}, bf16[4,64,256]{2,1,0:T(8,128)(2,1)S(1)}, f32[12,8,256]{2,1,0:T(8,128)S(1)}, bf16[4,128,256]{2,1,...) custom-call(s32[24,256]{1,0:T(8,128)S(1)} %get-tuple-element.22.plan, ...), custom_call_target="tpu_custom_call" | custom-call | flops 2000000000 | bytes 22000000 | tf_op jit(solution)/shard_map/image_and_transposed_products/pallas_call | solution.py:393
  55.2 1.6 %collective-permute-start.10 = (bf16[7,128,256]{2,1,0:T(8,128)(2,1)S(1)}, bf16[7,128,256]{2,1,0:T(8,128)(2,1)S(1)}, u32[]{:S(2)}, u32[]{:S(2)}) collective-permute-start(bf16[7,128,256]{2,1,0:T(8,128)(2,1)S(1)} %get-tuple-element.39), channel_id=1, source_target_pairs={{0,1},{1,0},{2,3},{3,2},{4,5},{5,4},{6,7},{7,6},{8,9},{9,8},{10,11... | collective-permute-start | bytes 1376264 | tf_op jit(solution)/shard_map/ppermute | solution.py:432
  56.8 1.4 %collective-permute-done.10.got = bf16[7,128,256]{2,1,0:T(8,128)(2,1)S(1)} collective-permute-done((bf16[7,128,256]{2,1,0:T(8,128)(2,1)S(1)}, bf16[7,128,256]{2,1,0:T(8,128)(2,1)S(1)}, u32[]{:S(2)}, u32[]{:S(2)}) %collective-permute-start.10) | collective-permute-done | bytes 458784 | tf_op jit(solution)/shard_map/ppermute | solution.py:432
  58.3 3.1 %collective-permute-start.11 = (bf16[4,128,256]{2,1,0:T(8,128)(2,1)S(1)}, bf16[4,128,256]{2,1,0:T(8,128)(2,1)S(1)}, u32[]{:S(2)}, u32[]{:S(2)}) collective-permute-start(bf16[4,128,256]{2,1,0:T(8,128)(2,1)S(1)} %get-tuple-element.47), channel_id=1, source_target_pairs={{0,2},{1,127},{2,4},{3,1},{4,6},{5,3},{6,8},{7,5},{8,10},{9,7},{10... | collective-permute-start | bytes 786440 | tf_op jit(solution)/shard_map/ppermute | solution.py:435
  61.4 0.5 collective-permute-start.12
  61.9 0.0 collective-permute-start.13
  61.9 14.1 %collective-permute-done.13.r3 = bf16[3,128,256]{2,1,0:T(8,128)(2,1)S(1)} collective-permute-done((bf16[3,128,256]{2,1,0:T(8,128)(2,1)S(1)}, bf16[3,128,256]{2,1,0:T(8,128)(2,1)S(1)}, u32[]{:S(2)}, u32[]{:S(2)}) %collective-permute-start.13) | collective-permute-done | bytes 196640 | tf_op jit(solution)/shard_map/ppermute | solution.py:435
  76.1 0.0 collective-permute-done.11.r1
  76.1 0.0 collective-permute-done.12.r2
  76.2 0.1 collective-permute-start.14
  76.3 1.6 %collective-permute-done.14.post = bf16[5,128,256]{2,1,0:T(8,128)(2,1)S(1)} collective-permute-done((bf16[5,128,256]{2,1,0:T(8,128)(2,1)S(1)}, bf16[5,128,256]{2,1,0:T(8,128)(2,1)S(1)}, u32[]{:S(2)}, u32[]{:S(2)}) %collective-permute-start.14) | collective-permute-done | bytes 327712 | tf_op jit(solution)/shard_map/ppermute | solution.py:432
  77.9 8.6 %second_image.1 = f32[64,1024]{1,0:T(8,128)} custom-call(s32[24,256]{1,0:T(8,128)S(1)} %get-tuple-element.22.plan, bf16[4,64,256]{2,1,0:T(8,128)(2,1)S(1)} %get-tuple-element.36.own, f32[12,8,256]{2,1,0:T(8,128)S(1)} %get-tuple-element.37.wanted, bf16[4,128,256]{2,1,0:T(8,128)(2,1)S(1)} %collective-permute-done.11.r1, ...), custom_call_target="tpu_custom_call" | custom-call | flops 2000000000 | bytes 22000000 | tf_op jit(solution)/shard_map/second_image/pallas_call | solution.py:408
  (11 shorter events, 0.2 us)
Async XLA Ops:
  0.6 2.7 %collective-permute-start = (bf16[64,1024]{1,0:T(8,128)(2,1)}, bf16[64,1024]{1,0:T(8,128)(2,1)S(1)}, u32[]{:S(2)}, u32[]{:S(2)}) collective-permute-start(bf16[64,1024]{1,0:T(8,128)(2,1)} %param.10), channel_id=1, source_target_pairs={{0,1},{1,0},{2,3},{3,2},{4,5},{5,4},{6,7},{7,6},{8,9},{9,8},{10,11... | collective-permute-start | bytes 393224 | tf_op jit(solution)/shard_map/ppermute | solution.py:432
  4.3 19.1 %collective-permute-start.3 = (bf16[2,64,1024]{2,1,0:T(8,128)(2,1)S(1)}, bf16[2,64,1024]{2,1,0:T(8,128)(2,1)S(1)}, u32[]{:S(2)}, u32[]{:S(2)}) collective-permute-start(bf16[2,64,1024]{2,1,0:T(8,128)(2,1)S(1)} %pad_maximum_fusion.3.both), channel_id=1, source_target_pairs={{0,6},{1,123},{2,8},{3,125},{4,10},{5,127},{6,12},{7,1},{8,14},{9,... | collective-permute-start | bytes 786440 | tf_op jit(solution)/shard_map/ppermute | solution.py:435
  10.7 12.7 %collective-permute-start.1 = (bf16[2,64,1024]{2,1,0:T(8,128)(2,1)S(1)}, bf16[2,64,1024]{2,1,0:T(8,128)(2,1)S(1)}, u32[]{:S(2)}, u32[]{:S(2)}) collective-permute-start(bf16[2,64,1024]{2,1,0:T(8,128)(2,1)S(1)} %pad_maximum_fusion.3.both), channel_id=1, source_target_pairs={{0,2},{1,127},{2,4},{3,1},{4,6},{5,3},{6,8},{7,5},{8,10},{9,7},{10... | collective-permute-start | bytes 786440 | tf_op jit(solution)/shard_map/ppermute | solution.py:435
  12.9 12.3 %collective-permute-start.2 = (bf16[2,64,1024]{2,1,0:T(8,128)(2,1)S(1)}, bf16[2,64,1024]{2,1,0:T(8,128)(2,1)S(1)}, u32[]{:S(2)}, u32[]{:S(2)}) collective-permute-start(bf16[2,64,1024]{2,1,0:T(8,128)(2,1)S(1)} %pad_maximum_fusion.3.both), channel_id=1, source_target_pairs={{0,4},{1,125},{2,6},{3,127},{4,8},{5,1},{6,10},{7,3},{8,12},{9,5},... | collective-permute-start | bytes 786440 | tf_op jit(solution)/shard_map/ppermute | solution.py:435
  23.3 7.5 %copy-start = (bf16[4,256,256]{2,1,0:T(8,128)(2,1)S(1)}, bf16[4,256,256]{2,1,0:T(8,128)(2,1)}, u32[]{:S(2)}) copy-start(bf16[4,256,256]{2,1,0:T(8,128)(2,1)} %diag.3) | copy-start | bytes 1572868
  23.3 2.1 %collective-permute-start.5 = (f32[7,72,256]{2,1,0:T(8,128)S(1)}, f32[7,72,256]{2,1,0:T(8,128)S(1)}, u32[]{:S(2)}, u32[]{:S(2)}) collective-permute-start(f32[7,72,256]{2,1,0:T(8,128)S(1)} %get-tuple-element.24), channel_id=1, source_target_pairs={{0,1},{1,0},{2,3},{3,2},{4,5},{5,4},{6,7},{7,6},{8,9},{9,8},{10,11... | collective-permute-start | bytes 1548296 | tf_op jit(solution)/shard_map/ppermute | solution.py:432
  25.3 5.4 %collective-permute-start.4 = (bf16[5,64,1024]{2,1,0:T(8,128)(2,1)S(1)}, bf16[5,64,1024]{2,1,0:T(8,128)(2,1)S(1)}, u32[]{:S(2)}, u32[]{:S(2)}) collective-permute-start(bf16[5,64,1024]{2,1,0:T(8,128)(2,1)S(1)} %pad_maximum_fusion), channel_id=1, source_target_pairs={{0,1},{1,0},{2,3},{3,2},{4,5},{5,4},{6,7},{7,6},{8,9},{9,8},{10,11... | collective-permute-start | bytes 1966088 | tf_op jit(solution)/shard_map/ppermute | solution.py:432
  25.5 20.3 %collective-permute-start.6 = (f32[4,72,256]{2,1,0:T(8,128)S(1)}, f32[4,72,256]{2,1,0:T(8,128)S(1)}, u32[]{:S(2)}, u32[]{:S(2)}) collective-permute-start(f32[4,72,256]{2,1,0:T(8,128)S(1)} %get-tuple-element.44), channel_id=1, source_target_pairs={{0,2},{1,127},{2,4},{3,1},{4,6},{5,3},{6,8},{7,5},{8,10},{9,7},{10... | collective-permute-start | bytes 884744 | tf_op jit(solution)/shard_map/ppermute | solution.py:435
  30.3 15.5 %collective-permute-start.7 = (f32[4,72,256]{2,1,0:T(8,128)S(1)}, f32[4,72,256]{2,1,0:T(8,128)S(1)}, u32[]{:S(2)}, u32[]{:S(2)}) collective-permute-start(f32[4,72,256]{2,1,0:T(8,128)S(1)} %get-tuple-element.43), channel_id=1, source_target_pairs={{0,4},{1,125},{2,6},{3,127},{4,8},{5,1},{6,10},{7,3},{8,12},{9,5},... | collective-permute-start | bytes 884744 | tf_op jit(solution)/shard_map/ppermute | solution.py:435
  30.3 15.5 %collective-permute-start.8 = (f32[3,72,256]{2,1,0:T(8,128)S(1)}, f32[3,72,256]{2,1,0:T(8,128)S(1)}, u32[]{:S(2)}, u32[]{:S(2)}) collective-permute-start(f32[3,72,256]{2,1,0:T(8,128)S(1)} %get-tuple-element.42), channel_id=1, source_target_pairs={{0,6},{1,123},{2,8},{3,125},{4,10},{5,127},{6,12},{7,1},{8,14},{9,... | collective-permute-start | bytes 663560 | tf_op jit(solution)/shard_map/ppermute | solution.py:435
  45.9 1.8 %collective-permute-start.9 = (f32[5,72,256]{2,1,0:T(8,128)S(1)}, f32[5,72,256]{2,1,0:T(8,128)S(1)}, u32[]{:S(2)}, u32[]{:S(2)}) collective-permute-start(f32[5,72,256]{2,1,0:T(8,128)S(1)} %pad_maximum_fusion.1), channel_id=1, source_target_pairs={{0,1},{1,0},{2,3},{3,2},{4,5},{5,4},{6,7},{7,6},{8,9},{9,8},{10,11... | collective-permute-start | bytes 1105928 | tf_op jit(solution)/shard_map/ppermute | solution.py:432
  55.2 3.0 %collective-permute-start.10 = (bf16[7,128,256]{2,1,0:T(8,128)(2,1)S(1)}, bf16[7,128,256]{2,1,0:T(8,128)(2,1)S(1)}, u32[]{:S(2)}, u32[]{:S(2)}) collective-permute-start(bf16[7,128,256]{2,1,0:T(8,128)(2,1)S(1)} %get-tuple-element.39), channel_id=1, source_target_pairs={{0,1},{1,0},{2,3},{3,2},{4,5},{5,4},{6,7},{7,6},{8,9},{9,8},{10,11... | collective-permute-start | bytes 1376264 | tf_op jit(solution)/shard_map/ppermute | solution.py:432
  58.3 17.8 %collective-permute-start.11 = (bf16[4,128,256]{2,1,0:T(8,128)(2,1)S(1)}, bf16[4,128,256]{2,1,0:T(8,128)(2,1)S(1)}, u32[]{:S(2)}, u32[]{:S(2)}) collective-permute-start(bf16[4,128,256]{2,1,0:T(8,128)(2,1)S(1)} %get-tuple-element.47), channel_id=1, source_target_pairs={{0,2},{1,127},{2,4},{3,1},{4,6},{5,3},{6,8},{7,5},{8,10},{9,7},{10... | collective-permute-start | bytes 786440 | tf_op jit(solution)/shard_map/ppermute | solution.py:435
  61.4 14.7 %collective-permute-start.12 = (bf16[4,128,256]{2,1,0:T(8,128)(2,1)S(1)}, bf16[4,128,256]{2,1,0:T(8,128)(2,1)S(1)}, u32[]{:S(2)}, u32[]{:S(2)}) collective-permute-start(bf16[4,128,256]{2,1,0:T(8,128)(2,1)S(1)} %get-tuple-element.46), channel_id=1, source_target_pairs={{0,4},{1,125},{2,6},{3,127},{4,8},{5,1},{6,10},{7,3},{8,12},{9,5},... | collective-permute-start | bytes 786440 | tf_op jit(solution)/shard_map/ppermute | solution.py:435
  61.9 14.1 %collective-permute-start.13 = (bf16[3,128,256]{2,1,0:T(8,128)(2,1)S(1)}, bf16[3,128,256]{2,1,0:T(8,128)(2,1)S(1)}, u32[]{:S(2)}, u32[]{:S(2)}) collective-permute-start(bf16[3,128,256]{2,1,0:T(8,128)(2,1)S(1)} %get-tuple-element.45), channel_id=1, source_target_pairs={{0,6},{1,123},{2,8},{3,125},{4,10},{5,127},{6,12},{7,1},{8,14},{9,... | collective-permute-start | bytes 589832 | tf_op jit(solution)/shard_map/ppermute | solution.py:435
  76.2 1.7 %collective-permute-start.14 = (bf16[5,128,256]{2,1,0:T(8,128)(2,1)S(1)}, bf16[5,128,256]{2,1,0:T(8,128)(2,1)S(1)}, u32[]{:S(2)}, u32[]{:S(2)}) collective-permute-start(bf16[5,128,256]{2,1,0:T(8,128)(2,1)S(1)} %pad_maximum_fusion.2), channel_id=1, source_target_pairs={{0,1},{1,0},{2,3},{3,2},{4,5},{5,4},{6,7},{7,6},{8,9},{9,8},{10,11... | collective-permute-start | bytes 983048 | tf_op jit(solution)/shard_map/ppermute | solution.py:432

commit v2 on v1

--- a/solution.py
+++ b/solution.py
@@ -39,8 +39,10 @@
     return 6 + 2 * (step - 1) + same if step < 3 or not same else DEAD
 
 
-PLAN = (24, 2 * SLOTS)
-COUNTS, WANTED = 4, 8
+PLAN = (4, 2 * SLOTS)
+COUNTS, WANTED = 64, 80
+STEP = 32
+GROUPS = 4
 
 
 class Blocks:
@@ -54,7 +56,11 @@
         target = (self.near, self.left, self.right)[which]
         return pltpu.make_async_copy(source.at[place], target.at[place], sem.at[chunk])
 
-    def start(self, near_chunks, far_chunks):
+    def start(self):
+        for which in (1, 2, 0):
+            self.copy(which, 0).start()
+
+    def start_rest(self, near_chunks, far_chunks):
         def far_start(chunk, carry):
             self.copy(1, chunk).start()
             self.copy(2, chunk).start()
@@ -64,8 +70,8 @@
             self.copy(0, chunk).start()
             return carry
 
-        lax.fori_loop(0, far_chunks, far_start, 0)
-        lax.fori_loop(0, near_chunks, near_start, 0)
+        lax.fori_loop(1, far_chunks, far_start, 0)
+        lax.fori_loop(1, near_chunks, near_start, 0)
 
     def far_loop(self, body):
         def arrived(chunk, carry):
@@ -74,12 +80,13 @@
             return carry
 
         if self.sources is not None:
-            lax.fori_loop(0, self.plan[COUNTS, 1], arrived, 0)
+            lax.fori_loop(0, self.plan[2, COUNTS + 1], arrived, 0)
 
         def step(index, carry):
-            for part in range(2):
-                first = index * 2 + part
-                entries = [self.plan[2, first * GROUP + k] for k in range(GROUP)]
+            groups = []
+            for part in range(GROUPS):
+                first = index * GROUPS + part
+                entries = [self.plan[1, first * GROUP + k] for k in range(GROUP)]
                 slots = [entry & 255 for entry in entries]
                 left = jnp.concatenate([self.left[slot] for slot in slots], axis=0)
                 right = jnp.concatenate([self.right[slot] for slot in slots], axis=0)
@@ -88,59 +95,83 @@
                 for k in range(GROUP):
                     rows = jnp.where(lane == k, entries[k] >> 8, rows)
                 rows = jnp.broadcast_to(rows, (RHS, B))
-                body(left, right, rows, [self.plan[3, 2 * first + half] for half in (0, 1)])
+                groups.append((left, right, rows, [self.plan[2, 2 * first + half] for half in (0, 1)]))
+            body(groups)
             return carry
 
-        lax.fori_loop(0, self.plan[COUNTS, 2], step, 0)
+        lax.fori_loop(0, self.plan[2, COUNTS + 2], step, 0)
 
     def near_loop(self, body):
-        def step(chunk, carry):
+        size = STEP if self.sources is None else CHUNK
+
+        def step(index, carry):
             if self.sources is not None:
-                self.copy(0, chunk).wait()
-            for part in range(CHUNK):
-                body(chunk * CHUNK + part)
+                self.copy(0, index).wait()
+            for part in range(size):
+                slot = index * size + part
+                code = self.plan[0, slot]
+                body(part, code & 7, code >> 3, self.near[slot])
             return carry
 
-        lax.fori_loop(0, self.plan[COUNTS, 0], step, 0)
+        lax.fori_loop(0, self.plan[2, COUNTS] * (STEP // size), step, 0)
+
+
+def halves(x, axis):
+    return (x[:HALF], x[HALF:]) if axis == 0 else (x[:, :HALF], x[:, HALF:])
 
 
 def back_products(blocks, own, acc):
-    plan = blocks.plan
-
-    def far(left, right, rows, partners):
-        every = dot_t(own[0:CL].reshape(CL * RHS, B), left)
-        coef = jnp.zeros((RHS, B), F32)
-        for cluster in range(CL):
-            coef = jnp.where(rows == cluster, every[cluster * RHS : (cluster + 1) * RHS], coef)
-        coef = coef.astype(BF16)
-        for half, partner in enumerate(partners):
-            part = slice(half * HALF, (half + 1) * HALF)
-            acc[partner] += dot(coef[:, part], right[part])
-
-    def near(slot):
-        acc[plan[1, slot]] += dot(own[plan[0, slot]], blocks.near[slot])
+    def far(groups):
+        coefs = []
+        for left, right, rows, partners in groups:
+            every = dot_t(own[0:CL].reshape(CL * RHS, B), left)
+            coef = jnp.zeros((RHS, B), F32)
+            for cluster in range(CL):
+                coef = jnp.where(rows == cluster, every[cluster * RHS : (cluster + 1) * RHS], coef)
+            coefs.append(coef.astype(BF16))
+        terms = []
+        for coef, (left, right, rows, partners) in zip(coefs, groups):
+            for part, block, partner in zip(halves(coef, 1), halves(right, 0), partners):
+                terms.append((partner, dot(part, block)))
+        for partner, term in terms:
+            acc[partner] += term
+
+    def near(part, row, partner, block):
+        acc[partner] += dot(own[row], block)
 
     blocks.far_loop(far)
     blocks.near_loop(near)
 
 
-def forward_products(blocks, fetched, acc):
-    plan = blocks.plan
-
-    def far(left, right, rows, partners):
-        coef = [
-            dot_t(fetched[partner], right[half * HALF : (half + 1) * HALF])
-            for half, partner in enumerate(partners)
-        ]
-        coef = jnp.concatenate(coef, axis=1).astype(BF16).astype(F32)
-        spread = [jnp.where(rows == cluster, coef, 0.0).astype(BF16) for cluster in range(CL)]
-        acc[0:CL] += dot(jnp.concatenate(spread, axis=0), left).reshape(CL, RHS, B)
-
-    def near(slot):
-        acc[plan[0, slot]] += dot_t(fetched[plan[1, slot]], blocks.near[slot])
+def forward_products(blocks, fetched, turned, acc, acc_turned):
+    turned[DEAD] = jnp.zeros((B, RHS), BF16)
+    for partner in range(PEERS):
+        turned[partner] = fetched[partner].T
+    acc_turned[...] = jnp.zeros_like(acc_turned)
+
+    def far(groups):
+        spreads = []
+        for left, right, rows, partners in groups:
+            coef = [dot_t(fetched[partner], block) for partner, block in zip(partners, halves(right, 0))]
+            coef = jnp.concatenate(coef, axis=1).astype(BF16).astype(F32)
+            spread = [jnp.where(rows == cluster, coef, 0.0).astype(BF16) for cluster in range(CL)]
+            spreads.append(jnp.concatenate(spread, axis=0))
+        terms = [dot(spread, group[0]) for spread, group in zip(spreads, groups)]
+        total = terms[0]
+        for term in terms[1:]:
+            total += term
+        acc[0:CL] += total.reshape(CL, RHS, B)
+
+    def near(part, row, partner, block):
+        if part % 2 == 0:
+            acc[row] += dot_t(fetched[partner], block)
+        else:
+            acc_turned[row] += dot(block, turned[partner])
 
     blocks.far_loop(far)
     blocks.near_loop(near)
+    for cluster in range(CL):
+        acc[cluster] += acc_turned[cluster].T
 
 
 def make_plan(me, lists, few, draft):
@@ -187,14 +218,13 @@
     codes = jnp.where(row16 == 0, wide(lane), jnp.where(row16 == 1, wide(far_row), 1)).astype(F32).astype(BF16)
     found = dot(codes, hits)
     entry = jnp.where(found[2:3] > 0.5, found[0:1] + 256.0 * found[1:2], 256.0 * CL).astype(jnp.int32)
-    draft[0:1, 0:SLOTS] = near_row
-    draft[1:2, 0:SLOTS] = near_rho
-    draft[2:3, :] = entry
-    draft[3:4, 0:SLOTS] = quad_rho
-    chunks = [(few[0, kind] + (CHUNK - 1)) // CHUNK for kind in (0, 1)]
-    numbers = jnp.where(lane == 0, chunks[0], jnp.where(lane == 1, chunks[1], (first + 15) >> 4))
-    draft[COUNTS : COUNTS + 1, 0:SLOTS] = numbers
-    draft[WANTED : WANTED + 16, 0:SLOTS] = wide(wanted).astype(jnp.int32)
+    wanted = jnp.sum(jnp.where(row16 + WANTED == wide(lane), wide(wanted), 0.0), axis=0, keepdims=True).astype(jnp.int32)
+    draft[0:1, 0:SLOTS] = near_row + 8 * near_rho
+    draft[1:2, :] = entry
+    numbers = jnp.where(lane == COUNTS, (few[0, 0] + (STEP - 1)) // STEP, jnp.where(lane < COUNTS, quad_rho, wanted))
+    numbers = jnp.where(lane == COUNTS + 1, (few[0, 1] + (CHUNK - 1)) // CHUNK, numbers)
+    steps = (first + (2 * GROUPS * QUAD - 1)) >> (GROUPS.bit_length() + 2)
+    draft[2:3, 0:SLOTS] = jnp.where(lane == COUNTS + 2, steps, numbers)
 
 
 def place_out(rho):
@@ -222,18 +252,20 @@
     m1, m2, m3, give, plan, near_held, left_held, right_held,
     own, acc, lists, few, draft, near_sem, left_sem, right_sem, list_sem,
 ):
+    blocks = Blocks(plan, near_held, left_held, right_held, ((near, near_sem), (left, left_sem), (right, right_sem)))
     copies = [pltpu.make_async_copy(counts, few, list_sem.at[4])]
     for index, source in enumerate((near_rows, near_cols, far_rows, far_cols)):
         copies.append(pltpu.make_async_copy(source, lists.at[pl.ds(index, 1)], list_sem.at[index]))
     for copy in copies:
         copy.start()
+    blocks.start()
     for cluster in range(CL):
         own[cluster] = both[0, :, cluster * B : (cluster + 1) * B]
     own[CL] = jnp.zeros((RHS, B), BF16)
     draft[...] = jnp.zeros_like(draft)
     copies[0].wait()
-    blocks = Blocks(plan, near_held, left_held, right_held, ((near, near_sem), (left, left_sem), (right, right_sem)))
-    blocks.start((few[0, 0] + (CHUNK - 1)) // CHUNK, (few[0, 1] + (CHUNK - 1)) // CHUNK)
+    near_steps = (few[0, 0] + (STEP - 1)) // STEP
+    blocks.start_rest(near_steps * (STEP // CHUNK), (few[0, 1] + (CHUNK - 1)) // CHUNK)
     for copy in copies[1:]:
         copy.wait()
     make_plan(me[0], lists, few, draft)
@@ -246,87 +278,88 @@
     for rho in range(PEERS):
         message, index = place_out(rho)
         outs[message][index, 0:RHS] = acc[rho]
-        outs[message][index, RHS:] = jnp.full((EXTRA, B), plan[WANTED + rho, 0].astype(F32), F32)
+        outs[message][index, RHS:] = jnp.full((EXTRA, B), plan[2, WANTED + rho].astype(F32), F32)
 
 
 def forward_first(
     plan, both, h1, h2, h3, post, diag, near, left, right,
     out,
-    fetched, acc, fetch_sem,
+    fetched, turned, acc, acc_turned,
 ):
     halo = (h1, h2, h3)
-    copies = []
     for rho in range(PEERS):
-        lanes = pl.ds(pl.multiple_of(plan[WANTED + rho, 0] * B, B), B)
+        lanes = pl.ds(pl.multiple_of(plan[2, WANTED + rho] * B, B), B)
         if rho == 11:
-            source = both.at[1, :, lanes]
+            fetched[rho] = both[1, :, lanes]
         elif rho < 6:
-            source = halo[rho // 2].at[rho % 2, :, lanes]
+            fetched[rho] = halo[rho // 2][rho % 2, :, lanes]
         else:
             k, same = divmod(rho - 6, 2)
-            source = post.at[2 * k + (1 - same if k < 2 else 0), :, lanes]
-        copies.append(pltpu.make_async_copy(source, fetched.at[rho], fetch_sem.at[rho]))
-    for copy in copies:
-        copy.start()
+            fetched[rho] = post[2 * k + (1 - same if k < 2 else 0), :, lanes]
     fetched[DEAD] = jnp.zeros((RHS, B), BF16)
     acc[CL] = jnp.zeros((RHS, B), F32)
     for cluster in range(CL):
         acc[cluster] = dot_t(both[0, :, cluster * B : (cluster + 1) * B], diag[cluster])
-    for copy in copies:
-        copy.wait()
-    forward_products(Blocks(plan, near, left, right), fetched, acc)
+    forward_products(Blocks(plan, near, left, right), fetched, turned, acc, acc_turned)
     out[...] = acc[0:CL]
+
+
+STRIP = 16
 
 
 def back_second(
     plan, partial, r1, r2, r3, post, got, near, left, right,
     image, rounded, wanted, m1, m2, m3, give,
-    own, acc,
+    own, acc, draft, sem,
 ):
     ins = (r1, r2, r3, post, got)
     own[CL] = jnp.zeros((RHS, B), BF16)
     acc[...] = jnp.zeros_like(acc)
     places = [place_in(rho) for rho in range(PEERS)]
-    for rho, (message, index) in enumerate(places):
-        wanted[rho] = ins[message][index, RHS:]
-    for cluster in range(CL):
-        total = partial[cluster]
-        for message, index in places:
-            mine = ins[message][index, RHS : RHS + 1] == float(cluster)
-            total += jnp.where(jnp.broadcast_to(mine, (RHS, B)), ins[message][index, 0:RHS], 0.0)
-        image[:, cluster * B : (cluster + 1) * B] = total
-        own[cluster] = total.astype(BF16)
-        rounded[cluster] = total.astype(BF16)
+    marks = [ins[message][index, RHS : RHS + 1] for message, index in places]
+    lane = lax.broadcasted_iota(jnp.int32, (1, SLOTS), 1)
+    packed = jnp.zeros((1, SLOTS), F32)
+    for rho, mark in enumerate(marks):
+        packed = jnp.where(lane == rho, mark[:, 0:SLOTS], packed)
+    draft[...] = packed.astype(jnp.int32)
+    copy = pltpu.make_async_copy(draft, wanted, sem)
+    copy.start()
+    for first in range(0, RHS, STRIP):
+        rows = slice(first, first + STRIP)
+        totals = [partial[cluster, rows] for cluster in range(CL)]
+        for (message, index), mark in zip(places, marks):
+            block = ins[message][index, rows]
+            mark = jnp.broadcast_to(mark, (STRIP, B))
+            for cluster in range(CL):
+                totals[cluster] += jnp.where(mark == float(cluster), block, 0.0)
+        for cluster in range(CL):
+            image[rows, cluster * B : (cluster + 1) * B] = totals[cluster]
+            own[cluster, rows] = totals[cluster].astype(BF16)
+            rounded[cluster, rows] = totals[cluster].astype(BF16)
     back_products(Blocks(plan, near, left, right), own, acc)
     outs = (m1, m2, m3, give)
+    copy.wait()
     for rho in range(PEERS):
         message, index = place_out(rho)
         outs[message][index, 0:RHS] = acc[rho].astype(BF16)
-        pick = jnp.broadcast_to(wanted[rho, 0:1], (RHS, B))
-        chosen = jnp.zeros((RHS, B), F32)
-        for cluster in range(CL):
-            chosen = jnp.where(pick == float(cluster), own[cluster].astype(F32), chosen)
-        outs[message][index, RHS:] = chosen.astype(BF16)
+        outs[message][index, RHS:] = own[wanted[0, rho]]
 
 
 def forward_second(
-    plan, own, wanted, r1, r2, r3, post, got, diag, near, left, right,
+    plan, wanted, own, r1, r2, r3, post, got, diag, near, left, right,
     image,
-    fetched, acc,
+    fetched, turned, acc, acc_turned,
 ):
     ins = (r1, r2, r3, post, got)
     fetched[DEAD] = jnp.zeros((RHS, B), BF16)
     acc[CL] = jnp.zeros((RHS, B), F32)
-    places = [place_in(rho) for rho in range(PEERS)]
-    for rho, (message, index) in enumerate(places):
+    for cluster in range(CL):
+        acc[cluster] = dot_t(own[cluster], diag[cluster])
+    for rho in range(PEERS):
+        message, index = place_in(rho)
         fetched[rho] = ins[message][index, RHS:]
-    for cluster in range(CL):
-        total = dot_t(own[cluster], diag[cluster])
-        for rho, (message, index) in enumerate(places):
-            mine = wanted[rho, 0:1] == float(cluster)
-            total += jnp.where(jnp.broadcast_to(mine, (RHS, B)), ins[message][index, 0:RHS].astype(F32), 0.0)
-        acc[cluster] = total
-    forward_products(Blocks(plan, near, left, right), fetched, acc)
+        acc[wanted[0, rho]] += ins[message][index, 0:RHS].astype(F32)
+    forward_products(Blocks(plan, near, left, right), fetched, turned, acc, acc_turned)
     for cluster in range(CL):
         image[:, cluster * B : (cluster + 1) * B] = acc[cluster]
 
@@ -376,16 +409,21 @@
     )(*args)
 
 
+def forward_scratch():
+    return [
+        pltpu.VMEM((PEERS + 1, RHS, B), BF16),
+        pltpu.VMEM((PEERS + 1, B, RHS), BF16),
+        pltpu.VMEM((CL + 1, RHS, B), F32),
+        pltpu.VMEM((CL + 1, B, RHS), F32),
+    ]
+
+
 def k2(*args):
     return call(
         forward_first, "forward_products",
         shaped((CL, RHS, B), F32), VMEM,
-        [SMEM] + [VMEM] + [ANY] * 4 + [VMEM] * 4,
-        [
-            pltpu.VMEM((PEERS + 1, RHS, B), BF16),
-            pltpu.VMEM((CL + 1, RHS, B), F32),
-            pltpu.SemaphoreType.DMA((PEERS,)),
-        ],
+        [SMEM] + [VMEM] * 9,
+        forward_scratch(),
     )(*args)
 
 
@@ -395,12 +433,17 @@
         [
             shaped((RHS, CL * B), F32),
             shaped((CL, RHS, B), BF16),
-            shaped((PEERS, EXTRA, B), F32),
+            shaped((1, SLOTS), jnp.int32),
         ]
         + message_shapes(2 * RHS, BF16),
-        [VMEM] * 7,
+        [VMEM] * 2 + [SMEM] + [VMEM] * 4,
         [SMEM] + [VMEM] * 9,
-        [pltpu.VMEM((CL + 1, RHS, B), BF16), pltpu.VMEM((PEERS + 1, RHS, B), F32)],
+        [
+            pltpu.VMEM((CL + 1, RHS, B), BF16),
+            pltpu.VMEM((PEERS + 1, RHS, B), F32),
+            pltpu.VMEM((1, SLOTS), jnp.int32),
+            pltpu.SemaphoreType.DMA,
+        ],
     )(*args)
 
 
@@ -408,8 +451,8 @@
     return call(
         forward_second, "second_image",
         shaped((RHS, CL * B), F32), VMEM,
-        [SMEM] + [VMEM] * 11,
-        [pltpu.VMEM((PEERS + 1, RHS, B), BF16), pltpu.VMEM((CL + 1, RHS, B), F32)],
+        [SMEM] * 2 + [VMEM] * 10,
+        forward_scratch(),
     )(*args)
 
 
@@ -463,7 +506,7 @@
     first_image, rounded, wanted, m1, m2, m3, give = k3(plan, partial, r1, r2, r3, post, got, *held)
     r1, r2, r3, got, messages = exchange(m1, m2, m3, give)
     post = passed_on(r1, r2, r3)
-    second_image = k4(plan, rounded, wanted, r1, r2, r3, post, got, diag_blocks, *held)
+    second_image = k4(plan, wanted, rounded, r1, r2, r3, post, got, diag_blocks, *held)
     return first_image, second_image
 
 

time: 85.1 us -> 80.9 us (0.951)
  Pallas kernels: 32.9 us -> 24.8 us
  waiting for transfers between devices: 29.1 us -> 32.9 us
    ppermute x9, waiting for transfers between devices: 23.2 us -> 26.6 us  [carry(): return lax.ppermute(block, 'rows', carriers(size, k))]
    pallas_call x1, Pallas kernels: 7.56 us -> 5.29 us  [k3(): call(back_second, 'image_and_transposed_products', [shaped((RHS, CL * B),...]
    pallas_call x1, Pallas kernels: 7.83 us -> 5.83 us  [k2(): call(forward_first, 'forward_products', shaped((CL, RHS, B), F32), VMEM,...]
    pallas_call x1, Pallas kernels: 8.58 us -> 6.66 us  [k4(): call(forward_second, 'second_image', shaped((RHS, CL * B), F32), VMEM, [S...]
    pallas_call x1, Pallas kernels: 8.95 us -> 7.04 us  [k1(): call(back_first, 'transposed_products', message_shapes(RHS + EXTRA, F32)...]
    ppermute x9, starting transfers between devices: 19 us -> 20.7 us  [carry(): return lax.ppermute(block, 'rows', carriers(size, k))]
    ppermute x6, starting transfers between devices: 3.45 us -> 1.93 us  [swap(): return lax.ppermute(block, 'rows', [(i, i ^ 1) for i in range(size)])]
  transfers between devices with their start and end apart: 15 -> 15, of which waited for: 7 -> 8; matrix products, arithmetic and copies ran while one was open for 0% -> 0% of each run, Pallas kernels for 19% -> 16%
where the time goes in v2:
time: 80.9 us; the launch traced here: 82.4 us
  waiting for transfers between devices  32.9 us (41%)
  Pallas kernels  24.8 us (31%)
  starting transfers between devices  22.6 us (28%)
  other arithmetic  1.08 us (1%)
  between operations  0.82 us (1%)
    ppermute x9, waiting for transfers between devices, carry(): return lax.ppermute(block, 'rows', carriers(size, k))  26.6 us
    ppermute x9, starting transfers between devices, carry(): return lax.ppermute(block, 'rows', carriers(size, k))  20.7 us
    pallas_call x1, Pallas kernels, k1(): call(back_first, 'transposed_products', message_shapes(RHS + EXTRA, F32)...  7.04 us
    pallas_call x1, Pallas kernels, k4(): call(forward_second, 'second_image', shaped((RHS, CL * B), F32), VMEM, [S...  6.66 us
    ppermute x6, waiting for transfers between devices, swap(): return lax.ppermute(block, 'rows', [(i, i ^ 1) for i in range(size)])  6.3 us
    pallas_call x1, Pallas kernels, k2(): call(forward_first, 'forward_products', shaped((CL, RHS, B), F32), VMEM,...  5.83 us
    pallas_call x1, Pallas kernels, k3(): call(back_second, 'image_and_transposed_products', [shaped((RHS, CL * B),...  5.29 us
    ppermute x6, starting transfers between devices, swap(): return lax.ppermute(block, 'rows', [(i, i ^ 1) for i in range(size)])  1.93 us
  transfers between devices with their start and end apart: 15, of which 8 were waited for; matrix products, arithmetic and copies ran while one was open for 0% of the time, Pallas kernels for 16%

profile of v2, /device:TPU:1, one launch (start us, length us, event | category | flops | bytes accessed | tf_op | source)
XLA Modules:
  0.0 82.4 jit_solution(12373267542114868261)
XLA Ops:
  0.6 1.5 %collective-permute-start = (bf16[64,1024]{1,0:T(8,128)(2,1)}, bf16[64,1024]{1,0:T(8,128)(2,1)S(1)}, u32[]{:S(2)}, u32[]{:S(2)}) collective-permute-start(bf16[64,1024]{1,0:T(8,128)(2,1)} %param.10), channel_id=1, source_target_pairs={{0,1},{1,0},{2,3},{3,2},{4,5},{5,4},{6,7},{7,6},{8,9},{9,8},{10,11... | collective-permute-start | bytes 393224 | tf_op jit(solution)/shard_map/ppermute | solution.py:475
  2.1 1.2 %collective-permute-done = bf16[64,1024]{1,0:T(8,128)(2,1)S(1)} collective-permute-done((bf16[64,1024]{1,0:T(8,128)(2,1)}, bf16[64,1024]{1,0:T(8,128)(2,1)S(1)}, u32[]{:S(2)}, u32[]{:S(2)}) %collective-permute-start) | collective-permute-done | bytes 131104 | tf_op jit(solution)/shard_map/ppermute | solution.py:475
  3.3 0.9 %pad_maximum_fusion.3.both = bf16[2,64,1024]{2,1,0:T(8,128)(2,1)S(1)} fusion(bf16[1,64,1024]{2,1,0:T(8,128)(2,1)S(1)} %bitcast.8, bf16[1,64,1024]{2,1,0:T(8,128)(2,1)} %bitcast.7), kind=kLoop, calls=%fused_computation.3 | loop fusion | flops 131072 | bytes 524288 | tf_op jit(solution)/shard_map/stack | solution.py:495
  4.3 6.4 %collective-permute-start.3 = (bf16[2,64,1024]{2,1,0:T(8,128)(2,1)S(1)}, bf16[2,64,1024]{2,1,0:T(8,128)(2,1)S(1)}, u32[]{:S(2)}, u32[]{:S(2)}) collective-permute-start(bf16[2,64,1024]{2,1,0:T(8,128)(2,1)S(1)} %pad_maximum_fusion.3.both), channel_id=1, source_target_pairs={{0,6},{1,123},{2,8},{3,125},{4,10},{5,127},{6,12},{7,1},{8,14},{9,... | collective-permute-start | bytes 786440 | tf_op jit(solution)/shard_map/ppermute | solution.py:478
  10.7 2.2 %collective-permute-start.1 = (bf16[2,64,1024]{2,1,0:T(8,128)(2,1)S(1)}, bf16[2,64,1024]{2,1,0:T(8,128)(2,1)S(1)}, u32[]{:S(2)}, u32[]{:S(2)}) collective-permute-start(bf16[2,64,1024]{2,1,0:T(8,128)(2,1)S(1)} %pad_maximum_fusion.3.both), channel_id=1, source_target_pairs={{0,2},{1,127},{2,4},{3,1},{4,6},{5,3},{6,8},{7,5},{8,10},{9,7},{10... | collective-permute-start | bytes 786440 | tf_op jit(solution)/shard_map/ppermute | solution.py:478
  12.9 1.4 %collective-permute-start.2 = (bf16[2,64,1024]{2,1,0:T(8,128)(2,1)S(1)}, bf16[2,64,1024]{2,1,0:T(8,128)(2,1)S(1)}, u32[]{:S(2)}, u32[]{:S(2)}) collective-permute-start(bf16[2,64,1024]{2,1,0:T(8,128)(2,1)S(1)} %pad_maximum_fusion.3.both), channel_id=1, source_target_pairs={{0,4},{1,125},{2,6},{3,127},{4,8},{5,1},{6,10},{7,3},{8,12},{9,5},... | collective-permute-start | bytes 786440 | tf_op jit(solution)/shard_map/ppermute | solution.py:478
  14.3 7.0 %transposed_products.1 = (f32[4,72,256]{2,1,0:T(8,128)S(1)}, f32[4,72,256]{2,1,0:T(8,128)S(1)}, f32[3,72,256]{2,1,0:T(8,128)S(1)}, f32[7,72,256]{2,1,0:T(8,128)S...) custom-call(s32[1]{0:T(128)} %bitcast.me, ...), custom_call_target="tpu_custom_call" | custom-call | flops 2000000000 | bytes 22000000 | tf_op jit(solution)/shard_map/transposed_products/pallas_call | solution.py:396
  21.3 0.0 copy-start
  21.4 0.1 collective-permute-start.5
  21.5 0.0 collective-permute-done.3.h3
  21.5 1.8 %collective-permute-done.1.h1 = bf16[2,64,1024]{2,1,0:T(8,128)(2,1)S(1)} collective-permute-done((bf16[2,64,1024]{2,1,0:T(8,128)(2,1)S(1)}, bf16[2,64,1024]{2,1,0:T(8,128)(2,1)S(1)}, u32[]{:S(2)}, u32[]{:S(2)}) %collective-permute-start.1) | collective-permute-done | bytes 262176 | tf_op jit(solution)/shard_map/ppermute | solution.py:478
  23.3 1.9 %collective-permute-done.2.h2 = bf16[2,64,1024]{2,1,0:T(8,128)(2,1)S(1)} collective-permute-done((bf16[2,64,1024]{2,1,0:T(8,128)(2,1)S(1)}, bf16[2,64,1024]{2,1,0:T(8,128)(2,1)S(1)}, u32[]{:S(2)}, u32[]{:S(2)}) %collective-permute-start.2) | collective-permute-done | bytes 262176 | tf_op jit(solution)/shard_map/ppermute | solution.py:478
  25.2 0.1 pad_maximum_fusion
  25.3 0.1 collective-permute-start.4
  25.4 0.0 collective-permute-done.5.got
  25.5 4.8 %collective-permute-start.6 = (f32[4,72,256]{2,1,0:T(8,128)S(1)}, f32[4,72,256]{2,1,0:T(8,128)S(1)}, u32[]{:S(2)}, u32[]{:S(2)}) collective-permute-start(f32[4,72,256]{2,1,0:T(8,128)S(1)} %get-tuple-element.44), channel_id=1, source_target_pairs={{0,2},{1,127},{2,4},{3,1},{4,6},{5,3},{6,8},{7,5},{8,10},{9,7},{10... | collective-permute-start | bytes 884744 | tf_op jit(solution)/shard_map/ppermute | solution.py:478
  30.3 0.0 collective-permute-start.7
  30.3 0.4 collective-permute-start.8
  30.7 0.0 collective-permute-done.4.post
  30.7 0.0 copy-done
  30.7 5.8 %forward_products.1.partial = f32[4,64,256]{2,1,0:T(8,128)S(1)} custom-call(s32[4,256]{1,0:T(4,128)S(1)} %get-tuple-element.22.plan, bf16[2,64,1024]{2,1,0:T(8,128)(2,1)S(1)} %pad_maximum_fusion.3.both, bf16[2,64,1024]{2,1,0:T(8,128)(2,1)S(1)} %collective-permute-done.1.h1, bf16[2,64,1024]{2,1,0:T(8,128)(2,1)S(1)} %collective-permute-done.2.h2, ...), custom_call_target="tpu_custom_call" | custom-call | flops 2000000000 | bytes 22000000 | tf_op jit(solution)/shard_map/forward_products/pallas_call | solution.py:422
  36.6 9.2 %collective-permute-done.8.r3 = f32[3,72,256]{2,1,0:T(8,128)S(1)} collective-permute-done((f32[3,72,256]{2,1,0:T(8,128)S(1)}, f32[3,72,256]{2,1,0:T(8,128)S(1)}, u32[]{:S(2)}, u32[]{:S(2)}) %collective-permute-start.8) | collective-permute-done | bytes 221216 | tf_op jit(solution)/shard_map/ppermute | solution.py:478
  45.8 0.0 collective-permute-done.6.r1
  45.8 0.0 collective-permute-done.7.r2
  45.9 0.1 collective-permute-start.9
  46.0 1.7 %collective-permute-done.9.post = f32[5,72,256]{2,1,0:T(8,128)S(1)} collective-permute-done((f32[5,72,256]{2,1,0:T(8,128)S(1)}, f32[5,72,256]{2,1,0:T(8,128)S(1)}, u32[]{:S(2)}, u32[]{:S(2)}) %collective-permute-start.9) | collective-permute-done | bytes 368672 | tf_op jit(solution)/shard_map/ppermute | solution.py:475
  47.6 5.3 %image_and_transposed_products.1 = (f32[64,1024]{1,0:T(8,128)}, bf16[4,64,256]{2,1,0:T(8,128)(2,1)S(1)}, s32[1,128]{1,0:T(1,128)S(1)}, bf16[4,128,256]{2,1,0:T(8...) custom-call(s32[4,256]{1,0:T(4,128)S(1)} %get-tuple-element.22.plan,, ...), custom_call_target="tpu_custom_call" | custom-call | flops 2000000000 | bytes 22000000 | tf_op jit(solution)/shard_map/image_and_transposed_products/pallas_call | solution.py:431
  52.9 0.1 collective-permute-start.10
  53.0 1.8 %collective-permute-done.10.got = bf16[7,128,256]{2,1,0:T(8,128)(2,1)S(1)} collective-permute-done((bf16[7,128,256]{2,1,0:T(8,128)(2,1)S(1)}, bf16[7,128,256]{2,1,0:T(8,128)(2,1)S(1)}, u32[]{:S(2)}, u32[]{:S(2)}) %collective-permute-start.10) | collective-permute-done | bytes 458784 | tf_op jit(solution)/shard_map/ppermute | solution.py:475
  54.9 5.4 %collective-permute-start.11 = (bf16[4,128,256]{2,1,0:T(8,128)(2,1)S(1)}, bf16[4,128,256]{2,1,0:T(8,128)(2,1)S(1)}, u32[]{:S(2)}, u32[]{:S(2)}) collective-permute-start(bf16[4,128,256]{2,1,0:T(8,128)(2,1)S(1)} %get-tuple-element.47), channel_id=1, source_target_pairs={{0,2},{1,127},{2,4},{3,1},{4,6},{5,3},{6,8},{7,5},{8,10},{9,7},{10... | collective-permute-start | bytes 786440 | tf_op jit(solution)/shard_map/ppermute | solution.py:478
  60.3 0.0 collective-permute-start.12
  60.3 0.0 collective-permute-start.13
  60.3 13.6 %collective-permute-done.13.r3 = bf16[3,128,256]{2,1,0:T(8,128)(2,1)S(1)} collective-permute-done((bf16[3,128,256]{2,1,0:T(8,128)(2,1)S(1)}, bf16[3,128,256]{2,1,0:T(8,128)(2,1)S(1)}, u32[]{:S(2)}, u32[]{:S(2)}) %collective-permute-start.13) | collective-permute-done | bytes 196640 | tf_op jit(solution)/shard_map/ppermute | solution.py:478
  73.9 0.0 collective-permute-done.11.r1
  73.9 0.0 collective-permute-done.12.r2
  74.0 0.1 collective-permute-start.14
  74.1 1.6 %collective-permute-done.14.post = bf16[5,128,256]{2,1,0:T(8,128)(2,1)S(1)} collective-permute-done((bf16[5,128,256]{2,1,0:T(8,128)(2,1)S(1)}, bf16[5,128,256]{2,1,0:T(8,128)(2,1)S(1)}, u32[]{:S(2)}, u32[]{:S(2)}) %collective-permute-start.14) | collective-permute-done | bytes 327712 | tf_op jit(solution)/shard_map/ppermute | solution.py:475
  75.7 6.7 %second_image.1 = f32[64,1024]{1,0:T(8,128)} custom-call(s32[4,256]{1,0:T(4,128)S(1)} %get-tuple-element.22.plan, s32[1,128]{1,0:T(1,128)S(1)} %get-tuple-element.36.wanted, bf16[4,64,256]{2,1,0:T(8,128)(2,1)S(1)} %get-tuple-element.37.own, bf16[4,128,256]{2,1,0:T(8,128)(2,1)S(1)} %collective-permute-done.11.r1, ...), custom_call_target="tpu_custom_call" | custom-call | flops 2000000000 | bytes 22000000 | tf_op jit(solution)/shard_map/second_image/pallas_call | solution.py:451
  (11 shorter events, 0.2 us)
Async XLA Ops:
  0.6 2.7 %collective-permute-start = (bf16[64,1024]{1,0:T(8,128)(2,1)}, bf16[64,1024]{1,0:T(8,128)(2,1)S(1)}, u32[]{:S(2)}, u32[]{:S(2)}) collective-permute-start(bf16[64,1024]{1,0:T(8,128)(2,1)} %param.10), channel_id=1, source_target_pairs={{0,1},{1,0},{2,3},{3,2},{4,5},{5,4},{6,7},{7,6},{8,9},{9,8},{10,11... | collective-permute-start | bytes 393224 | tf_op jit(solution)/shard_map/ppermute | solution.py:475
  4.3 17.2 %collective-permute-start.3 = (bf16[2,64,1024]{2,1,0:T(8,128)(2,1)S(1)}, bf16[2,64,1024]{2,1,0:T(8,128)(2,1)S(1)}, u32[]{:S(2)}, u32[]{:S(2)}) collective-permute-start(bf16[2,64,1024]{2,1,0:T(8,128)(2,1)S(1)} %pad_maximum_fusion.3.both), channel_id=1, source_target_pairs={{0,6},{1,123},{2,8},{3,125},{4,10},{5,127},{6,12},{7,1},{8,14},{9,... | collective-permute-start | bytes 786440 | tf_op jit(solution)/shard_map/ppermute | solution.py:478
  10.7 12.6 %collective-permute-start.1 = (bf16[2,64,1024]{2,1,0:T(8,128)(2,1)S(1)}, bf16[2,64,1024]{2,1,0:T(8,128)(2,1)S(1)}, u32[]{:S(2)}, u32[]{:S(2)}) collective-permute-start(bf16[2,64,1024]{2,1,0:T(8,128)(2,1)S(1)} %pad_maximum_fusion.3.both), channel_id=1, source_target_pairs={{0,2},{1,127},{2,4},{3,1},{4,6},{5,3},{6,8},{7,5},{8,10},{9,7},{10... | collective-permute-start | bytes 786440 | tf_op jit(solution)/shard_map/ppermute | solution.py:478
  12.9 12.3 %collective-permute-start.2 = (bf16[2,64,1024]{2,1,0:T(8,128)(2,1)S(1)}, bf16[2,64,1024]{2,1,0:T(8,128)(2,1)S(1)}, u32[]{:S(2)}, u32[]{:S(2)}) collective-permute-start(bf16[2,64,1024]{2,1,0:T(8,128)(2,1)S(1)} %pad_maximum_fusion.3.both), channel_id=1, source_target_pairs={{0,4},{1,125},{2,6},{3,127},{4,8},{5,1},{6,10},{7,3},{8,12},{9,5},... | collective-permute-start | bytes 786440 | tf_op jit(solution)/shard_map/ppermute | solution.py:478
  21.3 9.4 %copy-start = (bf16[4,256,256]{2,1,0:T(8,128)(2,1)S(1)}, bf16[4,256,256]{2,1,0:T(8,128)(2,1)}, u32[]{:S(2)}) copy-start(bf16[4,256,256]{2,1,0:T(8,128)(2,1)} %diag.3) | copy-start | bytes 1572868
  21.4 4.1 %collective-permute-start.5 = (f32[7,72,256]{2,1,0:T(8,128)S(1)}, f32[7,72,256]{2,1,0:T(8,128)S(1)}, u32[]{:S(2)}, u32[]{:S(2)}) collective-permute-start(f32[7,72,256]{2,1,0:T(8,128)S(1)} %get-tuple-element.24), channel_id=1, source_target_pairs={{0,1},{1,0},{2,3},{3,2},{4,5},{5,4},{6,7},{7,6},{8,9},{9,8},{10,11... | collective-permute-start | bytes 1548296 | tf_op jit(solution)/shard_map/ppermute | solution.py:475
  25.3 5.4 %collective-permute-start.4 = (bf16[5,64,1024]{2,1,0:T(8,128)(2,1)S(1)}, bf16[5,64,1024]{2,1,0:T(8,128)(2,1)S(1)}, u32[]{:S(2)}, u32[]{:S(2)}) collective-permute-start(bf16[5,64,1024]{2,1,0:T(8,128)(2,1)S(1)} %pad_maximum_fusion), channel_id=1, source_target_pairs={{0,1},{1,0},{2,3},{3,2},{4,5},{5,4},{6,7},{7,6},{8,9},{9,8},{10,11... | collective-permute-start | bytes 1966088 | tf_op jit(solution)/shard_map/ppermute | solution.py:475
  25.5 20.3 %collective-permute-start.6 = (f32[4,72,256]{2,1,0:T(8,128)S(1)}, f32[4,72,256]{2,1,0:T(8,128)S(1)}, u32[]{:S(2)}, u32[]{:S(2)}) collective-permute-start(f32[4,72,256]{2,1,0:T(8,128)S(1)} %get-tuple-element.44), channel_id=1, source_target_pairs={{0,2},{1,127},{2,4},{3,1},{4,6},{5,3},{6,8},{7,5},{8,10},{9,7},{10... | collective-permute-start | bytes 884744 | tf_op jit(solution)/shard_map/ppermute | solution.py:478
  30.3 15.5 %collective-permute-start.7 = (f32[4,72,256]{2,1,0:T(8,128)S(1)}, f32[4,72,256]{2,1,0:T(8,128)S(1)}, u32[]{:S(2)}, u32[]{:S(2)}) collective-permute-start(f32[4,72,256]{2,1,0:T(8,128)S(1)} %get-tuple-element.43), channel_id=1, source_target_pairs={{0,4},{1,125},{2,6},{3,127},{4,8},{5,1},{6,10},{7,3},{8,12},{9,5},... | collective-permute-start | bytes 884744 | tf_op jit(solution)/shard_map/ppermute | solution.py:478
  30.3 15.5 %collective-permute-start.8 = (f32[3,72,256]{2,1,0:T(8,128)S(1)}, f32[3,72,256]{2,1,0:T(8,128)S(1)}, u32[]{:S(2)}, u32[]{:S(2)}) collective-permute-start(f32[3,72,256]{2,1,0:T(8,128)S(1)} %get-tuple-element.42), channel_id=1, source_target_pairs={{0,6},{1,123},{2,8},{3,125},{4,10},{5,127},{6,12},{7,1},{8,14},{9,... | collective-permute-start | bytes 663560 | tf_op jit(solution)/shard_map/ppermute | solution.py:478
  45.9 1.8 %collective-permute-start.9 = (f32[5,72,256]{2,1,0:T(8,128)S(1)}, f32[5,72,256]{2,1,0:T(8,128)S(1)}, u32[]{:S(2)}, u32[]{:S(2)}) collective-permute-start(f32[5,72,256]{2,1,0:T(8,128)S(1)} %pad_maximum_fusion.1), channel_id=1, source_target_pairs={{0,1},{1,0},{2,3},{3,2},{4,5},{5,4},{6,7},{7,6},{8,9},{9,8},{10,11... | collective-permute-start | bytes 1105928 | tf_op jit(solution)/shard_map/ppermute | solution.py:475
  52.9 1.9 %collective-permute-start.10 = (bf16[7,128,256]{2,1,0:T(8,128)(2,1)S(1)}, bf16[7,128,256]{2,1,0:T(8,128)(2,1)S(1)}, u32[]{:S(2)}, u32[]{:S(2)}) collective-permute-start(bf16[7,128,256]{2,1,0:T(8,128)(2,1)S(1)} %get-tuple-element.39), channel_id=1, source_target_pairs={{0,1},{1,0},{2,3},{3,2},{4,5},{5,4},{6,7},{7,6},{8,9},{9,8},{10,11... | collective-permute-start | bytes 1376264 | tf_op jit(solution)/shard_map/ppermute | solution.py:475
  54.9 19.1 %collective-permute-start.11 = (bf16[4,128,256]{2,1,0:T(8,128)(2,1)S(1)}, bf16[4,128,256]{2,1,0:T(8,128)(2,1)S(1)}, u32[]{:S(2)}, u32[]{:S(2)}) collective-permute-start(bf16[4,128,256]{2,1,0:T(8,128)(2,1)S(1)} %get-tuple-element.47), channel_id=1, source_target_pairs={{0,2},{1,127},{2,4},{3,1},{4,6},{5,3},{6,8},{7,5},{8,10},{9,7},{10... | collective-permute-start | bytes 786440 | tf_op jit(solution)/shard_map/ppermute | solution.py:478
  60.3 13.7 %collective-permute-start.12 = (bf16[4,128,256]{2,1,0:T(8,128)(2,1)S(1)}, bf16[4,128,256]{2,1,0:T(8,128)(2,1)S(1)}, u32[]{:S(2)}, u32[]{:S(2)}) collective-permute-start(bf16[4,128,256]{2,1,0:T(8,128)(2,1)S(1)} %get-tuple-element.46), channel_id=1, source_target_pairs={{0,4},{1,125},{2,6},{3,127},{4,8},{5,1},{6,10},{7,3},{8,12},{9,5},... | collective-permute-start | bytes 786440 | tf_op jit(solution)/shard_map/ppermute | solution.py:478
  60.3 13.6 %collective-permute-start.13 = (bf16[3,128,256]{2,1,0:T(8,128)(2,1)S(1)}, bf16[3,128,256]{2,1,0:T(8,128)(2,1)S(1)}, u32[]{:S(2)}, u32[]{:S(2)}) collective-permute-start(bf16[3,128,256]{2,1,0:T(8,128)(2,1)S(1)} %get-tuple-element.45), channel_id=1, source_target_pairs={{0,6},{1,123},{2,8},{3,125},{4,10},{5,127},{6,12},{7,1},{8,14},{9,... | collective-permute-start | bytes 589832 | tf_op jit(solution)/shard_map/ppermute | solution.py:478
  74.0 1.7 %collective-permute-start.14 = (bf16[5,128,256]{2,1,0:T(8,128)(2,1)S(1)}, bf16[5,128,256]{2,1,0:T(8,128)(2,1)S(1)}, u32[]{:S(2)}, u32[]{:S(2)}) collective-permute-start(bf16[5,128,256]{2,1,0:T(8,128)(2,1)S(1)} %pad_maximum_fusion.2), channel_id=1, source_target_pairs={{0,1},{1,0},{2,3},{3,2},{4,5},{5,4},{6,7},{7,6},{8,9},{9,8},{10,11... | collective-permute-start | bytes 983048 | tf_op jit(solution)/shard_map/ppermute | solution.py:475

commit v3 on v2

--- a/solution.py
+++ b/solution.py
@@ -307,14 +307,12 @@
 STRIP = 16
 
 
-def back_second(
-    plan, partial, r1, r2, r3, post, got, near, left, right,
+def image_first(
+    partial, r1, r2, r3, post, got,
     image, rounded, wanted, m1, m2, m3, give,
-    own, acc, draft, sem,
+    draft, sem,
 ):
     ins = (r1, r2, r3, post, got)
-    own[CL] = jnp.zeros((RHS, B), BF16)
-    acc[...] = jnp.zeros_like(acc)
     places = [place_in(rho) for rho in range(PEERS)]
     marks = [ins[message][index, RHS : RHS + 1] for message, index in places]
     lane = lax.broadcasted_iota(jnp.int32, (1, SLOTS), 1)
@@ -334,32 +332,52 @@
                 totals[cluster] += jnp.where(mark == float(cluster), block, 0.0)
         for cluster in range(CL):
             image[rows, cluster * B : (cluster + 1) * B] = totals[cluster]
-            own[cluster, rows] = totals[cluster].astype(BF16)
             rounded[cluster, rows] = totals[cluster].astype(BF16)
+    copy.wait()
+    outs = (m1, m2, m3, give)
+    for rho in range(PEERS):
+        message, index = place_out(rho)
+        outs[message][index] = rounded[wanted[0, rho]]
+
+
+def back_second(
+    plan, rounded, near, left, right,
+    m1, m2, m3, give,
+    own, acc,
+):
+    own[0:CL] = rounded[...]
+    own[CL] = jnp.zeros((RHS, B), BF16)
+    acc[...] = jnp.zeros_like(acc)
     back_products(Blocks(plan, near, left, right), own, acc)
     outs = (m1, m2, m3, give)
-    copy.wait()
     for rho in range(PEERS):
         message, index = place_out(rho)
-        outs[message][index, 0:RHS] = acc[rho].astype(BF16)
-        outs[message][index, RHS:] = own[wanted[0, rho]]
+        outs[message][index] = acc[rho].astype(BF16)
 
 
 def forward_second(
-    plan, wanted, own, r1, r2, r3, post, got, diag, near, left, right,
-    image,
+    plan, own, r1, r2, r3, post, got, diag, near, left, right,
+    out,
     fetched, turned, acc, acc_turned,
 ):
     ins = (r1, r2, r3, post, got)
+    for rho in range(PEERS):
+        message, index = place_in(rho)
+        fetched[rho] = ins[message][index]
     fetched[DEAD] = jnp.zeros((RHS, B), BF16)
     acc[CL] = jnp.zeros((RHS, B), F32)
     for cluster in range(CL):
         acc[cluster] = dot_t(own[cluster], diag[cluster])
+    forward_products(Blocks(plan, near, left, right), fetched, turned, acc, acc_turned)
+    out[...] = acc[0:CL]
+
+
+def image_second(partial, wanted, r1, r2, r3, post, got, image, acc):
+    ins = (r1, r2, r3, post, got)
+    acc[...] = partial[...]
     for rho in range(PEERS):
         message, index = place_in(rho)
-        fetched[rho] = ins[message][index, RHS:]
-        acc[wanted[0, rho]] += ins[message][index, 0:RHS].astype(F32)
-    forward_products(Blocks(plan, near, left, right), fetched, turned, acc, acc_turned)
+        acc[wanted[0, rho]] += ins[message][index].astype(F32)
     for cluster in range(CL):
         image[:, cluster * B : (cluster + 1) * B] = acc[cluster]
 
@@ -429,30 +447,44 @@
 
 def k3(*args):
     return call(
-        back_second, "image_and_transposed_products",
+        image_first, "first_image",
         [
             shaped((RHS, CL * B), F32),
             shaped((CL, RHS, B), BF16),
             shaped((1, SLOTS), jnp.int32),
         ]
-        + message_shapes(2 * RHS, BF16),
+        + message_shapes(RHS, BF16),
         [VMEM] * 2 + [SMEM] + [VMEM] * 4,
-        [SMEM] + [VMEM] * 9,
-        [
-            pltpu.VMEM((CL + 1, RHS, B), BF16),
-            pltpu.VMEM((PEERS + 1, RHS, B), F32),
-            pltpu.VMEM((1, SLOTS), jnp.int32),
-            pltpu.SemaphoreType.DMA,
-        ],
+        [VMEM] * 6,
+        [pltpu.VMEM((1, SLOTS), jnp.int32), pltpu.SemaphoreType.DMA],
     )(*args)
 
 
 def k4(*args):
     return call(
-        forward_second, "second_image",
+        back_second, "second_transposed_products",
+        message_shapes(RHS, BF16),
+        [VMEM] * 4,
+        [SMEM] + [VMEM] * 4,
+        [pltpu.VMEM((CL + 1, RHS, B), BF16), pltpu.VMEM((PEERS + 1, RHS, B), F32)],
+    )(*args)
+
+
+def k5(*args):
+    return call(
+        forward_second, "second_forward_products",
+        shaped((CL, RHS, B), F32), VMEM,
+        [SMEM] + [VMEM] * 10,
+        forward_scratch(),
+    )(*args)
+
+
+def k6(*args):
+    return call(
+        image_second, "second_image",
         shaped((RHS, CL * B), F32), VMEM,
-        [SMEM] * 2 + [VMEM] * 10,
-        forward_scratch(),
+        [VMEM, SMEM] + [VMEM] * 5,
+        [pltpu.VMEM((CL, RHS, B), F32)],
     )(*args)
 
 
@@ -497,17 +529,25 @@
     m1, m2, m3, give, plan, *held = k1(
         me, *lists, in_hbm(counts), both, in_hbm(near_blocks), in_hbm(far_left), in_hbm(far_right)
     )
+    halo, m1 = lax.optimization_barrier((halo, m1))
     r1, r2, r3, got, messages = exchange(m1, m2, m3, give)
     halo_post = swap(jnp.concatenate([halo[0], halo[1], halo[2][1:]]))
     halo_post, messages = lax.optimization_barrier((halo_post, messages))
     partial = k2(plan, both, *halo, halo_post, diag_blocks, *held)
     partial, r1, r2, r3 = lax.optimization_barrier((partial, r1, r2, r3))
     post = passed_on(r1, r2, r3)
-    first_image, rounded, wanted, m1, m2, m3, give = k3(plan, partial, r1, r2, r3, post, got, *held)
+    first_image, rounded, wanted, m1, m2, m3, give = k3(partial, r1, r2, r3, post, got)
+    f1, f2, f3, f_got, messages = exchange(m1, m2, m3, give)
+    rounded, messages = lax.optimization_barrier((rounded, messages))
+    m1, m2, m3, give = k4(plan, rounded, *held)
+    f1, f2, f3, m1 = lax.optimization_barrier((f1, f2, f3, m1))
     r1, r2, r3, got, messages = exchange(m1, m2, m3, give)
+    f_post = passed_on(f1, f2, f3)
+    f_post, messages = lax.optimization_barrier((f_post, messages))
+    partial = k5(plan, rounded, f1, f2, f3, f_post, f_got, diag_blocks, *held)
+    partial, r1, r2, r3 = lax.optimization_barrier((partial, r1, r2, r3))
     post = passed_on(r1, r2, r3)
-    second_image = k4(plan, wanted, rounded, r1, r2, r3, post, got, diag_blocks, *held)
-    return first_image, second_image
+    return first_image, k6(partial, wanted, r1, r2, r3, post, got)
 
 
 def solution(mesh):

time: 80.9 us -> 84.8 us (1.048); the launches traced: 82.4 us -> 84.3 us
  starting transfers between devices: 22.6 us -> 34 us
  waiting for transfers between devices: 32.9 us -> 22.4 us
  Pallas kernels: 24.8 us -> 25.8 us
    ppermute x9 -> x12, waiting for transfers between devices: 26.6 us -> 16.8 us  [carry(): return lax.ppermute(block, 'rows', carriers(size, k))]
    ppermute x9 -> x12, starting transfers between devices: 20.7 us -> 28.3 us  [carry(): return lax.ppermute(block, 'rows', carriers(size, k))]
    ppermute x6 -> x8, starting transfers between devices: 1.93 us -> 5.76 us  [swap(): return lax.ppermute(block, 'rows', [(i, i ^ 1) for i in range(size)])]
    pallas_call x2 -> x4, Pallas kernels: 11.9 us -> 13 us  [the longest x1 5.88 us: k5(): call(forward_second, 'second_forward_products', shaped((CL, RHS, B), F32)...]
    ppermute x6 -> x8, waiting for transfers between devices: 6.3 us -> 5.62 us  [swap(): return lax.ppermute(block, 'rows', [(i, i ^ 1) for i in range(size)])]
  transfers between devices with their start and end apart: 15 -> 20, of which waited for: 8 -> 9; matrix products, arithmetic and copies ran while one was open for 0% -> 0% of each run, Pallas kernels for 16% -> 27%
where the time goes in v3:
time: 84.8 us; the launch traced here: 84.3 us
  starting transfers between devices  34 us (40%)
  Pallas kernels  25.8 us (30%)
  waiting for transfers between devices  22.4 us (26%)
  other arithmetic  1.09 us (1%)
  between operations  0.86 us (1%)
    ppermute x12, starting transfers between devices, carry(): return lax.ppermute(block, 'rows', carriers(size, k))  28.3 us
    ppermute x12, waiting for transfers between devices, carry(): return lax.ppermute(block, 'rows', carriers(size, k))  16.8 us
    pallas_call x1, Pallas kernels, k1(): call(back_first, 'transposed_products', message_shapes(RHS + EXTRA, F32)...  6.97 us
    pallas_call x1, Pallas kernels, k2(): call(forward_first, 'forward_products', shaped((CL, RHS, B), F32), VMEM,...  5.89 us
    pallas_call x1, Pallas kernels, k5(): call(forward_second, 'second_forward_products', shaped((CL, RHS, B), F32)...  5.88 us
    ppermute x8, starting transfers between devices, swap(): return lax.ppermute(block, 'rows', [(i, i ^ 1) for i in range(size)])  5.76 us
    ppermute x8, waiting for transfers between devices, swap(): return lax.ppermute(block, 'rows', [(i, i ^ 1) for i in range(size)])  5.62 us
    pallas_call x1, Pallas kernels, k4(): call(back_second, 'second_transposed_products', message_shapes(RHS, BF16)...  4.41 us
  transfers between devices with their start and end apart: 20, of which 9 were waited for; matrix products, arithmetic and copies ran while one was open for 0% of the time, Pallas kernels for 27%

profile of v3, /device:TPU:1, one launch (start us, length us, event | category | flops | bytes accessed | tf_op | source)
XLA Modules:
  0.0 84.3 jit_solution(1274811869896033415)
XLA Ops:
  0.6 1.5 %collective-permute-start = (bf16[64,1024]{1,0:T(8,128)(2,1)}, bf16[64,1024]{1,0:T(8,128)(2,1)S(1)}, u32[]{:S(2)}, u32[]{:S(2)}) collective-permute-start(bf16[64,1024]{1,0:T(8,128)(2,1)} %param.10), channel_id=1, source_target_pairs={{0,1},{1,0},{2,3},{3,2},{4,5},{5,4},{6,7},{7,6},{8,9},{9,8},{10,11... | collective-permute-start | bytes 393224 | tf_op jit(solution)/shard_map/ppermute | solution.py:507
  2.1 1.2 %collective-permute-done = bf16[64,1024]{1,0:T(8,128)(2,1)S(1)} collective-permute-done((bf16[64,1024]{1,0:T(8,128)(2,1)}, bf16[64,1024]{1,0:T(8,128)(2,1)S(1)}, u32[]{:S(2)}, u32[]{:S(2)}) %collective-permute-start) | collective-permute-done | bytes 131104 | tf_op jit(solution)/shard_map/ppermute | solution.py:507
  3.3 0.9 %pad_maximum_fusion.2.both = bf16[2,64,1024]{2,1,0:T(8,128)(2,1)S(1)} fusion(bf16[1,64,1024]{2,1,0:T(8,128)(2,1)S(1)} %bitcast.8, bf16[1,64,1024]{2,1,0:T(8,128)(2,1)} %bitcast.7), kind=kLoop, calls=%fused_computation.2 | loop fusion | flops 131072 | bytes 524288 | tf_op jit(solution)/shard_map/stack | solution.py:527
  4.3 8.6 %collective-permute-start.1 = (bf16[2,64,1024]{2,1,0:T(8,128)(2,1)S(1)}, bf16[2,64,1024]{2,1,0:T(8,128)(2,1)S(1)}, u32[]{:S(2)}, u32[]{:S(2)}) collective-permute-start(bf16[2,64,1024]{2,1,0:T(8,128)(2,1)S(1)} %pad_maximum_fusion.2.both), channel_id=1, source_target_pairs={{0,2},{1,127},{2,4},{3,1},{4,6},{5,3},{6,8},{7,5},{8,10},{9,7},{10... | collective-permute-start | bytes 786440 | tf_op jit(solution)/shard_map/ppermute | solution.py:510
  12.8 0.0 collective-permute-start.2
  12.8 0.9 %collective-permute-start.3 = (bf16[2,64,1024]{2,1,0:T(8,128)(2,1)S(1)}, bf16[2,64,1024]{2,1,0:T(8,128)(2,1)S(1)}, u32[]{:S(2)}, u32[]{:S(2)}) collective-permute-start(bf16[2,64,1024]{2,1,0:T(8,128)(2,1)S(1)} %pad_maximum_fusion.2.both), channel_id=1, source_target_pairs={{0,6},{1,123},{2,8},{3,125},{4,10},{5,127},{6,12},{7,1},{8,14},{9,... | collective-permute-start | bytes 786440 | tf_op jit(solution)/shard_map/ppermute | solution.py:510
  13.7 7.0 %transposed_products.1 = (f32[4,72,256]{2,1,0:T(8,128)S(1)}, f32[4,72,256]{2,1,0:T(8,128)S(1)}, f32[3,72,256]{2,1,0:T(8,128)S(1)}, f32[7,72,256]{2,1,0:T(8,128)S...) custom-call(s32[1]{0:T(128)} %bitcast.me, ...), custom_call_target="tpu_custom_call" | custom-call | flops 2000000000 | bytes 22000000 | tf_op jit(solution)/shard_map/transposed_products/pallas_call | solution.py:414
  20.7 0.0 copy-start
  20.7 0.1 collective-permute-start.5
  20.8 0.0 collective-permute-done.1.h1
  20.8 2.8 %collective-permute-done.2.h2 = bf16[2,64,1024]{2,1,0:T(8,128)(2,1)S(1)} collective-permute-done((bf16[2,64,1024]{2,1,0:T(8,128)(2,1)S(1)}, bf16[2,64,1024]{2,1,0:T(8,128)(2,1)S(1)}, u32[]{:S(2)}, u32[]{:S(2)}) %collective-permute-start.2) | collective-permute-done | bytes 262176 | tf_op jit(solution)/shard_map/ppermute | solution.py:510
  23.6 1.9 %collective-permute-done.3.h3 = bf16[2,64,1024]{2,1,0:T(8,128)(2,1)S(1)} collective-permute-done((bf16[2,64,1024]{2,1,0:T(8,128)(2,1)S(1)}, bf16[2,64,1024]{2,1,0:T(8,128)(2,1)S(1)}, u32[]{:S(2)}, u32[]{:S(2)}) %collective-permute-start.3) | collective-permute-done | bytes 262176 | tf_op jit(solution)/shard_map/ppermute | solution.py:510
  25.6 0.1 pad_maximum_fusion
  25.6 0.1 collective-permute-start.4
  25.7 0.0 collective-permute-done.5.got
  25.8 4.1 %collective-permute-start.6 = (f32[4,72,256]{2,1,0:T(8,128)S(1)}, f32[4,72,256]{2,1,0:T(8,128)S(1)}, u32[]{:S(2)}, u32[]{:S(2)}) collective-permute-start(f32[4,72,256]{2,1,0:T(8,128)S(1)} %get-tuple-element.80), channel_id=1, source_target_pairs={{0,2},{1,127},{2,4},{3,1},{4,6},{5,3},{6,8},{7,5},{8,10},{9,7},{10... | collective-permute-start | bytes 884744 | tf_op jit(solution)/shard_map/ppermute | solution.py:510
  29.9 2.5 %collective-permute-start.7 = (f32[4,72,256]{2,1,0:T(8,128)S(1)}, f32[4,72,256]{2,1,0:T(8,128)S(1)}, u32[]{:S(2)}, u32[]{:S(2)}) collective-permute-start(f32[4,72,256]{2,1,0:T(8,128)S(1)} %get-tuple-element.79), channel_id=1, source_target_pairs={{0,4},{1,125},{2,6},{3,127},{4,8},{5,1},{6,10},{7,3},{8,12},{9,5},... | collective-permute-start | bytes 884744 | tf_op jit(solution)/shard_map/ppermute | solution.py:510
  32.4 0.0 collective-permute-start.8
  32.4 0.0 collective-permute-done.4.post
  32.4 5.9 %forward_products.1.partial = f32[4,64,256]{2,1,0:T(8,128)S(1)} custom-call(s32[4,256]{1,0:T(4,128)S(1)} %get-tuple-element.40.plan, bf16[2,64,1024]{2,1,0:T(8,128)(2,1)S(1)} %pad_maximum_fusion.2.both, bf16[2,64,1024]{2,1,0:T(8,128)(2,1)S(1)} %collective-permute-done.1.h1, bf16[2,64,1024]{2,1,0:T(8,128)(2,1)S(1)} %collective-permute-done.2.h2, ...), custom_call_target="tpu_custom_call" | custom-call | flops 2000000000 | bytes 22000000 | tf_op jit(solution)/shard_map/forward_products/pallas_call | solution.py:440
  38.3 8.1 %collective-permute-done.8.r3 = f32[3,72,256]{2,1,0:T(8,128)S(1)} collective-permute-done((f32[3,72,256]{2,1,0:T(8,128)S(1)}, f32[3,72,256]{2,1,0:T(8,128)S(1)}, u32[]{:S(2)}, u32[]{:S(2)}) %collective-permute-start.8) | collective-permute-done | bytes 221216 | tf_op jit(solution)/shard_map/ppermute | solution.py:510
  46.4 0.0 collective-permute-done.6.r1
  46.4 0.0 collective-permute-done.7.r2
  46.5 0.1 collective-permute-start.9
  46.6 1.7 %collective-permute-done.9.post = f32[5,72,256]{2,1,0:T(8,128)S(1)} collective-permute-done((f32[5,72,256]{2,1,0:T(8,128)S(1)}, f32[5,72,256]{2,1,0:T(8,128)S(1)}, u32[]{:S(2)}, u32[]{:S(2)}) %collective-permute-start.9) | collective-permute-done | bytes 368672 | tf_op jit(solution)/shard_map/ppermute | solution.py:507
  48.3 1.3 %first_image.1 = (f32[64,1024]{1,0:T(8,128)}, bf16[4,64,256]{2,1,0:T(8,128)(2,1)S(1)}, s32[1,128]{1,0:T(1,128)S(1)}, bf16[4,64,256]{2,1,0:T(8,128)(2,1)S(1)}, bf...) custom-call(f32[4,64,256]{2,1,0:T(8,128)S(1)} %forward_products.1.partial, ...), custom_call_target="tpu_custom_call" | custom-call | flops 2000000000 | bytes 22000000 | tf_op jit(solution)/shard_map/first_image/pallas_call | solution.py:449
  49.6 0.2 collective-permute-start.10
  49.8 1.4 %collective-permute-done.10.got = bf16[7,64,256]{2,1,0:T(8,128)(2,1)S(1)} collective-permute-done((bf16[7,64,256]{2,1,0:T(8,128)(2,1)S(1)}, bf16[7,64,256]{2,1,0:T(8,128)(2,1)S(1)}, u32[]{:S(2)}, u32[]{:S(2)}) %collective-permute-start.10) | collective-permute-done | bytes 229408 | tf_op jit(solution)/shard_map/ppermute | solution.py:507
  51.2 3.4 %collective-permute-start.11 = (bf16[4,64,256]{2,1,0:T(8,128)(2,1)S(1)}, bf16[4,64,256]{2,1,0:T(8,128)(2,1)S(1)}, u32[]{:S(2)}, u32[]{:S(2)}) collective-permute-start(bf16[4,64,256]{2,1,0:T(8,128)(2,1)S(1)} %get-tuple-element.86), channel_id=1, source_target_pairs={{0,2},{1,127},{2,4},{3,1},{4,6},{5,3},{6,8},{7,5},{8,10},{9,7},{10... | collective-permute-start | bytes 393224 | tf_op jit(solution)/shard_map/ppermute | solution.py:510
  54.6 0.3 collective-permute-start.12
  54.9 4.4 %second_transposed_products.1 = (bf16[4,64,256]{2,1,0:T(8,128)(2,1)S(1)}, bf16[4,64,256]{2,1,0:T(8,128)(2,1)S(1)}, bf16[3,64,256]{2,1,0:T(8,128)(2,1)S(1)}, bf16[7,64,256]{2,1,0:T(8,128)(2,1)S(1)}) custom-call(s32[4,256]{1,0:T(4,128)S(1)} %get-tuple-element.40.plan, bf16[4,64,256]{2,1,0:T(8,128)(2,1)S(1)} %get-tuple-element.63.rounded.own, ...), custom_call_target="tpu_custom_call" | custom-call | flops 2000000000 | bytes 22000000 | tf_op jit(solution)/shard_map/second_transposed_products/pallas_call | solution.py:464
  59.3 0.1 collective-permute-start.15
  59.4 4.2 %collective-permute-start.13 = (bf16[3,64,256]{2,1,0:T(8,128)(2,1)S(1)}, bf16[3,64,256]{2,1,0:T(8,128)(2,1)S(1)}, u32[]{:S(2)}, u32[]{:S(2)}) collective-permute-start(bf16[3,64,256]{2,1,0:T(8,128)(2,1)S(1)} %get-tuple-element.84), channel_id=1, source_target_pairs={{0,6},{1,123},{2,8},{3,125},{4,10},{5,127},{6,12},{7,1},{8,14},{9,... | collective-permute-start | bytes 294920 | tf_op jit(solution)/shard_map/ppermute | solution.py:510
  63.5 1.6 %collective-permute-done.13.r3 = bf16[3,64,256]{2,1,0:T(8,128)(2,1)S(1)} collective-permute-done((bf16[3,64,256]{2,1,0:T(8,128)(2,1)S(1)}, bf16[3,64,256]{2,1,0:T(8,128)(2,1)S(1)}, u32[]{:S(2)}, u32[]{:S(2)}) %collective-permute-start.13) | collective-permute-done | bytes 98336 | tf_op jit(solution)/shard_map/ppermute | solution.py:510
  65.2 0.0 collective-permute-done.11.r1
  65.2 0.0 collective-permute-done.12.r2
  65.2 3.6 %collective-permute-start.14 = (bf16[5,64,256]{2,1,0:T(8,128)(2,1)S(1)}, bf16[5,64,256]{2,1,0:T(8,128)(2,1)S(1)}, u32[]{:S(2)}, u32[]{:S(2)}) collective-permute-start(bf16[5,64,256]{2,1,0:T(8,128)(2,1)S(1)} %pad_maximum_fusion.3), channel_id=1, source_target_pairs={{0,1},{1,0},{2,3},{3,2},{4,5},{5,4},{6,7},{7,6},{8,9},{9,8},{10,11... | collective-permute-start | bytes 491528 | tf_op jit(solution)/shard_map/ppermute | solution.py:507
  68.9 0.0 collective-permute-done.15.got
  68.9 2.4 %collective-permute-start.16 = (bf16[4,64,256]{2,1,0:T(8,128)(2,1)S(1)}, bf16[4,64,256]{2,1,0:T(8,128)(2,1)S(1)}, u32[]{:S(2)}, u32[]{:S(2)}) collective-permute-start(bf16[4,64,256]{2,1,0:T(8,128)(2,1)S(1)} %get-tuple-element.83), channel_id=1, source_target_pairs={{0,2},{1,127},{2,4},{3,1},{4,6},{5,3},{6,8},{7,5},{8,10},{9,7},{10... | collective-permute-start | bytes 393224 | tf_op jit(solution)/shard_map/ppermute | solution.py:510
  71.3 2.0 %collective-permute-start.17 = (bf16[4,64,256]{2,1,0:T(8,128)(2,1)S(1)}, bf16[4,64,256]{2,1,0:T(8,128)(2,1)S(1)}, u32[]{:S(2)}, u32[]{:S(2)}) collective-permute-start(bf16[4,64,256]{2,1,0:T(8,128)(2,1)S(1)} %get-tuple-element.82), channel_id=1, source_target_pairs={{0,4},{1,125},{2,6},{3,127},{4,8},{5,1},{6,10},{7,3},{8,12},{9,5},... | collective-permute-start | bytes 393224 | tf_op jit(solution)/shard_map/ppermute | solution.py:510
  73.3 0.0 collective-permute-start.18
  73.3 0.0 collective-permute-done.14.post
  73.3 5.9 %second_forward_products.1.partial = f32[4,64,256]{2,1,0:T(8,128)S(1)} custom-call(s32[4,256]{1,0:T(4,128)S(1)} %get-tuple-element.40.plan, bf16[4,64,256]{2,1,0:T(8,128)(2,1)S(1)} %get-tuple-element.63.rounded.own, bf16[4,64,256]{2,1,0:T(8,128)(2,1)S(1)} %collective-permute-done.11.r1, bf16[4,64,256]{2,1,0:T(8,128)(2,1)S(1)} %collective-permute-done.12.r2, ...), custom_call_target="tpu_custom_call" | custom-call | flops 2000000000 | bytes 22000000 | tf_op jit(solution)/shard_map/second_forward_products/pallas_call | solution.py:474
  79.2 2.2 %collective-permute-done.18.r3 = bf16[3,64,256]{2,1,0:T(8,128)(2,1)S(1)} collective-permute-done((bf16[3,64,256]{2,1,0:T(8,128)(2,1)S(1)}, bf16[3,64,256]{2,1,0:T(8,128)(2,1)S(1)}, u32[]{:S(2)}, u32[]{:S(2)}) %collective-permute-start.18) | collective-permute-done | bytes 98336 | tf_op jit(solution)/shard_map/ppermute | solution.py:510
  81.4 0.0 collective-permute-done.16.r1
  81.5 0.1 collective-permute-start.19
  81.6 1.4 %collective-permute-done.19.post = bf16[5,64,256]{2,1,0:T(8,128)(2,1)S(1)} collective-permute-done((bf16[5,64,256]{2,1,0:T(8,128)(2,1)S(1)}, bf16[5,64,256]{2,1,0:T(8,128)(2,1)S(1)}, u32[]{:S(2)}, u32[]{:S(2)}) %collective-permute-start.19) | collective-permute-done | bytes 163872 | tf_op jit(solution)/shard_map/ppermute | solution.py:507
  83.0 1.4 %second_image.1 = f32[64,1024]{1,0:T(8,128)} custom-call(f32[4,64,256]{2,1,0:T(8,128)S(1)} %second_forward_products.1.partial, s32[1,128]{1,0:T(1,128)S(1)} %get-tuple-element.74.wanted, bf16[4,64,256]{2,1,0:T(8,128)(2,1)S(1)} %collective-permute-done.16.r1, bf16[4,64,256]{2,1,0:T(8,128)(2,1)S(1)} %collective-permute-done.17.r2, ...), custom_call_target="tpu_custom_call" | custom-call | flops 2000000000 | bytes 22000000 | tf_op jit(solution)/shard_map/second_image/pallas_call | solution.py:483
  (18 shorter events, 0.2 us)
Async XLA Ops:
  0.6 2.7 %collective-permute-start = (bf16[64,1024]{1,0:T(8,128)(2,1)}, bf16[64,1024]{1,0:T(8,128)(2,1)S(1)}, u32[]{:S(2)}, u32[]{:S(2)}) collective-permute-start(bf16[64,1024]{1,0:T(8,128)(2,1)} %param.10), channel_id=1, source_target_pairs={{0,1},{1,0},{2,3},{3,2},{4,5},{5,4},{6,7},{7,6},{8,9},{9,8},{10,11... | collective-permute-start | bytes 393224 | tf_op jit(solution)/shard_map/ppermute | solution.py:507
  4.3 16.5 %collective-permute-start.1 = (bf16[2,64,1024]{2,1,0:T(8,128)(2,1)S(1)}, bf16[2,64,1024]{2,1,0:T(8,128)(2,1)S(1)}, u32[]{:S(2)}, u32[]{:S(2)}) collective-permute-start(bf16[2,64,1024]{2,1,0:T(8,128)(2,1)S(1)} %pad_maximum_fusion.2.both), channel_id=1, source_target_pairs={{0,2},{1,127},{2,4},{3,1},{4,6},{5,3},{6,8},{7,5},{8,10},{9,7},{10... | collective-permute-start | bytes 786440 | tf_op jit(solution)/shard_map/ppermute | solution.py:510
  12.8 10.8 %collective-permute-start.2 = (bf16[2,64,1024]{2,1,0:T(8,128)(2,1)S(1)}, bf16[2,64,1024]{2,1,0:T(8,128)(2,1)S(1)}, u32[]{:S(2)}, u32[]{:S(2)}) collective-permute-start(bf16[2,64,1024]{2,1,0:T(8,128)(2,1)S(1)} %pad_maximum_fusion.2.both), channel_id=1, source_target_pairs={{0,4},{1,125},{2,6},{3,127},{4,8},{5,1},{6,10},{7,3},{8,12},{9,5},... | collective-permute-start | bytes 786440 | tf_op jit(solution)/shard_map/ppermute | solution.py:510
  12.8 12.7 %collective-permute-start.3 = (bf16[2,64,1024]{2,1,0:T(8,128)(2,1)S(1)}, bf16[2,64,1024]{2,1,0:T(8,128)(2,1)S(1)}, u32[]{:S(2)}, u32[]{:S(2)}) collective-permute-start(bf16[2,64,1024]{2,1,0:T(8,128)(2,1)S(1)} %pad_maximum_fusion.2.both), channel_id=1, source_target_pairs={{0,6},{1,123},{2,8},{3,125},{4,10},{5,127},{6,12},{7,1},{8,14},{9,... | collective-permute-start | bytes 786440 | tf_op jit(solution)/shard_map/ppermute | solution.py:510
  20.7 11.7 %copy-start = (bf16[4,256,256]{2,1,0:T(8,128)(2,1)S(1)}, bf16[4,256,256]{2,1,0:T(8,128)(2,1)}, u32[]{:S(2)}) copy-start(bf16[4,256,256]{2,1,0:T(8,128)(2,1)} %diag.3) | copy-start | bytes 1572868
  20.7 5.1 %collective-permute-start.5 = (f32[7,72,256]{2,1,0:T(8,128)S(1)}, f32[7,72,256]{2,1,0:T(8,128)S(1)}, u32[]{:S(2)}, u32[]{:S(2)}) collective-permute-start(f32[7,72,256]{2,1,0:T(8,128)S(1)} %get-tuple-element.46), channel_id=1, source_target_pairs={{0,1},{1,0},{2,3},{3,2},{4,5},{5,4},{6,7},{7,6},{8,9},{9,8},{10,11... | collective-permute-start | bytes 1548296 | tf_op jit(solution)/shard_map/ppermute | solution.py:507
  25.6 6.8 %collective-permute-start.4 = (bf16[5,64,1024]{2,1,0:T(8,128)(2,1)S(1)}, bf16[5,64,1024]{2,1,0:T(8,128)(2,1)S(1)}, u32[]{:S(2)}, u32[]{:S(2)}) collective-permute-start(bf16[5,64,1024]{2,1,0:T(8,128)(2,1)S(1)} %pad_maximum_fusion), channel_id=1, source_target_pairs={{0,1},{1,0},{2,3},{3,2},{4,5},{5,4},{6,7},{7,6},{8,9},{9,8},{10,11... | collective-permute-start | bytes 1966088 | tf_op jit(solution)/shard_map/ppermute | solution.py:507
  25.8 20.6 %collective-permute-start.6 = (f32[4,72,256]{2,1,0:T(8,128)S(1)}, f32[4,72,256]{2,1,0:T(8,128)S(1)}, u32[]{:S(2)}, u32[]{:S(2)}) collective-permute-start(f32[4,72,256]{2,1,0:T(8,128)S(1)} %get-tuple-element.80), channel_id=1, source_target_pairs={{0,2},{1,127},{2,4},{3,1},{4,6},{5,3},{6,8},{7,5},{8,10},{9,7},{10... | collective-permute-start | bytes 884744 | tf_op jit(solution)/shard_map/ppermute | solution.py:510
  29.9 16.6 %collective-permute-start.7 = (f32[4,72,256]{2,1,0:T(8,128)S(1)}, f32[4,72,256]{2,1,0:T(8,128)S(1)}, u32[]{:S(2)}, u32[]{:S(2)}) collective-permute-start(f32[4,72,256]{2,1,0:T(8,128)S(1)} %get-tuple-element.79), channel_id=1, source_target_pairs={{0,4},{1,125},{2,6},{3,127},{4,8},{5,1},{6,10},{7,3},{8,12},{9,5},... | collective-permute-start | bytes 884744 | tf_op jit(solution)/shard_map/ppermute | solution.py:510
  32.4 14.0 %collective-permute-start.8 = (f32[3,72,256]{2,1,0:T(8,128)S(1)}, f32[3,72,256]{2,1,0:T(8,128)S(1)}, u32[]{:S(2)}, u32[]{:S(2)}) collective-permute-start(f32[3,72,256]{2,1,0:T(8,128)S(1)} %get-tuple-element.78), channel_id=1, source_target_pairs={{0,6},{1,123},{2,8},{3,125},{4,10},{5,127},{6,12},{7,1},{8,14},{9,... | collective-permute-start | bytes 663560 | tf_op jit(solution)/shard_map/ppermute | solution.py:510
  46.5 1.8 %collective-permute-start.9 = (f32[5,72,256]{2,1,0:T(8,128)S(1)}, f32[5,72,256]{2,1,0:T(8,128)S(1)}, u32[]{:S(2)}, u32[]{:S(2)}) collective-permute-start(f32[5,72,256]{2,1,0:T(8,128)S(1)} %pad_maximum_fusion.1), channel_id=1, source_target_pairs={{0,1},{1,0},{2,3},{3,2},{4,5},{5,4},{6,7},{7,6},{8,9},{9,8},{10,11... | collective-permute-start | bytes 1105928 | tf_op jit(solution)/shard_map/ppermute | solution.py:507
  49.6 1.6 %collective-permute-start.10 = (bf16[7,64,256]{2,1,0:T(8,128)(2,1)S(1)}, bf16[7,64,256]{2,1,0:T(8,128)(2,1)S(1)}, u32[]{:S(2)}, u32[]{:S(2)}) collective-permute-start(bf16[7,64,256]{2,1,0:T(8,128)(2,1)S(1)} %get-tuple-element.60), channel_id=1, source_target_pairs={{0,1},{1,0},{2,3},{3,2},{4,5},{5,4},{6,7},{7,6},{8,9},{9,8},{10,11... | collective-permute-start | bytes 688136 | tf_op jit(solution)/shard_map/ppermute | solution.py:507
  51.2 14.0 %collective-permute-start.11 = (bf16[4,64,256]{2,1,0:T(8,128)(2,1)S(1)}, bf16[4,64,256]{2,1,0:T(8,128)(2,1)S(1)}, u32[]{:S(2)}, u32[]{:S(2)}) collective-permute-start(bf16[4,64,256]{2,1,0:T(8,128)(2,1)S(1)} %get-tuple-element.86), channel_id=1, source_target_pairs={{0,2},{1,127},{2,4},{3,1},{4,6},{5,3},{6,8},{7,5},{8,10},{9,7},{10... | collective-permute-start | bytes 393224 | tf_op jit(solution)/shard_map/ppermute | solution.py:510
  54.6 10.6 %collective-permute-start.12 = (bf16[4,64,256]{2,1,0:T(8,128)(2,1)S(1)}, bf16[4,64,256]{2,1,0:T(8,128)(2,1)S(1)}, u32[]{:S(2)}, u32[]{:S(2)}) collective-permute-start(bf16[4,64,256]{2,1,0:T(8,128)(2,1)S(1)} %get-tuple-element.85), channel_id=1, source_target_pairs={{0,4},{1,125},{2,6},{3,127},{4,8},{5,1},{6,10},{7,3},{8,12},{9,5},... | collective-permute-start | bytes 393224 | tf_op jit(solution)/shard_map/ppermute | solution.py:510
  59.3 9.6 %collective-permute-start.15 = (bf16[7,64,256]{2,1,0:T(8,128)(2,1)S(1)}, bf16[7,64,256]{2,1,0:T(8,128)(2,1)S(1)}, u32[]{:S(2)}, u32[]{:S(2)}) collective-permute-start(bf16[7,64,256]{2,1,0:T(8,128)(2,1)S(1)} %get-tuple-element.69), channel_id=1, source_target_pairs={{0,1},{1,0},{2,3},{3,2},{4,5},{5,4},{6,7},{7,6},{8,9},{9,8},{10,11... | collective-permute-start | bytes 688136 | tf_op jit(solution)/shard_map/ppermute | solution.py:507
  59.4 5.8 %collective-permute-start.13 = (bf16[3,64,256]{2,1,0:T(8,128)(2,1)S(1)}, bf16[3,64,256]{2,1,0:T(8,128)(2,1)S(1)}, u32[]{:S(2)}, u32[]{:S(2)}) collective-permute-start(bf16[3,64,256]{2,1,0:T(8,128)(2,1)S(1)} %get-tuple-element.84), channel_id=1, source_target_pairs={{0,6},{1,123},{2,8},{3,125},{4,10},{5,127},{6,12},{7,1},{8,14},{9,... | collective-permute-start | bytes 294920 | tf_op jit(solution)/shard_map/ppermute | solution.py:510
  65.2 8.0 %collective-permute-start.14 = (bf16[5,64,256]{2,1,0:T(8,128)(2,1)S(1)}, bf16[5,64,256]{2,1,0:T(8,128)(2,1)S(1)}, u32[]{:S(2)}, u32[]{:S(2)}) collective-permute-start(bf16[5,64,256]{2,1,0:T(8,128)(2,1)S(1)} %pad_maximum_fusion.3), channel_id=1, source_target_pairs={{0,1},{1,0},{2,3},{3,2},{4,5},{5,4},{6,7},{7,6},{8,9},{9,8},{10,11... | collective-permute-start | bytes 491528 | tf_op jit(solution)/shard_map/ppermute | solution.py:507
  68.9 12.5 %collective-permute-start.16 = (bf16[4,64,256]{2,1,0:T(8,128)(2,1)S(1)}, bf16[4,64,256]{2,1,0:T(8,128)(2,1)S(1)}, u32[]{:S(2)}, u32[]{:S(2)}) collective-permute-start(bf16[4,64,256]{2,1,0:T(8,128)(2,1)S(1)} %get-tuple-element.83), channel_id=1, source_target_pairs={{0,2},{1,127},{2,4},{3,1},{4,6},{5,3},{6,8},{7,5},{8,10},{9,7},{10... | collective-permute-start | bytes 393224 | tf_op jit(solution)/shard_map/ppermute | solution.py:510
  71.3 10.1 %collective-permute-start.17 = (bf16[4,64,256]{2,1,0:T(8,128)(2,1)S(1)}, bf16[4,64,256]{2,1,0:T(8,128)(2,1)S(1)}, u32[]{:S(2)}, u32[]{:S(2)}) collective-permute-start(bf16[4,64,256]{2,1,0:T(8,128)(2,1)S(1)} %get-tuple-element.82), channel_id=1, source_target_pairs={{0,4},{1,125},{2,6},{3,127},{4,8},{5,1},{6,10},{7,3},{8,12},{9,5},... | collective-permute-start | bytes 393224 | tf_op jit(solution)/shard_map/ppermute | solution.py:510
  73.3 8.1 %collective-permute-start.18 = (bf16[3,64,256]{2,1,0:T(8,128)(2,1)S(1)}, bf16[3,64,256]{2,1,0:T(8,128)(2,1)S(1)}, u32[]{:S(2)}, u32[]{:S(2)}) collective-permute-start(bf16[3,64,256]{2,1,0:T(8,128)(2,1)S(1)} %get-tuple-element.81), channel_id=1, source_target_pairs={{0,6},{1,123},{2,8},{3,125},{4,10},{5,127},{6,12},{7,1},{8,14},{9,... | collective-permute-start | bytes 294920 | tf_op jit(solution)/shard_map/ppermute | solution.py:510
  81.5 1.5 %collective-permute-start.19 = (bf16[5,64,256]{2,1,0:T(8,128)(2,1)S(1)}, bf16[5,64,256]{2,1,0:T(8,128)(2,1)S(1)}, u32[]{:S(2)}, u32[]{:S(2)}) collective-permute-start(bf16[5,64,256]{2,1,0:T(8,128)(2,1)S(1)} %pad_maximum_fusion.4), channel_id=1, source_target_pairs={{0,1},{1,0},{2,3},{3,2},{4,5},{5,4},{6,7},{7,6},{8,9},{9,8},{10,11... | collective-permute-start | bytes 491528 | tf_op jit(solution)/shard_map/ppermute | solution.py:507

commit v4 on v3

--- a/solution.py
+++ b/solution.py
@@ -14,7 +14,10 @@
 HALF = B // 2
 PEERS = 12
 DEAD = 12
-EXTRA = 8
+EXTRA = 16
+LEVELS = 32766.0
+TINY = 2.0**-100
+LN2 = 0.6931471805599453
 QUAD = 4
 VMEM_BYTES = 16 * 2**20
 F32, BF16 = jnp.float32, jnp.bfloat16
@@ -277,8 +280,9 @@
     outs = (m1, m2, m3, give)
     for rho in range(PEERS):
         message, index = place_out(rho)
-        outs[message][index, 0:RHS] = acc[rho]
-        outs[message][index, RHS:] = jnp.full((EXTRA, B), plan[2, WANTED + rho].astype(F32), F32)
+        outs[message][index, 0:RHS], power = coded(acc[rho])
+        half = lax.broadcasted_iota(jnp.int32, (EXTRA, B), 0) < EXTRA // 2
+        outs[message][index, RHS:] = jnp.where(half, power, plan[2, WANTED + rho]).astype(jnp.int16)
 
 
 def forward_first(
@@ -307,6 +311,13 @@
 STRIP = 16
 
 
+def coded(block):
+    top = jnp.maximum(jnp.max(jnp.abs(block), axis=0, keepdims=True), TINY)
+    power = jnp.ceil(jnp.log(top * (1.0 / LEVELS)) * (1.0 / LN2) + 1e-3)
+    scaled = block * jnp.exp(power * -LN2)
+    return jnp.floor(scaled + 0.5).astype(jnp.int32).astype(jnp.int16), power.astype(jnp.int32)
+
+
 def image_first(
     partial, r1, r2, r3, post, got,
     image, rounded, wanted, m1, m2, m3, give,
@@ -314,22 +325,24 @@
 ):
     ins = (r1, r2, r3, post, got)
     places = [place_in(rho) for rho in range(PEERS)]
-    marks = [ins[message][index, RHS : RHS + 1] for message, index in places]
+    extras = [ins[message][index, RHS:].astype(jnp.int32) for message, index in places]
+    units = [jnp.exp(extra[0:1].astype(F32) * LN2) for extra in extras]
+    marks = [extra[EXTRA // 2 : EXTRA // 2 + 1] for extra in extras]
     lane = lax.broadcasted_iota(jnp.int32, (1, SLOTS), 1)
-    packed = jnp.zeros((1, SLOTS), F32)
+    packed = jnp.zeros((1, SLOTS), jnp.int32)
     for rho, mark in enumerate(marks):
         packed = jnp.where(lane == rho, mark[:, 0:SLOTS], packed)
-    draft[...] = packed.astype(jnp.int32)
+    draft[...] = packed
     copy = pltpu.make_async_copy(draft, wanted, sem)
     copy.start()
     for first in range(0, RHS, STRIP):
         rows = slice(first, first + STRIP)
         totals = [partial[cluster, rows] for cluster in range(CL)]
-        for (message, index), mark in zip(places, marks):
-            block = ins[message][index, rows]
+        for (message, index), mark, unit in zip(places, marks, units):
+            block = ins[message][index, rows].astype(jnp.int32).astype(F32) * unit
             mark = jnp.broadcast_to(mark, (STRIP, B))
             for cluster in range(CL):
-                totals[cluster] += jnp.where(mark == float(cluster), block, 0.0)
+                totals[cluster] += jnp.where(mark == cluster, block, 0.0)
         for cluster in range(CL):
             image[rows, cluster * B : (cluster + 1) * B] = totals[cluster]
             rounded[cluster, rows] = totals[cluster].astype(BF16)
@@ -413,7 +426,7 @@
     held = [pltpu.VMEM(shape, BF16) for shape in ((SLOTS, B, B), (SLOTS, K, B), (SLOTS, K, B))]
     return call(
         back_first, "transposed_products",
-        message_shapes(RHS + EXTRA, F32) + [shaped(PLAN, jnp.int32)] + held,
+        message_shapes(RHS + EXTRA, jnp.int16) + [shaped(PLAN, jnp.int32)] + held,
         [VMEM] * 4 + [SMEM] + [VMEM] * 3,
         [SMEM] + [HBM] * 5 + [VMEM] + [HBM] * 3,
         [
@@ -540,7 +553,7 @@
     f1, f2, f3, f_got, messages = exchange(m1, m2, m3, give)
     rounded, messages = lax.optimization_barrier((rounded, messages))
     m1, m2, m3, give = k4(plan, rounded, *held)
-    f1, f2, f3, m1 = lax.optimization_barrier((f1, f2, f3, m1))
+    f1, f2, f3, give = lax.optimization_barrier((f1, f2, f3, give))
     r1, r2, r3, got, messages = exchange(m1, m2, m3, give)
     f_post = passed_on(f1, f2, f3)
     f_post, messages = lax.optimization_barrier((f_post, messages))

time: 84.8 us -> 78.2 us (0.922)
  starting transfers between devices: 34 us -> 27.3 us
  waiting for transfers between devices: 22.4 us -> 24.8 us
  Pallas kernels: 25.8 us -> 23.9 us
    ppermute x12, starting transfers between devices: 28.3 us -> 24.2 us  [carry(): return lax.ppermute(block, 'rows', carriers(size, k))]
    ppermute x8, starting transfers between devices: 5.76 us -> 3.06 us  [swap(): return lax.ppermute(block, 'rows', [(i, i ^ 1) for i in range(size)])]
    ppermute x8, waiting for transfers between devices: 5.62 us -> 8.21 us  [swap(): return lax.ppermute(block, 'rows', [(i, i ^ 1) for i in range(size)])]
  transfers between devices with their start and end apart: 20 -> 20, of which waited for: 9 -> 11; matrix products, arithmetic and copies ran while one was open for 0% -> 0% of each run, Pallas kernels for 27% -> 27%
where the time goes in v4:
time: 78.2 us; the launch traced here: 78 us
  starting transfers between devices  27.3 us (35%)
  waiting for transfers between devices  24.8 us (32%)
  Pallas kernels  23.9 us (31%)
  other arithmetic  1.07 us (1%)
  between operations  0.83 us (1%)
    ppermute x12, starting transfers between devices, carry(): return lax.ppermute(block, 'rows', carriers(size, k))  24.2 us
    ppermute x12, waiting for transfers between devices, carry(): return lax.ppermute(block, 'rows', carriers(size, k))  16.6 us
    ppermute x8, waiting for transfers between devices, swap(): return lax.ppermute(block, 'rows', [(i, i ^ 1) for i in range(size)])  8.21 us
    pallas_call x1, Pallas kernels, k1(): call(back_first, 'transposed_products', message_shapes(RHS + EXTRA, jnp.i...  6.79 us
    pallas_call x1, Pallas kernels, k2(): call(forward_first, 'forward_products', shaped((CL, RHS, B), F32), VMEM,...  5.21 us
    pallas_call x1, Pallas kernels, k5(): call(forward_second, 'second_forward_products', shaped((CL, RHS, B), F32)...  5.21 us
    pallas_call x1, Pallas kernels, k4(): call(back_second, 'second_transposed_products', message_shapes(RHS, BF16)...  4.02 us
    ppermute x8, starting transfers between devices, swap(): return lax.ppermute(block, 'rows', [(i, i ^ 1) for i in range(size)])  3.06 us
  transfers between devices with their start and end apart: 20, of which 11 were waited for; matrix products, arithmetic and copies ran while one was open for 0% of the time, Pallas kernels for 27%

profile of v4, /device:TPU:1, one launch (start us, length us, event | category | flops | bytes accessed | tf_op | source)
XLA Modules:
  0.0 78.0 jit_solution(10910120887658675994)
XLA Ops:
  0.6 1.5 %collective-permute-start = (bf16[64,1024]{1,0:T(8,128)(2,1)}, bf16[64,1024]{1,0:T(8,128)(2,1)S(1)}, u32[]{:S(2)}, u32[]{:S(2)}) collective-permute-start(bf16[64,1024]{1,0:T(8,128)(2,1)} %param.10), channel_id=1, source_target_pairs={{0,1},{1,0},{2,3},{3,2},{4,5},{5,4},{6,7},{7,6},{8,9},{9,8},{10,11... | collective-permute-start | bytes 393224 | tf_op jit(solution)/shard_map/ppermute | solution.py:520
  2.1 1.2 %collective-permute-done = bf16[64,1024]{1,0:T(8,128)(2,1)S(1)} collective-permute-done((bf16[64,1024]{1,0:T(8,128)(2,1)}, bf16[64,1024]{1,0:T(8,128)(2,1)S(1)}, u32[]{:S(2)}, u32[]{:S(2)}) %collective-permute-start) | collective-permute-done | bytes 131104 | tf_op jit(solution)/shard_map/ppermute | solution.py:520
  3.3 0.9 %pad_maximum_fusion.1.both = bf16[2,64,1024]{2,1,0:T(8,128)(2,1)S(1)} fusion(bf16[1,64,1024]{2,1,0:T(8,128)(2,1)S(1)} %bitcast.8, bf16[1,64,1024]{2,1,0:T(8,128)(2,1)} %bitcast.7), kind=kLoop, calls=%fused_computation.1 | loop fusion | flops 131072 | bytes 524288 | tf_op jit(solution)/shard_map/stack | solution.py:540
  4.3 8.6 %collective-permute-start.1 = (bf16[2,64,1024]{2,1,0:T(8,128)(2,1)S(1)}, bf16[2,64,1024]{2,1,0:T(8,128)(2,1)S(1)}, u32[]{:S(2)}, u32[]{:S(2)}) collective-permute-start(bf16[2,64,1024]{2,1,0:T(8,128)(2,1)S(1)} %pad_maximum_fusion.1.both), channel_id=1, source_target_pairs={{0,2},{1,127},{2,4},{3,1},{4,6},{5,3},{6,8},{7,5},{8,10},{9,7},{10... | collective-permute-start | bytes 786440 | tf_op jit(solution)/shard_map/ppermute | solution.py:523
  12.8 0.0 collective-permute-start.2
  12.8 0.9 %collective-permute-start.3 = (bf16[2,64,1024]{2,1,0:T(8,128)(2,1)S(1)}, bf16[2,64,1024]{2,1,0:T(8,128)(2,1)S(1)}, u32[]{:S(2)}, u32[]{:S(2)}) collective-permute-start(bf16[2,64,1024]{2,1,0:T(8,128)(2,1)S(1)} %pad_maximum_fusion.1.both), channel_id=1, source_target_pairs={{0,6},{1,123},{2,8},{3,125},{4,10},{5,127},{6,12},{7,1},{8,14},{9,... | collective-permute-start | bytes 786440 | tf_op jit(solution)/shard_map/ppermute | solution.py:523
  13.7 6.8 %transposed_products.1 = (s16[4,80,256]{2,1,0:T(8,128)(2,1)S(1)}, s16[4,80,256]{2,1,0:T(8,128)(2,1)S(1)}, s16[3,80,256]{2,1,0:T(8,128)(2,1)S(1)}, s16[7,80,256]{...) custom-call(s32[1]{0:T(128)} %bitcast.me, ...), custom_call_target="tpu_custom_call" | custom-call | flops 2000000000 | bytes 22000000 | tf_op jit(solution)/shard_map/transposed_products/pallas_call | solution.py:427
  20.5 0.0 copy-start
  20.5 0.0 collective-permute-done.1.h1
  20.5 3.1 %collective-permute-done.2.h2 = bf16[2,64,1024]{2,1,0:T(8,128)(2,1)S(1)} collective-permute-done((bf16[2,64,1024]{2,1,0:T(8,128)(2,1)S(1)}, bf16[2,64,1024]{2,1,0:T(8,128)(2,1)S(1)}, u32[]{:S(2)}, u32[]{:S(2)}) %collective-permute-start.2) | collective-permute-done | bytes 262176 | tf_op jit(solution)/shard_map/ppermute | solution.py:523
  23.6 1.9 %collective-permute-done.3.h3 = bf16[2,64,1024]{2,1,0:T(8,128)(2,1)S(1)} collective-permute-done((bf16[2,64,1024]{2,1,0:T(8,128)(2,1)S(1)}, bf16[2,64,1024]{2,1,0:T(8,128)(2,1)S(1)}, u32[]{:S(2)}, u32[]{:S(2)}) %collective-permute-start.3) | collective-permute-done | bytes 262176 | tf_op jit(solution)/shard_map/ppermute | solution.py:523
  25.6 0.1 pad_maximum_fusion
  25.6 0.1 collective-permute-start.4
  25.7 0.5 collective-permute-start.5
  26.2 2.0 %collective-permute-done.5.got = s16[7,80,256]{2,1,0:T(8,128)(2,1)S(1)} collective-permute-done((s16[7,80,256]{2,1,0:T(8,128)(2,1)S(1)}, s16[7,80,256]{2,1,0:T(8,128)(2,1)S(1)}, u32[]{:S(2)}, u32[]{:S(2)}) %collective-permute-start.5) | collective-permute-done | bytes 286752 | tf_op jit(solution)/shard_map/ppermute | solution.py:520
  28.3 3.7 %collective-permute-start.6 = (s16[4,80,256]{2,1,0:T(8,128)(2,1)S(1)}, s16[4,80,256]{2,1,0:T(8,128)(2,1)S(1)}, u32[]{:S(2)}, u32[]{:S(2)}) collective-permute-start(s16[4,80,256]{2,1,0:T(8,128)(2,1)S(1)} %get-tuple-element.80), channel_id=1, source_target_pairs={{0,2},{1,127},{2,4},{3,1},{4,6},{5,3},{6,8},{7,5},{8,10},{9,7},{10... | collective-permute-start | bytes 491528 | tf_op jit(solution)/shard_map/ppermute | solution.py:523
  32.0 2.9 %collective-permute-start.7 = (s16[4,80,256]{2,1,0:T(8,128)(2,1)S(1)}, s16[4,80,256]{2,1,0:T(8,128)(2,1)S(1)}, u32[]{:S(2)}, u32[]{:S(2)}) collective-permute-start(s16[4,80,256]{2,1,0:T(8,128)(2,1)S(1)} %get-tuple-element.79), channel_id=1, source_target_pairs={{0,4},{1,125},{2,6},{3,127},{4,8},{5,1},{6,10},{7,3},{8,12},{9,5},... | collective-permute-start | bytes 491528 | tf_op jit(solution)/shard_map/ppermute | solution.py:523
  34.9 0.0 collective-permute-start.8
  34.9 0.0 collective-permute-done.4.post
  34.9 5.2 %forward_products.1.partial = f32[4,64,256]{2,1,0:T(8,128)S(1)} custom-call(s32[4,256]{1,0:T(4,128)S(1)} %get-tuple-element.40.plan, bf16[2,64,1024]{2,1,0:T(8,128)(2,1)S(1)} %pad_maximum_fusion.1.both, bf16[2,64,1024]{2,1,0:T(8,128)(2,1)S(1)} %collective-permute-done.1.h1, bf16[2,64,1024]{2,1,0:T(8,128)(2,1)S(1)} %collective-permute-done.2.h2, ...), custom_call_target="tpu_custom_call" | custom-call | flops 2000000000 | bytes 22000000 | tf_op jit(solution)/shard_map/forward_products/pallas_call | solution.py:453
  40.1 3.0 %collective-permute-done.8.r3 = s16[3,80,256]{2,1,0:T(8,128)(2,1)S(1)} collective-permute-done((s16[3,80,256]{2,1,0:T(8,128)(2,1)S(1)}, s16[3,80,256]{2,1,0:T(8,128)(2,1)S(1)}, u32[]{:S(2)}, u32[]{:S(2)}) %collective-permute-start.8) | collective-permute-done | bytes 122912 | tf_op jit(solution)/shard_map/ppermute | solution.py:523
  43.1 0.0 collective-permute-done.6.r1
  43.1 0.0 collective-permute-done.7.r2
  43.2 0.1 collective-permute-start.9
  43.3 1.4 %collective-permute-done.9.post = s16[5,80,256]{2,1,0:T(8,128)(2,1)S(1)} collective-permute-done((s16[5,80,256]{2,1,0:T(8,128)(2,1)S(1)}, s16[5,80,256]{2,1,0:T(8,128)(2,1)S(1)}, u32[]{:S(2)}, u32[]{:S(2)}) %collective-permute-start.9) | collective-permute-done | bytes 204832 | tf_op jit(solution)/shard_map/ppermute | solution.py:520
  44.7 1.3 %first_image.1 = (f32[64,1024]{1,0:T(8,128)}, bf16[4,64,256]{2,1,0:T(8,128)(2,1)S(1)}, s32[1,128]{1,0:T(1,128)S(1)}, bf16[4,64,256]{2,1,0:T(8,128)(2,1)S(1)}, bf...) custom-call(f32[4,64,256]{2,1,0:T(8,128)S(1)} %forward_products.1.partial, ...), custom_call_target="tpu_custom_call" | custom-call | flops 2000000000 | bytes 22000000 | tf_op jit(solution)/shard_map/first_image/pallas_call | solution.py:462
  46.0 0.2 collective-permute-start.10
  46.2 1.4 %collective-permute-done.10.got = bf16[7,64,256]{2,1,0:T(8,128)(2,1)S(1)} collective-permute-done((bf16[7,64,256]{2,1,0:T(8,128)(2,1)S(1)}, bf16[7,64,256]{2,1,0:T(8,128)(2,1)S(1)}, u32[]{:S(2)}, u32[]{:S(2)}) %collective-permute-start.10) | collective-permute-done | bytes 229408 | tf_op jit(solution)/shard_map/ppermute | solution.py:520
  47.6 3.6 %collective-permute-start.11 = (bf16[4,64,256]{2,1,0:T(8,128)(2,1)S(1)}, bf16[4,64,256]{2,1,0:T(8,128)(2,1)S(1)}, u32[]{:S(2)}, u32[]{:S(2)}) collective-permute-start(bf16[4,64,256]{2,1,0:T(8,128)(2,1)S(1)} %get-tuple-element.86), channel_id=1, source_target_pairs={{0,2},{1,127},{2,4},{3,1},{4,6},{5,3},{6,8},{7,5},{8,10},{9,7},{10... | collective-permute-start | bytes 393224 | tf_op jit(solution)/shard_map/ppermute | solution.py:523
  51.2 0.0 collective-permute-start.12
  51.2 0.0 collective-permute-start.13
  51.2 4.0 %second_transposed_products.1 = (bf16[4,64,256]{2,1,0:T(8,128)(2,1)S(1)}, bf16[4,64,256]{2,1,0:T(8,128)(2,1)S(1)}, bf16[3,64,256]{2,1,0:T(8,128)(2,1)S(1)}, bf16[7,64,256]{2,1,0:T(8,128)(2,1)S(1)}) custom-call(s32[4,256]{1,0:T(4,128)S(1)} %get-tuple-element.40.plan, bf16[4,64,256]{2,1,0:T(8,128)(2,1)S(1)} %get-tuple-element.63.rounded.own, ...), custom_call_target="tpu_custom_call" | custom-call | flops 2000000000 | bytes 22000000 | tf_op jit(solution)/shard_map/second_transposed_products/pallas_call | solution.py:477
  55.2 4.9 %collective-permute-done.13.r3 = bf16[3,64,256]{2,1,0:T(8,128)(2,1)S(1)} collective-permute-done((bf16[3,64,256]{2,1,0:T(8,128)(2,1)S(1)}, bf16[3,64,256]{2,1,0:T(8,128)(2,1)S(1)}, u32[]{:S(2)}, u32[]{:S(2)}) %collective-permute-start.13) | collective-permute-done | bytes 98336 | tf_op jit(solution)/shard_map/ppermute | solution.py:523
  60.1 0.0 collective-permute-done.11.r1
  60.1 0.0 collective-permute-done.12.r2
  60.1 0.1 collective-permute-start.15
  60.3 0.5 collective-permute-start.14
  60.7 0.8 %collective-permute-done.15.got = bf16[7,64,256]{2,1,0:T(8,128)(2,1)S(1)} collective-permute-done((bf16[7,64,256]{2,1,0:T(8,128)(2,1)S(1)}, bf16[7,64,256]{2,1,0:T(8,128)(2,1)S(1)}, u32[]{:S(2)}, u32[]{:S(2)}) %collective-permute-start.15) | collective-permute-done | bytes 229408 | tf_op jit(solution)/shard_map/ppermute | solution.py:520
  61.6 4.6 %collective-permute-start.16 = (bf16[4,64,256]{2,1,0:T(8,128)(2,1)S(1)}, bf16[4,64,256]{2,1,0:T(8,128)(2,1)S(1)}, u32[]{:S(2)}, u32[]{:S(2)}) collective-permute-start(bf16[4,64,256]{2,1,0:T(8,128)(2,1)S(1)} %get-tuple-element.83), channel_id=1, source_target_pairs={{0,2},{1,127},{2,4},{3,1},{4,6},{5,3},{6,8},{7,5},{8,10},{9,7},{10... | collective-permute-start | bytes 393224 | tf_op jit(solution)/shard_map/ppermute | solution.py:523
  66.2 0.0 collective-permute-start.17
  66.2 0.0 collective-permute-start.18
  66.2 0.0 collective-permute-done.14.post
  66.2 5.2 %second_forward_products.1.partial = f32[4,64,256]{2,1,0:T(8,128)S(1)} custom-call(s32[4,256]{1,0:T(4,128)S(1)} %get-tuple-element.40.plan, bf16[4,64,256]{2,1,0:T(8,128)(2,1)S(1)} %get-tuple-element.63.rounded.own, bf16[4,64,256]{2,1,0:T(8,128)(2,1)S(1)} %collective-permute-done.11.r1, bf16[4,64,256]{2,1,0:T(8,128)(2,1)S(1)} %collective-permute-done.12.r2, ...), custom_call_target="tpu_custom_call" | custom-call | flops 2000000000 | bytes 22000000 | tf_op jit(solution)/shard_map/second_forward_products/pallas_call | solution.py:487
  71.4 3.7 %collective-permute-done.18.r3 = bf16[3,64,256]{2,1,0:T(8,128)(2,1)S(1)} collective-permute-done((bf16[3,64,256]{2,1,0:T(8,128)(2,1)S(1)}, bf16[3,64,256]{2,1,0:T(8,128)(2,1)S(1)}, u32[]{:S(2)}, u32[]{:S(2)}) %collective-permute-start.18) | collective-permute-done | bytes 98336 | tf_op jit(solution)/shard_map/ppermute | solution.py:523
  75.1 0.0 collective-permute-done.16.r1
  75.2 0.1 collective-permute-start.19
  75.3 1.4 %collective-permute-done.19.post = bf16[5,64,256]{2,1,0:T(8,128)(2,1)S(1)} collective-permute-done((bf16[5,64,256]{2,1,0:T(8,128)(2,1)S(1)}, bf16[5,64,256]{2,1,0:T(8,128)(2,1)S(1)}, u32[]{:S(2)}, u32[]{:S(2)}) %collective-permute-start.19) | collective-permute-done | bytes 163872 | tf_op jit(solution)/shard_map/ppermute | solution.py:520
  76.6 1.4 %second_image.1 = f32[64,1024]{1,0:T(8,128)} custom-call(f32[4,64,256]{2,1,0:T(8,128)S(1)} %second_forward_products.1.partial, s32[1,128]{1,0:T(1,128)S(1)} %get-tuple-element.74.wanted, bf16[4,64,256]{2,1,0:T(8,128)(2,1)S(1)} %collective-permute-done.16.r1, bf16[4,64,256]{2,1,0:T(8,128)(2,1)S(1)} %collective-permute-done.17.r2, ...), custom_call_target="tpu_custom_call" | custom-call | flops 2000000000 | bytes 22000000 | tf_op jit(solution)/shard_map/second_image/pallas_call | solution.py:496
  (18 shorter events, 0.2 us)
Async XLA Ops:
  0.6 2.7 %collective-permute-start = (bf16[64,1024]{1,0:T(8,128)(2,1)}, bf16[64,1024]{1,0:T(8,128)(2,1)S(1)}, u32[]{:S(2)}, u32[]{:S(2)}) collective-permute-start(bf16[64,1024]{1,0:T(8,128)(2,1)} %param.10), channel_id=1, source_target_pairs={{0,1},{1,0},{2,3},{3,2},{4,5},{5,4},{6,7},{7,6},{8,9},{9,8},{10,11... | collective-permute-start | bytes 393224 | tf_op jit(solution)/shard_map/ppermute | solution.py:520
  4.3 16.2 %collective-permute-start.1 = (bf16[2,64,1024]{2,1,0:T(8,128)(2,1)S(1)}, bf16[2,64,1024]{2,1,0:T(8,128)(2,1)S(1)}, u32[]{:S(2)}, u32[]{:S(2)}) collective-permute-start(bf16[2,64,1024]{2,1,0:T(8,128)(2,1)S(1)} %pad_maximum_fusion.1.both), channel_id=1, source_target_pairs={{0,2},{1,127},{2,4},{3,1},{4,6},{5,3},{6,8},{7,5},{8,10},{9,7},{10... | collective-permute-start | bytes 786440 | tf_op jit(solution)/shard_map/ppermute | solution.py:523
  12.8 10.8 %collective-permute-start.2 = (bf16[2,64,1024]{2,1,0:T(8,128)(2,1)S(1)}, bf16[2,64,1024]{2,1,0:T(8,128)(2,1)S(1)}, u32[]{:S(2)}, u32[]{:S(2)}) collective-permute-start(bf16[2,64,1024]{2,1,0:T(8,128)(2,1)S(1)} %pad_maximum_fusion.1.both), channel_id=1, source_target_pairs={{0,4},{1,125},{2,6},{3,127},{4,8},{5,1},{6,10},{7,3},{8,12},{9,5},... | collective-permute-start | bytes 786440 | tf_op jit(solution)/shard_map/ppermute | solution.py:523
  12.8 12.7 %collective-permute-start.3 = (bf16[2,64,1024]{2,1,0:T(8,128)(2,1)S(1)}, bf16[2,64,1024]{2,1,0:T(8,128)(2,1)S(1)}, u32[]{:S(2)}, u32[]{:S(2)}) collective-permute-start(bf16[2,64,1024]{2,1,0:T(8,128)(2,1)S(1)} %pad_maximum_fusion.1.both), channel_id=1, source_target_pairs={{0,6},{1,123},{2,8},{3,125},{4,10},{5,127},{6,12},{7,1},{8,14},{9,... | collective-permute-start | bytes 786440 | tf_op jit(solution)/shard_map/ppermute | solution.py:523
  20.5 14.4 %copy-start = (bf16[4,256,256]{2,1,0:T(8,128)(2,1)S(1)}, bf16[4,256,256]{2,1,0:T(8,128)(2,1)}, u32[]{:S(2)}) copy-start(bf16[4,256,256]{2,1,0:T(8,128)(2,1)} %diag.3) | copy-start | bytes 1572868
  25.6 9.2 %collective-permute-start.4 = (bf16[5,64,1024]{2,1,0:T(8,128)(2,1)S(1)}, bf16[5,64,1024]{2,1,0:T(8,128)(2,1)S(1)}, u32[]{:S(2)}, u32[]{:S(2)}) collective-permute-start(bf16[5,64,1024]{2,1,0:T(8,128)(2,1)S(1)} %pad_maximum_fusion), channel_id=1, source_target_pairs={{0,1},{1,0},{2,3},{3,2},{4,5},{5,4},{6,7},{7,6},{8,9},{9,8},{10,11... | collective-permute-start | bytes 1966088 | tf_op jit(solution)/shard_map/ppermute | solution.py:520
  25.7 2.5 %collective-permute-start.5 = (s16[7,80,256]{2,1,0:T(8,128)(2,1)S(1)}, s16[7,80,256]{2,1,0:T(8,128)(2,1)S(1)}, u32[]{:S(2)}, u32[]{:S(2)}) collective-permute-start(s16[7,80,256]{2,1,0:T(8,128)(2,1)S(1)} %get-tuple-element.46), channel_id=1, source_target_pairs={{0,1},{1,0},{2,3},{3,2},{4,5},{5,4},{6,7},{7,6},{8,9},{9,8},{10,11... | collective-permute-start | bytes 860168 | tf_op jit(solution)/shard_map/ppermute | solution.py:520
  28.3 14.9 %collective-permute-start.6 = (s16[4,80,256]{2,1,0:T(8,128)(2,1)S(1)}, s16[4,80,256]{2,1,0:T(8,128)(2,1)S(1)}, u32[]{:S(2)}, u32[]{:S(2)}) collective-permute-start(s16[4,80,256]{2,1,0:T(8,128)(2,1)S(1)} %get-tuple-element.80), channel_id=1, source_target_pairs={{0,2},{1,127},{2,4},{3,1},{4,6},{5,3},{6,8},{7,5},{8,10},{9,7},{10... | collective-permute-start | bytes 491528 | tf_op jit(solution)/shard_map/ppermute | solution.py:523
  32.0 11.2 %collective-permute-start.7 = (s16[4,80,256]{2,1,0:T(8,128)(2,1)S(1)}, s16[4,80,256]{2,1,0:T(8,128)(2,1)S(1)}, u32[]{:S(2)}, u32[]{:S(2)}) collective-permute-start(s16[4,80,256]{2,1,0:T(8,128)(2,1)S(1)} %get-tuple-element.79), channel_id=1, source_target_pairs={{0,4},{1,125},{2,6},{3,127},{4,8},{5,1},{6,10},{7,3},{8,12},{9,5},... | collective-permute-start | bytes 491528 | tf_op jit(solution)/shard_map/ppermute | solution.py:523
  34.9 8.3 %collective-permute-start.8 = (s16[3,80,256]{2,1,0:T(8,128)(2,1)S(1)}, s16[3,80,256]{2,1,0:T(8,128)(2,1)S(1)}, u32[]{:S(2)}, u32[]{:S(2)}) collective-permute-start(s16[3,80,256]{2,1,0:T(8,128)(2,1)S(1)} %get-tuple-element.78), channel_id=1, source_target_pairs={{0,6},{1,123},{2,8},{3,125},{4,10},{5,127},{6,12},{7,1},{8,14},{9,... | collective-permute-start | bytes 368648 | tf_op jit(solution)/shard_map/ppermute | solution.py:523
  43.2 1.5 %collective-permute-start.9 = (s16[5,80,256]{2,1,0:T(8,128)(2,1)S(1)}, s16[5,80,256]{2,1,0:T(8,128)(2,1)S(1)}, u32[]{:S(2)}, u32[]{:S(2)}) collective-permute-start(s16[5,80,256]{2,1,0:T(8,128)(2,1)S(1)} %pad_add_fusion), channel_id=1, source_target_pairs={{0,1},{1,0},{2,3},{3,2},{4,5},{5,4},{6,7},{7,6},{8,9},{9,8},{10,11... | collective-permute-start | bytes 614408 | tf_op jit(solution)/shard_map/ppermute | solution.py:520
  46.0 1.6 %collective-permute-start.10 = (bf16[7,64,256]{2,1,0:T(8,128)(2,1)S(1)}, bf16[7,64,256]{2,1,0:T(8,128)(2,1)S(1)}, u32[]{:S(2)}, u32[]{:S(2)}) collective-permute-start(bf16[7,64,256]{2,1,0:T(8,128)(2,1)S(1)} %get-tuple-element.60), channel_id=1, source_target_pairs={{0,1},{1,0},{2,3},{3,2},{4,5},{5,4},{6,7},{7,6},{8,9},{9,8},{10,11... | collective-permute-start | bytes 688136 | tf_op jit(solution)/shard_map/ppermute | solution.py:520
  47.6 12.5 %collective-permute-start.11 = (bf16[4,64,256]{2,1,0:T(8,128)(2,1)S(1)}, bf16[4,64,256]{2,1,0:T(8,128)(2,1)S(1)}, u32[]{:S(2)}, u32[]{:S(2)}) collective-permute-start(bf16[4,64,256]{2,1,0:T(8,128)(2,1)S(1)} %get-tuple-element.86), channel_id=1, source_target_pairs={{0,2},{1,127},{2,4},{3,1},{4,6},{5,3},{6,8},{7,5},{8,10},{9,7},{10... | collective-permute-start | bytes 393224 | tf_op jit(solution)/shard_map/ppermute | solution.py:523
  51.2 8.9 %collective-permute-start.12 = (bf16[4,64,256]{2,1,0:T(8,128)(2,1)S(1)}, bf16[4,64,256]{2,1,0:T(8,128)(2,1)S(1)}, u32[]{:S(2)}, u32[]{:S(2)}) collective-permute-start(bf16[4,64,256]{2,1,0:T(8,128)(2,1)S(1)} %get-tuple-element.85), channel_id=1, source_target_pairs={{0,4},{1,125},{2,6},{3,127},{4,8},{5,1},{6,10},{7,3},{8,12},{9,5},... | collective-permute-start | bytes 393224 | tf_op jit(solution)/shard_map/ppermute | solution.py:523
  51.2 8.9 %collective-permute-start.13 = (bf16[3,64,256]{2,1,0:T(8,128)(2,1)S(1)}, bf16[3,64,256]{2,1,0:T(8,128)(2,1)S(1)}, u32[]{:S(2)}, u32[]{:S(2)}) collective-permute-start(bf16[3,64,256]{2,1,0:T(8,128)(2,1)S(1)} %get-tuple-element.84), channel_id=1, source_target_pairs={{0,6},{1,123},{2,8},{3,125},{4,10},{5,127},{6,12},{7,1},{8,14},{9,... | collective-permute-start | bytes 294920 | tf_op jit(solution)/shard_map/ppermute | solution.py:523
  60.1 1.5 %collective-permute-start.15 = (bf16[7,64,256]{2,1,0:T(8,128)(2,1)S(1)}, bf16[7,64,256]{2,1,0:T(8,128)(2,1)S(1)}, u32[]{:S(2)}, u32[]{:S(2)}) collective-permute-start(bf16[7,64,256]{2,1,0:T(8,128)(2,1)S(1)} %get-tuple-element.69), channel_id=1, source_target_pairs={{0,1},{1,0},{2,3},{3,2},{4,5},{5,4},{6,7},{7,6},{8,9},{9,8},{10,11... | collective-permute-start | bytes 688136 | tf_op jit(solution)/shard_map/ppermute | solution.py:520
  60.3 6.0 %collective-permute-start.14 = (bf16[5,64,256]{2,1,0:T(8,128)(2,1)S(1)}, bf16[5,64,256]{2,1,0:T(8,128)(2,1)S(1)}, u32[]{:S(2)}, u32[]{:S(2)}) collective-permute-start(bf16[5,64,256]{2,1,0:T(8,128)(2,1)S(1)} %pad_maximum_fusion.2), channel_id=1, source_target_pairs={{0,1},{1,0},{2,3},{3,2},{4,5},{5,4},{6,7},{7,6},{8,9},{9,8},{10,11... | collective-permute-start | bytes 491528 | tf_op jit(solution)/shard_map/ppermute | solution.py:520
  61.6 13.5 %collective-permute-start.16 = (bf16[4,64,256]{2,1,0:T(8,128)(2,1)S(1)}, bf16[4,64,256]{2,1,0:T(8,128)(2,1)S(1)}, u32[]{:S(2)}, u32[]{:S(2)}) collective-permute-start(bf16[4,64,256]{2,1,0:T(8,128)(2,1)S(1)} %get-tuple-element.83), channel_id=1, source_target_pairs={{0,2},{1,127},{2,4},{3,1},{4,6},{5,3},{6,8},{7,5},{8,10},{9,7},{10... | collective-permute-start | bytes 393224 | tf_op jit(solution)/shard_map/ppermute | solution.py:523
  66.2 8.9 %collective-permute-start.17 = (bf16[4,64,256]{2,1,0:T(8,128)(2,1)S(1)}, bf16[4,64,256]{2,1,0:T(8,128)(2,1)S(1)}, u32[]{:S(2)}, u32[]{:S(2)}) collective-permute-start(bf16[4,64,256]{2,1,0:T(8,128)(2,1)S(1)} %get-tuple-element.82), channel_id=1, source_target_pairs={{0,4},{1,125},{2,6},{3,127},{4,8},{5,1},{6,10},{7,3},{8,12},{9,5},... | collective-permute-start | bytes 393224 | tf_op jit(solution)/shard_map/ppermute | solution.py:523
  66.2 8.9 %collective-permute-start.18 = (bf16[3,64,256]{2,1,0:T(8,128)(2,1)S(1)}, bf16[3,64,256]{2,1,0:T(8,128)(2,1)S(1)}, u32[]{:S(2)}, u32[]{:S(2)}) collective-permute-start(bf16[3,64,256]{2,1,0:T(8,128)(2,1)S(1)} %get-tuple-element.81), channel_id=1, source_target_pairs={{0,6},{1,123},{2,8},{3,125},{4,10},{5,127},{6,12},{7,1},{8,14},{9,... | collective-permute-start | bytes 294920 | tf_op jit(solution)/shard_map/ppermute | solution.py:523
  75.2 1.5 %collective-permute-start.19 = (bf16[5,64,256]{2,1,0:T(8,128)(2,1)S(1)}, bf16[5,64,256]{2,1,0:T(8,128)(2,1)S(1)}, u32[]{:S(2)}, u32[]{:S(2)}) collective-permute-start(bf16[5,64,256]{2,1,0:T(8,128)(2,1)S(1)} %pad_maximum_fusion.3), channel_id=1, source_target_pairs={{0,1},{1,0},{2,3},{3,2},{4,5},{5,4},{6,7},{7,6},{8,9},{9,8},{10,11... | collective-permute-start | bytes 491528 | tf_op jit(solution)/shard_map/ppermute | solution.py:520

commit v5 on v4

--- a/solution.py
+++ b/solution.py
@@ -422,6 +422,16 @@
     return [shaped((n, rows, B), dtype) for n in MESSAGE + (7,)]
 
 
+def stage(source, target, sem):
+    copy = pltpu.make_async_copy(source, target.at[0], sem)
+    copy.start()
+    copy.wait()
+
+
+def staged(vectors):
+    return call(stage, "staged", shaped((2, *vectors.shape), BF16), VMEM, [HBM], [pltpu.SemaphoreType.DMA])(vectors)
+
+
 def k1(*args):
     held = [pltpu.VMEM(shape, BF16) for shape in ((SLOTS, B, B), (SLOTS, K, B), (SLOTS, K, B))]
     return call(
@@ -462,7 +472,7 @@
     return call(
         image_first, "first_image",
         [
-            shaped((RHS, CL * B), F32),
+            pltpu.VMEM((RHS, CL * B), F32),
             shaped((CL, RHS, B), BF16),
             shaped((1, SLOTS), jnp.int32),
         ]
@@ -522,12 +532,16 @@
     def carry(block, k):
         return lax.ppermute(block, "rows", carriers(size, k))
 
+    def carried(messages):
+        second = carry(messages[1], 2)
+        return [carry(messages[0], 1), second, carry(messages[2], 3)]
+
     def exchange(m1, m2, m3, give):
         got = swap(give)
         messages = []
         for k, message in enumerate((m1, m2, m3)):
             messages.append(lax.dynamic_update_slice(message, got[2 * k : 2 * k + 2], (1, 0, 0)))
-        return [carry(message, k + 1) for k, message in enumerate(messages)] + [got, messages]
+        return carried(messages) + [got, messages]
 
     def passed_on(r1, r2, r3):
         return swap(jnp.concatenate([r1[2:4], r2[2:4], r3[2:3]]))
@@ -537,8 +551,8 @@
 
     lists = [in_hbm(x.reshape(1, SLOTS)) for x in (near_rows, near_cols, far_rows, far_cols)]
     sib = swap(vectors)
-    both = jnp.stack([vectors, sib])
-    halo = [carry(both, k) for k in (1, 2, 3)]
+    both = lax.dynamic_update_slice(staged(in_hbm(vectors)), sib[None], (1, 0, 0))
+    halo = carried([both] * 3)
     m1, m2, m3, give, plan, *held = k1(
         me, *lists, in_hbm(counts), both, in_hbm(near_blocks), in_hbm(far_left), in_hbm(far_right)
     )

time: 78.2 us -> 77.1 us (0.986)
  waiting for transfers between devices: 24.8 us -> 23.2 us
  other arithmetic: 1.07 us -> 0.14 us
  Pallas kernels: 23.9 us -> 24.7 us
    ppermute x8, waiting for transfers between devices: 8.21 us -> 6.59 us  [swap(): return lax.ppermute(block, 'rows', [(i, i ^ 1) for i in range(size)])]
    another operation x1 -> x0, other arithmetic: 0.93 us -> none  [per_device(): both = jnp.stack([vectors, sib])]
    pallas_call x1 -> x2, Pallas kernels: 1.3 us -> 2.06 us  [the longest x1 1.15 us: k3(): call(image_first, 'first_image', [pltpu.VMEM((RHS, CL * B), F32), shaped(...]
  transfers between devices with their start and end apart: 20 -> 20, of which waited for: 11 -> 11; matrix products, arithmetic and copies ran while one was open for 0% -> 1% of each run, Pallas kernels for 27% -> 29%
where the time goes in v5:
time: 77.1 us; the launch traced here: 76.9 us
  starting transfers between devices  27.3 us (35%)
  Pallas kernels  24.7 us (32%)
  waiting for transfers between devices  23.2 us (30%)
  between operations  0.84 us (1%)
  local copies, waits for them, and re-layouts  0.82 us (1%)
    ppermute x12, starting transfers between devices, carry(): return lax.ppermute(block, 'rows', carriers(size, k))  24.2 us
    ppermute x12, waiting for transfers between devices, carry(): return lax.ppermute(block, 'rows', carriers(size, k))  16.6 us
    pallas_call x1, Pallas kernels, k1(): call(back_first, 'transposed_products', message_shapes(RHS + EXTRA, jnp.i...  6.79 us
    ppermute x8, waiting for transfers between devices, swap(): return lax.ppermute(block, 'rows', [(i, i ^ 1) for i in range(size)])  6.59 us
    pallas_call x1, Pallas kernels, k5(): call(forward_second, 'second_forward_products', shaped((CL, RHS, B), F32)...  5.22 us
    pallas_call x1, Pallas kernels, k2(): call(forward_first, 'forward_products', shaped((CL, RHS, B), F32), VMEM,...  5.21 us
    pallas_call x1, Pallas kernels, k4(): call(back_second, 'second_transposed_products', message_shapes(RHS, BF16)...  4.03 us
    ppermute x8, starting transfers between devices, swap(): return lax.ppermute(block, 'rows', [(i, i ^ 1) for i in range(size)])  3.06 us
  transfers between devices with their start and end apart: 20, of which 11 were waited for; matrix products, arithmetic and copies ran while one was open for 1% of the time, Pallas kernels for 29%

profile of v5, /device:TPU:1, one launch (start us, length us, event | category | flops | bytes accessed | tf_op | source)
XLA Modules:
  0.0 76.9 jit_solution(13294976075727313102)
XLA Ops:
  0.6 1.5 %collective-permute-start = (bf16[64,1024]{1,0:T(8,128)(2,1)}, bf16[64,1024]{1,0:T(8,128)(2,1)S(1)}, u32[]{:S(2)}, u32[]{:S(2)}) collective-permute-start(bf16[64,1024]{1,0:T(8,128)(2,1)} %source.1), channel_id=1, source_target_pairs={{0,1},{1,0},{2,3},{3,2},{4,5},{5,4},{6,7},{7,6},{8,9},{9,8},{10,11... | collective-permute-start | bytes 393224 | tf_op jit(solution)/shard_map/ppermute | solution.py:530
  2.1 0.9 %staged.1 = bf16[2,64,1024]{2,1,0:T(8,128)(2,1)S(1)} custom-call(bf16[64,1024]{1,0:T(8,128)(2,1)} %source.1), custom_call_target="tpu_custom_call" | custom-call | flops 2000000000 | bytes 22000000 | tf_op jit(solution)/shard_map/staged/pallas_call | solution.py:432
  3.0 0.3 collective-permute-done
  3.3 8.6 %collective-permute-start.1 = (bf16[2,64,1024]{2,1,0:T(8,128)(2,1)S(1)}, bf16[2,64,1024]{2,1,0:T(8,128)(2,1)S(1)}, u32[]{:S(2)}, u32[]{:S(2)}) collective-permute-start(bf16[2,64,1024]{2,1,0:T(8,128)(2,1)S(1)} %bitcast_dynamic-update-slice_fusion.both), channel_id=1, source_target_pairs={{0,2},{1,127},{2,4},{3,1},{4,6},{5,3},{6,8},{7,5},{8,10},{9,7},{10... | collective-permute-start | bytes 786440 | tf_op jit(solution)/shard_map/ppermute | solution.py:533
  11.9 0.0 collective-permute-start.2
  11.9 0.9 %collective-permute-start.3 = (bf16[2,64,1024]{2,1,0:T(8,128)(2,1)S(1)}, bf16[2,64,1024]{2,1,0:T(8,128)(2,1)S(1)}, u32[]{:S(2)}, u32[]{:S(2)}) collective-permute-start(bf16[2,64,1024]{2,1,0:T(8,128)(2,1)S(1)} %bitcast_dynamic-update-slice_fusion.both), channel_id=1, source_target_pairs={{0,6},{1,123},{2,8},{3,125},{4,10},{5,127},{6,12},{7,1},{8,14},{9,... | collective-permute-start | bytes 786440 | tf_op jit(solution)/shard_map/ppermute | solution.py:533
  12.8 6.8 %transposed_products.1 = (s16[4,80,256]{2,1,0:T(8,128)(2,1)S(1)}, s16[4,80,256]{2,1,0:T(8,128)(2,1)S(1)}, s16[3,80,256]{2,1,0:T(8,128)(2,1)S(1)}, s16[7,80,256]{...) custom-call(s32[1]{0:T(128)} %bitcast.me, ...), custom_call_target="tpu_custom_call" | custom-call | flops 2000000000 | bytes 22000000 | tf_op jit(solution)/shard_map/transposed_products/pallas_call | solution.py:437
  19.6 0.0 copy-start
  19.6 0.0 collective-permute-done.1.h1
  19.6 3.1 %collective-permute-done.2.h2 = bf16[2,64,1024]{2,1,0:T(8,128)(2,1)S(1)} collective-permute-done((bf16[2,64,1024]{2,1,0:T(8,128)(2,1)S(1)}, bf16[2,64,1024]{2,1,0:T(8,128)(2,1)S(1)}, u32[]{:S(2)}, u32[]{:S(2)}) %collective-permute-start.2) | collective-permute-done | bytes 262176 | tf_op jit(solution)/shard_map/ppermute | solution.py:533
  22.7 1.9 %collective-permute-done.3.h3 = bf16[2,64,1024]{2,1,0:T(8,128)(2,1)S(1)} collective-permute-done((bf16[2,64,1024]{2,1,0:T(8,128)(2,1)S(1)}, bf16[2,64,1024]{2,1,0:T(8,128)(2,1)S(1)}, u32[]{:S(2)}, u32[]{:S(2)}) %collective-permute-start.3) | collective-permute-done | bytes 262176 | tf_op jit(solution)/shard_map/ppermute | solution.py:533
  24.6 0.1 pad_maximum_fusion
  24.7 0.1 collective-permute-start.4
  24.8 0.5 collective-permute-start.5
  25.3 2.0 %collective-permute-done.5.got = s16[7,80,256]{2,1,0:T(8,128)(2,1)S(1)} collective-permute-done((s16[7,80,256]{2,1,0:T(8,128)(2,1)S(1)}, s16[7,80,256]{2,1,0:T(8,128)(2,1)S(1)}, u32[]{:S(2)}, u32[]{:S(2)}) %collective-permute-start.5) | collective-permute-done | bytes 286752 | tf_op jit(solution)/shard_map/ppermute | solution.py:530
  27.3 3.7 %collective-permute-start.6 = (s16[4,80,256]{2,1,0:T(8,128)(2,1)S(1)}, s16[4,80,256]{2,1,0:T(8,128)(2,1)S(1)}, u32[]{:S(2)}, u32[]{:S(2)}) collective-permute-start(s16[4,80,256]{2,1,0:T(8,128)(2,1)S(1)} %get-tuple-element.80), channel_id=1, source_target_pairs={{0,2},{1,127},{2,4},{3,1},{4,6},{5,3},{6,8},{7,5},{8,10},{9,7},{10... | collective-permute-start | bytes 491528 | tf_op jit(solution)/shard_map/ppermute | solution.py:533
  31.0 2.9 %collective-permute-start.7 = (s16[4,80,256]{2,1,0:T(8,128)(2,1)S(1)}, s16[4,80,256]{2,1,0:T(8,128)(2,1)S(1)}, u32[]{:S(2)}, u32[]{:S(2)}) collective-permute-start(s16[4,80,256]{2,1,0:T(8,128)(2,1)S(1)} %get-tuple-element.79), channel_id=1, source_target_pairs={{0,4},{1,125},{2,6},{3,127},{4,8},{5,1},{6,10},{7,3},{8,12},{9,5},... | collective-permute-start | bytes 491528 | tf_op jit(solution)/shard_map/ppermute | solution.py:533
  33.9 0.0 collective-permute-start.8
  33.9 0.0 collective-permute-done.4.post
  34.0 5.2 %forward_products.1.partial = f32[4,64,256]{2,1,0:T(8,128)S(1)} custom-call(s32[4,256]{1,0:T(4,128)S(1)} %get-tuple-element.40.plan, bf16[2,64,1024]{2,1,0:T(8,128)(2,1)S(1)} %bitcast_dynamic-update-slice_fusion.both, bf16[2,64,1024]{2,1,0:T(8,128)(2,1)S(1)} %collective-permute-done.1.h1, bf16[2,64,1024]{2,1,0:T(8,128)(2,1)S(1)} %collective-permute-done.2.h2, ...), custom_call_target="tpu_custom_call" | custom-call | flops 2000000000 | bytes 22000000 | tf_op jit(solution)/shard_map/forward_products/pallas_call | solution.py:463
  39.2 3.0 %collective-permute-done.8.r3 = s16[3,80,256]{2,1,0:T(8,128)(2,1)S(1)} collective-permute-done((s16[3,80,256]{2,1,0:T(8,128)(2,1)S(1)}, s16[3,80,256]{2,1,0:T(8,128)(2,1)S(1)}, u32[]{:S(2)}, u32[]{:S(2)}) %collective-permute-start.8) | collective-permute-done | bytes 122912 | tf_op jit(solution)/shard_map/ppermute | solution.py:533
  42.2 0.0 collective-permute-done.6.r1
  42.2 0.0 collective-permute-done.7.r2
  42.3 0.1 collective-permute-start.9
  42.4 1.4 %collective-permute-done.9.post = s16[5,80,256]{2,1,0:T(8,128)(2,1)S(1)} collective-permute-done((s16[5,80,256]{2,1,0:T(8,128)(2,1)S(1)}, s16[5,80,256]{2,1,0:T(8,128)(2,1)S(1)}, u32[]{:S(2)}, u32[]{:S(2)}) %collective-permute-start.9) | collective-permute-done | bytes 204832 | tf_op jit(solution)/shard_map/ppermute | solution.py:530
  43.8 1.2 %first_image.1 = (f32[64,1024]{1,0:T(8,128)S(1)}, bf16[4,64,256]{2,1,0:T(8,128)(2,1)S(1)}, s32[1,128]{1,0:T(1,128)S(1)}, bf16[4,64,256]{2,1,0:T(8,128)(2,1)S(1)}...) custom-call(f32[4,64,256]{2,1,0:T(8,128)S(1)} %forward_products.1.partial, ...), custom_call_target="tpu_custom_call" | custom-call | flops 2000000000 | bytes 22000000 | tf_op jit(solution)/shard_map/first_image/pallas_call | solution.py:472
  45.0 0.2 collective-permute-start.10
  45.2 1.4 %collective-permute-done.10.got = bf16[7,64,256]{2,1,0:T(8,128)(2,1)S(1)} collective-permute-done((bf16[7,64,256]{2,1,0:T(8,128)(2,1)S(1)}, bf16[7,64,256]{2,1,0:T(8,128)(2,1)S(1)}, u32[]{:S(2)}, u32[]{:S(2)}) %collective-permute-start.10) | collective-permute-done | bytes 229408 | tf_op jit(solution)/shard_map/ppermute | solution.py:530
  46.5 3.6 %collective-permute-start.11 = (bf16[4,64,256]{2,1,0:T(8,128)(2,1)S(1)}, bf16[4,64,256]{2,1,0:T(8,128)(2,1)S(1)}, u32[]{:S(2)}, u32[]{:S(2)}) collective-permute-start(bf16[4,64,256]{2,1,0:T(8,128)(2,1)S(1)} %get-tuple-element.86), channel_id=1, source_target_pairs={{0,2},{1,127},{2,4},{3,1},{4,6},{5,3},{6,8},{7,5},{8,10},{9,7},{10... | collective-permute-start | bytes 393224 | tf_op jit(solution)/shard_map/ppermute | solution.py:533
  50.1 0.0 collective-permute-start.12
  50.1 0.0 collective-permute-start.13
  50.1 4.0 %second_transposed_products.1 = (bf16[4,64,256]{2,1,0:T(8,128)(2,1)S(1)}, bf16[4,64,256]{2,1,0:T(8,128)(2,1)S(1)}, bf16[3,64,256]{2,1,0:T(8,128)(2,1)S(1)}, bf16[7,64,256]{2,1,0:T(8,128)(2,1)S(1)}) custom-call(s32[4,256]{1,0:T(4,128)S(1)} %get-tuple-element.40.plan, bf16[4,64,256]{2,1,0:T(8,128)(2,1)S(1)} %get-tuple-element.63.rounded.own, ...), custom_call_target="tpu_custom_call" | custom-call | flops 2000000000 | bytes 22000000 | tf_op jit(solution)/shard_map/second_transposed_products/pallas_call | solution.py:487
  54.2 4.9 %collective-permute-done.13.r3 = bf16[3,64,256]{2,1,0:T(8,128)(2,1)S(1)} collective-permute-done((bf16[3,64,256]{2,1,0:T(8,128)(2,1)S(1)}, bf16[3,64,256]{2,1,0:T(8,128)(2,1)S(1)}, u32[]{:S(2)}, u32[]{:S(2)}) %collective-permute-start.13) | collective-permute-done | bytes 98336 | tf_op jit(solution)/shard_map/ppermute | solution.py:533
  59.0 0.0 collective-permute-done.11.r1
  59.0 0.0 collective-permute-done.12.r2
  59.0 0.1 collective-permute-start.15
  59.2 0.5 collective-permute-start.14
  59.7 0.8 %collective-permute-done.15.got = bf16[7,64,256]{2,1,0:T(8,128)(2,1)S(1)} collective-permute-done((bf16[7,64,256]{2,1,0:T(8,128)(2,1)S(1)}, bf16[7,64,256]{2,1,0:T(8,128)(2,1)S(1)}, u32[]{:S(2)}, u32[]{:S(2)}) %collective-permute-start.15) | collective-permute-done | bytes 229408 | tf_op jit(solution)/shard_map/ppermute | solution.py:530
  60.5 4.6 %collective-permute-start.16 = (bf16[4,64,256]{2,1,0:T(8,128)(2,1)S(1)}, bf16[4,64,256]{2,1,0:T(8,128)(2,1)S(1)}, u32[]{:S(2)}, u32[]{:S(2)}) collective-permute-start(bf16[4,64,256]{2,1,0:T(8,128)(2,1)S(1)} %get-tuple-element.83), channel_id=1, source_target_pairs={{0,2},{1,127},{2,4},{3,1},{4,6},{5,3},{6,8},{7,5},{8,10},{9,7},{10... | collective-permute-start | bytes 393224 | tf_op jit(solution)/shard_map/ppermute | solution.py:533
  65.1 0.0 collective-permute-start.17
  65.1 0.0 collective-permute-start.18
  65.1 5.2 %second_forward_products.1.partial = f32[4,64,256]{2,1,0:T(8,128)S(1)} custom-call(s32[4,256]{1,0:T(4,128)S(1)} %get-tuple-element.40.plan, bf16[4,64,256]{2,1,0:T(8,128)(2,1)S(1)} %get-tuple-element.63.rounded.own, bf16[4,64,256]{2,1,0:T(8,128)(2,1)S(1)} %collective-permute-done.11.r1, bf16[4,64,256]{2,1,0:T(8,128)(2,1)S(1)} %collective-permute-done.12.r2, ...), custom_call_target="tpu_custom_call" | custom-call | flops 2000000000 | bytes 22000000 | tf_op jit(solution)/shard_map/second_forward_products/pallas_call | solution.py:497
  70.4 3.7 %collective-permute-done.18.r3 = bf16[3,64,256]{2,1,0:T(8,128)(2,1)S(1)} collective-permute-done((bf16[3,64,256]{2,1,0:T(8,128)(2,1)S(1)}, bf16[3,64,256]{2,1,0:T(8,128)(2,1)S(1)}, u32[]{:S(2)}, u32[]{:S(2)}) %collective-permute-start.18) | collective-permute-done | bytes 98336 | tf_op jit(solution)/shard_map/ppermute | solution.py:533
  74.0 0.0 collective-permute-done.17.r2
  74.1 0.1 collective-permute-start.19
  74.2 0.7 copy.22
  74.9 0.7 collective-permute-done.19.post
  75.6 1.4 %second_image.1 = f32[64,1024]{1,0:T(8,128)} custom-call(f32[4,64,256]{2,1,0:T(8,128)S(1)} %second_forward_products.1.partial, s32[1,128]{1,0:T(1,128)S(1)} %get-tuple-element.74.wanted, bf16[4,64,256]{2,1,0:T(8,128)(2,1)S(1)} %collective-permute-done.16.r1, bf16[4,64,256]{2,1,0:T(8,128)(2,1)S(1)} %collective-permute-done.17.r2, ...), custom_call_target="tpu_custom_call" | custom-call | flops 2000000000 | bytes 22000000 | tf_op jit(solution)/shard_map/second_image/pallas_call | solution.py:506
  (20 shorter events, 0.2 us)
Async XLA Ops:
  0.6 2.7 %collective-permute-start = (bf16[64,1024]{1,0:T(8,128)(2,1)}, bf16[64,1024]{1,0:T(8,128)(2,1)S(1)}, u32[]{:S(2)}, u32[]{:S(2)}) collective-permute-start(bf16[64,1024]{1,0:T(8,128)(2,1)} %source.1), channel_id=1, source_target_pairs={{0,1},{1,0},{2,3},{3,2},{4,5},{5,4},{6,7},{7,6},{8,9},{9,8},{10,11... | collective-permute-start | bytes 393224 | tf_op jit(solution)/shard_map/ppermute | solution.py:530
  3.3 16.3 %collective-permute-start.1 = (bf16[2,64,1024]{2,1,0:T(8,128)(2,1)S(1)}, bf16[2,64,1024]{2,1,0:T(8,128)(2,1)S(1)}, u32[]{:S(2)}, u32[]{:S(2)}) collective-permute-start(bf16[2,64,1024]{2,1,0:T(8,128)(2,1)S(1)} %bitcast_dynamic-update-slice_fusion.both), channel_id=1, source_target_pairs={{0,2},{1,127},{2,4},{3,1},{4,6},{5,3},{6,8},{7,5},{8,10},{9,7},{10... | collective-permute-start | bytes 786440 | tf_op jit(solution)/shard_map/ppermute | solution.py:533
  11.9 10.8 %collective-permute-start.2 = (bf16[2,64,1024]{2,1,0:T(8,128)(2,1)S(1)}, bf16[2,64,1024]{2,1,0:T(8,128)(2,1)S(1)}, u32[]{:S(2)}, u32[]{:S(2)}) collective-permute-start(bf16[2,64,1024]{2,1,0:T(8,128)(2,1)S(1)} %bitcast_dynamic-update-slice_fusion.both), channel_id=1, source_target_pairs={{0,4},{1,125},{2,6},{3,127},{4,8},{5,1},{6,10},{7,3},{8,12},{9,5},... | collective-permute-start | bytes 786440 | tf_op jit(solution)/shard_map/ppermute | solution.py:533
  11.9 12.7 %collective-permute-start.3 = (bf16[2,64,1024]{2,1,0:T(8,128)(2,1)S(1)}, bf16[2,64,1024]{2,1,0:T(8,128)(2,1)S(1)}, u32[]{:S(2)}, u32[]{:S(2)}) collective-permute-start(bf16[2,64,1024]{2,1,0:T(8,128)(2,1)S(1)} %bitcast_dynamic-update-slice_fusion.both), channel_id=1, source_target_pairs={{0,6},{1,123},{2,8},{3,125},{4,10},{5,127},{6,12},{7,1},{8,14},{9,... | collective-permute-start | bytes 786440 | tf_op jit(solution)/shard_map/ppermute | solution.py:533
  19.6 14.4 %copy-start = (bf16[4,256,256]{2,1,0:T(8,128)(2,1)S(1)}, bf16[4,256,256]{2,1,0:T(8,128)(2,1)}, u32[]{:S(2)}) copy-start(bf16[4,256,256]{2,1,0:T(8,128)(2,1)} %diag.3) | copy-start | bytes 1572868
  24.7 9.2 %collective-permute-start.4 = (bf16[5,64,1024]{2,1,0:T(8,128)(2,1)S(1)}, bf16[5,64,1024]{2,1,0:T(8,128)(2,1)S(1)}, u32[]{:S(2)}, u32[]{:S(2)}) collective-permute-start(bf16[5,64,1024]{2,1,0:T(8,128)(2,1)S(1)} %pad_maximum_fusion), channel_id=1, source_target_pairs={{0,1},{1,0},{2,3},{3,2},{4,5},{5,4},{6,7},{7,6},{8,9},{9,8},{10,11... | collective-permute-start | bytes 1966088 | tf_op jit(solution)/shard_map/ppermute | solution.py:530
  24.8 2.5 %collective-permute-start.5 = (s16[7,80,256]{2,1,0:T(8,128)(2,1)S(1)}, s16[7,80,256]{2,1,0:T(8,128)(2,1)S(1)}, u32[]{:S(2)}, u32[]{:S(2)}) collective-permute-start(s16[7,80,256]{2,1,0:T(8,128)(2,1)S(1)} %get-tuple-element.46), channel_id=1, source_target_pairs={{0,1},{1,0},{2,3},{3,2},{4,5},{5,4},{6,7},{7,6},{8,9},{9,8},{10,11... | collective-permute-start | bytes 860168 | tf_op jit(solution)/shard_map/ppermute | solution.py:530
  27.3 14.9 %collective-permute-start.6 = (s16[4,80,256]{2,1,0:T(8,128)(2,1)S(1)}, s16[4,80,256]{2,1,0:T(8,128)(2,1)S(1)}, u32[]{:S(2)}, u32[]{:S(2)}) collective-permute-start(s16[4,80,256]{2,1,0:T(8,128)(2,1)S(1)} %get-tuple-element.80), channel_id=1, source_target_pairs={{0,2},{1,127},{2,4},{3,1},{4,6},{5,3},{6,8},{7,5},{8,10},{9,7},{10... | collective-permute-start | bytes 491528 | tf_op jit(solution)/shard_map/ppermute | solution.py:533
  31.0 11.2 %collective-permute-start.7 = (s16[4,80,256]{2,1,0:T(8,128)(2,1)S(1)}, s16[4,80,256]{2,1,0:T(8,128)(2,1)S(1)}, u32[]{:S(2)}, u32[]{:S(2)}) collective-permute-start(s16[4,80,256]{2,1,0:T(8,128)(2,1)S(1)} %get-tuple-element.79), channel_id=1, source_target_pairs={{0,4},{1,125},{2,6},{3,127},{4,8},{5,1},{6,10},{7,3},{8,12},{9,5},... | collective-permute-start | bytes 491528 | tf_op jit(solution)/shard_map/ppermute | solution.py:533
  33.9 8.3 %collective-permute-start.8 = (s16[3,80,256]{2,1,0:T(8,128)(2,1)S(1)}, s16[3,80,256]{2,1,0:T(8,128)(2,1)S(1)}, u32[]{:S(2)}, u32[]{:S(2)}) collective-permute-start(s16[3,80,256]{2,1,0:T(8,128)(2,1)S(1)} %get-tuple-element.78), channel_id=1, source_target_pairs={{0,6},{1,123},{2,8},{3,125},{4,10},{5,127},{6,12},{7,1},{8,14},{9,... | collective-permute-start | bytes 368648 | tf_op jit(solution)/shard_map/ppermute | solution.py:533
  42.3 1.5 %collective-permute-start.9 = (s16[5,80,256]{2,1,0:T(8,128)(2,1)S(1)}, s16[5,80,256]{2,1,0:T(8,128)(2,1)S(1)}, u32[]{:S(2)}, u32[]{:S(2)}) collective-permute-start(s16[5,80,256]{2,1,0:T(8,128)(2,1)S(1)} %pad_add_fusion), channel_id=1, source_target_pairs={{0,1},{1,0},{2,3},{3,2},{4,5},{5,4},{6,7},{7,6},{8,9},{9,8},{10,11... | collective-permute-start | bytes 614408 | tf_op jit(solution)/shard_map/ppermute | solution.py:530
  45.0 1.6 %collective-permute-start.10 = (bf16[7,64,256]{2,1,0:T(8,128)(2,1)S(1)}, bf16[7,64,256]{2,1,0:T(8,128)(2,1)S(1)}, u32[]{:S(2)}, u32[]{:S(2)}) collective-permute-start(bf16[7,64,256]{2,1,0:T(8,128)(2,1)S(1)} %get-tuple-element.60), channel_id=1, source_target_pairs={{0,1},{1,0},{2,3},{3,2},{4,5},{5,4},{6,7},{7,6},{8,9},{9,8},{10,11... | collective-permute-start | bytes 688136 | tf_op jit(solution)/shard_map/ppermute | solution.py:530
  46.5 12.5 %collective-permute-start.11 = (bf16[4,64,256]{2,1,0:T(8,128)(2,1)S(1)}, bf16[4,64,256]{2,1,0:T(8,128)(2,1)S(1)}, u32[]{:S(2)}, u32[]{:S(2)}) collective-permute-start(bf16[4,64,256]{2,1,0:T(8,128)(2,1)S(1)} %get-tuple-element.86), channel_id=1, source_target_pairs={{0,2},{1,127},{2,4},{3,1},{4,6},{5,3},{6,8},{7,5},{8,10},{9,7},{10... | collective-permute-start | bytes 393224 | tf_op jit(solution)/shard_map/ppermute | solution.py:533
  50.1 8.9 %collective-permute-start.12 = (bf16[4,64,256]{2,1,0:T(8,128)(2,1)S(1)}, bf16[4,64,256]{2,1,0:T(8,128)(2,1)S(1)}, u32[]{:S(2)}, u32[]{:S(2)}) collective-permute-start(bf16[4,64,256]{2,1,0:T(8,128)(2,1)S(1)} %get-tuple-element.85), channel_id=1, source_target_pairs={{0,4},{1,125},{2,6},{3,127},{4,8},{5,1},{6,10},{7,3},{8,12},{9,5},... | collective-permute-start | bytes 393224 | tf_op jit(solution)/shard_map/ppermute | solution.py:533
  50.1 8.9 %collective-permute-start.13 = (bf16[3,64,256]{2,1,0:T(8,128)(2,1)S(1)}, bf16[3,64,256]{2,1,0:T(8,128)(2,1)S(1)}, u32[]{:S(2)}, u32[]{:S(2)}) collective-permute-start(bf16[3,64,256]{2,1,0:T(8,128)(2,1)S(1)} %get-tuple-element.84), channel_id=1, source_target_pairs={{0,6},{1,123},{2,8},{3,125},{4,10},{5,127},{6,12},{7,1},{8,14},{9,... | collective-permute-start | bytes 294920 | tf_op jit(solution)/shard_map/ppermute | solution.py:533
  59.0 1.5 %collective-permute-start.15 = (bf16[7,64,256]{2,1,0:T(8,128)(2,1)S(1)}, bf16[7,64,256]{2,1,0:T(8,128)(2,1)S(1)}, u32[]{:S(2)}, u32[]{:S(2)}) collective-permute-start(bf16[7,64,256]{2,1,0:T(8,128)(2,1)S(1)} %get-tuple-element.69), channel_id=1, source_target_pairs={{0,1},{1,0},{2,3},{3,2},{4,5},{5,4},{6,7},{7,6},{8,9},{9,8},{10,11... | collective-permute-start | bytes 688136 | tf_op jit(solution)/shard_map/ppermute | solution.py:530
  59.2 6.0 %collective-permute-start.14 = (bf16[5,64,256]{2,1,0:T(8,128)(2,1)S(1)}, bf16[5,64,256]{2,1,0:T(8,128)(2,1)S(1)}, u32[]{:S(2)}, u32[]{:S(2)}) collective-permute-start(bf16[5,64,256]{2,1,0:T(8,128)(2,1)S(1)} %pad_maximum_fusion.1), channel_id=1, source_target_pairs={{0,1},{1,0},{2,3},{3,2},{4,5},{5,4},{6,7},{7,6},{8,9},{9,8},{10,11... | collective-permute-start | bytes 491528 | tf_op jit(solution)/shard_map/ppermute | solution.py:530
  60.5 13.5 %collective-permute-start.16 = (bf16[4,64,256]{2,1,0:T(8,128)(2,1)S(1)}, bf16[4,64,256]{2,1,0:T(8,128)(2,1)S(1)}, u32[]{:S(2)}, u32[]{:S(2)}) collective-permute-start(bf16[4,64,256]{2,1,0:T(8,128)(2,1)S(1)} %get-tuple-element.83), channel_id=1, source_target_pairs={{0,2},{1,127},{2,4},{3,1},{4,6},{5,3},{6,8},{7,5},{8,10},{9,7},{10... | collective-permute-start | bytes 393224 | tf_op jit(solution)/shard_map/ppermute | solution.py:533
  65.1 8.9 %collective-permute-start.17 = (bf16[4,64,256]{2,1,0:T(8,128)(2,1)S(1)}, bf16[4,64,256]{2,1,0:T(8,128)(2,1)S(1)}, u32[]{:S(2)}, u32[]{:S(2)}) collective-permute-start(bf16[4,64,256]{2,1,0:T(8,128)(2,1)S(1)} %get-tuple-element.82), channel_id=1, source_target_pairs={{0,4},{1,125},{2,6},{3,127},{4,8},{5,1},{6,10},{7,3},{8,12},{9,5},... | collective-permute-start | bytes 393224 | tf_op jit(solution)/shard_map/ppermute | solution.py:533
  65.1 8.9 %collective-permute-start.18 = (bf16[3,64,256]{2,1,0:T(8,128)(2,1)S(1)}, bf16[3,64,256]{2,1,0:T(8,128)(2,1)S(1)}, u32[]{:S(2)}, u32[]{:S(2)}) collective-permute-start(bf16[3,64,256]{2,1,0:T(8,128)(2,1)S(1)} %get-tuple-element.81), channel_id=1, source_target_pairs={{0,6},{1,123},{2,8},{3,125},{4,10},{5,127},{6,12},{7,1},{8,14},{9,... | collective-permute-start | bytes 294920 | tf_op jit(solution)/shard_map/ppermute | solution.py:533
  74.1 1.5 %collective-permute-start.19 = (bf16[5,64,256]{2,1,0:T(8,128)(2,1)S(1)}, bf16[5,64,256]{2,1,0:T(8,128)(2,1)S(1)}, u32[]{:S(2)}, u32[]{:S(2)}) collective-permute-start(bf16[5,64,256]{2,1,0:T(8,128)(2,1)S(1)} %pad_maximum_fusion.2), channel_id=1, source_target_pairs={{0,1},{1,0},{2,3},{3,2},{4,5},{5,4},{6,7},{7,6},{8,9},{9,8},{10,11... | collective-permute-start | bytes 491528 | tf_op jit(solution)/shard_map/ppermute | solution.py:530

commit v6 on v5

--- a/solution.py
+++ b/solution.py
@@ -320,8 +320,8 @@
 
 def image_first(
     partial, r1, r2, r3, post, got,
-    image, rounded, wanted, m1, m2, m3, give,
-    draft, sem,
+    image, rounded, marked, m1, m2, m3, give,
+    draft, wanted, sem,
 ):
     ins = (r1, r2, r3, post, got)
     places = [place_in(rho) for rho in range(PEERS)]
@@ -332,6 +332,7 @@
     packed = jnp.zeros((1, SLOTS), jnp.int32)
     for rho, mark in enumerate(marks):
         packed = jnp.where(lane == rho, mark[:, 0:SLOTS], packed)
+        marked[rho : rho + 1] = mark
     draft[...] = packed
     copy = pltpu.make_async_copy(draft, wanted, sem)
     copy.start()
@@ -385,14 +386,25 @@
     out[...] = acc[0:CL]
 
 
-def image_second(partial, wanted, r1, r2, r3, post, got, image, acc):
+def image_second(partial, marked, r1, r2, r3, post, got, image, acc, sem):
     ins = (r1, r2, r3, post, got)
-    acc[...] = partial[...]
-    for rho in range(PEERS):
-        message, index = place_in(rho)
-        acc[wanted[0, rho]] += ins[message][index].astype(F32)
-    for cluster in range(CL):
-        image[:, cluster * B : (cluster + 1) * B] = acc[cluster]
+    places = [place_in(rho) for rho in range(PEERS)]
+    marks = [marked[rho : rho + 1] for rho in range(PEERS)]
+    copies = []
+    for first in range(0, RHS, STRIP):
+        rows = slice(first, first + STRIP)
+        totals = [partial[cluster, rows] for cluster in range(CL)]
+        for (message, index), mark in zip(places, marks):
+            block = ins[message][index, rows].astype(F32)
+            mark = jnp.broadcast_to(mark, (STRIP, B))
+            for cluster in range(CL):
+                totals[cluster] += jnp.where(mark == cluster, block, 0.0)
+        for cluster in range(CL):
+            acc[rows, cluster * B : (cluster + 1) * B] = totals[cluster]
+        copies.append(pltpu.make_async_copy(acc.at[rows], image.at[rows], sem.at[first // STRIP]))
+        copies[-1].start()
+    for copy in copies:
+        copy.wait()
 
 
 SMEM = pl.BlockSpec(memory_space=pltpu.SMEM)
@@ -474,12 +486,12 @@
         [
             pltpu.VMEM((RHS, CL * B), F32),
             shaped((CL, RHS, B), BF16),
-            shaped((1, SLOTS), jnp.int32),
+            shaped((16, B), jnp.int32),
         ]
         + message_shapes(RHS, BF16),
-        [VMEM] * 2 + [SMEM] + [VMEM] * 4,
+        [VMEM] * 7,
         [VMEM] * 6,
-        [pltpu.VMEM((1, SLOTS), jnp.int32), pltpu.SemaphoreType.DMA],
+        [pltpu.VMEM((1, SLOTS), jnp.int32), pltpu.SMEM((1, SLOTS), jnp.int32), pltpu.SemaphoreType.DMA],
     )(*args)
 
 
@@ -505,9 +517,9 @@
 def k6(*args):
     return call(
         image_second, "second_image",
-        shaped((RHS, CL * B), F32), VMEM,
-        [VMEM, SMEM] + [VMEM] * 5,
-        [pltpu.VMEM((CL, RHS, B), F32)],
+        shaped((RHS, CL * B), F32), HBM,
+        [VMEM] * 7,
+        [pltpu.VMEM((RHS, CL * B), F32), pltpu.SemaphoreType.DMA((RHS // STRIP,))],
     )(*args)
 
 
@@ -556,14 +568,15 @@
     m1, m2, m3, give, plan, *held = k1(
         me, *lists, in_hbm(counts), both, in_hbm(near_blocks), in_hbm(far_left), in_hbm(far_right)
     )
-    halo, m1 = lax.optimization_barrier((halo, m1))
+    halo, give = lax.optimization_barrier((halo, give))
     r1, r2, r3, got, messages = exchange(m1, m2, m3, give)
+    halo, got = lax.optimization_barrier((halo, got))
     halo_post = swap(jnp.concatenate([halo[0], halo[1], halo[2][1:]]))
     halo_post, messages = lax.optimization_barrier((halo_post, messages))
     partial = k2(plan, both, *halo, halo_post, diag_blocks, *held)
     partial, r1, r2, r3 = lax.optimization_barrier((partial, r1, r2, r3))
     post = passed_on(r1, r2, r3)
-    first_image, rounded, wanted, m1, m2, m3, give = k3(partial, r1, r2, r3, post, got)
+    first_image, rounded, marked, m1, m2, m3, give = k3(partial, r1, r2, r3, post, got)
     f1, f2, f3, f_got, messages = exchange(m1, m2, m3, give)
     rounded, messages = lax.optimization_barrier((rounded, messages))
     m1, m2, m3, give = k4(plan, rounded, *held)
@@ -574,7 +587,7 @@
     partial = k5(plan, rounded, f1, f2, f3, f_post, f_got, diag_blocks, *held)
     partial, r1, r2, r3 = lax.optimization_barrier((partial, r1, r2, r3))
     post = passed_on(r1, r2, r3)
-    return first_image, k6(partial, wanted, r1, r2, r3, post, got)
+    return first_image, k6(partial, marked, r1, r2, r3, post, got)
 
 
 def solution(mesh):

time: 77.1 us -> 75.7 us (0.982)
  waiting for transfers between devices: 23.2 us -> 18.4 us
  Pallas kernels: 24.7 us -> 28.1 us
    ppermute x12, waiting for transfers between devices: 16.6 us -> 12.2 us  [carry(): return lax.ppermute(block, 'rows', carriers(size, k))]
    pallas_call x1, Pallas kernels: 5.21 us -> 6.44 us  [k2(): call(forward_first, 'forward_products', shaped((CL, RHS, B), F32), VMEM,...]
    pallas_call x1, Pallas kernels: 5.22 us -> 6.44 us  [k5(): call(forward_second, 'second_forward_products', shaped((CL, RHS, B), F32)...]
    pallas_call x1, Pallas kernels: 6.79 us -> 7.8 us  [k1(): call(back_first, 'transposed_products', message_shapes(RHS + EXTRA, jnp.i...]
    pallas_call x1, Pallas kernels: 4.03 us -> 4.92 us  [k4(): call(back_second, 'second_transposed_products', message_shapes(RHS, BF16)...]
  transfers between devices with their start and end apart: 20 -> 20, of which waited for: 11 -> 11; matrix products, arithmetic and copies ran while one was open for 1% -> 1% of each run, Pallas kernels for 29% -> 35%
where the time goes in v6:
time: 75.7 us; the launch traced here: 75.6 us
  Pallas kernels  28.1 us (37%)
  starting transfers between devices  27.1 us (36%)
  waiting for transfers between devices  18.4 us (24%)
  between operations  1.01 us (1%)
  local copies, waits for them, and re-layouts  0.83 us (1%)
    ppermute x12, starting transfers between devices, carry(): return lax.ppermute(block, 'rows', carriers(size, k))  24.5 us
    ppermute x12, waiting for transfers between devices, carry(): return lax.ppermute(block, 'rows', carriers(size, k))  12.2 us
    pallas_call x1, Pallas kernels, k1(): call(back_first, 'transposed_products', message_shapes(RHS + EXTRA, jnp.i...  7.8 us
    pallas_call x1, Pallas kernels, k5(): call(forward_second, 'second_forward_products', shaped((CL, RHS, B), F32)...  6.44 us
    pallas_call x1, Pallas kernels, k2(): call(forward_first, 'forward_products', shaped((CL, RHS, B), F32), VMEM,...  6.44 us
    ppermute x8, waiting for transfers between devices, swap(): return lax.ppermute(block, 'rows', [(i, i ^ 1) for i in range(size)])  6.16 us
    pallas_call x1, Pallas kernels, k4(): call(back_second, 'second_transposed_products', message_shapes(RHS, BF16)...  4.92 us
    ppermute x8, starting transfers between devices, swap(): return lax.ppermute(block, 'rows', [(i, i ^ 1) for i in range(size)])  2.68 us
  transfers between devices with their start and end apart: 20, of which 11 were waited for; matrix products, arithmetic and copies ran while one was open for 1% of the time, Pallas kernels for 35%

profile of v6, /device:TPU:1, one launch (start us, length us, event | category | flops | bytes accessed | tf_op | source)
XLA Modules:
  0.0 75.6 jit_solution(1414384453328055468)
XLA Ops:
  0.6 1.5 %collective-permute-start = (bf16[64,1024]{1,0:T(8,128)(2,1)}, bf16[64,1024]{1,0:T(8,128)(2,1)S(1)}, u32[]{:S(2)}, u32[]{:S(2)}) collective-permute-start(bf16[64,1024]{1,0:T(8,128)(2,1)} %source.1), channel_id=1, source_target_pairs={{0,1},{1,0},{2,3},{3,2},{4,5},{5,4},{6,7},{7,6},{8,9},{9,8},{10,11... | collective-permute-start | bytes 393224 | tf_op jit(solution)/shard_map/ppermute | solution.py:542
  2.1 0.9 %staged.1 = bf16[2,64,1024]{2,1,0:T(8,128)(2,1)S(1)} custom-call(bf16[64,1024]{1,0:T(8,128)(2,1)} %source.1), custom_call_target="tpu_custom_call" | custom-call | flops 2000000000 | bytes 22000000 | tf_op jit(solution)/shard_map/staged/pallas_call | solution.py:444
  3.0 0.3 collective-permute-done
  3.3 8.6 %collective-permute-start.1 = (bf16[2,64,1024]{2,1,0:T(8,128)(2,1)S(1)}, bf16[2,64,1024]{2,1,0:T(8,128)(2,1)S(1)}, u32[]{:S(2)}, u32[]{:S(2)}) collective-permute-start(bf16[2,64,1024]{2,1,0:T(8,128)(2,1)S(1)} %bitcast_dynamic-update-slice_fusion.both), channel_id=1, source_target_pairs={{0,2},{1,127},{2,4},{3,1},{4,6},{5,3},{6,8},{7,5},{8,10},{9,7},{10... | collective-permute-start | bytes 786440 | tf_op jit(solution)/shard_map/ppermute | solution.py:545
  11.9 0.0 collective-permute-start.2
  11.9 0.9 %collective-permute-start.3 = (bf16[2,64,1024]{2,1,0:T(8,128)(2,1)S(1)}, bf16[2,64,1024]{2,1,0:T(8,128)(2,1)S(1)}, u32[]{:S(2)}, u32[]{:S(2)}) collective-permute-start(bf16[2,64,1024]{2,1,0:T(8,128)(2,1)S(1)} %bitcast_dynamic-update-slice_fusion.both), channel_id=1, source_target_pairs={{0,6},{1,123},{2,8},{3,125},{4,10},{5,127},{6,12},{7,1},{8,14},{9,... | collective-permute-start | bytes 786440 | tf_op jit(solution)/shard_map/ppermute | solution.py:545
  12.8 7.8 %transposed_products.1 = (s16[4,80,256]{2,1,0:T(8,128)(2,1)S(1)}, s16[4,80,256]{2,1,0:T(8,128)(2,1)S(1)}, s16[3,80,256]{2,1,0:T(8,128)(2,1)S(1)}, s16[7,80,256]{...) custom-call(s32[1]{0:T(128)} %bitcast.me, ...), custom_call_target="tpu_custom_call" | custom-call | flops 2000000000 | bytes 22000000 | tf_op jit(solution)/shard_map/transposed_products/pallas_call | solution.py:449
  20.6 0.0 copy-start
  20.6 0.0 collective-permute-done.1.h1
  20.6 2.1 %collective-permute-done.2.h2 = bf16[2,64,1024]{2,1,0:T(8,128)(2,1)S(1)} collective-permute-done((bf16[2,64,1024]{2,1,0:T(8,128)(2,1)S(1)}, bf16[2,64,1024]{2,1,0:T(8,128)(2,1)S(1)}, u32[]{:S(2)}, u32[]{:S(2)}) %collective-permute-start.2) | collective-permute-done | bytes 262176 | tf_op jit(solution)/shard_map/ppermute | solution.py:545
  22.7 1.9 %collective-permute-done.3.h3 = bf16[2,64,1024]{2,1,0:T(8,128)(2,1)S(1)} collective-permute-done((bf16[2,64,1024]{2,1,0:T(8,128)(2,1)S(1)}, bf16[2,64,1024]{2,1,0:T(8,128)(2,1)S(1)}, u32[]{:S(2)}, u32[]{:S(2)}) %collective-permute-start.3) | collective-permute-done | bytes 262176 | tf_op jit(solution)/shard_map/ppermute | solution.py:545
  24.6 0.0 collective-permute-start.4
  24.6 1.6 %collective-permute-done.4.got = s16[7,80,256]{2,1,0:T(8,128)(2,1)S(1)} collective-permute-done((s16[7,80,256]{2,1,0:T(8,128)(2,1)S(1)}, s16[7,80,256]{2,1,0:T(8,128)(2,1)S(1)}, u32[]{:S(2)}, u32[]{:S(2)}) %collective-permute-start.4) | collective-permute-done | bytes 286752 | tf_op jit(solution)/shard_map/ppermute | solution.py:542
  26.2 0.1 pad_maximum_fusion
  26.3 0.2 collective-permute-start.5
  26.5 3.9 %collective-permute-start.6 = (s16[4,80,256]{2,1,0:T(8,128)(2,1)S(1)}, s16[4,80,256]{2,1,0:T(8,128)(2,1)S(1)}, u32[]{:S(2)}, u32[]{:S(2)}) collective-permute-start(s16[4,80,256]{2,1,0:T(8,128)(2,1)S(1)} %get-tuple-element.88), channel_id=1, source_target_pairs={{0,2},{1,127},{2,4},{3,1},{4,6},{5,3},{6,8},{7,5},{8,10},{9,7},{10... | collective-permute-start | bytes 491528 | tf_op jit(solution)/shard_map/ppermute | solution.py:545
  30.5 2.7 %collective-permute-start.7 = (s16[4,80,256]{2,1,0:T(8,128)(2,1)S(1)}, s16[4,80,256]{2,1,0:T(8,128)(2,1)S(1)}, u32[]{:S(2)}, u32[]{:S(2)}) collective-permute-start(s16[4,80,256]{2,1,0:T(8,128)(2,1)S(1)} %get-tuple-element.87), channel_id=1, source_target_pairs={{0,4},{1,125},{2,6},{3,127},{4,8},{5,1},{6,10},{7,3},{8,12},{9,5},... | collective-permute-start | bytes 491528 | tf_op jit(solution)/shard_map/ppermute | solution.py:545
  33.1 0.0 collective-permute-start.8
  33.1 0.0 collective-permute-done.5.post
  33.2 6.4 %forward_products.1.partial = f32[4,64,256]{2,1,0:T(8,128)S(1)} custom-call(s32[4,256]{1,0:T(4,128)S(1)} %get-tuple-element.44.plan, bf16[2,64,1024]{2,1,0:T(8,128)(2,1)S(1)} %bitcast_dynamic-update-slice_fusion.both, bf16[2,64,1024]{2,1,0:T(8,128)(2,1)S(1)} %collective-permute-done.1.h1, bf16[2,64,1024]{2,1,0:T(8,128)(2,1)S(1)} %collective-permute-done.2.h2, ...), custom_call_target="tpu_custom_call" | custom-call | flops 2000000000 | bytes 22000000 | tf_op jit(solution)/shard_map/forward_products/pallas_call | solution.py:475
  39.6 1.8 %collective-permute-done.8.r3 = s16[3,80,256]{2,1,0:T(8,128)(2,1)S(1)} collective-permute-done((s16[3,80,256]{2,1,0:T(8,128)(2,1)S(1)}, s16[3,80,256]{2,1,0:T(8,128)(2,1)S(1)}, u32[]{:S(2)}, u32[]{:S(2)}) %collective-permute-start.8) | collective-permute-done | bytes 122912 | tf_op jit(solution)/shard_map/ppermute | solution.py:545
  41.4 0.0 collective-permute-done.6.r1
  41.4 0.0 collective-permute-done.7.r2
  41.5 0.1 collective-permute-start.9
  41.6 1.4 %collective-permute-done.9.post = s16[5,80,256]{2,1,0:T(8,128)(2,1)S(1)} collective-permute-done((s16[5,80,256]{2,1,0:T(8,128)(2,1)S(1)}, s16[5,80,256]{2,1,0:T(8,128)(2,1)S(1)}, u32[]{:S(2)}, u32[]{:S(2)}) %collective-permute-start.9) | collective-permute-done | bytes 204832 | tf_op jit(solution)/shard_map/ppermute | solution.py:542
  43.0 0.6 first_image.1
  43.6 0.2 collective-permute-start.10
  43.8 1.4 %collective-permute-done.10.got = bf16[7,64,256]{2,1,0:T(8,128)(2,1)S(1)} collective-permute-done((bf16[7,64,256]{2,1,0:T(8,128)(2,1)S(1)}, bf16[7,64,256]{2,1,0:T(8,128)(2,1)S(1)}, u32[]{:S(2)}, u32[]{:S(2)}) %collective-permute-start.10) | collective-permute-done | bytes 229408 | tf_op jit(solution)/shard_map/ppermute | solution.py:542
  45.2 3.8 %collective-permute-start.11 = (bf16[4,64,256]{2,1,0:T(8,128)(2,1)S(1)}, bf16[4,64,256]{2,1,0:T(8,128)(2,1)S(1)}, u32[]{:S(2)}, u32[]{:S(2)}) collective-permute-start(bf16[4,64,256]{2,1,0:T(8,128)(2,1)S(1)} %get-tuple-element.94), channel_id=1, source_target_pairs={{0,2},{1,127},{2,4},{3,1},{4,6},{5,3},{6,8},{7,5},{8,10},{9,7},{10... | collective-permute-start | bytes 393224 | tf_op jit(solution)/shard_map/ppermute | solution.py:545
  49.0 0.0 collective-permute-start.12
  49.0 0.0 collective-permute-start.13
  49.0 4.9 %second_transposed_products.1 = (bf16[4,64,256]{2,1,0:T(8,128)(2,1)S(1)}, bf16[4,64,256]{2,1,0:T(8,128)(2,1)S(1)}, bf16[3,64,256]{2,1,0:T(8,128)(2,1)S(1)}, bf16[7,64,256]{2,1,0:T(8,128)(2,1)S(1)}) custom-call(s32[4,256]{1,0:T(4,128)S(1)} %get-tuple-element.44.plan, bf16[4,64,256]{2,1,0:T(8,128)(2,1)S(1)} %get-tuple-element.71.rounded.own, ...), custom_call_target="tpu_custom_call" | custom-call | flops 2000000000 | bytes 22000000 | tf_op jit(solution)/shard_map/second_transposed_products/pallas_call | solution.py:499
  53.9 4.0 %collective-permute-done.13.r3 = bf16[3,64,256]{2,1,0:T(8,128)(2,1)S(1)} collective-permute-done((bf16[3,64,256]{2,1,0:T(8,128)(2,1)S(1)}, bf16[3,64,256]{2,1,0:T(8,128)(2,1)S(1)}, u32[]{:S(2)}, u32[]{:S(2)}) %collective-permute-start.13) | collective-permute-done | bytes 98336 | tf_op jit(solution)/shard_map/ppermute | solution.py:545
  57.9 0.0 collective-permute-done.11.r1
  57.9 0.0 collective-permute-done.12.r2
  57.9 0.0 collective-permute-start.15
  58.0 0.6 collective-permute-start.14
  58.5 0.8 %collective-permute-done.15.got = bf16[7,64,256]{2,1,0:T(8,128)(2,1)S(1)} collective-permute-done((bf16[7,64,256]{2,1,0:T(8,128)(2,1)S(1)}, bf16[7,64,256]{2,1,0:T(8,128)(2,1)S(1)}, u32[]{:S(2)}, u32[]{:S(2)}) %collective-permute-start.15) | collective-permute-done | bytes 229408 | tf_op jit(solution)/shard_map/ppermute | solution.py:542
  59.4 4.6 %collective-permute-start.16 = (bf16[4,64,256]{2,1,0:T(8,128)(2,1)S(1)}, bf16[4,64,256]{2,1,0:T(8,128)(2,1)S(1)}, u32[]{:S(2)}, u32[]{:S(2)}) collective-permute-start(bf16[4,64,256]{2,1,0:T(8,128)(2,1)S(1)} %get-tuple-element.91), channel_id=1, source_target_pairs={{0,2},{1,127},{2,4},{3,1},{4,6},{5,3},{6,8},{7,5},{8,10},{9,7},{10... | collective-permute-start | bytes 393224 | tf_op jit(solution)/shard_map/ppermute | solution.py:545
  64.0 0.0 collective-permute-start.17
  64.0 0.0 collective-permute-start.18
  64.0 0.0 collective-permute-done.14.post
  64.0 6.4 %second_forward_products.1.partial = f32[4,64,256]{2,1,0:T(8,128)S(1)} custom-call(s32[4,256]{1,0:T(4,128)S(1)} %get-tuple-element.44.plan, bf16[4,64,256]{2,1,0:T(8,128)(2,1)S(1)} %get-tuple-element.71.rounded.own, bf16[4,64,256]{2,1,0:T(8,128)(2,1)S(1)} %collective-permute-done.11.r1, bf16[4,64,256]{2,1,0:T(8,128)(2,1)S(1)} %collective-permute-done.12.r2, ...), custom_call_target="tpu_custom_call" | custom-call | flops 2000000000 | bytes 22000000 | tf_op jit(solution)/shard_map/second_forward_products/pallas_call | solution.py:509
  70.5 2.4 %collective-permute-done.18.r3 = bf16[3,64,256]{2,1,0:T(8,128)(2,1)S(1)} collective-permute-done((bf16[3,64,256]{2,1,0:T(8,128)(2,1)S(1)}, bf16[3,64,256]{2,1,0:T(8,128)(2,1)S(1)}, u32[]{:S(2)}, u32[]{:S(2)}) %collective-permute-start.18) | collective-permute-done | bytes 98336 | tf_op jit(solution)/shard_map/ppermute | solution.py:545
  73.0 0.1 collective-permute-start.19
  73.1 0.7 copy.22
  73.8 0.7 collective-permute-done.19.post
  74.4 1.0 %second_image.1 = f32[64,1024]{1,0:T(8,128)} custom-call(f32[4,64,256]{2,1,0:T(8,128)S(1)} %second_forward_products.1.partial, s32[16,256]{1,0:T(8,128)S(1)} %get-tuple-element.82.marked, bf16[4,64,256]{2,1,0:T(8,128)(2,1)S(1)} %collective-permute-done.16.r1, bf16[4,64,256]{2,1,0:T(8,128)(2,1)S(1)} %collective-permute-done.17.r2, ...), custom_call_target="tpu_custom_call" | custom-call | flops 2000000000 | bytes 22000000 | tf_op jit(solution)/shard_map/second_image/pallas_call | solution.py:518
  (20 shorter events, 0.2 us)
Async XLA Ops:
  0.6 2.7 %collective-permute-start = (bf16[64,1024]{1,0:T(8,128)(2,1)}, bf16[64,1024]{1,0:T(8,128)(2,1)S(1)}, u32[]{:S(2)}, u32[]{:S(2)}) collective-permute-start(bf16[64,1024]{1,0:T(8,128)(2,1)} %source.1), channel_id=1, source_target_pairs={{0,1},{1,0},{2,3},{3,2},{4,5},{5,4},{6,7},{7,6},{8,9},{9,8},{10,11... | collective-permute-start | bytes 393224 | tf_op jit(solution)/shard_map/ppermute | solution.py:542
  3.3 17.3 %collective-permute-start.1 = (bf16[2,64,1024]{2,1,0:T(8,128)(2,1)S(1)}, bf16[2,64,1024]{2,1,0:T(8,128)(2,1)S(1)}, u32[]{:S(2)}, u32[]{:S(2)}) collective-permute-start(bf16[2,64,1024]{2,1,0:T(8,128)(2,1)S(1)} %bitcast_dynamic-update-slice_fusion.both), channel_id=1, source_target_pairs={{0,2},{1,127},{2,4},{3,1},{4,6},{5,3},{6,8},{7,5},{8,10},{9,7},{10... | collective-permute-start | bytes 786440 | tf_op jit(solution)/shard_map/ppermute | solution.py:545
  11.9 10.8 %collective-permute-start.2 = (bf16[2,64,1024]{2,1,0:T(8,128)(2,1)S(1)}, bf16[2,64,1024]{2,1,0:T(8,128)(2,1)S(1)}, u32[]{:S(2)}, u32[]{:S(2)}) collective-permute-start(bf16[2,64,1024]{2,1,0:T(8,128)(2,1)S(1)} %bitcast_dynamic-update-slice_fusion.both), channel_id=1, source_target_pairs={{0,4},{1,125},{2,6},{3,127},{4,8},{5,1},{6,10},{7,3},{8,12},{9,5},... | collective-permute-start | bytes 786440 | tf_op jit(solution)/shard_map/ppermute | solution.py:545
  11.9 12.7 %collective-permute-start.3 = (bf16[2,64,1024]{2,1,0:T(8,128)(2,1)S(1)}, bf16[2,64,1024]{2,1,0:T(8,128)(2,1)S(1)}, u32[]{:S(2)}, u32[]{:S(2)}) collective-permute-start(bf16[2,64,1024]{2,1,0:T(8,128)(2,1)S(1)} %bitcast_dynamic-update-slice_fusion.both), channel_id=1, source_target_pairs={{0,6},{1,123},{2,8},{3,125},{4,10},{5,127},{6,12},{7,1},{8,14},{9,... | collective-permute-start | bytes 786440 | tf_op jit(solution)/shard_map/ppermute | solution.py:545
  20.6 12.6 %copy-start = (bf16[4,256,256]{2,1,0:T(8,128)(2,1)S(1)}, bf16[4,256,256]{2,1,0:T(8,128)(2,1)}, u32[]{:S(2)}) copy-start(bf16[4,256,256]{2,1,0:T(8,128)(2,1)} %diag.3) | copy-start | bytes 1572868
  24.6 1.6 %collective-permute-start.4 = (s16[7,80,256]{2,1,0:T(8,128)(2,1)S(1)}, s16[7,80,256]{2,1,0:T(8,128)(2,1)S(1)}, u32[]{:S(2)}, u32[]{:S(2)}) collective-permute-start(s16[7,80,256]{2,1,0:T(8,128)(2,1)S(1)} %get-tuple-element.49), channel_id=1, source_target_pairs={{0,1},{1,0},{2,3},{3,2},{4,5},{5,4},{6,7},{7,6},{8,9},{9,8},{10,11... | collective-permute-start | bytes 860168 | tf_op jit(solution)/shard_map/ppermute | solution.py:542
  26.3 6.8 %collective-permute-start.5 = (bf16[5,64,1024]{2,1,0:T(8,128)(2,1)S(1)}, bf16[5,64,1024]{2,1,0:T(8,128)(2,1)S(1)}, u32[]{:S(2)}, u32[]{:S(2)}) collective-permute-start(bf16[5,64,1024]{2,1,0:T(8,128)(2,1)S(1)} %pad_maximum_fusion), channel_id=1, source_target_pairs={{0,1},{1,0},{2,3},{3,2},{4,5},{5,4},{6,7},{7,6},{8,9},{9,8},{10,11... | collective-permute-start | bytes 1966088 | tf_op jit(solution)/shard_map/ppermute | solution.py:542
  26.5 14.9 %collective-permute-start.6 = (s16[4,80,256]{2,1,0:T(8,128)(2,1)S(1)}, s16[4,80,256]{2,1,0:T(8,128)(2,1)S(1)}, u32[]{:S(2)}, u32[]{:S(2)}) collective-permute-start(s16[4,80,256]{2,1,0:T(8,128)(2,1)S(1)} %get-tuple-element.88), channel_id=1, source_target_pairs={{0,2},{1,127},{2,4},{3,1},{4,6},{5,3},{6,8},{7,5},{8,10},{9,7},{10... | collective-permute-start | bytes 491528 | tf_op jit(solution)/shard_map/ppermute | solution.py:545
  30.5 10.9 %collective-permute-start.7 = (s16[4,80,256]{2,1,0:T(8,128)(2,1)S(1)}, s16[4,80,256]{2,1,0:T(8,128)(2,1)S(1)}, u32[]{:S(2)}, u32[]{:S(2)}) collective-permute-start(s16[4,80,256]{2,1,0:T(8,128)(2,1)S(1)} %get-tuple-element.87), channel_id=1, source_target_pairs={{0,4},{1,125},{2,6},{3,127},{4,8},{5,1},{6,10},{7,3},{8,12},{9,5},... | collective-permute-start | bytes 491528 | tf_op jit(solution)/shard_map/ppermute | solution.py:545
  33.1 8.3 %collective-permute-start.8 = (s16[3,80,256]{2,1,0:T(8,128)(2,1)S(1)}, s16[3,80,256]{2,1,0:T(8,128)(2,1)S(1)}, u32[]{:S(2)}, u32[]{:S(2)}) collective-permute-start(s16[3,80,256]{2,1,0:T(8,128)(2,1)S(1)} %get-tuple-element.86), channel_id=1, source_target_pairs={{0,6},{1,123},{2,8},{3,125},{4,10},{5,127},{6,12},{7,1},{8,14},{9,... | collective-permute-start | bytes 368648 | tf_op jit(solution)/shard_map/ppermute | solution.py:545
  41.5 1.5 %collective-permute-start.9 = (s16[5,80,256]{2,1,0:T(8,128)(2,1)S(1)}, s16[5,80,256]{2,1,0:T(8,128)(2,1)S(1)}, u32[]{:S(2)}, u32[]{:S(2)}) collective-permute-start(s16[5,80,256]{2,1,0:T(8,128)(2,1)S(1)} %pad_add_fusion), channel_id=1, source_target_pairs={{0,1},{1,0},{2,3},{3,2},{4,5},{5,4},{6,7},{7,6},{8,9},{9,8},{10,11... | collective-permute-start | bytes 614408 | tf_op jit(solution)/shard_map/ppermute | solution.py:542
  43.6 1.6 %collective-permute-start.10 = (bf16[7,64,256]{2,1,0:T(8,128)(2,1)S(1)}, bf16[7,64,256]{2,1,0:T(8,128)(2,1)S(1)}, u32[]{:S(2)}, u32[]{:S(2)}) collective-permute-start(bf16[7,64,256]{2,1,0:T(8,128)(2,1)S(1)} %get-tuple-element.68), channel_id=1, source_target_pairs={{0,1},{1,0},{2,3},{3,2},{4,5},{5,4},{6,7},{7,6},{8,9},{9,8},{10,11... | collective-permute-start | bytes 688136 | tf_op jit(solution)/shard_map/ppermute | solution.py:542
  45.2 12.7 %collective-permute-start.11 = (bf16[4,64,256]{2,1,0:T(8,128)(2,1)S(1)}, bf16[4,64,256]{2,1,0:T(8,128)(2,1)S(1)}, u32[]{:S(2)}, u32[]{:S(2)}) collective-permute-start(bf16[4,64,256]{2,1,0:T(8,128)(2,1)S(1)} %get-tuple-element.94), channel_id=1, source_target_pairs={{0,2},{1,127},{2,4},{3,1},{4,6},{5,3},{6,8},{7,5},{8,10},{9,7},{10... | collective-permute-start | bytes 393224 | tf_op jit(solution)/shard_map/ppermute | solution.py:545
  49.0 8.9 %collective-permute-start.12 = (bf16[4,64,256]{2,1,0:T(8,128)(2,1)S(1)}, bf16[4,64,256]{2,1,0:T(8,128)(2,1)S(1)}, u32[]{:S(2)}, u32[]{:S(2)}) collective-permute-start(bf16[4,64,256]{2,1,0:T(8,128)(2,1)S(1)} %get-tuple-element.93), channel_id=1, source_target_pairs={{0,4},{1,125},{2,6},{3,127},{4,8},{5,1},{6,10},{7,3},{8,12},{9,5},... | collective-permute-start | bytes 393224 | tf_op jit(solution)/shard_map/ppermute | solution.py:545
  49.0 8.9 %collective-permute-start.13 = (bf16[3,64,256]{2,1,0:T(8,128)(2,1)S(1)}, bf16[3,64,256]{2,1,0:T(8,128)(2,1)S(1)}, u32[]{:S(2)}, u32[]{:S(2)}) collective-permute-start(bf16[3,64,256]{2,1,0:T(8,128)(2,1)S(1)} %get-tuple-element.92), channel_id=1, source_target_pairs={{0,6},{1,123},{2,8},{3,125},{4,10},{5,127},{6,12},{7,1},{8,14},{9,... | collective-permute-start | bytes 294920 | tf_op jit(solution)/shard_map/ppermute | solution.py:545
  57.9 1.5 %collective-permute-start.15 = (bf16[7,64,256]{2,1,0:T(8,128)(2,1)S(1)}, bf16[7,64,256]{2,1,0:T(8,128)(2,1)S(1)}, u32[]{:S(2)}, u32[]{:S(2)}) collective-permute-start(bf16[7,64,256]{2,1,0:T(8,128)(2,1)S(1)} %get-tuple-element.77), channel_id=1, source_target_pairs={{0,1},{1,0},{2,3},{3,2},{4,5},{5,4},{6,7},{7,6},{8,9},{9,8},{10,11... | collective-permute-start | bytes 688136 | tf_op jit(solution)/shard_map/ppermute | solution.py:542
  58.0 6.0 %collective-permute-start.14 = (bf16[5,64,256]{2,1,0:T(8,128)(2,1)S(1)}, bf16[5,64,256]{2,1,0:T(8,128)(2,1)S(1)}, u32[]{:S(2)}, u32[]{:S(2)}) collective-permute-start(bf16[5,64,256]{2,1,0:T(8,128)(2,1)S(1)} %pad_maximum_fusion.1), channel_id=1, source_target_pairs={{0,1},{1,0},{2,3},{3,2},{4,5},{5,4},{6,7},{7,6},{8,9},{9,8},{10,11... | collective-permute-start | bytes 491528 | tf_op jit(solution)/shard_map/ppermute | solution.py:542
  59.4 13.5 %collective-permute-start.16 = (bf16[4,64,256]{2,1,0:T(8,128)(2,1)S(1)}, bf16[4,64,256]{2,1,0:T(8,128)(2,1)S(1)}, u32[]{:S(2)}, u32[]{:S(2)}) collective-permute-start(bf16[4,64,256]{2,1,0:T(8,128)(2,1)S(1)} %get-tuple-element.91), channel_id=1, source_target_pairs={{0,2},{1,127},{2,4},{3,1},{4,6},{5,3},{6,8},{7,5},{8,10},{9,7},{10... | collective-permute-start | bytes 393224 | tf_op jit(solution)/shard_map/ppermute | solution.py:545
  64.0 8.9 %collective-permute-start.17 = (bf16[4,64,256]{2,1,0:T(8,128)(2,1)S(1)}, bf16[4,64,256]{2,1,0:T(8,128)(2,1)S(1)}, u32[]{:S(2)}, u32[]{:S(2)}) collective-permute-start(bf16[4,64,256]{2,1,0:T(8,128)(2,1)S(1)} %get-tuple-element.90), channel_id=1, source_target_pairs={{0,4},{1,125},{2,6},{3,127},{4,8},{5,1},{6,10},{7,3},{8,12},{9,5},... | collective-permute-start | bytes 393224 | tf_op jit(solution)/shard_map/ppermute | solution.py:545
  64.0 8.9 %collective-permute-start.18 = (bf16[3,64,256]{2,1,0:T(8,128)(2,1)S(1)}, bf16[3,64,256]{2,1,0:T(8,128)(2,1)S(1)}, u32[]{:S(2)}, u32[]{:S(2)}) collective-permute-start(bf16[3,64,256]{2,1,0:T(8,128)(2,1)S(1)} %get-tuple-element.89), channel_id=1, source_target_pairs={{0,6},{1,123},{2,8},{3,125},{4,10},{5,127},{6,12},{7,1},{8,14},{9,... | collective-permute-start | bytes 294920 | tf_op jit(solution)/shard_map/ppermute | solution.py:545
  73.0 1.5 %collective-permute-start.19 = (bf16[5,64,256]{2,1,0:T(8,128)(2,1)S(1)}, bf16[5,64,256]{2,1,0:T(8,128)(2,1)S(1)}, u32[]{:S(2)}, u32[]{:S(2)}) collective-permute-start(bf16[5,64,256]{2,1,0:T(8,128)(2,1)S(1)} %pad_maximum_fusion.2), channel_id=1, source_target_pairs={{0,1},{1,0},{2,3},{3,2},{4,5},{5,4},{6,7},{7,6},{8,9},{9,8},{10,11... | collective-permute-start | bytes 491528 | tf_op jit(solution)/shard_map/ppermute | solution.py:542

commit v7 on v6

--- a/solution.py
+++ b/solution.py
@@ -252,8 +252,8 @@
 
 def back_first(
     me, near_rows, near_cols, far_rows, far_cols, counts, both, near, left, right,
-    m1, m2, m3, give, plan, near_held, left_held, right_held,
-    own, acc, lists, few, draft, near_sem, left_sem, right_sem, list_sem,
+    m1, m2, m3, give, draft, near_held, left_held, right_held,
+    own, acc, lists, few, plan, near_sem, left_sem, right_sem, list_sem,
 ):
     blocks = Blocks(plan, near_held, left_held, right_held, ((near, near_sem), (left, left_sem), (right, right_sem)))
     copies = [pltpu.make_async_copy(counts, few, list_sem.at[4])]
@@ -286,10 +286,17 @@
 
 
 def forward_first(
-    plan, both, h1, h2, h3, post, diag, near, left, right,
+    draft, both, h1, h2, h3, post, diag, near, left, right,
     out,
-    fetched, turned, acc, acc_turned,
+    fetched, turned, acc, acc_turned, plan, sem,
 ):
+    copy = pltpu.make_async_copy(draft, plan, sem)
+    copy.start()
+    fetched[DEAD] = jnp.zeros((RHS, B), BF16)
+    acc[CL] = jnp.zeros((RHS, B), F32)
+    for cluster in range(CL):
+        acc[cluster] = dot_t(both[0, :, cluster * B : (cluster + 1) * B], diag[cluster])
+    copy.wait()
     halo = (h1, h2, h3)
     for rho in range(PEERS):
         lanes = pl.ds(pl.multiple_of(plan[2, WANTED + rho] * B, B), B)
@@ -300,10 +307,6 @@
         else:
             k, same = divmod(rho - 6, 2)
             fetched[rho] = post[2 * k + (1 - same if k < 2 else 0), :, lanes]
-    fetched[DEAD] = jnp.zeros((RHS, B), BF16)
-    acc[CL] = jnp.zeros((RHS, B), F32)
-    for cluster in range(CL):
-        acc[cluster] = dot_t(both[0, :, cluster * B : (cluster + 1) * B], diag[cluster])
     forward_products(Blocks(plan, near, left, right), fetched, turned, acc, acc_turned)
     out[...] = acc[0:CL]
 
@@ -355,13 +358,16 @@
 
 
 def back_second(
-    plan, rounded, near, left, right,
+    draft, rounded, near, left, right,
     m1, m2, m3, give,
-    own, acc,
+    own, acc, plan, sem,
 ):
+    copy = pltpu.make_async_copy(draft, plan, sem)
+    copy.start()
     own[0:CL] = rounded[...]
     own[CL] = jnp.zeros((RHS, B), BF16)
     acc[...] = jnp.zeros_like(acc)
+    copy.wait()
     back_products(Blocks(plan, near, left, right), own, acc)
     outs = (m1, m2, m3, give)
     for rho in range(PEERS):
@@ -370,10 +376,12 @@
 
 
 def forward_second(
-    plan, own, r1, r2, r3, post, got, diag, near, left, right,
+    draft, own, r1, r2, r3, post, got, diag, near, left, right,
     out,
-    fetched, turned, acc, acc_turned,
+    fetched, turned, acc, acc_turned, plan, sem,
 ):
+    copy = pltpu.make_async_copy(draft, plan, sem)
+    copy.start()
     ins = (r1, r2, r3, post, got)
     for rho in range(PEERS):
         message, index = place_in(rho)
@@ -382,6 +390,7 @@
     acc[CL] = jnp.zeros((RHS, B), F32)
     for cluster in range(CL):
         acc[cluster] = dot_t(own[cluster], diag[cluster])
+    copy.wait()
     forward_products(Blocks(plan, near, left, right), fetched, turned, acc, acc_turned)
     out[...] = acc[0:CL]
 
@@ -449,17 +458,21 @@
     return call(
         back_first, "transposed_products",
         message_shapes(RHS + EXTRA, jnp.int16) + [shaped(PLAN, jnp.int32)] + held,
-        [VMEM] * 4 + [SMEM] + [VMEM] * 3,
+        [VMEM] * 8,
         [SMEM] + [HBM] * 5 + [VMEM] + [HBM] * 3,
         [
             pltpu.VMEM((CL + 1, RHS, B), BF16),
             pltpu.VMEM((PEERS + 1, RHS, B), F32),
             pltpu.VMEM((8, SLOTS), jnp.int32),
             pltpu.SMEM((1, 2), jnp.int32),
-            pltpu.VMEM(PLAN, jnp.int32),
+            pltpu.SMEM(PLAN, jnp.int32),
         ]
         + [pltpu.SemaphoreType.DMA((n,)) for n in (CHUNKS, CHUNKS, CHUNKS, 6)],
     )(*args)
+
+
+def plan_scratch():
+    return [pltpu.SMEM(PLAN, jnp.int32), pltpu.SemaphoreType.DMA]
 
 
 def forward_scratch():
@@ -468,14 +481,14 @@
         pltpu.VMEM((PEERS + 1, B, RHS), BF16),
         pltpu.VMEM((CL + 1, RHS, B), F32),
         pltpu.VMEM((CL + 1, B, RHS), F32),
-    ]
+    ] + plan_scratch()
 
 
 def k2(*args):
     return call(
         forward_first, "forward_products",
         shaped((CL, RHS, B), F32), VMEM,
-        [SMEM] + [VMEM] * 9,
+        [VMEM] * 10,
         forward_scratch(),
     )(*args)
 
@@ -500,8 +513,8 @@
         back_second, "second_transposed_products",
         message_shapes(RHS, BF16),
         [VMEM] * 4,
-        [SMEM] + [VMEM] * 4,
-        [pltpu.VMEM((CL + 1, RHS, B), BF16), pltpu.VMEM((PEERS + 1, RHS, B), F32)],
+        [VMEM] * 5,
+        [pltpu.VMEM((CL + 1, RHS, B), BF16), pltpu.VMEM((PEERS + 1, RHS, B), F32)] + plan_scratch(),
     )(*args)
 
 
@@ -509,7 +522,7 @@
     return call(
         forward_second, "second_forward_products",
         shaped((CL, RHS, B), F32), VMEM,
-        [SMEM] + [VMEM] * 10,
+        [VMEM] * 11,
         forward_scratch(),
     )(*args)
 

time: 75.7 us -> 75.7 us (level)
  Pallas kernels: 28.1 us -> 25.2 us
  waiting for transfers between devices: 18.4 us -> 21.3 us
    ppermute x12, waiting for transfers between devices: 12.2 us -> 15.1 us  [carry(): return lax.ppermute(block, 'rows', carriers(size, k))]
    pallas_call x1, Pallas kernels: 7.8 us -> 6.56 us  [k1(): call(back_first, 'transposed_products', message_shapes(RHS + EXTRA, jnp.i...]
  transfers between devices with their start and end apart: 20 -> 20, of which waited for: 11 -> 11; matrix products, arithmetic and copies ran while one was open for 1% -> 1% of each run, Pallas kernels for 35% -> 31%
where the time goes in v7:
time: 75.7 us; the launch traced here: 75.6 us
  starting transfers between devices  27.1 us (36%)
  Pallas kernels  25.2 us (33%)
  waiting for transfers between devices  21.3 us (28%)
  between operations  1.01 us (1%)
  local copies, waits for them, and re-layouts  0.83 us (1%)
    ppermute x12, starting transfers between devices, carry(): return lax.ppermute(block, 'rows', carriers(size, k))  24.5 us
    ppermute x12, waiting for transfers between devices, carry(): return lax.ppermute(block, 'rows', carriers(size, k))  15.1 us
    pallas_call x1, Pallas kernels, k1(): call(back_first, 'transposed_products', message_shapes(RHS + EXTRA, jnp.i...  6.56 us
    ppermute x8, waiting for transfers between devices, swap(): return lax.ppermute(block, 'rows', [(i, i ^ 1) for i in range(size)])  6.16 us
    pallas_call x1, Pallas kernels, k2(): call(forward_first, 'forward_products', shaped((CL, RHS, B), F32), VMEM,...  5.88 us
    pallas_call x1, Pallas kernels, k5(): call(forward_second, 'second_forward_products', shaped((CL, RHS, B), F32)...  5.88 us
    pallas_call x1, Pallas kernels, k4(): call(back_second, 'second_transposed_products', message_shapes(RHS, BF16)...  4.36 us
    ppermute x8, starting transfers between devices, swap(): return lax.ppermute(block, 'rows', [(i, i ^ 1) for i in range(size)])  2.68 us
  transfers between devices with their start and end apart: 20, of which 11 were waited for; matrix products, arithmetic and copies ran while one was open for 1% of the time, Pallas kernels for 31%

profile of v7, /device:TPU:1, one launch (start us, length us, event | category | flops | bytes accessed | tf_op | source)
XLA Modules:
  0.0 75.6 jit_solution(2161858353637853634)
XLA Ops:
  0.6 1.5 %collective-permute-start = (bf16[64,1024]{1,0:T(8,128)(2,1)}, bf16[64,1024]{1,0:T(8,128)(2,1)S(1)}, u32[]{:S(2)}, u32[]{:S(2)}) collective-permute-start(bf16[64,1024]{1,0:T(8,128)(2,1)} %source.1), channel_id=1, source_target_pairs={{0,1},{1,0},{2,3},{3,2},{4,5},{5,4},{6,7},{7,6},{8,9},{9,8},{10,11... | collective-permute-start | bytes 393224 | tf_op jit(solution)/shard_map/ppermute | solution.py:555
  2.1 0.9 %staged.1 = bf16[2,64,1024]{2,1,0:T(8,128)(2,1)S(1)} custom-call(bf16[64,1024]{1,0:T(8,128)(2,1)} %source.1), custom_call_target="tpu_custom_call" | custom-call | flops 2000000000 | bytes 22000000 | tf_op jit(solution)/shard_map/staged/pallas_call | solution.py:453
  3.0 0.3 collective-permute-done
  3.3 8.6 %collective-permute-start.1 = (bf16[2,64,1024]{2,1,0:T(8,128)(2,1)S(1)}, bf16[2,64,1024]{2,1,0:T(8,128)(2,1)S(1)}, u32[]{:S(2)}, u32[]{:S(2)}) collective-permute-start(bf16[2,64,1024]{2,1,0:T(8,128)(2,1)S(1)} %bitcast_dynamic-update-slice_fusion.both), channel_id=1, source_target_pairs={{0,2},{1,127},{2,4},{3,1},{4,6},{5,3},{6,8},{7,5},{8,10},{9,7},{10... | collective-permute-start | bytes 786440 | tf_op jit(solution)/shard_map/ppermute | solution.py:558
  11.9 0.0 collective-permute-start.2
  11.9 0.9 %collective-permute-start.3 = (bf16[2,64,1024]{2,1,0:T(8,128)(2,1)S(1)}, bf16[2,64,1024]{2,1,0:T(8,128)(2,1)S(1)}, u32[]{:S(2)}, u32[]{:S(2)}) collective-permute-start(bf16[2,64,1024]{2,1,0:T(8,128)(2,1)S(1)} %bitcast_dynamic-update-slice_fusion.both), channel_id=1, source_target_pairs={{0,6},{1,123},{2,8},{3,125},{4,10},{5,127},{6,12},{7,1},{8,14},{9,... | collective-permute-start | bytes 786440 | tf_op jit(solution)/shard_map/ppermute | solution.py:558
  12.8 6.6 %transposed_products.1 = (s16[4,80,256]{2,1,0:T(8,128)(2,1)S(1)}, s16[4,80,256]{2,1,0:T(8,128)(2,1)S(1)}, s16[3,80,256]{2,1,0:T(8,128)(2,1)S(1)}, s16[7,80,256]{...) custom-call(s32[1]{0:T(128)} %bitcast.me, ...), custom_call_target="tpu_custom_call" | custom-call | flops 2000000000 | bytes 22000000 | tf_op jit(solution)/shard_map/transposed_products/pallas_call | solution.py:458
  19.3 0.0 copy-start
  19.4 0.0 collective-permute-done.1.h1
  19.4 3.3 %collective-permute-done.2.h2 = bf16[2,64,1024]{2,1,0:T(8,128)(2,1)S(1)} collective-permute-done((bf16[2,64,1024]{2,1,0:T(8,128)(2,1)S(1)}, bf16[2,64,1024]{2,1,0:T(8,128)(2,1)S(1)}, u32[]{:S(2)}, u32[]{:S(2)}) %collective-permute-start.2) | collective-permute-done | bytes 262176 | tf_op jit(solution)/shard_map/ppermute | solution.py:558
  22.7 1.9 %collective-permute-done.3.h3 = bf16[2,64,1024]{2,1,0:T(8,128)(2,1)S(1)} collective-permute-done((bf16[2,64,1024]{2,1,0:T(8,128)(2,1)S(1)}, bf16[2,64,1024]{2,1,0:T(8,128)(2,1)S(1)}, u32[]{:S(2)}, u32[]{:S(2)}) %collective-permute-start.3) | collective-permute-done | bytes 262176 | tf_op jit(solution)/shard_map/ppermute | solution.py:558
  24.6 0.0 collective-permute-start.4
  24.6 1.6 %collective-permute-done.4.got = s16[7,80,256]{2,1,0:T(8,128)(2,1)S(1)} collective-permute-done((s16[7,80,256]{2,1,0:T(8,128)(2,1)S(1)}, s16[7,80,256]{2,1,0:T(8,128)(2,1)S(1)}, u32[]{:S(2)}, u32[]{:S(2)}) %collective-permute-start.4) | collective-permute-done | bytes 286752 | tf_op jit(solution)/shard_map/ppermute | solution.py:555
  26.2 0.1 pad_maximum_fusion
  26.3 0.2 collective-permute-start.5
  26.5 3.9 %collective-permute-start.6 = (s16[4,80,256]{2,1,0:T(8,128)(2,1)S(1)}, s16[4,80,256]{2,1,0:T(8,128)(2,1)S(1)}, u32[]{:S(2)}, u32[]{:S(2)}) collective-permute-start(s16[4,80,256]{2,1,0:T(8,128)(2,1)S(1)} %get-tuple-element.88), channel_id=1, source_target_pairs={{0,2},{1,127},{2,4},{3,1},{4,6},{5,3},{6,8},{7,5},{8,10},{9,7},{10... | collective-permute-start | bytes 491528 | tf_op jit(solution)/shard_map/ppermute | solution.py:558
  30.5 2.7 %collective-permute-start.7 = (s16[4,80,256]{2,1,0:T(8,128)(2,1)S(1)}, s16[4,80,256]{2,1,0:T(8,128)(2,1)S(1)}, u32[]{:S(2)}, u32[]{:S(2)}) collective-permute-start(s16[4,80,256]{2,1,0:T(8,128)(2,1)S(1)} %get-tuple-element.87), channel_id=1, source_target_pairs={{0,4},{1,125},{2,6},{3,127},{4,8},{5,1},{6,10},{7,3},{8,12},{9,5},... | collective-permute-start | bytes 491528 | tf_op jit(solution)/shard_map/ppermute | solution.py:558
  33.1 0.0 collective-permute-start.8
  33.1 0.0 collective-permute-done.5.post
  33.2 5.9 %forward_products.1.partial = f32[4,64,256]{2,1,0:T(8,128)S(1)} custom-call(s32[4,256]{1,0:T(4,128)S(1)} %get-tuple-element.44.draft, bf16[2,64,1024]{2,1,0:T(8,128)(2,1)S(1)} %bitcast_dynamic-update-slice_fusion.both, bf16[2,64,1024]{2,1,0:T(8,128)(2,1)S(1)} %collective-permute-done.1.h1, bf16[2,64,1024]{2,1,0:T(8,128)(2,1)S(1)} %collective-permute-done.2.h2, ...), custom_call_target="tpu_custom_call" | custom-call | flops 2000000000 | bytes 22000000 | tf_op jit(solution)/shard_map/forward_products/pallas_call | solution.py:488
  39.0 2.3 %collective-permute-done.8.r3 = s16[3,80,256]{2,1,0:T(8,128)(2,1)S(1)} collective-permute-done((s16[3,80,256]{2,1,0:T(8,128)(2,1)S(1)}, s16[3,80,256]{2,1,0:T(8,128)(2,1)S(1)}, u32[]{:S(2)}, u32[]{:S(2)}) %collective-permute-start.8) | collective-permute-done | bytes 122912 | tf_op jit(solution)/shard_map/ppermute | solution.py:558
  41.4 0.0 collective-permute-done.6.r1
  41.4 0.0 collective-permute-done.7.r2
  41.5 0.1 collective-permute-start.9
  41.6 1.4 %collective-permute-done.9.post = s16[5,80,256]{2,1,0:T(8,128)(2,1)S(1)} collective-permute-done((s16[5,80,256]{2,1,0:T(8,128)(2,1)S(1)}, s16[5,80,256]{2,1,0:T(8,128)(2,1)S(1)}, u32[]{:S(2)}, u32[]{:S(2)}) %collective-permute-start.9) | collective-permute-done | bytes 204832 | tf_op jit(solution)/shard_map/ppermute | solution.py:555
  43.0 0.6 first_image.1
  43.6 0.2 collective-permute-start.10
  43.8 1.4 %collective-permute-done.10.got = bf16[7,64,256]{2,1,0:T(8,128)(2,1)S(1)} collective-permute-done((bf16[7,64,256]{2,1,0:T(8,128)(2,1)S(1)}, bf16[7,64,256]{2,1,0:T(8,128)(2,1)S(1)}, u32[]{:S(2)}, u32[]{:S(2)}) %collective-permute-start.10) | collective-permute-done | bytes 229408 | tf_op jit(solution)/shard_map/ppermute | solution.py:555
  45.2 3.8 %collective-permute-start.11 = (bf16[4,64,256]{2,1,0:T(8,128)(2,1)S(1)}, bf16[4,64,256]{2,1,0:T(8,128)(2,1)S(1)}, u32[]{:S(2)}, u32[]{:S(2)}) collective-permute-start(bf16[4,64,256]{2,1,0:T(8,128)(2,1)S(1)} %get-tuple-element.94), channel_id=1, source_target_pairs={{0,2},{1,127},{2,4},{3,1},{4,6},{5,3},{6,8},{7,5},{8,10},{9,7},{10... | collective-permute-start | bytes 393224 | tf_op jit(solution)/shard_map/ppermute | solution.py:558
  49.0 0.0 collective-permute-start.12
  49.0 0.0 collective-permute-start.13
  49.0 4.4 %second_transposed_products.1 = (bf16[4,64,256]{2,1,0:T(8,128)(2,1)S(1)}, bf16[4,64,256]{2,1,0:T(8,128)(2,1)S(1)}, bf16[3,64,256]{2,1,0:T(8,128)(2,1)S(1)}, bf16[7,64,256]{2,1,0:T(8,128)(2,1)S(1)}) custom-call(s32[4,256]{1,0:T(4,128)S(1)} %get-tuple-element.44.draft, bf16[4,64,256]{2,1,0:T(8,128)(2,1)S(1)} %get-tuple-element.71.rounded.own, ...), custom_call_target="tpu_custom_call" | custom-call | flops 2000000000 | bytes 22000000 | tf_op jit(solution)/shard_map/second_transposed_products/pallas_call | solution.py:512
  53.4 4.5 %collective-permute-done.13.r3 = bf16[3,64,256]{2,1,0:T(8,128)(2,1)S(1)} collective-permute-done((bf16[3,64,256]{2,1,0:T(8,128)(2,1)S(1)}, bf16[3,64,256]{2,1,0:T(8,128)(2,1)S(1)}, u32[]{:S(2)}, u32[]{:S(2)}) %collective-permute-start.13) | collective-permute-done | bytes 98336 | tf_op jit(solution)/shard_map/ppermute | solution.py:558
  57.9 0.0 collective-permute-done.11.r1
  57.9 0.0 collective-permute-done.12.r2
  57.9 0.0 collective-permute-start.15
  58.0 0.6 collective-permute-start.14
  58.5 0.8 %collective-permute-done.15.got = bf16[7,64,256]{2,1,0:T(8,128)(2,1)S(1)} collective-permute-done((bf16[7,64,256]{2,1,0:T(8,128)(2,1)S(1)}, bf16[7,64,256]{2,1,0:T(8,128)(2,1)S(1)}, u32[]{:S(2)}, u32[]{:S(2)}) %collective-permute-start.15) | collective-permute-done | bytes 229408 | tf_op jit(solution)/shard_map/ppermute | solution.py:555
  59.4 4.6 %collective-permute-start.16 = (bf16[4,64,256]{2,1,0:T(8,128)(2,1)S(1)}, bf16[4,64,256]{2,1,0:T(8,128)(2,1)S(1)}, u32[]{:S(2)}, u32[]{:S(2)}) collective-permute-start(bf16[4,64,256]{2,1,0:T(8,128)(2,1)S(1)} %get-tuple-element.91), channel_id=1, source_target_pairs={{0,2},{1,127},{2,4},{3,1},{4,6},{5,3},{6,8},{7,5},{8,10},{9,7},{10... | collective-permute-start | bytes 393224 | tf_op jit(solution)/shard_map/ppermute | solution.py:558
  64.0 0.0 collective-permute-start.17
  64.0 0.0 collective-permute-start.18
  64.0 0.0 collective-permute-done.14.post
  64.0 5.9 %second_forward_products.1.partial = f32[4,64,256]{2,1,0:T(8,128)S(1)} custom-call(s32[4,256]{1,0:T(4,128)S(1)} %get-tuple-element.44.draft, bf16[4,64,256]{2,1,0:T(8,128)(2,1)S(1)} %get-tuple-element.71.rounded.own, bf16[4,64,256]{2,1,0:T(8,128)(2,1)S(1)} %collective-permute-done.11.r1, bf16[4,64,256]{2,1,0:T(8,128)(2,1)S(1)} %collective-permute-done.12.r2, ...), custom_call_target="tpu_custom_call" | custom-call | flops 2000000000 | bytes 22000000 | tf_op jit(solution)/shard_map/second_forward_products/pallas_call | solution.py:522
  69.9 3.0 %collective-permute-done.18.r3 = bf16[3,64,256]{2,1,0:T(8,128)(2,1)S(1)} collective-permute-done((bf16[3,64,256]{2,1,0:T(8,128)(2,1)S(1)}, bf16[3,64,256]{2,1,0:T(8,128)(2,1)S(1)}, u32[]{:S(2)}, u32[]{:S(2)}) %collective-permute-start.18) | collective-permute-done | bytes 98336 | tf_op jit(solution)/shard_map/ppermute | solution.py:558
  73.0 0.1 collective-permute-start.19
  73.1 0.7 copy.22
  73.8 0.7 collective-permute-done.19.post
  74.4 1.0 %second_image.1 = f32[64,1024]{1,0:T(8,128)} custom-call(f32[4,64,256]{2,1,0:T(8,128)S(1)} %second_forward_products.1.partial, s32[16,256]{1,0:T(8,128)S(1)} %get-tuple-element.82.marked, bf16[4,64,256]{2,1,0:T(8,128)(2,1)S(1)} %collective-permute-done.16.r1, bf16[4,64,256]{2,1,0:T(8,128)(2,1)S(1)} %collective-permute-done.17.r2, ...), custom_call_target="tpu_custom_call" | custom-call | flops 2000000000 | bytes 22000000 | tf_op jit(solution)/shard_map/second_image/pallas_call | solution.py:531
  (20 shorter events, 0.2 us)
Async XLA Ops:
  0.6 2.7 %collective-permute-start = (bf16[64,1024]{1,0:T(8,128)(2,1)}, bf16[64,1024]{1,0:T(8,128)(2,1)S(1)}, u32[]{:S(2)}, u32[]{:S(2)}) collective-permute-start(bf16[64,1024]{1,0:T(8,128)(2,1)} %source.1), channel_id=1, source_target_pairs={{0,1},{1,0},{2,3},{3,2},{4,5},{5,4},{6,7},{7,6},{8,9},{9,8},{10,11... | collective-permute-start | bytes 393224 | tf_op jit(solution)/shard_map/ppermute | solution.py:555
  3.3 16.0 %collective-permute-start.1 = (bf16[2,64,1024]{2,1,0:T(8,128)(2,1)S(1)}, bf16[2,64,1024]{2,1,0:T(8,128)(2,1)S(1)}, u32[]{:S(2)}, u32[]{:S(2)}) collective-permute-start(bf16[2,64,1024]{2,1,0:T(8,128)(2,1)S(1)} %bitcast_dynamic-update-slice_fusion.both), channel_id=1, source_target_pairs={{0,2},{1,127},{2,4},{3,1},{4,6},{5,3},{6,8},{7,5},{8,10},{9,7},{10... | collective-permute-start | bytes 786440 | tf_op jit(solution)/shard_map/ppermute | solution.py:558
  11.9 10.8 %collective-permute-start.2 = (bf16[2,64,1024]{2,1,0:T(8,128)(2,1)S(1)}, bf16[2,64,1024]{2,1,0:T(8,128)(2,1)S(1)}, u32[]{:S(2)}, u32[]{:S(2)}) collective-permute-start(bf16[2,64,1024]{2,1,0:T(8,128)(2,1)S(1)} %bitcast_dynamic-update-slice_fusion.both), channel_id=1, source_target_pairs={{0,4},{1,125},{2,6},{3,127},{4,8},{5,1},{6,10},{7,3},{8,12},{9,5},... | collective-permute-start | bytes 786440 | tf_op jit(solution)/shard_map/ppermute | solution.py:558
  11.9 12.7 %collective-permute-start.3 = (bf16[2,64,1024]{2,1,0:T(8,128)(2,1)S(1)}, bf16[2,64,1024]{2,1,0:T(8,128)(2,1)S(1)}, u32[]{:S(2)}, u32[]{:S(2)}) collective-permute-start(bf16[2,64,1024]{2,1,0:T(8,128)(2,1)S(1)} %bitcast_dynamic-update-slice_fusion.both), channel_id=1, source_target_pairs={{0,6},{1,123},{2,8},{3,125},{4,10},{5,127},{6,12},{7,1},{8,14},{9,... | collective-permute-start | bytes 786440 | tf_op jit(solution)/shard_map/ppermute | solution.py:558
  19.3 13.8 %copy-start = (bf16[4,256,256]{2,1,0:T(8,128)(2,1)S(1)}, bf16[4,256,256]{2,1,0:T(8,128)(2,1)}, u32[]{:S(2)}) copy-start(bf16[4,256,256]{2,1,0:T(8,128)(2,1)} %diag.3) | copy-start | bytes 1572868
  24.6 1.6 %collective-permute-start.4 = (s16[7,80,256]{2,1,0:T(8,128)(2,1)S(1)}, s16[7,80,256]{2,1,0:T(8,128)(2,1)S(1)}, u32[]{:S(2)}, u32[]{:S(2)}) collective-permute-start(s16[7,80,256]{2,1,0:T(8,128)(2,1)S(1)} %get-tuple-element.49), channel_id=1, source_target_pairs={{0,1},{1,0},{2,3},{3,2},{4,5},{5,4},{6,7},{7,6},{8,9},{9,8},{10,11... | collective-permute-start | bytes 860168 | tf_op jit(solution)/shard_map/ppermute | solution.py:555
  26.3 6.8 %collective-permute-start.5 = (bf16[5,64,1024]{2,1,0:T(8,128)(2,1)S(1)}, bf16[5,64,1024]{2,1,0:T(8,128)(2,1)S(1)}, u32[]{:S(2)}, u32[]{:S(2)}) collective-permute-start(bf16[5,64,1024]{2,1,0:T(8,128)(2,1)S(1)} %pad_maximum_fusion), channel_id=1, source_target_pairs={{0,1},{1,0},{2,3},{3,2},{4,5},{5,4},{6,7},{7,6},{8,9},{9,8},{10,11... | collective-permute-start | bytes 1966088 | tf_op jit(solution)/shard_map/ppermute | solution.py:555
  26.5 14.9 %collective-permute-start.6 = (s16[4,80,256]{2,1,0:T(8,128)(2,1)S(1)}, s16[4,80,256]{2,1,0:T(8,128)(2,1)S(1)}, u32[]{:S(2)}, u32[]{:S(2)}) collective-permute-start(s16[4,80,256]{2,1,0:T(8,128)(2,1)S(1)} %get-tuple-element.88), channel_id=1, source_target_pairs={{0,2},{1,127},{2,4},{3,1},{4,6},{5,3},{6,8},{7,5},{8,10},{9,7},{10... | collective-permute-start | bytes 491528 | tf_op jit(solution)/shard_map/ppermute | solution.py:558
  30.5 10.9 %collective-permute-start.7 = (s16[4,80,256]{2,1,0:T(8,128)(2,1)S(1)}, s16[4,80,256]{2,1,0:T(8,128)(2,1)S(1)}, u32[]{:S(2)}, u32[]{:S(2)}) collective-permute-start(s16[4,80,256]{2,1,0:T(8,128)(2,1)S(1)} %get-tuple-element.87), channel_id=1, source_target_pairs={{0,4},{1,125},{2,6},{3,127},{4,8},{5,1},{6,10},{7,3},{8,12},{9,5},... | collective-permute-start | bytes 491528 | tf_op jit(solution)/shard_map/ppermute | solution.py:558
  33.1 8.3 %collective-permute-start.8 = (s16[3,80,256]{2,1,0:T(8,128)(2,1)S(1)}, s16[3,80,256]{2,1,0:T(8,128)(2,1)S(1)}, u32[]{:S(2)}, u32[]{:S(2)}) collective-permute-start(s16[3,80,256]{2,1,0:T(8,128)(2,1)S(1)} %get-tuple-element.86), channel_id=1, source_target_pairs={{0,6},{1,123},{2,8},{3,125},{4,10},{5,127},{6,12},{7,1},{8,14},{9,... | collective-permute-start | bytes 368648 | tf_op jit(solution)/shard_map/ppermute | solution.py:558
  41.5 1.5 %collective-permute-start.9 = (s16[5,80,256]{2,1,0:T(8,128)(2,1)S(1)}, s16[5,80,256]{2,1,0:T(8,128)(2,1)S(1)}, u32[]{:S(2)}, u32[]{:S(2)}) collective-permute-start(s16[5,80,256]{2,1,0:T(8,128)(2,1)S(1)} %pad_add_fusion), channel_id=1, source_target_pairs={{0,1},{1,0},{2,3},{3,2},{4,5},{5,4},{6,7},{7,6},{8,9},{9,8},{10,11... | collective-permute-start | bytes 614408 | tf_op jit(solution)/shard_map/ppermute | solution.py:555
  43.6 1.6 %collective-permute-start.10 = (bf16[7,64,256]{2,1,0:T(8,128)(2,1)S(1)}, bf16[7,64,256]{2,1,0:T(8,128)(2,1)S(1)}, u32[]{:S(2)}, u32[]{:S(2)}) collective-permute-start(bf16[7,64,256]{2,1,0:T(8,128)(2,1)S(1)} %get-tuple-element.68), channel_id=1, source_target_pairs={{0,1},{1,0},{2,3},{3,2},{4,5},{5,4},{6,7},{7,6},{8,9},{9,8},{10,11... | collective-permute-start | bytes 688136 | tf_op jit(solution)/shard_map/ppermute | solution.py:555
  45.2 12.7 %collective-permute-start.11 = (bf16[4,64,256]{2,1,0:T(8,128)(2,1)S(1)}, bf16[4,64,256]{2,1,0:T(8,128)(2,1)S(1)}, u32[]{:S(2)}, u32[]{:S(2)}) collective-permute-start(bf16[4,64,256]{2,1,0:T(8,128)(2,1)S(1)} %get-tuple-element.94), channel_id=1, source_target_pairs={{0,2},{1,127},{2,4},{3,1},{4,6},{5,3},{6,8},{7,5},{8,10},{9,7},{10... | collective-permute-start | bytes 393224 | tf_op jit(solution)/shard_map/ppermute | solution.py:558
  49.0 8.9 %collective-permute-start.12 = (bf16[4,64,256]{2,1,0:T(8,128)(2,1)S(1)}, bf16[4,64,256]{2,1,0:T(8,128)(2,1)S(1)}, u32[]{:S(2)}, u32[]{:S(2)}) collective-permute-start(bf16[4,64,256]{2,1,0:T(8,128)(2,1)S(1)} %get-tuple-element.93), channel_id=1, source_target_pairs={{0,4},{1,125},{2,6},{3,127},{4,8},{5,1},{6,10},{7,3},{8,12},{9,5},... | collective-permute-start | bytes 393224 | tf_op jit(solution)/shard_map/ppermute | solution.py:558
  49.0 8.9 %collective-permute-start.13 = (bf16[3,64,256]{2,1,0:T(8,128)(2,1)S(1)}, bf16[3,64,256]{2,1,0:T(8,128)(2,1)S(1)}, u32[]{:S(2)}, u32[]{:S(2)}) collective-permute-start(bf16[3,64,256]{2,1,0:T(8,128)(2,1)S(1)} %get-tuple-element.92), channel_id=1, source_target_pairs={{0,6},{1,123},{2,8},{3,125},{4,10},{5,127},{6,12},{7,1},{8,14},{9,... | collective-permute-start | bytes 294920 | tf_op jit(solution)/shard_map/ppermute | solution.py:558
  57.9 1.5 %collective-permute-start.15 = (bf16[7,64,256]{2,1,0:T(8,128)(2,1)S(1)}, bf16[7,64,256]{2,1,0:T(8,128)(2,1)S(1)}, u32[]{:S(2)}, u32[]{:S(2)}) collective-permute-start(bf16[7,64,256]{2,1,0:T(8,128)(2,1)S(1)} %get-tuple-element.77), channel_id=1, source_target_pairs={{0,1},{1,0},{2,3},{3,2},{4,5},{5,4},{6,7},{7,6},{8,9},{9,8},{10,11... | collective-permute-start | bytes 688136 | tf_op jit(solution)/shard_map/ppermute | solution.py:555
  58.0 6.0 %collective-permute-start.14 = (bf16[5,64,256]{2,1,0:T(8,128)(2,1)S(1)}, bf16[5,64,256]{2,1,0:T(8,128)(2,1)S(1)}, u32[]{:S(2)}, u32[]{:S(2)}) collective-permute-start(bf16[5,64,256]{2,1,0:T(8,128)(2,1)S(1)} %pad_maximum_fusion.1), channel_id=1, source_target_pairs={{0,1},{1,0},{2,3},{3,2},{4,5},{5,4},{6,7},{7,6},{8,9},{9,8},{10,11... | collective-permute-start | bytes 491528 | tf_op jit(solution)/shard_map/ppermute | solution.py:555
  59.4 13.5 %collective-permute-start.16 = (bf16[4,64,256]{2,1,0:T(8,128)(2,1)S(1)}, bf16[4,64,256]{2,1,0:T(8,128)(2,1)S(1)}, u32[]{:S(2)}, u32[]{:S(2)}) collective-permute-start(bf16[4,64,256]{2,1,0:T(8,128)(2,1)S(1)} %get-tuple-element.91), channel_id=1, source_target_pairs={{0,2},{1,127},{2,4},{3,1},{4,6},{5,3},{6,8},{7,5},{8,10},{9,7},{10... | collective-permute-start | bytes 393224 | tf_op jit(solution)/shard_map/ppermute | solution.py:558
  64.0 8.9 %collective-permute-start.17 = (bf16[4,64,256]{2,1,0:T(8,128)(2,1)S(1)}, bf16[4,64,256]{2,1,0:T(8,128)(2,1)S(1)}, u32[]{:S(2)}, u32[]{:S(2)}) collective-permute-start(bf16[4,64,256]{2,1,0:T(8,128)(2,1)S(1)} %get-tuple-element.90), channel_id=1, source_target_pairs={{0,4},{1,125},{2,6},{3,127},{4,8},{5,1},{6,10},{7,3},{8,12},{9,5},... | collective-permute-start | bytes 393224 | tf_op jit(solution)/shard_map/ppermute | solution.py:558
  64.0 8.9 %collective-permute-start.18 = (bf16[3,64,256]{2,1,0:T(8,128)(2,1)S(1)}, bf16[3,64,256]{2,1,0:T(8,128)(2,1)S(1)}, u32[]{:S(2)}, u32[]{:S(2)}) collective-permute-start(bf16[3,64,256]{2,1,0:T(8,128)(2,1)S(1)} %get-tuple-element.89), channel_id=1, source_target_pairs={{0,6},{1,123},{2,8},{3,125},{4,10},{5,127},{6,12},{7,1},{8,14},{9,... | collective-permute-start | bytes 294920 | tf_op jit(solution)/shard_map/ppermute | solution.py:558
  73.0 1.5 %collective-permute-start.19 = (bf16[5,64,256]{2,1,0:T(8,128)(2,1)S(1)}, bf16[5,64,256]{2,1,0:T(8,128)(2,1)S(1)}, u32[]{:S(2)}, u32[]{:S(2)}) collective-permute-start(bf16[5,64,256]{2,1,0:T(8,128)(2,1)S(1)} %pad_maximum_fusion.2), channel_id=1, source_target_pairs={{0,1},{1,0},{2,3},{3,2},{4,5},{5,4},{6,7},{7,6},{8,9},{9,8},{10,11... | collective-permute-start | bytes 491528 | tf_op jit(solution)/shard_map/ppermute | solution.py:555

commit v8 on v7

--- a/solution.py
+++ b/solution.py
@@ -439,8 +439,8 @@
     return jax.ShapeDtypeStruct(shape, dtype)
 
 
-def message_shapes(rows, dtype):
-    return [shaped((n, rows, B), dtype) for n in MESSAGE + (7,)]
+def message_shapes(rows, dtype, given=7):
+    return [shaped((n, rows, B), dtype) for n in MESSAGE + (given,)]
 
 
 def stage(source, target, sem):
@@ -457,7 +457,7 @@
     held = [pltpu.VMEM(shape, BF16) for shape in ((SLOTS, B, B), (SLOTS, K, B), (SLOTS, K, B))]
     return call(
         back_first, "transposed_products",
-        message_shapes(RHS + EXTRA, jnp.int16) + [shaped(PLAN, jnp.int32)] + held,
+        message_shapes(RHS + EXTRA, jnp.int16, 11) + [shaped(PLAN, jnp.int32)] + held,
         [VMEM] * 8,
         [SMEM] + [HBM] * 5 + [VMEM] + [HBM] * 3,
         [
@@ -581,9 +581,8 @@
     m1, m2, m3, give, plan, *held = k1(
         me, *lists, in_hbm(counts), both, in_hbm(near_blocks), in_hbm(far_left), in_hbm(far_right)
     )
-    halo, give = lax.optimization_barrier((halo, give))
+    halo, m1 = lax.optimization_barrier((halo, m1))
     r1, r2, r3, got, messages = exchange(m1, m2, m3, give)
-    halo, got = lax.optimization_barrier((halo, got))
     halo_post = swap(jnp.concatenate([halo[0], halo[1], halo[2][1:]]))
     halo_post, messages = lax.optimization_barrier((halo_post, messages))
     partial = k2(plan, both, *halo, halo_post, diag_blocks, *held)

time: 75.7 us -> 74.2 us (0.980)
  waiting for transfers between devices: 21.3 us -> 19.1 us
    ppermute x8, waiting for transfers between devices: 6.16 us -> 4.59 us  [swap(): return lax.ppermute(block, 'rows', [(i, i ^ 1) for i in range(size)])]
  transfers between devices with their start and end apart: 20 -> 20, of which waited for: 11 -> 10; matrix products, arithmetic and copies ran while one was open for 1% -> 1% of each run, Pallas kernels for 31% -> 33%
where the time goes in v8:
time: 74.2 us; the launch traced here: 74 us
  starting transfers between devices  27.2 us (37%)
  Pallas kernels  25.7 us (35%)
  waiting for transfers between devices  19.1 us (26%)
  between operations  1.04 us (1%)
  local copies, waits for them, and re-layouts  0.83 us (1%)
    ppermute x12, starting transfers between devices, carry(): return lax.ppermute(block, 'rows', carriers(size, k))  24.6 us
    ppermute x12, waiting for transfers between devices, carry(): return lax.ppermute(block, 'rows', carriers(size, k))  14.5 us
    pallas_call x1, Pallas kernels, k1(): call(back_first, 'transposed_products', message_shapes(RHS + EXTRA, jnp.i...  7.21 us
    pallas_call x1, Pallas kernels, k2(): call(forward_first, 'forward_products', shaped((CL, RHS, B), F32), VMEM,...  5.75 us
    pallas_call x1, Pallas kernels, k5(): call(forward_second, 'second_forward_products', shaped((CL, RHS, B), F32)...  5.73 us
    ppermute x8, waiting for transfers between devices, swap(): return lax.ppermute(block, 'rows', [(i, i ^ 1) for i in range(size)])  4.59 us
    pallas_call x1, Pallas kernels, k4(): call(back_second, 'second_transposed_products', message_shapes(RHS, BF16)...  4.49 us
    ppermute x8, starting transfers between devices, swap(): return lax.ppermute(block, 'rows', [(i, i ^ 1) for i in range(size)])  2.63 us
  transfers between devices with their start and end apart: 20, of which 10 were waited for; matrix products, arithmetic and copies ran while one was open for 1% of the time, Pallas kernels for 33%

profile of v8, /device:TPU:1, one launch (start us, length us, event | category | flops | bytes accessed | tf_op | source)
XLA Modules:
  0.0 74.0 jit_solution(9987694225637699233)
XLA Ops:
  0.6 1.5 %collective-permute-start = (bf16[64,1024]{1,0:T(8,128)(2,1)}, bf16[64,1024]{1,0:T(8,128)(2,1)S(1)}, u32[]{:S(2)}, u32[]{:S(2)}) collective-permute-start(bf16[64,1024]{1,0:T(8,128)(2,1)} %source.1), channel_id=1, source_target_pairs={{0,1},{1,0},{2,3},{3,2},{4,5},{5,4},{6,7},{7,6},{8,9},{9,8},{10,11... | collective-permute-start | bytes 393224 | tf_op jit(solution)/shard_map/ppermute | solution.py:555
  2.1 0.9 %staged.1 = bf16[2,64,1024]{2,1,0:T(8,128)(2,1)S(1)} custom-call(bf16[64,1024]{1,0:T(8,128)(2,1)} %source.1), custom_call_target="tpu_custom_call" | custom-call | flops 2000000000 | bytes 22000000 | tf_op jit(solution)/shard_map/staged/pallas_call | solution.py:453
  3.0 0.3 collective-permute-done
  3.3 8.6 %collective-permute-start.1 = (bf16[2,64,1024]{2,1,0:T(8,128)(2,1)S(1)}, bf16[2,64,1024]{2,1,0:T(8,128)(2,1)S(1)}, u32[]{:S(2)}, u32[]{:S(2)}) collective-permute-start(bf16[2,64,1024]{2,1,0:T(8,128)(2,1)S(1)} %bitcast_dynamic-update-slice_fusion.both), channel_id=1, source_target_pairs={{0,2},{1,127},{2,4},{3,1},{4,6},{5,3},{6,8},{7,5},{8,10},{9,7},{10... | collective-permute-start | bytes 786440 | tf_op jit(solution)/shard_map/ppermute | solution.py:558
  11.9 0.0 collective-permute-start.2
  11.9 0.9 %collective-permute-start.3 = (bf16[2,64,1024]{2,1,0:T(8,128)(2,1)S(1)}, bf16[2,64,1024]{2,1,0:T(8,128)(2,1)S(1)}, u32[]{:S(2)}, u32[]{:S(2)}) collective-permute-start(bf16[2,64,1024]{2,1,0:T(8,128)(2,1)S(1)} %bitcast_dynamic-update-slice_fusion.both), channel_id=1, source_target_pairs={{0,6},{1,123},{2,8},{3,125},{4,10},{5,127},{6,12},{7,1},{8,14},{9,... | collective-permute-start | bytes 786440 | tf_op jit(solution)/shard_map/ppermute | solution.py:558
  12.8 7.2 %transposed_products.1 = (s16[4,80,256]{2,1,0:T(8,128)(2,1)S(1)}, s16[4,80,256]{2,1,0:T(8,128)(2,1)S(1)}, s16[3,80,256]{2,1,0:T(8,128)(2,1)S(1)}, s16[11,80,256]...) custom-call(s32[1]{0:T(128)} %bitcast.me, ...), custom_call_target="tpu_custom_call" | custom-call | flops 2000000000 | bytes 22000000 | tf_op jit(solution)/shard_map/transposed_products/pallas_call | solution.py:458
  20.0 0.0 copy-start
  20.0 0.1 collective-permute-start.5
  20.1 0.0 collective-permute-done.1.h1
  20.1 2.6 %collective-permute-done.2.h2 = bf16[2,64,1024]{2,1,0:T(8,128)(2,1)S(1)} collective-permute-done((bf16[2,64,1024]{2,1,0:T(8,128)(2,1)S(1)}, bf16[2,64,1024]{2,1,0:T(8,128)(2,1)S(1)}, u32[]{:S(2)}, u32[]{:S(2)}) %collective-permute-start.2) | collective-permute-done | bytes 262176 | tf_op jit(solution)/shard_map/ppermute | solution.py:558
  22.7 1.9 %collective-permute-done.3.h3 = bf16[2,64,1024]{2,1,0:T(8,128)(2,1)S(1)} collective-permute-done((bf16[2,64,1024]{2,1,0:T(8,128)(2,1)S(1)}, bf16[2,64,1024]{2,1,0:T(8,128)(2,1)S(1)}, u32[]{:S(2)}, u32[]{:S(2)}) %collective-permute-start.3) | collective-permute-done | bytes 262176 | tf_op jit(solution)/shard_map/ppermute | solution.py:558
  24.6 0.1 pad_maximum_fusion
  24.7 0.1 collective-permute-start.4
  24.8 0.0 collective-permute-done.5.got
  24.9 4.1 %collective-permute-start.6 = (s16[4,80,256]{2,1,0:T(8,128)(2,1)S(1)}, s16[4,80,256]{2,1,0:T(8,128)(2,1)S(1)}, u32[]{:S(2)}, u32[]{:S(2)}) collective-permute-start(s16[4,80,256]{2,1,0:T(8,128)(2,1)S(1)} %get-tuple-element.80), channel_id=1, source_target_pairs={{0,2},{1,127},{2,4},{3,1},{4,6},{5,3},{6,8},{7,5},{8,10},{9,7},{10... | collective-permute-start | bytes 491528 | tf_op jit(solution)/shard_map/ppermute | solution.py:558
  28.9 2.5 %collective-permute-start.7 = (s16[4,80,256]{2,1,0:T(8,128)(2,1)S(1)}, s16[4,80,256]{2,1,0:T(8,128)(2,1)S(1)}, u32[]{:S(2)}, u32[]{:S(2)}) collective-permute-start(s16[4,80,256]{2,1,0:T(8,128)(2,1)S(1)} %get-tuple-element.79), channel_id=1, source_target_pairs={{0,4},{1,125},{2,6},{3,127},{4,8},{5,1},{6,10},{7,3},{8,12},{9,5},... | collective-permute-start | bytes 491528 | tf_op jit(solution)/shard_map/ppermute | solution.py:558
  31.5 0.0 collective-permute-done.4.post
  31.5 5.8 %forward_products.1.partial = f32[4,64,256]{2,1,0:T(8,128)S(1)} custom-call(s32[4,256]{1,0:T(4,128)S(1)} %get-tuple-element.40.draft, bf16[2,64,1024]{2,1,0:T(8,128)(2,1)S(1)} %bitcast_dynamic-update-slice_fusion.both, bf16[2,64,1024]{2,1,0:T(8,128)(2,1)S(1)} %collective-permute-done.1.h1, bf16[2,64,1024]{2,1,0:T(8,128)(2,1)S(1)} %collective-permute-done.2.h2, ...), custom_call_target="tpu_custom_call" | custom-call | flops 2000000000 | bytes 22000000 | tf_op jit(solution)/shard_map/forward_products/pallas_call | solution.py:488
  37.2 2.5 %collective-permute-done.8.r3 = s16[3,80,256]{2,1,0:T(8,128)(2,1)S(1)} collective-permute-done((s16[3,80,256]{2,1,0:T(8,128)(2,1)S(1)}, s16[3,80,256]{2,1,0:T(8,128)(2,1)S(1)}, u32[]{:S(2)}, u32[]{:S(2)}) %collective-permute-start.8) | collective-permute-done | bytes 122912 | tf_op jit(solution)/shard_map/ppermute | solution.py:558
  39.7 0.0 collective-permute-done.6.r1
  39.7 0.0 collective-permute-done.7.r2
  39.8 0.1 collective-permute-start.9
  39.9 1.4 %collective-permute-done.9.post = s16[5,80,256]{2,1,0:T(8,128)(2,1)S(1)} collective-permute-done((s16[5,80,256]{2,1,0:T(8,128)(2,1)S(1)}, s16[5,80,256]{2,1,0:T(8,128)(2,1)S(1)}, u32[]{:S(2)}, u32[]{:S(2)}) %collective-permute-start.9) | collective-permute-done | bytes 204832 | tf_op jit(solution)/shard_map/ppermute | solution.py:555
  41.3 0.6 first_image.1
  41.9 0.2 collective-permute-start.10
  42.1 1.4 %collective-permute-done.10.got = bf16[7,64,256]{2,1,0:T(8,128)(2,1)S(1)} collective-permute-done((bf16[7,64,256]{2,1,0:T(8,128)(2,1)S(1)}, bf16[7,64,256]{2,1,0:T(8,128)(2,1)S(1)}, u32[]{:S(2)}, u32[]{:S(2)}) %collective-permute-start.10) | collective-permute-done | bytes 229408 | tf_op jit(solution)/shard_map/ppermute | solution.py:555
  43.5 3.9 %collective-permute-start.11 = (bf16[4,64,256]{2,1,0:T(8,128)(2,1)S(1)}, bf16[4,64,256]{2,1,0:T(8,128)(2,1)S(1)}, u32[]{:S(2)}, u32[]{:S(2)}) collective-permute-start(bf16[4,64,256]{2,1,0:T(8,128)(2,1)S(1)} %get-tuple-element.86), channel_id=1, source_target_pairs={{0,2},{1,127},{2,4},{3,1},{4,6},{5,3},{6,8},{7,5},{8,10},{9,7},{10... | collective-permute-start | bytes 393224 | tf_op jit(solution)/shard_map/ppermute | solution.py:558
  47.4 0.0 collective-permute-start.12
  47.4 0.0 collective-permute-start.13
  47.4 4.5 %second_transposed_products.1 = (bf16[4,64,256]{2,1,0:T(8,128)(2,1)S(1)}, bf16[4,64,256]{2,1,0:T(8,128)(2,1)S(1)}, bf16[3,64,256]{2,1,0:T(8,128)(2,1)S(1)}, bf16[7,64,256]{2,1,0:T(8,128)(2,1)S(1)}) custom-call(s32[4,256]{1,0:T(4,128)S(1)} %get-tuple-element.40.draft, bf16[4,64,256]{2,1,0:T(8,128)(2,1)S(1)} %get-tuple-element.63.rounded.own, ...), custom_call_target="tpu_custom_call" | custom-call | flops 2000000000 | bytes 22000000 | tf_op jit(solution)/shard_map/second_transposed_products/pallas_call | solution.py:512
  51.9 4.4 %collective-permute-done.13.r3 = bf16[3,64,256]{2,1,0:T(8,128)(2,1)S(1)} collective-permute-done((bf16[3,64,256]{2,1,0:T(8,128)(2,1)S(1)}, bf16[3,64,256]{2,1,0:T(8,128)(2,1)S(1)}, u32[]{:S(2)}, u32[]{:S(2)}) %collective-permute-start.13) | collective-permute-done | bytes 98336 | tf_op jit(solution)/shard_map/ppermute | solution.py:558
  56.3 0.0 collective-permute-done.11.r1
  56.3 0.0 collective-permute-done.12.r2
  56.3 0.0 collective-permute-start.15
  56.4 0.6 collective-permute-start.14
  57.0 0.8 %collective-permute-done.15.got = bf16[7,64,256]{2,1,0:T(8,128)(2,1)S(1)} collective-permute-done((bf16[7,64,256]{2,1,0:T(8,128)(2,1)S(1)}, bf16[7,64,256]{2,1,0:T(8,128)(2,1)S(1)}, u32[]{:S(2)}, u32[]{:S(2)}) %collective-permute-start.15) | collective-permute-done | bytes 229408 | tf_op jit(solution)/shard_map/ppermute | solution.py:555
  57.8 4.6 %collective-permute-start.16 = (bf16[4,64,256]{2,1,0:T(8,128)(2,1)S(1)}, bf16[4,64,256]{2,1,0:T(8,128)(2,1)S(1)}, u32[]{:S(2)}, u32[]{:S(2)}) collective-permute-start(bf16[4,64,256]{2,1,0:T(8,128)(2,1)S(1)} %get-tuple-element.83), channel_id=1, source_target_pairs={{0,2},{1,127},{2,4},{3,1},{4,6},{5,3},{6,8},{7,5},{8,10},{9,7},{10... | collective-permute-start | bytes 393224 | tf_op jit(solution)/shard_map/ppermute | solution.py:558
  62.4 0.0 collective-permute-start.17
  62.4 0.0 collective-permute-start.18
  62.4 0.0 collective-permute-done.14.post
  62.4 5.7 %second_forward_products.1.partial = f32[4,64,256]{2,1,0:T(8,128)S(1)} custom-call(s32[4,256]{1,0:T(4,128)S(1)} %get-tuple-element.40.draft, bf16[4,64,256]{2,1,0:T(8,128)(2,1)S(1)} %get-tuple-element.63.rounded.own, bf16[4,64,256]{2,1,0:T(8,128)(2,1)S(1)} %collective-permute-done.11.r1, bf16[4,64,256]{2,1,0:T(8,128)(2,1)S(1)} %collective-permute-done.12.r2, ...), custom_call_target="tpu_custom_call" | custom-call | flops 2000000000 | bytes 22000000 | tf_op jit(solution)/shard_map/second_forward_products/pallas_call | solution.py:522
  68.2 3.1 %collective-permute-done.18.r3 = bf16[3,64,256]{2,1,0:T(8,128)(2,1)S(1)} collective-permute-done((bf16[3,64,256]{2,1,0:T(8,128)(2,1)S(1)}, bf16[3,64,256]{2,1,0:T(8,128)(2,1)S(1)}, u32[]{:S(2)}, u32[]{:S(2)}) %collective-permute-start.18) | collective-permute-done | bytes 98336 | tf_op jit(solution)/shard_map/ppermute | solution.py:558
  71.3 0.0 collective-permute-done.16.r1
  71.4 0.1 collective-permute-start.19
  71.5 0.7 copy.22
  72.2 0.7 collective-permute-done.19.post
  72.9 1.0 %second_image.1 = f32[64,1024]{1,0:T(8,128)} custom-call(f32[4,64,256]{2,1,0:T(8,128)S(1)} %second_forward_products.1.partial, s32[16,256]{1,0:T(8,128)S(1)} %get-tuple-element.74.marked, bf16[4,64,256]{2,1,0:T(8,128)(2,1)S(1)} %collective-permute-done.16.r1, bf16[4,64,256]{2,1,0:T(8,128)(2,1)S(1)} %collective-permute-done.17.r2, ...), custom_call_target="tpu_custom_call" | custom-call | flops 2000000000 | bytes 22000000 | tf_op jit(solution)/shard_map/second_image/pallas_call | solution.py:531
  (20 shorter events, 0.2 us)
Async XLA Ops:
  0.6 2.7 %collective-permute-start = (bf16[64,1024]{1,0:T(8,128)(2,1)}, bf16[64,1024]{1,0:T(8,128)(2,1)S(1)}, u32[]{:S(2)}, u32[]{:S(2)}) collective-permute-start(bf16[64,1024]{1,0:T(8,128)(2,1)} %source.1), channel_id=1, source_target_pairs={{0,1},{1,0},{2,3},{3,2},{4,5},{5,4},{6,7},{7,6},{8,9},{9,8},{10,11... | collective-permute-start | bytes 393224 | tf_op jit(solution)/shard_map/ppermute | solution.py:555
  3.3 16.8 %collective-permute-start.1 = (bf16[2,64,1024]{2,1,0:T(8,128)(2,1)S(1)}, bf16[2,64,1024]{2,1,0:T(8,128)(2,1)S(1)}, u32[]{:S(2)}, u32[]{:S(2)}) collective-permute-start(bf16[2,64,1024]{2,1,0:T(8,128)(2,1)S(1)} %bitcast_dynamic-update-slice_fusion.both), channel_id=1, source_target_pairs={{0,2},{1,127},{2,4},{3,1},{4,6},{5,3},{6,8},{7,5},{8,10},{9,7},{10... | collective-permute-start | bytes 786440 | tf_op jit(solution)/shard_map/ppermute | solution.py:558
  11.9 10.8 %collective-permute-start.2 = (bf16[2,64,1024]{2,1,0:T(8,128)(2,1)S(1)}, bf16[2,64,1024]{2,1,0:T(8,128)(2,1)S(1)}, u32[]{:S(2)}, u32[]{:S(2)}) collective-permute-start(bf16[2,64,1024]{2,1,0:T(8,128)(2,1)S(1)} %bitcast_dynamic-update-slice_fusion.both), channel_id=1, source_target_pairs={{0,4},{1,125},{2,6},{3,127},{4,8},{5,1},{6,10},{7,3},{8,12},{9,5},... | collective-permute-start | bytes 786440 | tf_op jit(solution)/shard_map/ppermute | solution.py:558
  11.9 12.7 %collective-permute-start.3 = (bf16[2,64,1024]{2,1,0:T(8,128)(2,1)S(1)}, bf16[2,64,1024]{2,1,0:T(8,128)(2,1)S(1)}, u32[]{:S(2)}, u32[]{:S(2)}) collective-permute-start(bf16[2,64,1024]{2,1,0:T(8,128)(2,1)S(1)} %bitcast_dynamic-update-slice_fusion.both), channel_id=1, source_target_pairs={{0,6},{1,123},{2,8},{3,125},{4,10},{5,127},{6,12},{7,1},{8,14},{9,... | collective-permute-start | bytes 786440 | tf_op jit(solution)/shard_map/ppermute | solution.py:558
  20.0 11.5 %copy-start = (bf16[4,256,256]{2,1,0:T(8,128)(2,1)S(1)}, bf16[4,256,256]{2,1,0:T(8,128)(2,1)}, u32[]{:S(2)}) copy-start(bf16[4,256,256]{2,1,0:T(8,128)(2,1)} %diag.3) | copy-start | bytes 1572868
  20.0 4.8 %collective-permute-start.5 = (s16[11,80,256]{2,1,0:T(8,128)(2,1)S(1)}, s16[11,80,256]{2,1,0:T(8,128)(2,1)S(1)}, u32[]{:S(2)}, u32[]{:S(2)}) collective-permute-start(s16[11,80,256]{2,1,0:T(8,128)(2,1)S(1)} %get-tuple-element.46), channel_id=1, source_target_pairs={{0,1},{1,0},{2,3},{3,2},{4,5},{5,4},{6,7},{7,6},{8,9},{9,8},{10,11... | collective-permute-start | bytes 1351688 | tf_op jit(solution)/shard_map/ppermute | solution.py:555
  24.7 6.7 %collective-permute-start.4 = (bf16[5,64,1024]{2,1,0:T(8,128)(2,1)S(1)}, bf16[5,64,1024]{2,1,0:T(8,128)(2,1)S(1)}, u32[]{:S(2)}, u32[]{:S(2)}) collective-permute-start(bf16[5,64,1024]{2,1,0:T(8,128)(2,1)S(1)} %pad_maximum_fusion), channel_id=1, source_target_pairs={{0,1},{1,0},{2,3},{3,2},{4,5},{5,4},{6,7},{7,6},{8,9},{9,8},{10,11... | collective-permute-start | bytes 1966088 | tf_op jit(solution)/shard_map/ppermute | solution.py:555
  24.9 14.9 %collective-permute-start.6 = (s16[4,80,256]{2,1,0:T(8,128)(2,1)S(1)}, s16[4,80,256]{2,1,0:T(8,128)(2,1)S(1)}, u32[]{:S(2)}, u32[]{:S(2)}) collective-permute-start(s16[4,80,256]{2,1,0:T(8,128)(2,1)S(1)} %get-tuple-element.80), channel_id=1, source_target_pairs={{0,2},{1,127},{2,4},{3,1},{4,6},{5,3},{6,8},{7,5},{8,10},{9,7},{10... | collective-permute-start | bytes 491528 | tf_op jit(solution)/shard_map/ppermute | solution.py:558
  28.9 10.8 %collective-permute-start.7 = (s16[4,80,256]{2,1,0:T(8,128)(2,1)S(1)}, s16[4,80,256]{2,1,0:T(8,128)(2,1)S(1)}, u32[]{:S(2)}, u32[]{:S(2)}) collective-permute-start(s16[4,80,256]{2,1,0:T(8,128)(2,1)S(1)} %get-tuple-element.79), channel_id=1, source_target_pairs={{0,4},{1,125},{2,6},{3,127},{4,8},{5,1},{6,10},{7,3},{8,12},{9,5},... | collective-permute-start | bytes 491528 | tf_op jit(solution)/shard_map/ppermute | solution.py:558
  31.5 8.3 %collective-permute-start.8 = (s16[3,80,256]{2,1,0:T(8,128)(2,1)S(1)}, s16[3,80,256]{2,1,0:T(8,128)(2,1)S(1)}, u32[]{:S(2)}, u32[]{:S(2)}) collective-permute-start(s16[3,80,256]{2,1,0:T(8,128)(2,1)S(1)} %get-tuple-element.78), channel_id=1, source_target_pairs={{0,6},{1,123},{2,8},{3,125},{4,10},{5,127},{6,12},{7,1},{8,14},{9,... | collective-permute-start | bytes 368648 | tf_op jit(solution)/shard_map/ppermute | solution.py:558
  39.8 1.5 %collective-permute-start.9 = (s16[5,80,256]{2,1,0:T(8,128)(2,1)S(1)}, s16[5,80,256]{2,1,0:T(8,128)(2,1)S(1)}, u32[]{:S(2)}, u32[]{:S(2)}) collective-permute-start(s16[5,80,256]{2,1,0:T(8,128)(2,1)S(1)} %pad_add_fusion), channel_id=1, source_target_pairs={{0,1},{1,0},{2,3},{3,2},{4,5},{5,4},{6,7},{7,6},{8,9},{9,8},{10,11... | collective-permute-start | bytes 614408 | tf_op jit(solution)/shard_map/ppermute | solution.py:555
  41.9 1.6 %collective-permute-start.10 = (bf16[7,64,256]{2,1,0:T(8,128)(2,1)S(1)}, bf16[7,64,256]{2,1,0:T(8,128)(2,1)S(1)}, u32[]{:S(2)}, u32[]{:S(2)}) collective-permute-start(bf16[7,64,256]{2,1,0:T(8,128)(2,1)S(1)} %get-tuple-element.60), channel_id=1, source_target_pairs={{0,1},{1,0},{2,3},{3,2},{4,5},{5,4},{6,7},{7,6},{8,9},{9,8},{10,11... | collective-permute-start | bytes 688136 | tf_op jit(solution)/shard_map/ppermute | solution.py:555
  43.5 12.8 %collective-permute-start.11 = (bf16[4,64,256]{2,1,0:T(8,128)(2,1)S(1)}, bf16[4,64,256]{2,1,0:T(8,128)(2,1)S(1)}, u32[]{:S(2)}, u32[]{:S(2)}) collective-permute-start(bf16[4,64,256]{2,1,0:T(8,128)(2,1)S(1)} %get-tuple-element.86), channel_id=1, source_target_pairs={{0,2},{1,127},{2,4},{3,1},{4,6},{5,3},{6,8},{7,5},{8,10},{9,7},{10... | collective-permute-start | bytes 393224 | tf_op jit(solution)/shard_map/ppermute | solution.py:558
  47.4 8.9 %collective-permute-start.12 = (bf16[4,64,256]{2,1,0:T(8,128)(2,1)S(1)}, bf16[4,64,256]{2,1,0:T(8,128)(2,1)S(1)}, u32[]{:S(2)}, u32[]{:S(2)}) collective-permute-start(bf16[4,64,256]{2,1,0:T(8,128)(2,1)S(1)} %get-tuple-element.85), channel_id=1, source_target_pairs={{0,4},{1,125},{2,6},{3,127},{4,8},{5,1},{6,10},{7,3},{8,12},{9,5},... | collective-permute-start | bytes 393224 | tf_op jit(solution)/shard_map/ppermute | solution.py:558
  47.4 8.9 %collective-permute-start.13 = (bf16[3,64,256]{2,1,0:T(8,128)(2,1)S(1)}, bf16[3,64,256]{2,1,0:T(8,128)(2,1)S(1)}, u32[]{:S(2)}, u32[]{:S(2)}) collective-permute-start(bf16[3,64,256]{2,1,0:T(8,128)(2,1)S(1)} %get-tuple-element.84), channel_id=1, source_target_pairs={{0,6},{1,123},{2,8},{3,125},{4,10},{5,127},{6,12},{7,1},{8,14},{9,... | collective-permute-start | bytes 294920 | tf_op jit(solution)/shard_map/ppermute | solution.py:558
  56.3 1.5 %collective-permute-start.15 = (bf16[7,64,256]{2,1,0:T(8,128)(2,1)S(1)}, bf16[7,64,256]{2,1,0:T(8,128)(2,1)S(1)}, u32[]{:S(2)}, u32[]{:S(2)}) collective-permute-start(bf16[7,64,256]{2,1,0:T(8,128)(2,1)S(1)} %get-tuple-element.69), channel_id=1, source_target_pairs={{0,1},{1,0},{2,3},{3,2},{4,5},{5,4},{6,7},{7,6},{8,9},{9,8},{10,11... | collective-permute-start | bytes 688136 | tf_op jit(solution)/shard_map/ppermute | solution.py:555
  56.4 6.0 %collective-permute-start.14 = (bf16[5,64,256]{2,1,0:T(8,128)(2,1)S(1)}, bf16[5,64,256]{2,1,0:T(8,128)(2,1)S(1)}, u32[]{:S(2)}, u32[]{:S(2)}) collective-permute-start(bf16[5,64,256]{2,1,0:T(8,128)(2,1)S(1)} %pad_maximum_fusion.1), channel_id=1, source_target_pairs={{0,1},{1,0},{2,3},{3,2},{4,5},{5,4},{6,7},{7,6},{8,9},{9,8},{10,11... | collective-permute-start | bytes 491528 | tf_op jit(solution)/shard_map/ppermute | solution.py:555
  57.8 13.5 %collective-permute-start.16 = (bf16[4,64,256]{2,1,0:T(8,128)(2,1)S(1)}, bf16[4,64,256]{2,1,0:T(8,128)(2,1)S(1)}, u32[]{:S(2)}, u32[]{:S(2)}) collective-permute-start(bf16[4,64,256]{2,1,0:T(8,128)(2,1)S(1)} %get-tuple-element.83), channel_id=1, source_target_pairs={{0,2},{1,127},{2,4},{3,1},{4,6},{5,3},{6,8},{7,5},{8,10},{9,7},{10... | collective-permute-start | bytes 393224 | tf_op jit(solution)/shard_map/ppermute | solution.py:558
  62.4 8.9 %collective-permute-start.17 = (bf16[4,64,256]{2,1,0:T(8,128)(2,1)S(1)}, bf16[4,64,256]{2,1,0:T(8,128)(2,1)S(1)}, u32[]{:S(2)}, u32[]{:S(2)}) collective-permute-start(bf16[4,64,256]{2,1,0:T(8,128)(2,1)S(1)} %get-tuple-element.82), channel_id=1, source_target_pairs={{0,4},{1,125},{2,6},{3,127},{4,8},{5,1},{6,10},{7,3},{8,12},{9,5},... | collective-permute-start | bytes 393224 | tf_op jit(solution)/shard_map/ppermute | solution.py:558
  62.4 8.9 %collective-permute-start.18 = (bf16[3,64,256]{2,1,0:T(8,128)(2,1)S(1)}, bf16[3,64,256]{2,1,0:T(8,128)(2,1)S(1)}, u32[]{:S(2)}, u32[]{:S(2)}) collective-permute-start(bf16[3,64,256]{2,1,0:T(8,128)(2,1)S(1)} %get-tuple-element.81), channel_id=1, source_target_pairs={{0,6},{1,123},{2,8},{3,125},{4,10},{5,127},{6,12},{7,1},{8,14},{9,... | collective-permute-start | bytes 294920 | tf_op jit(solution)/shard_map/ppermute | solution.py:558
  71.4 1.5 %collective-permute-start.19 = (bf16[5,64,256]{2,1,0:T(8,128)(2,1)S(1)}, bf16[5,64,256]{2,1,0:T(8,128)(2,1)S(1)}, u32[]{:S(2)}, u32[]{:S(2)}) collective-permute-start(bf16[5,64,256]{2,1,0:T(8,128)(2,1)S(1)} %pad_maximum_fusion.2), channel_id=1, source_target_pairs={{0,1},{1,0},{2,3},{3,2},{4,5},{5,4},{6,7},{7,6},{8,9},{9,8},{10,11... | collective-permute-start | bytes 491528 | tf_op jit(solution)/shard_map/ppermute | solution.py:555

commit v9 on v8

--- a/solution.py
+++ b/solution.py
@@ -247,9 +247,6 @@
     return 3, rho - 6
 
 
-MESSAGE = (4, 4, 3)
-
-
 def back_first(
     me, near_rows, near_cols, far_rows, far_cols, counts, both, near, left, right,
     m1, m2, m3, give, draft, near_held, left_held, right_held,
@@ -439,8 +436,8 @@
     return jax.ShapeDtypeStruct(shape, dtype)
 
 
-def message_shapes(rows, dtype, given=7):
-    return [shaped((n, rows, B), dtype) for n in MESSAGE + (given,)]
+def message_shapes(rows, dtype, given=7, third=3):
+    return [shaped((n, rows, B), dtype) for n in (4, 4, third, given)]
 
 
 def stage(source, target, sem):
@@ -501,7 +498,7 @@
             shaped((CL, RHS, B), BF16),
             shaped((16, B), jnp.int32),
         ]
-        + message_shapes(RHS, BF16),
+        + message_shapes(RHS, BF16, third=4),
         [VMEM] * 7,
         [VMEM] * 6,
         [pltpu.VMEM((1, SLOTS), jnp.int32), pltpu.SMEM((1, SLOTS), jnp.int32), pltpu.SemaphoreType.DMA],
@@ -558,8 +555,8 @@
         return lax.ppermute(block, "rows", carriers(size, k))
 
     def carried(messages):
-        second = carry(messages[1], 2)
-        return [carry(messages[0], 1), second, carry(messages[2], 3)]
+        second, first, third = [carry(messages[k - 1], k) for k in (2, 1, 3)]
+        return [first, second, third]
 
     def exchange(m1, m2, m3, give):
         got = swap(give)
@@ -581,23 +578,24 @@
     m1, m2, m3, give, plan, *held = k1(
         me, *lists, in_hbm(counts), both, in_hbm(near_blocks), in_hbm(far_left), in_hbm(far_right)
     )
-    halo, m1 = lax.optimization_barrier((halo, m1))
+    far_halo, halo_1, halo_3, m1 = lax.optimization_barrier((halo[1], halo[0], halo[2], m1))
+    halo = (halo_1, far_halo, halo_3)
     r1, r2, r3, got, messages = exchange(m1, m2, m3, give)
     halo_post = swap(jnp.concatenate([halo[0], halo[1], halo[2][1:]]))
     halo_post, messages = lax.optimization_barrier((halo_post, messages))
     partial = k2(plan, both, *halo, halo_post, diag_blocks, *held)
-    partial, r1, r2, r3 = lax.optimization_barrier((partial, r1, r2, r3))
+    partial, r2, r1, r3 = lax.optimization_barrier((partial, r2, r1, r3))
     post = passed_on(r1, r2, r3)
     first_image, rounded, marked, m1, m2, m3, give = k3(partial, r1, r2, r3, post, got)
     f1, f2, f3, f_got, messages = exchange(m1, m2, m3, give)
     rounded, messages = lax.optimization_barrier((rounded, messages))
     m1, m2, m3, give = k4(plan, rounded, *held)
-    f1, f2, f3, give = lax.optimization_barrier((f1, f2, f3, give))
+    f1, f2, f3, m1 = lax.optimization_barrier((f1, f2, f3, m1))
     r1, r2, r3, got, messages = exchange(m1, m2, m3, give)
     f_post = passed_on(f1, f2, f3)
     f_post, messages = lax.optimization_barrier((f_post, messages))
     partial = k5(plan, rounded, f1, f2, f3, f_post, f_got, diag_blocks, *held)
-    partial, r1, r2, r3 = lax.optimization_barrier((partial, r1, r2, r3))
+    partial, r2, r1, r3 = lax.optimization_barrier((partial, r2, r1, r3))
     post = passed_on(r1, r2, r3)
     return first_image, k6(partial, marked, r1, r2, r3, post, got)
 

time: 74.2 us -> 70.4 us (0.949)
  starting transfers between devices: 27.2 us -> 32.8 us
  waiting for transfers between devices: 19.1 us -> 14 us
  Pallas kernels: 25.7 us -> 21.3 us
    ppermute x12, waiting for transfers between devices: 14.5 us -> 10.6 us  [carry(): return lax.ppermute(block, 'rows', carriers(size, k))]
    ppermute x8, starting transfers between devices: 2.63 us -> 5.96 us  [swap(): return lax.ppermute(block, 'rows', [(i, i ^ 1) for i in range(size)])]
    ppermute x12, starting transfers between devices: 24.6 us -> 26.9 us  [carry(): return lax.ppermute(block, 'rows', carriers(size, k))]
    pallas_call x1, Pallas kernels: 5.73 us -> 4.5 us  [k5(): call(forward_second, 'second_forward_products', shaped((CL, RHS, B), F32)...]
    pallas_call x1, Pallas kernels: 5.75 us -> 4.52 us  [k2(): call(forward_first, 'forward_products', shaped((CL, RHS, B), F32), VMEM,...]
    ppermute x8, waiting for transfers between devices: 4.59 us -> 3.4 us  [swap(): return lax.ppermute(block, 'rows', [(i, i ^ 1) for i in range(size)])]
    pallas_call x1, Pallas kernels: 7.21 us -> 6.2 us  [k1(): call(back_first, 'transposed_products', message_shapes(RHS + EXTRA, jnp.i...]
    pallas_call x1, Pallas kernels: 4.49 us -> 3.6 us  [k4(): call(back_second, 'second_transposed_products', message_shapes(RHS, BF16)...]
  transfers between devices with their start and end apart: 20 -> 20, of which waited for: 10 -> 10; matrix products, arithmetic and copies ran while one was open for 1% -> 1% of each run, Pallas kernels for 33% -> 28%
where the time goes in v9:
time: 70.4 us; the launch traced here: 70.2 us
  starting transfers between devices  32.8 us (47%)
  Pallas kernels  21.3 us (30%)
  waiting for transfers between devices  14 us (20%)
  between operations  1.03 us (1%)
  local copies, waits for them, and re-layouts  0.83 us (1%)
    ppermute x12, starting transfers between devices, carry(): return lax.ppermute(block, 'rows', carriers(size, k))  26.9 us
    ppermute x12, waiting for transfers between devices, carry(): return lax.ppermute(block, 'rows', carriers(size, k))  10.6 us
    pallas_call x1, Pallas kernels, k1(): call(back_first, 'transposed_products', message_shapes(RHS + EXTRA, jnp.i...  6.2 us
    ppermute x8, starting transfers between devices, swap(): return lax.ppermute(block, 'rows', [(i, i ^ 1) for i in range(size)])  5.96 us
    pallas_call x1, Pallas kernels, k2(): call(forward_first, 'forward_products', shaped((CL, RHS, B), F32), VMEM,...  4.52 us
    pallas_call x1, Pallas kernels, k5(): call(forward_second, 'second_forward_products', shaped((CL, RHS, B), F32)...  4.5 us
    pallas_call x1, Pallas kernels, k4(): call(back_second, 'second_transposed_products', message_shapes(RHS, BF16)...  3.6 us
    ppermute x8, waiting for transfers between devices, swap(): return lax.ppermute(block, 'rows', [(i, i ^ 1) for i in range(size)])  3.4 us
  transfers between devices with their start and end apart: 20, of which 10 were waited for; matrix products, arithmetic and copies ran while one was open for 1% of the time, Pallas kernels for 28%

profile of v9, /device:TPU:1, one launch (start us, length us, event | category | flops | bytes accessed | tf_op | source)
XLA Modules:
  0.0 70.2 jit_solution(3507943809032241298)
XLA Ops:
  0.6 1.5 %collective-permute-start = (bf16[64,1024]{1,0:T(8,128)(2,1)}, bf16[64,1024]{1,0:T(8,128)(2,1)S(1)}, u32[]{:S(2)}, u32[]{:S(2)}) collective-permute-start(bf16[64,1024]{1,0:T(8,128)(2,1)} %source.1), channel_id=1, source_target_pairs={{0,1},{1,0},{2,3},{3,2},{4,5},{5,4},{6,7},{7,6},{8,9},{9,8},{10,11... | collective-permute-start | bytes 393224 | tf_op jit(solution)/shard_map/ppermute | solution.py:552
  2.1 0.9 %staged.1 = bf16[2,64,1024]{2,1,0:T(8,128)(2,1)S(1)} custom-call(bf16[64,1024]{1,0:T(8,128)(2,1)} %source.1), custom_call_target="tpu_custom_call" | custom-call | flops 2000000000 | bytes 22000000 | tf_op jit(solution)/shard_map/staged/pallas_call | solution.py:450
  3.0 0.3 collective-permute-done
  3.3 8.4 %collective-permute-start.1 = (bf16[2,64,1024]{2,1,0:T(8,128)(2,1)S(1)}, bf16[2,64,1024]{2,1,0:T(8,128)(2,1)S(1)}, u32[]{:S(2)}, u32[]{:S(2)}) collective-permute-start(bf16[2,64,1024]{2,1,0:T(8,128)(2,1)S(1)} %bitcast_dynamic-update-slice_fusion.both), channel_id=1, source_target_pairs={{0,4},{1,125},{2,6},{3,127},{4,8},{5,1},{6,10},{7,3},{8,12},{9,5},... | collective-permute-start | bytes 786440 | tf_op jit(solution)/shard_map/ppermute | solution.py:555
  11.7 0.4 collective-permute-start.2
  12.2 1.2 %collective-permute-start.3 = (bf16[2,64,1024]{2,1,0:T(8,128)(2,1)S(1)}, bf16[2,64,1024]{2,1,0:T(8,128)(2,1)S(1)}, u32[]{:S(2)}, u32[]{:S(2)}) collective-permute-start(bf16[2,64,1024]{2,1,0:T(8,128)(2,1)S(1)} %bitcast_dynamic-update-slice_fusion.both), channel_id=1, source_target_pairs={{0,6},{1,123},{2,8},{3,125},{4,10},{5,127},{6,12},{7,1},{8,14},{9,... | collective-permute-start | bytes 786440 | tf_op jit(solution)/shard_map/ppermute | solution.py:555
  13.4 6.2 %transposed_products.1 = (s16[4,80,256]{2,1,0:T(8,128)(2,1)S(1)}, s16[4,80,256]{2,1,0:T(8,128)(2,1)S(1)}, s16[3,80,256]{2,1,0:T(8,128)(2,1)S(1)}, s16[11,80,256]...) custom-call(s32[1]{0:T(128)} %bitcast.me, ...), custom_call_target="tpu_custom_call" | custom-call | flops 2000000000 | bytes 22000000 | tf_op jit(solution)/shard_map/transposed_products/pallas_call | solution.py:455
  19.6 0.0 copy-start
  19.6 0.1 collective-permute-start.5
  19.7 0.0 collective-permute-done.1.h2
  19.7 1.8 %collective-permute-done.2.h1 = bf16[2,64,1024]{2,1,0:T(8,128)(2,1)S(1)} collective-permute-done((bf16[2,64,1024]{2,1,0:T(8,128)(2,1)S(1)}, bf16[2,64,1024]{2,1,0:T(8,128)(2,1)S(1)}, u32[]{:S(2)}, u32[]{:S(2)}) %collective-permute-start.2) | collective-permute-done | bytes 262176 | tf_op jit(solution)/shard_map/ppermute | solution.py:555
  21.5 1.3 %collective-permute-done.3.h3 = bf16[2,64,1024]{2,1,0:T(8,128)(2,1)S(1)} collective-permute-done((bf16[2,64,1024]{2,1,0:T(8,128)(2,1)S(1)}, bf16[2,64,1024]{2,1,0:T(8,128)(2,1)S(1)}, u32[]{:S(2)}, u32[]{:S(2)}) %collective-permute-start.3) | collective-permute-done | bytes 262176 | tf_op jit(solution)/shard_map/ppermute | solution.py:555
  22.8 0.1 pad_maximum_fusion
  22.9 0.1 collective-permute-start.4
  23.0 0.0 collective-permute-done.5.got
  23.0 5.2 %collective-permute-start.6 = (s16[4,80,256]{2,1,0:T(8,128)(2,1)S(1)}, s16[4,80,256]{2,1,0:T(8,128)(2,1)S(1)}, u32[]{:S(2)}, u32[]{:S(2)}) collective-permute-start(s16[4,80,256]{2,1,0:T(8,128)(2,1)S(1)} %get-tuple-element.79), channel_id=1, source_target_pairs={{0,4},{1,125},{2,6},{3,127},{4,8},{5,1},{6,10},{7,3},{8,12},{9,5},... | collective-permute-start | bytes 491528 | tf_op jit(solution)/shard_map/ppermute | solution.py:555
  28.2 2.2 %collective-permute-start.7 = (s16[4,80,256]{2,1,0:T(8,128)(2,1)S(1)}, s16[4,80,256]{2,1,0:T(8,128)(2,1)S(1)}, u32[]{:S(2)}, u32[]{:S(2)}) collective-permute-start(s16[4,80,256]{2,1,0:T(8,128)(2,1)S(1)} %get-tuple-element.80), channel_id=1, source_target_pairs={{0,2},{1,127},{2,4},{3,1},{4,6},{5,3},{6,8},{7,5},{8,10},{9,7},{10... | collective-permute-start | bytes 491528 | tf_op jit(solution)/shard_map/ppermute | solution.py:555
  30.4 0.0 collective-permute-start.8
  30.5 0.0 collective-permute-done.4.post
  30.5 4.5 %forward_products.1.partial = f32[4,64,256]{2,1,0:T(8,128)S(1)} custom-call(s32[4,256]{1,0:T(4,128)S(1)} %get-tuple-element.40.draft, bf16[2,64,1024]{2,1,0:T(8,128)(2,1)S(1)} %bitcast_dynamic-update-slice_fusion.both, bf16[2,64,1024]{2,1,0:T(8,128)(2,1)S(1)} %collective-permute-done.2.h1, bf16[2,64,1024]{2,1,0:T(8,128)(2,1)S(1)} %collective-permute-done.1.h2, ...), custom_call_target="tpu_custom_call" | custom-call | flops 2000000000 | bytes 22000000 | tf_op jit(solution)/shard_map/forward_products/pallas_call | solution.py:485
  35.0 2.1 %collective-permute-done.8.r3 = s16[3,80,256]{2,1,0:T(8,128)(2,1)S(1)} collective-permute-done((s16[3,80,256]{2,1,0:T(8,128)(2,1)S(1)}, s16[3,80,256]{2,1,0:T(8,128)(2,1)S(1)}, u32[]{:S(2)}, u32[]{:S(2)}) %collective-permute-start.8) | collective-permute-done | bytes 122912 | tf_op jit(solution)/shard_map/ppermute | solution.py:555
  37.1 0.0 collective-permute-done.6.r2
  37.1 0.0 collective-permute-done.7.r1
  37.2 0.1 collective-permute-start.9
  37.3 1.4 %collective-permute-done.9.post = s16[5,80,256]{2,1,0:T(8,128)(2,1)S(1)} collective-permute-done((s16[5,80,256]{2,1,0:T(8,128)(2,1)S(1)}, s16[5,80,256]{2,1,0:T(8,128)(2,1)S(1)}, u32[]{:S(2)}, u32[]{:S(2)}) %collective-permute-start.9) | collective-permute-done | bytes 204832 | tf_op jit(solution)/shard_map/ppermute | solution.py:552
  38.7 0.6 first_image.1
  39.3 0.2 collective-permute-start.10
  39.5 1.4 %collective-permute-done.10.got = bf16[7,64,256]{2,1,0:T(8,128)(2,1)S(1)} collective-permute-done((bf16[7,64,256]{2,1,0:T(8,128)(2,1)S(1)}, bf16[7,64,256]{2,1,0:T(8,128)(2,1)S(1)}, u32[]{:S(2)}, u32[]{:S(2)}) %collective-permute-start.10) | collective-permute-done | bytes 229408 | tf_op jit(solution)/shard_map/ppermute | solution.py:552
  40.9 4.7 %collective-permute-start.11 = (bf16[4,64,256]{2,1,0:T(8,128)(2,1)S(1)}, bf16[4,64,256]{2,1,0:T(8,128)(2,1)S(1)}, u32[]{:S(2)}, u32[]{:S(2)}) collective-permute-start(bf16[4,64,256]{2,1,0:T(8,128)(2,1)S(1)} %get-tuple-element.86), channel_id=1, source_target_pairs={{0,2},{1,127},{2,4},{3,1},{4,6},{5,3},{6,8},{7,5},{8,10},{9,7},{10... | collective-permute-start | bytes 393224 | tf_op jit(solution)/shard_map/ppermute | solution.py:555
  45.6 0.2 collective-permute-start.12
  45.8 0.0 collective-permute-start.13
  45.8 3.6 %second_transposed_products.1 = (bf16[4,64,256]{2,1,0:T(8,128)(2,1)S(1)}, bf16[4,64,256]{2,1,0:T(8,128)(2,1)S(1)}, bf16[3,64,256]{2,1,0:T(8,128)(2,1)S(1)}, bf16[7,64,256]{2,1,0:T(8,128)(2,1)S(1)}) custom-call(s32[4,256]{1,0:T(4,128)S(1)} %get-tuple-element.40.draft, bf16[4,64,256]{2,1,0:T(8,128)(2,1)S(1)} %get-tuple-element.63.rounded.own, ...), custom_call_target="tpu_custom_call" | custom-call | flops 2000000000 | bytes 22000000 | tf_op jit(solution)/shard_map/second_transposed_products/pallas_call | solution.py:509
  49.4 0.4 collective-permute-start.15
  49.8 4.1 %collective-permute-done.12.r2 = bf16[4,64,256]{2,1,0:T(8,128)(2,1)S(1)} collective-permute-done((bf16[4,64,256]{2,1,0:T(8,128)(2,1)S(1)}, bf16[4,64,256]{2,1,0:T(8,128)(2,1)S(1)}, u32[]{:S(2)}, u32[]{:S(2)}) %collective-permute-start.12) | collective-permute-done | bytes 131104 | tf_op jit(solution)/shard_map/ppermute | solution.py:555
  54.0 1.1 %collective-permute-done.13.r3 = bf16[4,64,256]{2,1,0:T(8,128)(2,1)S(1)} collective-permute-done((bf16[4,64,256]{2,1,0:T(8,128)(2,1)S(1)}, bf16[4,64,256]{2,1,0:T(8,128)(2,1)S(1)}, u32[]{:S(2)}, u32[]{:S(2)}) %collective-permute-start.13) | collective-permute-done | bytes 131104 | tf_op jit(solution)/shard_map/ppermute | solution.py:555
  55.1 0.1 collective-permute-start.14
  55.2 0.0 collective-permute-done.15.got
  55.2 2.4 %collective-permute-start.16 = (bf16[4,64,256]{2,1,0:T(8,128)(2,1)S(1)}, bf16[4,64,256]{2,1,0:T(8,128)(2,1)S(1)}, u32[]{:S(2)}, u32[]{:S(2)}) collective-permute-start(bf16[4,64,256]{2,1,0:T(8,128)(2,1)S(1)} %get-tuple-element.82), channel_id=1, source_target_pairs={{0,4},{1,125},{2,6},{3,127},{4,8},{5,1},{6,10},{7,3},{8,12},{9,5},... | collective-permute-start | bytes 393224 | tf_op jit(solution)/shard_map/ppermute | solution.py:555
  57.7 1.8 %collective-permute-start.17 = (bf16[4,64,256]{2,1,0:T(8,128)(2,1)S(1)}, bf16[4,64,256]{2,1,0:T(8,128)(2,1)S(1)}, u32[]{:S(2)}, u32[]{:S(2)}) collective-permute-start(bf16[4,64,256]{2,1,0:T(8,128)(2,1)S(1)} %get-tuple-element.83), channel_id=1, source_target_pairs={{0,2},{1,127},{2,4},{3,1},{4,6},{5,3},{6,8},{7,5},{8,10},{9,7},{10... | collective-permute-start | bytes 393224 | tf_op jit(solution)/shard_map/ppermute | solution.py:555
  59.4 0.3 collective-permute-start.18
  59.7 0.0 collective-permute-done.14.post
  59.7 4.5 %second_forward_products.1.partial = f32[4,64,256]{2,1,0:T(8,128)S(1)} custom-call(s32[4,256]{1,0:T(4,128)S(1)} %get-tuple-element.40.draft, bf16[4,64,256]{2,1,0:T(8,128)(2,1)S(1)} %get-tuple-element.63.rounded.own, bf16[4,64,256]{2,1,0:T(8,128)(2,1)S(1)} %collective-permute-done.11.r1, bf16[4,64,256]{2,1,0:T(8,128)(2,1)S(1)} %collective-permute-done.12.r2, ...), custom_call_target="tpu_custom_call" | custom-call | flops 2000000000 | bytes 22000000 | tf_op jit(solution)/shard_map/second_forward_products/pallas_call | solution.py:519
  64.2 0.2 collective-permute-done.18.r3
  64.4 0.0 collective-permute-done.16.r2
  64.5 3.5 %collective-permute-start.19 = (bf16[5,64,256]{2,1,0:T(8,128)(2,1)S(1)}, bf16[5,64,256]{2,1,0:T(8,128)(2,1)S(1)}, u32[]{:S(2)}, u32[]{:S(2)}) collective-permute-start(bf16[5,64,256]{2,1,0:T(8,128)(2,1)S(1)} %pad_maximum_fusion.2), channel_id=1, source_target_pairs={{0,1},{1,0},{2,3},{3,2},{4,5},{5,4},{6,7},{7,6},{8,9},{9,8},{10,11... | collective-permute-start | bytes 491528 | tf_op jit(solution)/shard_map/ppermute | solution.py:552
  68.0 0.7 %copy.22 = f32[64,1024]{1,0:T(8,128)} copy(f32[64,1024]{1,0:T(8,128)S(1)} %get-tuple-element.87) | data formatting | bytes 524288
  68.7 0.3 collective-permute-done.19.post
  69.0 1.0 %second_image.1 = f32[64,1024]{1,0:T(8,128)} custom-call(f32[4,64,256]{2,1,0:T(8,128)S(1)} %second_forward_products.1.partial, s32[16,256]{1,0:T(8,128)S(1)} %get-tuple-element.74.marked, bf16[4,64,256]{2,1,0:T(8,128)(2,1)S(1)} %collective-permute-done.17.r1, bf16[4,64,256]{2,1,0:T(8,128)(2,1)S(1)} %collective-permute-done.16.r2, ...), custom_call_target="tpu_custom_call" | custom-call | flops 2000000000 | bytes 22000000 | tf_op jit(solution)/shard_map/second_image/pallas_call | solution.py:528
  (20 shorter events, 0.2 us)
Async XLA Ops:
  0.6 2.7 %collective-permute-start = (bf16[64,1024]{1,0:T(8,128)(2,1)}, bf16[64,1024]{1,0:T(8,128)(2,1)S(1)}, u32[]{:S(2)}, u32[]{:S(2)}) collective-permute-start(bf16[64,1024]{1,0:T(8,128)(2,1)} %source.1), channel_id=1, source_target_pairs={{0,1},{1,0},{2,3},{3,2},{4,5},{5,4},{6,7},{7,6},{8,9},{9,8},{10,11... | collective-permute-start | bytes 393224 | tf_op jit(solution)/shard_map/ppermute | solution.py:552
  3.3 16.4 %collective-permute-start.1 = (bf16[2,64,1024]{2,1,0:T(8,128)(2,1)S(1)}, bf16[2,64,1024]{2,1,0:T(8,128)(2,1)S(1)}, u32[]{:S(2)}, u32[]{:S(2)}) collective-permute-start(bf16[2,64,1024]{2,1,0:T(8,128)(2,1)S(1)} %bitcast_dynamic-update-slice_fusion.both), channel_id=1, source_target_pairs={{0,4},{1,125},{2,6},{3,127},{4,8},{5,1},{6,10},{7,3},{8,12},{9,5},... | collective-permute-start | bytes 786440 | tf_op jit(solution)/shard_map/ppermute | solution.py:555
  11.7 9.7 %collective-permute-start.2 = (bf16[2,64,1024]{2,1,0:T(8,128)(2,1)S(1)}, bf16[2,64,1024]{2,1,0:T(8,128)(2,1)S(1)}, u32[]{:S(2)}, u32[]{:S(2)}) collective-permute-start(bf16[2,64,1024]{2,1,0:T(8,128)(2,1)S(1)} %bitcast_dynamic-update-slice_fusion.both), channel_id=1, source_target_pairs={{0,2},{1,127},{2,4},{3,1},{4,6},{5,3},{6,8},{7,5},{8,10},{9,7},{10... | collective-permute-start | bytes 786440 | tf_op jit(solution)/shard_map/ppermute | solution.py:555
  12.2 10.6 %collective-permute-start.3 = (bf16[2,64,1024]{2,1,0:T(8,128)(2,1)S(1)}, bf16[2,64,1024]{2,1,0:T(8,128)(2,1)S(1)}, u32[]{:S(2)}, u32[]{:S(2)}) collective-permute-start(bf16[2,64,1024]{2,1,0:T(8,128)(2,1)S(1)} %bitcast_dynamic-update-slice_fusion.both), channel_id=1, source_target_pairs={{0,6},{1,123},{2,8},{3,125},{4,10},{5,127},{6,12},{7,1},{8,14},{9,... | collective-permute-start | bytes 786440 | tf_op jit(solution)/shard_map/ppermute | solution.py:555
  19.6 10.9 %copy-start = (bf16[4,256,256]{2,1,0:T(8,128)(2,1)S(1)}, bf16[4,256,256]{2,1,0:T(8,128)(2,1)}, u32[]{:S(2)}) copy-start(bf16[4,256,256]{2,1,0:T(8,128)(2,1)} %diag.3) | copy-start | bytes 1572868
  19.6 3.4 %collective-permute-start.5 = (s16[11,80,256]{2,1,0:T(8,128)(2,1)S(1)}, s16[11,80,256]{2,1,0:T(8,128)(2,1)S(1)}, u32[]{:S(2)}, u32[]{:S(2)}) collective-permute-start(s16[11,80,256]{2,1,0:T(8,128)(2,1)S(1)} %get-tuple-element.46), channel_id=1, source_target_pairs={{0,1},{1,0},{2,3},{3,2},{4,5},{5,4},{6,7},{7,6},{8,9},{9,8},{10,11... | collective-permute-start | bytes 1351688 | tf_op jit(solution)/shard_map/ppermute | solution.py:552
  22.9 7.6 %collective-permute-start.4 = (bf16[5,64,1024]{2,1,0:T(8,128)(2,1)S(1)}, bf16[5,64,1024]{2,1,0:T(8,128)(2,1)S(1)}, u32[]{:S(2)}, u32[]{:S(2)}) collective-permute-start(bf16[5,64,1024]{2,1,0:T(8,128)(2,1)S(1)} %pad_maximum_fusion), channel_id=1, source_target_pairs={{0,1},{1,0},{2,3},{3,2},{4,5},{5,4},{6,7},{7,6},{8,9},{9,8},{10,11... | collective-permute-start | bytes 1966088 | tf_op jit(solution)/shard_map/ppermute | solution.py:552
  23.0 14.1 %collective-permute-start.6 = (s16[4,80,256]{2,1,0:T(8,128)(2,1)S(1)}, s16[4,80,256]{2,1,0:T(8,128)(2,1)S(1)}, u32[]{:S(2)}, u32[]{:S(2)}) collective-permute-start(s16[4,80,256]{2,1,0:T(8,128)(2,1)S(1)} %get-tuple-element.79), channel_id=1, source_target_pairs={{0,4},{1,125},{2,6},{3,127},{4,8},{5,1},{6,10},{7,3},{8,12},{9,5},... | collective-permute-start | bytes 491528 | tf_op jit(solution)/shard_map/ppermute | solution.py:555
  28.2 8.9 %collective-permute-start.7 = (s16[4,80,256]{2,1,0:T(8,128)(2,1)S(1)}, s16[4,80,256]{2,1,0:T(8,128)(2,1)S(1)}, u32[]{:S(2)}, u32[]{:S(2)}) collective-permute-start(s16[4,80,256]{2,1,0:T(8,128)(2,1)S(1)} %get-tuple-element.80), channel_id=1, source_target_pairs={{0,2},{1,127},{2,4},{3,1},{4,6},{5,3},{6,8},{7,5},{8,10},{9,7},{10... | collective-permute-start | bytes 491528 | tf_op jit(solution)/shard_map/ppermute | solution.py:555
  30.4 6.7 %collective-permute-start.8 = (s16[3,80,256]{2,1,0:T(8,128)(2,1)S(1)}, s16[3,80,256]{2,1,0:T(8,128)(2,1)S(1)}, u32[]{:S(2)}, u32[]{:S(2)}) collective-permute-start(s16[3,80,256]{2,1,0:T(8,128)(2,1)S(1)} %get-tuple-element.78), channel_id=1, source_target_pairs={{0,6},{1,123},{2,8},{3,125},{4,10},{5,127},{6,12},{7,1},{8,14},{9,... | collective-permute-start | bytes 368648 | tf_op jit(solution)/shard_map/ppermute | solution.py:555
  37.2 1.5 %collective-permute-start.9 = (s16[5,80,256]{2,1,0:T(8,128)(2,1)S(1)}, s16[5,80,256]{2,1,0:T(8,128)(2,1)S(1)}, u32[]{:S(2)}, u32[]{:S(2)}) collective-permute-start(s16[5,80,256]{2,1,0:T(8,128)(2,1)S(1)} %pad_add_fusion), channel_id=1, source_target_pairs={{0,1},{1,0},{2,3},{3,2},{4,5},{5,4},{6,7},{7,6},{8,9},{9,8},{10,11... | collective-permute-start | bytes 614408 | tf_op jit(solution)/shard_map/ppermute | solution.py:552
  39.3 1.6 %collective-permute-start.10 = (bf16[7,64,256]{2,1,0:T(8,128)(2,1)S(1)}, bf16[7,64,256]{2,1,0:T(8,128)(2,1)S(1)}, u32[]{:S(2)}, u32[]{:S(2)}) collective-permute-start(bf16[7,64,256]{2,1,0:T(8,128)(2,1)S(1)} %get-tuple-element.60), channel_id=1, source_target_pairs={{0,1},{1,0},{2,3},{3,2},{4,5},{5,4},{6,7},{7,6},{8,9},{9,8},{10,11... | collective-permute-start | bytes 688136 | tf_op jit(solution)/shard_map/ppermute | solution.py:552
  40.9 8.9 %collective-permute-start.11 = (bf16[4,64,256]{2,1,0:T(8,128)(2,1)S(1)}, bf16[4,64,256]{2,1,0:T(8,128)(2,1)S(1)}, u32[]{:S(2)}, u32[]{:S(2)}) collective-permute-start(bf16[4,64,256]{2,1,0:T(8,128)(2,1)S(1)} %get-tuple-element.86), channel_id=1, source_target_pairs={{0,2},{1,127},{2,4},{3,1},{4,6},{5,3},{6,8},{7,5},{8,10},{9,7},{10... | collective-permute-start | bytes 393224 | tf_op jit(solution)/shard_map/ppermute | solution.py:555
  45.6 8.4 %collective-permute-start.12 = (bf16[4,64,256]{2,1,0:T(8,128)(2,1)S(1)}, bf16[4,64,256]{2,1,0:T(8,128)(2,1)S(1)}, u32[]{:S(2)}, u32[]{:S(2)}) collective-permute-start(bf16[4,64,256]{2,1,0:T(8,128)(2,1)S(1)} %get-tuple-element.85), channel_id=1, source_target_pairs={{0,4},{1,125},{2,6},{3,127},{4,8},{5,1},{6,10},{7,3},{8,12},{9,5},... | collective-permute-start | bytes 393224 | tf_op jit(solution)/shard_map/ppermute | solution.py:555
  45.8 9.2 %collective-permute-start.13 = (bf16[4,64,256]{2,1,0:T(8,128)(2,1)S(1)}, bf16[4,64,256]{2,1,0:T(8,128)(2,1)S(1)}, u32[]{:S(2)}, u32[]{:S(2)}) collective-permute-start(bf16[4,64,256]{2,1,0:T(8,128)(2,1)S(1)} %get-tuple-element.84), channel_id=1, source_target_pairs={{0,6},{1,123},{2,8},{3,125},{4,10},{5,127},{6,12},{7,1},{8,14},{9,... | collective-permute-start | bytes 393224 | tf_op jit(solution)/shard_map/ppermute | solution.py:555
  49.4 5.8 %collective-permute-start.15 = (bf16[7,64,256]{2,1,0:T(8,128)(2,1)S(1)}, bf16[7,64,256]{2,1,0:T(8,128)(2,1)S(1)}, u32[]{:S(2)}, u32[]{:S(2)}) collective-permute-start(bf16[7,64,256]{2,1,0:T(8,128)(2,1)S(1)} %get-tuple-element.69), channel_id=1, source_target_pairs={{0,1},{1,0},{2,3},{3,2},{4,5},{5,4},{6,7},{7,6},{8,9},{9,8},{10,11... | collective-permute-start | bytes 688136 | tf_op jit(solution)/shard_map/ppermute | solution.py:552
  55.1 4.7 %collective-permute-start.14 = (bf16[5,64,256]{2,1,0:T(8,128)(2,1)S(1)}, bf16[5,64,256]{2,1,0:T(8,128)(2,1)S(1)}, u32[]{:S(2)}, u32[]{:S(2)}) collective-permute-start(bf16[5,64,256]{2,1,0:T(8,128)(2,1)S(1)} %pad_maximum_fusion.1), channel_id=1, source_target_pairs={{0,1},{1,0},{2,3},{3,2},{4,5},{5,4},{6,7},{7,6},{8,9},{9,8},{10,11... | collective-permute-start | bytes 491528 | tf_op jit(solution)/shard_map/ppermute | solution.py:552
  55.2 9.2 %collective-permute-start.16 = (bf16[4,64,256]{2,1,0:T(8,128)(2,1)S(1)}, bf16[4,64,256]{2,1,0:T(8,128)(2,1)S(1)}, u32[]{:S(2)}, u32[]{:S(2)}) collective-permute-start(bf16[4,64,256]{2,1,0:T(8,128)(2,1)S(1)} %get-tuple-element.82), channel_id=1, source_target_pairs={{0,4},{1,125},{2,6},{3,127},{4,8},{5,1},{6,10},{7,3},{8,12},{9,5},... | collective-permute-start | bytes 393224 | tf_op jit(solution)/shard_map/ppermute | solution.py:555
  57.7 6.8 %collective-permute-start.17 = (bf16[4,64,256]{2,1,0:T(8,128)(2,1)S(1)}, bf16[4,64,256]{2,1,0:T(8,128)(2,1)S(1)}, u32[]{:S(2)}, u32[]{:S(2)}) collective-permute-start(bf16[4,64,256]{2,1,0:T(8,128)(2,1)S(1)} %get-tuple-element.83), channel_id=1, source_target_pairs={{0,2},{1,127},{2,4},{3,1},{4,6},{5,3},{6,8},{7,5},{8,10},{9,7},{10... | collective-permute-start | bytes 393224 | tf_op jit(solution)/shard_map/ppermute | solution.py:555
  59.4 5.0 %collective-permute-start.18 = (bf16[3,64,256]{2,1,0:T(8,128)(2,1)S(1)}, bf16[3,64,256]{2,1,0:T(8,128)(2,1)S(1)}, u32[]{:S(2)}, u32[]{:S(2)}) collective-permute-start(bf16[3,64,256]{2,1,0:T(8,128)(2,1)S(1)} %get-tuple-element.81), channel_id=1, source_target_pairs={{0,6},{1,123},{2,8},{3,125},{4,10},{5,127},{6,12},{7,1},{8,14},{9,... | collective-permute-start | bytes 294920 | tf_op jit(solution)/shard_map/ppermute | solution.py:555
  64.5 4.5 %collective-permute-start.19 = (bf16[5,64,256]{2,1,0:T(8,128)(2,1)S(1)}, bf16[5,64,256]{2,1,0:T(8,128)(2,1)S(1)}, u32[]{:S(2)}, u32[]{:S(2)}) collective-permute-start(bf16[5,64,256]{2,1,0:T(8,128)(2,1)S(1)} %pad_maximum_fusion.2), channel_id=1, source_target_pairs={{0,1},{1,0},{2,3},{3,2},{4,5},{5,4},{6,7},{7,6},{8,9},{9,8},{10,11... | collective-permute-start | bytes 491528 | tf_op jit(solution)/shard_map/ppermute | solution.py:552

commit v10 on v9

--- a/solution.py
+++ b/solution.py
@@ -590,7 +590,7 @@
     f1, f2, f3, f_got, messages = exchange(m1, m2, m3, give)
     rounded, messages = lax.optimization_barrier((rounded, messages))
     m1, m2, m3, give = k4(plan, rounded, *held)
-    f1, f2, f3, m1 = lax.optimization_barrier((f1, f2, f3, m1))
+    f2, f1, f3, m1 = lax.optimization_barrier((f2, f1, f3, m1))
     r1, r2, r3, got, messages = exchange(m1, m2, m3, give)
     f_post = passed_on(f1, f2, f3)
     f_post, messages = lax.optimization_barrier((f_post, messages))

time: 70.4 us -> 70.4 us (level)
  Pallas kernels: 21.3 us -> 19 us
  starting transfers between devices: 32.8 us -> 34.4 us
    ppermute x12, starting transfers between devices: 26.9 us -> 27.8 us  [carry(): return lax.ppermute(block, 'rows', carriers(size, k))]
  transfers between devices with their start and end apart: 20 -> 20, of which waited for: 10 -> 9; matrix products, arithmetic and copies ran while one was open for 1% -> 1% of each run, Pallas kernels for 28% -> 25%
where the time goes in v10:
time: 70.4 us; the launch traced here: 70 us
  starting transfers between devices  34.4 us (49%)
  Pallas kernels  19 us (27%)
  waiting for transfers between devices  14.5 us (21%)
  between operations  1.02 us (1%)
  local copies, waits for them, and re-layouts  0.83 us (1%)
    ppermute x12, starting transfers between devices, carry(): return lax.ppermute(block, 'rows', carriers(size, k))  27.8 us
    ppermute x12, waiting for transfers between devices, carry(): return lax.ppermute(block, 'rows', carriers(size, k))  11.1 us
    ppermute x8, starting transfers between devices, swap(): return lax.ppermute(block, 'rows', [(i, i ^ 1) for i in range(size)])  6.6 us
    pallas_call x1, Pallas kernels, k1(): call(back_first, 'transposed_products', message_shapes(RHS + EXTRA, jnp.i...  5.54 us
    pallas_call x1, Pallas kernels, k2(): call(forward_first, 'forward_products', shaped((CL, RHS, B), F32), VMEM,...  3.97 us
    pallas_call x1, Pallas kernels, k5(): call(forward_second, 'second_forward_products', shaped((CL, RHS, B), F32)...  3.95 us
    ppermute x8, waiting for transfers between devices, swap(): return lax.ppermute(block, 'rows', [(i, i ^ 1) for i in range(size)])  3.4 us
    pallas_call x1, Pallas kernels, k4(): call(back_second, 'second_transposed_products', message_shapes(RHS, BF16)...  3.08 us
  transfers between devices with their start and end apart: 20, of which 9 were waited for; matrix products, arithmetic and copies ran while one was open for 1% of the time, Pallas kernels for 25%

profile of v10, /device:TPU:1, one launch (start us, length us, event | category | flops | bytes accessed | tf_op | source)
XLA Modules:
  0.0 70.0 jit_solution(9610955993132679488)
XLA Ops:
  0.6 1.5 %collective-permute-start = (bf16[64,1024]{1,0:T(8,128)(2,1)}, bf16[64,1024]{1,0:T(8,128)(2,1)S(1)}, u32[]{:S(2)}, u32[]{:S(2)}) collective-permute-start(bf16[64,1024]{1,0:T(8,128)(2,1)} %source.1), channel_id=1, source_target_pairs={{0,1},{1,0},{2,3},{3,2},{4,5},{5,4},{6,7},{7,6},{8,9},{9,8},{10,11... | collective-permute-start | bytes 393224 | tf_op jit(solution)/shard_map/ppermute | solution.py:552
  2.1 0.9 %staged.1 = bf16[2,64,1024]{2,1,0:T(8,128)(2,1)S(1)} custom-call(bf16[64,1024]{1,0:T(8,128)(2,1)} %source.1), custom_call_target="tpu_custom_call" | custom-call | flops 2000000000 | bytes 22000000 | tf_op jit(solution)/shard_map/staged/pallas_call | solution.py:450
  3.0 0.3 collective-permute-done
  3.3 8.4 %collective-permute-start.1 = (bf16[2,64,1024]{2,1,0:T(8,128)(2,1)S(1)}, bf16[2,64,1024]{2,1,0:T(8,128)(2,1)S(1)}, u32[]{:S(2)}, u32[]{:S(2)}) collective-permute-start(bf16[2,64,1024]{2,1,0:T(8,128)(2,1)S(1)} %bitcast_dynamic-update-slice_fusion.both), channel_id=1, source_target_pairs={{0,4},{1,125},{2,6},{3,127},{4,8},{5,1},{6,10},{7,3},{8,12},{9,5},... | collective-permute-start | bytes 786440 | tf_op jit(solution)/shard_map/ppermute | solution.py:555
  11.7 0.4 collective-permute-start.2
  12.2 1.2 %collective-permute-start.3 = (bf16[2,64,1024]{2,1,0:T(8,128)(2,1)S(1)}, bf16[2,64,1024]{2,1,0:T(8,128)(2,1)S(1)}, u32[]{:S(2)}, u32[]{:S(2)}) collective-permute-start(bf16[2,64,1024]{2,1,0:T(8,128)(2,1)S(1)} %bitcast_dynamic-update-slice_fusion.both), channel_id=1, source_target_pairs={{0,6},{1,123},{2,8},{3,125},{4,10},{5,127},{6,12},{7,1},{8,14},{9,... | collective-permute-start | bytes 786440 | tf_op jit(solution)/shard_map/ppermute | solution.py:555
  13.4 5.5 %transposed_products.1 = (s16[4,80,256]{2,1,0:T(8,128)(2,1)S(1)}, s16[4,80,256]{2,1,0:T(8,128)(2,1)S(1)}, s16[3,80,256]{2,1,0:T(8,128)(2,1)S(1)}, s16[11,80,256]...) custom-call(s32[1]{0:T(128)} %bitcast.me, ...), custom_call_target="tpu_custom_call" | custom-call | flops 2000000000 | bytes 22000000 | tf_op jit(solution)/shard_map/transposed_products/pallas_call | solution.py:455
  18.9 0.0 copy-start
  18.9 0.5 collective-permute-start.5
  19.5 0.0 collective-permute-done.1.h2
  19.5 2.0 %collective-permute-done.2.h1 = bf16[2,64,1024]{2,1,0:T(8,128)(2,1)S(1)} collective-permute-done((bf16[2,64,1024]{2,1,0:T(8,128)(2,1)S(1)}, bf16[2,64,1024]{2,1,0:T(8,128)(2,1)S(1)}, u32[]{:S(2)}, u32[]{:S(2)}) %collective-permute-start.2) | collective-permute-done | bytes 262176 | tf_op jit(solution)/shard_map/ppermute | solution.py:555
  21.5 1.3 %collective-permute-done.3.h3 = bf16[2,64,1024]{2,1,0:T(8,128)(2,1)S(1)} collective-permute-done((bf16[2,64,1024]{2,1,0:T(8,128)(2,1)S(1)}, bf16[2,64,1024]{2,1,0:T(8,128)(2,1)S(1)}, u32[]{:S(2)}, u32[]{:S(2)}) %collective-permute-start.3) | collective-permute-done | bytes 262176 | tf_op jit(solution)/shard_map/ppermute | solution.py:555
  22.8 0.1 pad_maximum_fusion
  22.9 0.1 collective-permute-start.4
  23.0 0.0 collective-permute-done.5.got
  23.0 5.2 %collective-permute-start.6 = (s16[4,80,256]{2,1,0:T(8,128)(2,1)S(1)}, s16[4,80,256]{2,1,0:T(8,128)(2,1)S(1)}, u32[]{:S(2)}, u32[]{:S(2)}) collective-permute-start(s16[4,80,256]{2,1,0:T(8,128)(2,1)S(1)} %get-tuple-element.79), channel_id=1, source_target_pairs={{0,4},{1,125},{2,6},{3,127},{4,8},{5,1},{6,10},{7,3},{8,12},{9,5},... | collective-permute-start | bytes 491528 | tf_op jit(solution)/shard_map/ppermute | solution.py:555
  28.2 2.2 %collective-permute-start.7 = (s16[4,80,256]{2,1,0:T(8,128)(2,1)S(1)}, s16[4,80,256]{2,1,0:T(8,128)(2,1)S(1)}, u32[]{:S(2)}, u32[]{:S(2)}) collective-permute-start(s16[4,80,256]{2,1,0:T(8,128)(2,1)S(1)} %get-tuple-element.80), channel_id=1, source_target_pairs={{0,2},{1,127},{2,4},{3,1},{4,6},{5,3},{6,8},{7,5},{8,10},{9,7},{10... | collective-permute-start | bytes 491528 | tf_op jit(solution)/shard_map/ppermute | solution.py:555
  30.4 0.0 collective-permute-start.8
  30.5 0.0 collective-permute-done.4.post
  30.5 4.0 %forward_products.1.partial = f32[4,64,256]{2,1,0:T(8,128)S(1)} custom-call(s32[4,256]{1,0:T(4,128)S(1)} %get-tuple-element.40.draft, bf16[2,64,1024]{2,1,0:T(8,128)(2,1)S(1)} %bitcast_dynamic-update-slice_fusion.both, bf16[2,64,1024]{2,1,0:T(8,128)(2,1)S(1)} %collective-permute-done.2.h1, bf16[2,64,1024]{2,1,0:T(8,128)(2,1)S(1)} %collective-permute-done.1.h2, ...), custom_call_target="tpu_custom_call" | custom-call | flops 2000000000 | bytes 22000000 | tf_op jit(solution)/shard_map/forward_products/pallas_call | solution.py:485
  34.4 2.7 %collective-permute-done.8.r3 = s16[3,80,256]{2,1,0:T(8,128)(2,1)S(1)} collective-permute-done((s16[3,80,256]{2,1,0:T(8,128)(2,1)S(1)}, s16[3,80,256]{2,1,0:T(8,128)(2,1)S(1)}, u32[]{:S(2)}, u32[]{:S(2)}) %collective-permute-start.8) | collective-permute-done | bytes 122912 | tf_op jit(solution)/shard_map/ppermute | solution.py:555
  37.1 0.0 collective-permute-done.6.r2
  37.1 0.0 collective-permute-done.7.r1
  37.2 0.1 collective-permute-start.9
  37.3 1.4 %collective-permute-done.9.post = s16[5,80,256]{2,1,0:T(8,128)(2,1)S(1)} collective-permute-done((s16[5,80,256]{2,1,0:T(8,128)(2,1)S(1)}, s16[5,80,256]{2,1,0:T(8,128)(2,1)S(1)}, u32[]{:S(2)}, u32[]{:S(2)}) %collective-permute-start.9) | collective-permute-done | bytes 204832 | tf_op jit(solution)/shard_map/ppermute | solution.py:552
  38.7 0.6 first_image.1
  39.3 0.2 collective-permute-start.10
  39.5 1.4 %collective-permute-done.10.got = bf16[7,64,256]{2,1,0:T(8,128)(2,1)S(1)} collective-permute-done((bf16[7,64,256]{2,1,0:T(8,128)(2,1)S(1)}, bf16[7,64,256]{2,1,0:T(8,128)(2,1)S(1)}, u32[]{:S(2)}, u32[]{:S(2)}) %collective-permute-start.10) | collective-permute-done | bytes 229408 | tf_op jit(solution)/shard_map/ppermute | solution.py:552
  40.9 3.5 %collective-permute-start.11 = (bf16[4,64,256]{2,1,0:T(8,128)(2,1)S(1)}, bf16[4,64,256]{2,1,0:T(8,128)(2,1)S(1)}, u32[]{:S(2)}, u32[]{:S(2)}) collective-permute-start(bf16[4,64,256]{2,1,0:T(8,128)(2,1)S(1)} %get-tuple-element.85), channel_id=1, source_target_pairs={{0,4},{1,125},{2,6},{3,127},{4,8},{5,1},{6,10},{7,3},{8,12},{9,5},... | collective-permute-start | bytes 393224 | tf_op jit(solution)/shard_map/ppermute | solution.py:555
  44.4 2.0 %collective-permute-start.12 = (bf16[4,64,256]{2,1,0:T(8,128)(2,1)S(1)}, bf16[4,64,256]{2,1,0:T(8,128)(2,1)S(1)}, u32[]{:S(2)}, u32[]{:S(2)}) collective-permute-start(bf16[4,64,256]{2,1,0:T(8,128)(2,1)S(1)} %get-tuple-element.86), channel_id=1, source_target_pairs={{0,2},{1,127},{2,4},{3,1},{4,6},{5,3},{6,8},{7,5},{8,10},{9,7},{10... | collective-permute-start | bytes 393224 | tf_op jit(solution)/shard_map/ppermute | solution.py:555
  46.4 0.0 collective-permute-start.13
  46.4 3.1 %second_transposed_products.1 = (bf16[4,64,256]{2,1,0:T(8,128)(2,1)S(1)}, bf16[4,64,256]{2,1,0:T(8,128)(2,1)S(1)}, bf16[3,64,256]{2,1,0:T(8,128)(2,1)S(1)}, bf16[7,64,256]{2,1,0:T(8,128)(2,1)S(1)}) custom-call(s32[4,256]{1,0:T(4,128)S(1)} %get-tuple-element.40.draft, bf16[4,64,256]{2,1,0:T(8,128)(2,1)S(1)} %get-tuple-element.63.rounded.own, ...), custom_call_target="tpu_custom_call" | custom-call | flops 2000000000 | bytes 22000000 | tf_op jit(solution)/shard_map/second_transposed_products/pallas_call | solution.py:509
  49.5 1.8 %collective-permute-start.15 = (bf16[7,64,256]{2,1,0:T(8,128)(2,1)S(1)}, bf16[7,64,256]{2,1,0:T(8,128)(2,1)S(1)}, u32[]{:S(2)}, u32[]{:S(2)}) collective-permute-start(bf16[7,64,256]{2,1,0:T(8,128)(2,1)S(1)} %get-tuple-element.69), channel_id=1, source_target_pairs={{0,1},{1,0},{2,3},{3,2},{4,5},{5,4},{6,7},{7,6},{8,9},{9,8},{10,11... | collective-permute-start | bytes 688136 | tf_op jit(solution)/shard_map/ppermute | solution.py:552
  51.3 0.0 collective-permute-done.11.r2
  51.3 2.7 %collective-permute-done.13.r3 = bf16[4,64,256]{2,1,0:T(8,128)(2,1)S(1)} collective-permute-done((bf16[4,64,256]{2,1,0:T(8,128)(2,1)S(1)}, bf16[4,64,256]{2,1,0:T(8,128)(2,1)S(1)}, u32[]{:S(2)}, u32[]{:S(2)}) %collective-permute-start.13) | collective-permute-done | bytes 131104 | tf_op jit(solution)/shard_map/ppermute | solution.py:555
  54.1 0.1 collective-permute-start.14
  54.2 0.0 collective-permute-done.15.got
  54.2 2.0 %collective-permute-start.16 = (bf16[4,64,256]{2,1,0:T(8,128)(2,1)S(1)}, bf16[4,64,256]{2,1,0:T(8,128)(2,1)S(1)}, u32[]{:S(2)}, u32[]{:S(2)}) collective-permute-start(bf16[4,64,256]{2,1,0:T(8,128)(2,1)S(1)} %get-tuple-element.82), channel_id=1, source_target_pairs={{0,4},{1,125},{2,6},{3,127},{4,8},{5,1},{6,10},{7,3},{8,12},{9,5},... | collective-permute-start | bytes 393224 | tf_op jit(solution)/shard_map/ppermute | solution.py:555
  56.2 2.9 %collective-permute-start.17 = (bf16[4,64,256]{2,1,0:T(8,128)(2,1)S(1)}, bf16[4,64,256]{2,1,0:T(8,128)(2,1)S(1)}, u32[]{:S(2)}, u32[]{:S(2)}) collective-permute-start(bf16[4,64,256]{2,1,0:T(8,128)(2,1)S(1)} %get-tuple-element.83), channel_id=1, source_target_pairs={{0,2},{1,127},{2,4},{3,1},{4,6},{5,3},{6,8},{7,5},{8,10},{9,7},{10... | collective-permute-start | bytes 393224 | tf_op jit(solution)/shard_map/ppermute | solution.py:555
  59.0 0.0 collective-permute-start.18
  59.0 4.0 %second_forward_products.1.partial = f32[4,64,256]{2,1,0:T(8,128)S(1)} custom-call(s32[4,256]{1,0:T(4,128)S(1)} %get-tuple-element.40.draft, bf16[4,64,256]{2,1,0:T(8,128)(2,1)S(1)} %get-tuple-element.63.rounded.own, bf16[4,64,256]{2,1,0:T(8,128)(2,1)S(1)} %collective-permute-done.12.r1, bf16[4,64,256]{2,1,0:T(8,128)(2,1)S(1)} %collective-permute-done.11.r2, ...), custom_call_target="tpu_custom_call" | custom-call | flops 2000000000 | bytes 22000000 | tf_op jit(solution)/shard_map/second_forward_products/pallas_call | solution.py:519
  63.0 2.4 %collective-permute-done.18.r3 = bf16[3,64,256]{2,1,0:T(8,128)(2,1)S(1)} collective-permute-done((bf16[3,64,256]{2,1,0:T(8,128)(2,1)S(1)}, bf16[3,64,256]{2,1,0:T(8,128)(2,1)S(1)}, u32[]{:S(2)}, u32[]{:S(2)}) %collective-permute-start.18) | collective-permute-done | bytes 98336 | tf_op jit(solution)/shard_map/ppermute | solution.py:555
  65.4 0.0 collective-permute-done.16.r2
  65.4 0.0 collective-permute-done.17.r1
  65.5 2.3 %collective-permute-start.19 = (bf16[5,64,256]{2,1,0:T(8,128)(2,1)S(1)}, bf16[5,64,256]{2,1,0:T(8,128)(2,1)S(1)}, u32[]{:S(2)}, u32[]{:S(2)}) collective-permute-start(bf16[5,64,256]{2,1,0:T(8,128)(2,1)S(1)} %pad_maximum_fusion.2), channel_id=1, source_target_pairs={{0,1},{1,0},{2,3},{3,2},{4,5},{5,4},{6,7},{7,6},{8,9},{9,8},{10,11... | collective-permute-start | bytes 491528 | tf_op jit(solution)/shard_map/ppermute | solution.py:552
  67.8 0.7 %copy.22 = f32[64,1024]{1,0:T(8,128)} copy(f32[64,1024]{1,0:T(8,128)S(1)} %get-tuple-element.87) | data formatting | bytes 524288
  68.5 0.3 collective-permute-done.19.post
  68.8 1.0 %second_image.1 = f32[64,1024]{1,0:T(8,128)} custom-call(f32[4,64,256]{2,1,0:T(8,128)S(1)} %second_forward_products.1.partial, s32[16,256]{1,0:T(8,128)S(1)} %get-tuple-element.74.marked, bf16[4,64,256]{2,1,0:T(8,128)(2,1)S(1)} %collective-permute-done.17.r1, bf16[4,64,256]{2,1,0:T(8,128)(2,1)S(1)} %collective-permute-done.16.r2, ...), custom_call_target="tpu_custom_call" | custom-call | flops 2000000000 | bytes 22000000 | tf_op jit(solution)/shard_map/second_image/pallas_call | solution.py:528
  (20 shorter events, 0.2 us)
Async XLA Ops:
  0.6 2.7 %collective-permute-start = (bf16[64,1024]{1,0:T(8,128)(2,1)}, bf16[64,1024]{1,0:T(8,128)(2,1)S(1)}, u32[]{:S(2)}, u32[]{:S(2)}) collective-permute-start(bf16[64,1024]{1,0:T(8,128)(2,1)} %source.1), channel_id=1, source_target_pairs={{0,1},{1,0},{2,3},{3,2},{4,5},{5,4},{6,7},{7,6},{8,9},{9,8},{10,11... | collective-permute-start | bytes 393224 | tf_op jit(solution)/shard_map/ppermute | solution.py:552
  3.3 16.1 %collective-permute-start.1 = (bf16[2,64,1024]{2,1,0:T(8,128)(2,1)S(1)}, bf16[2,64,1024]{2,1,0:T(8,128)(2,1)S(1)}, u32[]{:S(2)}, u32[]{:S(2)}) collective-permute-start(bf16[2,64,1024]{2,1,0:T(8,128)(2,1)S(1)} %bitcast_dynamic-update-slice_fusion.both), channel_id=1, source_target_pairs={{0,4},{1,125},{2,6},{3,127},{4,8},{5,1},{6,10},{7,3},{8,12},{9,5},... | collective-permute-start | bytes 786440 | tf_op jit(solution)/shard_map/ppermute | solution.py:555
  11.7 9.7 %collective-permute-start.2 = (bf16[2,64,1024]{2,1,0:T(8,128)(2,1)S(1)}, bf16[2,64,1024]{2,1,0:T(8,128)(2,1)S(1)}, u32[]{:S(2)}, u32[]{:S(2)}) collective-permute-start(bf16[2,64,1024]{2,1,0:T(8,128)(2,1)S(1)} %bitcast_dynamic-update-slice_fusion.both), channel_id=1, source_target_pairs={{0,2},{1,127},{2,4},{3,1},{4,6},{5,3},{6,8},{7,5},{8,10},{9,7},{10... | collective-permute-start | bytes 786440 | tf_op jit(solution)/shard_map/ppermute | solution.py:555
  12.2 10.6 %collective-permute-start.3 = (bf16[2,64,1024]{2,1,0:T(8,128)(2,1)S(1)}, bf16[2,64,1024]{2,1,0:T(8,128)(2,1)S(1)}, u32[]{:S(2)}, u32[]{:S(2)}) collective-permute-start(bf16[2,64,1024]{2,1,0:T(8,128)(2,1)S(1)} %bitcast_dynamic-update-slice_fusion.both), channel_id=1, source_target_pairs={{0,6},{1,123},{2,8},{3,125},{4,10},{5,127},{6,12},{7,1},{8,14},{9,... | collective-permute-start | bytes 786440 | tf_op jit(solution)/shard_map/ppermute | solution.py:555
  18.9 11.5 %copy-start = (bf16[4,256,256]{2,1,0:T(8,128)(2,1)S(1)}, bf16[4,256,256]{2,1,0:T(8,128)(2,1)}, u32[]{:S(2)}) copy-start(bf16[4,256,256]{2,1,0:T(8,128)(2,1)} %diag.3) | copy-start | bytes 1572868
  18.9 4.1 %collective-permute-start.5 = (s16[11,80,256]{2,1,0:T(8,128)(2,1)S(1)}, s16[11,80,256]{2,1,0:T(8,128)(2,1)S(1)}, u32[]{:S(2)}, u32[]{:S(2)}) collective-permute-start(s16[11,80,256]{2,1,0:T(8,128)(2,1)S(1)} %get-tuple-element.46), channel_id=1, source_target_pairs={{0,1},{1,0},{2,3},{3,2},{4,5},{5,4},{6,7},{7,6},{8,9},{9,8},{10,11... | collective-permute-start | bytes 1351688 | tf_op jit(solution)/shard_map/ppermute | solution.py:552
  22.9 7.6 %collective-permute-start.4 = (bf16[5,64,1024]{2,1,0:T(8,128)(2,1)S(1)}, bf16[5,64,1024]{2,1,0:T(8,128)(2,1)S(1)}, u32[]{:S(2)}, u32[]{:S(2)}) collective-permute-start(bf16[5,64,1024]{2,1,0:T(8,128)(2,1)S(1)} %pad_maximum_fusion), channel_id=1, source_target_pairs={{0,1},{1,0},{2,3},{3,2},{4,5},{5,4},{6,7},{7,6},{8,9},{9,8},{10,11... | collective-permute-start | bytes 1966088 | tf_op jit(solution)/shard_map/ppermute | solution.py:552
  23.0 14.1 %collective-permute-start.6 = (s16[4,80,256]{2,1,0:T(8,128)(2,1)S(1)}, s16[4,80,256]{2,1,0:T(8,128)(2,1)S(1)}, u32[]{:S(2)}, u32[]{:S(2)}) collective-permute-start(s16[4,80,256]{2,1,0:T(8,128)(2,1)S(1)} %get-tuple-element.79), channel_id=1, source_target_pairs={{0,4},{1,125},{2,6},{3,127},{4,8},{5,1},{6,10},{7,3},{8,12},{9,5},... | collective-permute-start | bytes 491528 | tf_op jit(solution)/shard_map/ppermute | solution.py:555
  28.2 8.9 %collective-permute-start.7 = (s16[4,80,256]{2,1,0:T(8,128)(2,1)S(1)}, s16[4,80,256]{2,1,0:T(8,128)(2,1)S(1)}, u32[]{:S(2)}, u32[]{:S(2)}) collective-permute-start(s16[4,80,256]{2,1,0:T(8,128)(2,1)S(1)} %get-tuple-element.80), channel_id=1, source_target_pairs={{0,2},{1,127},{2,4},{3,1},{4,6},{5,3},{6,8},{7,5},{8,10},{9,7},{10... | collective-permute-start | bytes 491528 | tf_op jit(solution)/shard_map/ppermute | solution.py:555
  30.4 6.7 %collective-permute-start.8 = (s16[3,80,256]{2,1,0:T(8,128)(2,1)S(1)}, s16[3,80,256]{2,1,0:T(8,128)(2,1)S(1)}, u32[]{:S(2)}, u32[]{:S(2)}) collective-permute-start(s16[3,80,256]{2,1,0:T(8,128)(2,1)S(1)} %get-tuple-element.78), channel_id=1, source_target_pairs={{0,6},{1,123},{2,8},{3,125},{4,10},{5,127},{6,12},{7,1},{8,14},{9,... | collective-permute-start | bytes 368648 | tf_op jit(solution)/shard_map/ppermute | solution.py:555
  37.2 1.5 %collective-permute-start.9 = (s16[5,80,256]{2,1,0:T(8,128)(2,1)S(1)}, s16[5,80,256]{2,1,0:T(8,128)(2,1)S(1)}, u32[]{:S(2)}, u32[]{:S(2)}) collective-permute-start(s16[5,80,256]{2,1,0:T(8,128)(2,1)S(1)} %pad_add_fusion), channel_id=1, source_target_pairs={{0,1},{1,0},{2,3},{3,2},{4,5},{5,4},{6,7},{7,6},{8,9},{9,8},{10,11... | collective-permute-start | bytes 614408 | tf_op jit(solution)/shard_map/ppermute | solution.py:552
  39.3 1.6 %collective-permute-start.10 = (bf16[7,64,256]{2,1,0:T(8,128)(2,1)S(1)}, bf16[7,64,256]{2,1,0:T(8,128)(2,1)S(1)}, u32[]{:S(2)}, u32[]{:S(2)}) collective-permute-start(bf16[7,64,256]{2,1,0:T(8,128)(2,1)S(1)} %get-tuple-element.60), channel_id=1, source_target_pairs={{0,1},{1,0},{2,3},{3,2},{4,5},{5,4},{6,7},{7,6},{8,9},{9,8},{10,11... | collective-permute-start | bytes 688136 | tf_op jit(solution)/shard_map/ppermute | solution.py:552
  40.9 10.4 %collective-permute-start.11 = (bf16[4,64,256]{2,1,0:T(8,128)(2,1)S(1)}, bf16[4,64,256]{2,1,0:T(8,128)(2,1)S(1)}, u32[]{:S(2)}, u32[]{:S(2)}) collective-permute-start(bf16[4,64,256]{2,1,0:T(8,128)(2,1)S(1)} %get-tuple-element.85), channel_id=1, source_target_pairs={{0,4},{1,125},{2,6},{3,127},{4,8},{5,1},{6,10},{7,3},{8,12},{9,5},... | collective-permute-start | bytes 393224 | tf_op jit(solution)/shard_map/ppermute | solution.py:555
  44.4 6.9 %collective-permute-start.12 = (bf16[4,64,256]{2,1,0:T(8,128)(2,1)S(1)}, bf16[4,64,256]{2,1,0:T(8,128)(2,1)S(1)}, u32[]{:S(2)}, u32[]{:S(2)}) collective-permute-start(bf16[4,64,256]{2,1,0:T(8,128)(2,1)S(1)} %get-tuple-element.86), channel_id=1, source_target_pairs={{0,2},{1,127},{2,4},{3,1},{4,6},{5,3},{6,8},{7,5},{8,10},{9,7},{10... | collective-permute-start | bytes 393224 | tf_op jit(solution)/shard_map/ppermute | solution.py:555
  46.4 7.6 %collective-permute-start.13 = (bf16[4,64,256]{2,1,0:T(8,128)(2,1)S(1)}, bf16[4,64,256]{2,1,0:T(8,128)(2,1)S(1)}, u32[]{:S(2)}, u32[]{:S(2)}) collective-permute-start(bf16[4,64,256]{2,1,0:T(8,128)(2,1)S(1)} %get-tuple-element.84), channel_id=1, source_target_pairs={{0,6},{1,123},{2,8},{3,125},{4,10},{5,127},{6,12},{7,1},{8,14},{9,... | collective-permute-start | bytes 393224 | tf_op jit(solution)/shard_map/ppermute | solution.py:555
  49.5 4.7 %collective-permute-start.15 = (bf16[7,64,256]{2,1,0:T(8,128)(2,1)S(1)}, bf16[7,64,256]{2,1,0:T(8,128)(2,1)S(1)}, u32[]{:S(2)}, u32[]{:S(2)}) collective-permute-start(bf16[7,64,256]{2,1,0:T(8,128)(2,1)S(1)} %get-tuple-element.69), channel_id=1, source_target_pairs={{0,1},{1,0},{2,3},{3,2},{4,5},{5,4},{6,7},{7,6},{8,9},{9,8},{10,11... | collective-permute-start | bytes 688136 | tf_op jit(solution)/shard_map/ppermute | solution.py:552
  54.1 5.0 %collective-permute-start.14 = (bf16[5,64,256]{2,1,0:T(8,128)(2,1)S(1)}, bf16[5,64,256]{2,1,0:T(8,128)(2,1)S(1)}, u32[]{:S(2)}, u32[]{:S(2)}) collective-permute-start(bf16[5,64,256]{2,1,0:T(8,128)(2,1)S(1)} %pad_maximum_fusion.1), channel_id=1, source_target_pairs={{0,1},{1,0},{2,3},{3,2},{4,5},{5,4},{6,7},{7,6},{8,9},{9,8},{10,11... | collective-permute-start | bytes 491528 | tf_op jit(solution)/shard_map/ppermute | solution.py:552
  54.2 11.2 %collective-permute-start.16 = (bf16[4,64,256]{2,1,0:T(8,128)(2,1)S(1)}, bf16[4,64,256]{2,1,0:T(8,128)(2,1)S(1)}, u32[]{:S(2)}, u32[]{:S(2)}) collective-permute-start(bf16[4,64,256]{2,1,0:T(8,128)(2,1)S(1)} %get-tuple-element.82), channel_id=1, source_target_pairs={{0,4},{1,125},{2,6},{3,127},{4,8},{5,1},{6,10},{7,3},{8,12},{9,5},... | collective-permute-start | bytes 393224 | tf_op jit(solution)/shard_map/ppermute | solution.py:555
  56.2 9.3 %collective-permute-start.17 = (bf16[4,64,256]{2,1,0:T(8,128)(2,1)S(1)}, bf16[4,64,256]{2,1,0:T(8,128)(2,1)S(1)}, u32[]{:S(2)}, u32[]{:S(2)}) collective-permute-start(bf16[4,64,256]{2,1,0:T(8,128)(2,1)S(1)} %get-tuple-element.83), channel_id=1, source_target_pairs={{0,2},{1,127},{2,4},{3,1},{4,6},{5,3},{6,8},{7,5},{8,10},{9,7},{10... | collective-permute-start | bytes 393224 | tf_op jit(solution)/shard_map/ppermute | solution.py:555
  59.0 6.4 %collective-permute-start.18 = (bf16[3,64,256]{2,1,0:T(8,128)(2,1)S(1)}, bf16[3,64,256]{2,1,0:T(8,128)(2,1)S(1)}, u32[]{:S(2)}, u32[]{:S(2)}) collective-permute-start(bf16[3,64,256]{2,1,0:T(8,128)(2,1)S(1)} %get-tuple-element.81), channel_id=1, source_target_pairs={{0,6},{1,123},{2,8},{3,125},{4,10},{5,127},{6,12},{7,1},{8,14},{9,... | collective-permute-start | bytes 294920 | tf_op jit(solution)/shard_map/ppermute | solution.py:555
  65.5 3.3 %collective-permute-start.19 = (bf16[5,64,256]{2,1,0:T(8,128)(2,1)S(1)}, bf16[5,64,256]{2,1,0:T(8,128)(2,1)S(1)}, u32[]{:S(2)}, u32[]{:S(2)}) collective-permute-start(bf16[5,64,256]{2,1,0:T(8,128)(2,1)S(1)} %pad_maximum_fusion.2), channel_id=1, source_target_pairs={{0,1},{1,0},{2,3},{3,2},{4,5},{5,4},{6,7},{7,6},{8,9},{9,8},{10,11... | collective-permute-start | bytes 491528 | tf_op jit(solution)/shard_map/ppermute | solution.py:552

commit v11 on v10

--- a/solution.py
+++ b/solution.py
@@ -578,24 +578,24 @@
     m1, m2, m3, give, plan, *held = k1(
         me, *lists, in_hbm(counts), both, in_hbm(near_blocks), in_hbm(far_left), in_hbm(far_right)
     )
-    far_halo, halo_1, halo_3, m1 = lax.optimization_barrier((halo[1], halo[0], halo[2], m1))
+    far_halo, halo_3, halo_1, m1 = lax.optimization_barrier((halo[1], halo[2], halo[0], m1))
     halo = (halo_1, far_halo, halo_3)
     r1, r2, r3, got, messages = exchange(m1, m2, m3, give)
     halo_post = swap(jnp.concatenate([halo[0], halo[1], halo[2][1:]]))
     halo_post, messages = lax.optimization_barrier((halo_post, messages))
     partial = k2(plan, both, *halo, halo_post, diag_blocks, *held)
-    partial, r2, r1, r3 = lax.optimization_barrier((partial, r2, r1, r3))
+    partial, r2, r3, r1 = lax.optimization_barrier((partial, r2, r3, r1))
     post = passed_on(r1, r2, r3)
     first_image, rounded, marked, m1, m2, m3, give = k3(partial, r1, r2, r3, post, got)
     f1, f2, f3, f_got, messages = exchange(m1, m2, m3, give)
     rounded, messages = lax.optimization_barrier((rounded, messages))
     m1, m2, m3, give = k4(plan, rounded, *held)
-    f2, f1, f3, m1 = lax.optimization_barrier((f2, f1, f3, m1))
+    f2, f3, f1, m1 = lax.optimization_barrier((f2, f3, f1, m1))
     r1, r2, r3, got, messages = exchange(m1, m2, m3, give)
     f_post = passed_on(f1, f2, f3)
     f_post, messages = lax.optimization_barrier((f_post, messages))
     partial = k5(plan, rounded, f1, f2, f3, f_post, f_got, diag_blocks, *held)
-    partial, r2, r1, r3 = lax.optimization_barrier((partial, r2, r1, r3))
+    partial, r2, r3, r1 = lax.optimization_barrier((partial, r2, r3, r1))
     post = passed_on(r1, r2, r3)
     return first_image, k6(partial, marked, r1, r2, r3, post, got)
 

time: 70.4 us -> 69.7 us (0.990)
  waiting for transfers between devices: 14.5 us -> 5.14 us
  Pallas kernels: 19 us -> 27.6 us
    ppermute x12, waiting for transfers between devices: 11.1 us -> 0.81 us  [carry(): return lax.ppermute(block, 'rows', carriers(size, k))]
    pallas_call x1, Pallas kernels: 3.97 us -> 6.43 us  [k2(): call(forward_first, 'forward_products', shaped((CL, RHS, B), F32), VMEM,...]
    pallas_call x1, Pallas kernels: 3.95 us -> 6.41 us  [k5(): call(forward_second, 'second_forward_products', shaped((CL, RHS, B), F32)...]
    pallas_call x1, Pallas kernels: 5.54 us -> 7.39 us  [k1(): call(back_first, 'transposed_products', message_shapes(RHS + EXTRA, jnp.i...]
    pallas_call x1, Pallas kernels: 3.08 us -> 4.87 us  [k4(): call(back_second, 'second_transposed_products', message_shapes(RHS, BF16)...]
    ppermute x8, starting transfers between devices: 6.6 us -> 8.07 us  [swap(): return lax.ppermute(block, 'rows', [(i, i ^ 1) for i in range(size)])]
    ppermute x12, starting transfers between devices: 27.8 us -> 26.5 us  [carry(): return lax.ppermute(block, 'rows', carriers(size, k))]
    ppermute x8, waiting for transfers between devices: 3.4 us -> 4.33 us  [swap(): return lax.ppermute(block, 'rows', [(i, i ^ 1) for i in range(size)])]
  transfers between devices with their start and end apart: 20 -> 20, of which waited for: 9 -> 6; matrix products, arithmetic and copies ran while one was open for 1% -> 1% of each run, Pallas kernels for 25% -> 38%
where the time goes in v11:
time: 69.7 us; the launch traced here: 69.3 us
  starting transfers between devices  34.6 us (50%)
  Pallas kernels  27.6 us (40%)
  waiting for transfers between devices  5.14 us (7%)
  between operations  1.08 us (2%)
  local copies, waits for them, and re-layouts  0.82 us (1%)
    ppermute x12, starting transfers between devices, carry(): return lax.ppermute(block, 'rows', carriers(size, k))  26.5 us
    ppermute x8, starting transfers between devices, swap(): return lax.ppermute(block, 'rows', [(i, i ^ 1) for i in range(size)])  8.07 us
    pallas_call x1, Pallas kernels, k1(): call(back_first, 'transposed_products', message_shapes(RHS + EXTRA, jnp.i...  7.39 us
    pallas_call x1, Pallas kernels, k2(): call(forward_first, 'forward_products', shaped((CL, RHS, B), F32), VMEM,...  6.43 us
    pallas_call x1, Pallas kernels, k5(): call(forward_second, 'second_forward_products', shaped((CL, RHS, B), F32)...  6.41 us
    pallas_call x1, Pallas kernels, k4(): call(back_second, 'second_transposed_products', message_shapes(RHS, BF16)...  4.87 us
    ppermute x8, waiting for transfers between devices, swap(): return lax.ppermute(block, 'rows', [(i, i ^ 1) for i in range(size)])  4.33 us
  transfers between devices with their start and end apart: 20, of which 6 were waited for; matrix products, arithmetic and copies ran while one was open for 1% of the time, Pallas kernels for 38%

profile of v11, /device:TPU:1, one launch (start us, length us, event | category | flops | bytes accessed | tf_op | source)
XLA Modules:
  0.0 69.3 jit_solution(4680383092197158728)
XLA Ops:
  0.6 1.5 %collective-permute-start = (bf16[64,1024]{1,0:T(8,128)(2,1)}, bf16[64,1024]{1,0:T(8,128)(2,1)S(1)}, u32[]{:S(2)}, u32[]{:S(2)}) collective-permute-start(bf16[64,1024]{1,0:T(8,128)(2,1)} %source.1), channel_id=1, source_target_pairs={{0,1},{1,0},{2,3},{3,2},{4,5},{5,4},{6,7},{7,6},{8,9},{9,8},{10,11... | collective-permute-start | bytes 393224 | tf_op jit(solution)/shard_map/ppermute | solution.py:552
  2.1 0.9 %staged.1 = bf16[2,64,1024]{2,1,0:T(8,128)(2,1)S(1)} custom-call(bf16[64,1024]{1,0:T(8,128)(2,1)} %source.1), custom_call_target="tpu_custom_call" | custom-call | flops 2000000000 | bytes 22000000 | tf_op jit(solution)/shard_map/staged/pallas_call | solution.py:450
  3.0 0.3 collective-permute-done
  3.3 8.4 %collective-permute-start.1 = (bf16[2,64,1024]{2,1,0:T(8,128)(2,1)S(1)}, bf16[2,64,1024]{2,1,0:T(8,128)(2,1)S(1)}, u32[]{:S(2)}, u32[]{:S(2)}) collective-permute-start(bf16[2,64,1024]{2,1,0:T(8,128)(2,1)S(1)} %bitcast_dynamic-update-slice_fusion.both), channel_id=1, source_target_pairs={{0,4},{1,125},{2,6},{3,127},{4,8},{5,1},{6,10},{7,3},{8,12},{9,5},... | collective-permute-start | bytes 786440 | tf_op jit(solution)/shard_map/ppermute | solution.py:555
  11.7 0.9 %collective-permute-start.2 = (bf16[2,64,1024]{2,1,0:T(8,128)(2,1)S(1)}, bf16[2,64,1024]{2,1,0:T(8,128)(2,1)S(1)}, u32[]{:S(2)}, u32[]{:S(2)}) collective-permute-start(bf16[2,64,1024]{2,1,0:T(8,128)(2,1)S(1)} %bitcast_dynamic-update-slice_fusion.both), channel_id=1, source_target_pairs={{0,6},{1,123},{2,8},{3,125},{4,10},{5,127},{6,12},{7,1},{8,14},{9,... | collective-permute-start | bytes 786440 | tf_op jit(solution)/shard_map/ppermute | solution.py:555
  12.7 1.9 %collective-permute-start.3 = (bf16[2,64,1024]{2,1,0:T(8,128)(2,1)S(1)}, bf16[2,64,1024]{2,1,0:T(8,128)(2,1)S(1)}, u32[]{:S(2)}, u32[]{:S(2)}) collective-permute-start(bf16[2,64,1024]{2,1,0:T(8,128)(2,1)S(1)} %bitcast_dynamic-update-slice_fusion.both), channel_id=1, source_target_pairs={{0,2},{1,127},{2,4},{3,1},{4,6},{5,3},{6,8},{7,5},{8,10},{9,7},{10... | collective-permute-start | bytes 786440 | tf_op jit(solution)/shard_map/ppermute | solution.py:555
  14.6 7.4 %transposed_products.1 = (s16[4,80,256]{2,1,0:T(8,128)(2,1)S(1)}, s16[4,80,256]{2,1,0:T(8,128)(2,1)S(1)}, s16[3,80,256]{2,1,0:T(8,128)(2,1)S(1)}, s16[11,80,256]...) custom-call(s32[1]{0:T(128)} %bitcast.me, ...), custom_call_target="tpu_custom_call" | custom-call | flops 2000000000 | bytes 22000000 | tf_op jit(solution)/shard_map/transposed_products/pallas_call | solution.py:455
  22.0 0.0 copy-start
  22.0 0.1 collective-permute-start.5
  22.1 0.0 collective-permute-done.1.h2
  22.1 0.0 collective-permute-done.2.h3
  22.1 0.0 collective-permute-done.3.h1
  22.1 0.1 pad_maximum_fusion
  22.2 0.7 %collective-permute-start.4 = (bf16[5,64,1024]{2,1,0:T(8,128)(2,1)S(1)}, bf16[5,64,1024]{2,1,0:T(8,128)(2,1)S(1)}, u32[]{:S(2)}, u32[]{:S(2)}) collective-permute-start(bf16[5,64,1024]{2,1,0:T(8,128)(2,1)S(1)} %pad_maximum_fusion), channel_id=1, source_target_pairs={{0,1},{1,0},{2,3},{3,2},{4,5},{5,4},{6,7},{7,6},{8,9},{9,8},{10,11... | collective-permute-start | bytes 1966088 | tf_op jit(solution)/shard_map/ppermute | solution.py:552
  23.0 0.9 %collective-permute-done.5.got = s16[11,80,256]{2,1,0:T(8,128)(2,1)S(1)} collective-permute-done((s16[11,80,256]{2,1,0:T(8,128)(2,1)S(1)}, s16[11,80,256]{2,1,0:T(8,128)(2,1)S(1)}, u32[]{:S(2)}, u32[]{:S(2)}) %collective-permute-start.5) | collective-permute-done | bytes 450592 | tf_op jit(solution)/shard_map/ppermute | solution.py:552
  23.9 4.8 %collective-permute-start.6 = (s16[4,80,256]{2,1,0:T(8,128)(2,1)S(1)}, s16[4,80,256]{2,1,0:T(8,128)(2,1)S(1)}, u32[]{:S(2)}, u32[]{:S(2)}) collective-permute-start(s16[4,80,256]{2,1,0:T(8,128)(2,1)S(1)} %get-tuple-element.79), channel_id=1, source_target_pairs={{0,4},{1,125},{2,6},{3,127},{4,8},{5,1},{6,10},{7,3},{8,12},{9,5},... | collective-permute-start | bytes 491528 | tf_op jit(solution)/shard_map/ppermute | solution.py:555
  28.7 0.9 %collective-permute-start.8 = (s16[4,80,256]{2,1,0:T(8,128)(2,1)S(1)}, s16[4,80,256]{2,1,0:T(8,128)(2,1)S(1)}, u32[]{:S(2)}, u32[]{:S(2)}) collective-permute-start(s16[4,80,256]{2,1,0:T(8,128)(2,1)S(1)} %get-tuple-element.80), channel_id=1, source_target_pairs={{0,2},{1,127},{2,4},{3,1},{4,6},{5,3},{6,8},{7,5},{8,10},{9,7},{10... | collective-permute-start | bytes 491528 | tf_op jit(solution)/shard_map/ppermute | solution.py:555
  29.6 0.7 %collective-permute-start.7 = (s16[3,80,256]{2,1,0:T(8,128)(2,1)S(1)}, s16[3,80,256]{2,1,0:T(8,128)(2,1)S(1)}, u32[]{:S(2)}, u32[]{:S(2)}) collective-permute-start(s16[3,80,256]{2,1,0:T(8,128)(2,1)S(1)} %get-tuple-element.78), channel_id=1, source_target_pairs={{0,6},{1,123},{2,8},{3,125},{4,10},{5,127},{6,12},{7,1},{8,14},{9,... | collective-permute-start | bytes 368648 | tf_op jit(solution)/shard_map/ppermute | solution.py:555
  30.3 0.0 collective-permute-done.4.post
  30.3 6.4 %forward_products.1.partial = f32[4,64,256]{2,1,0:T(8,128)S(1)} custom-call(s32[4,256]{1,0:T(4,128)S(1)} %get-tuple-element.40.draft, bf16[2,64,1024]{2,1,0:T(8,128)(2,1)S(1)} %bitcast_dynamic-update-slice_fusion.both, bf16[2,64,1024]{2,1,0:T(8,128)(2,1)S(1)} %collective-permute-done.3.h1, bf16[2,64,1024]{2,1,0:T(8,128)(2,1)S(1)} %collective-permute-done.1.h2, ...), custom_call_target="tpu_custom_call" | custom-call | flops 2000000000 | bytes 22000000 | tf_op jit(solution)/shard_map/forward_products/pallas_call | solution.py:485
  36.8 0.8 %collective-permute-done.7.r3 = s16[3,80,256]{2,1,0:T(8,128)(2,1)S(1)} collective-permute-done((s16[3,80,256]{2,1,0:T(8,128)(2,1)S(1)}, s16[3,80,256]{2,1,0:T(8,128)(2,1)S(1)}, u32[]{:S(2)}, u32[]{:S(2)}) %collective-permute-start.7) | collective-permute-done | bytes 122912 | tf_op jit(solution)/shard_map/ppermute | solution.py:555
  37.5 0.0 collective-permute-done.6.r2
  37.6 0.0 collective-permute-done.8.r1
  37.6 0.1 collective-permute-start.9
  37.7 1.4 %collective-permute-done.9.post = s16[5,80,256]{2,1,0:T(8,128)(2,1)S(1)} collective-permute-done((s16[5,80,256]{2,1,0:T(8,128)(2,1)S(1)}, s16[5,80,256]{2,1,0:T(8,128)(2,1)S(1)}, u32[]{:S(2)}, u32[]{:S(2)}) %collective-permute-start.9) | collective-permute-done | bytes 204832 | tf_op jit(solution)/shard_map/ppermute | solution.py:552
  39.2 0.6 first_image.1
  39.7 0.2 collective-permute-start.10
  40.0 1.4 %collective-permute-done.10.got = bf16[7,64,256]{2,1,0:T(8,128)(2,1)S(1)} collective-permute-done((bf16[7,64,256]{2,1,0:T(8,128)(2,1)S(1)}, bf16[7,64,256]{2,1,0:T(8,128)(2,1)S(1)}, u32[]{:S(2)}, u32[]{:S(2)}) %collective-permute-start.10) | collective-permute-done | bytes 229408 | tf_op jit(solution)/shard_map/ppermute | solution.py:552
  41.3 2.5 %collective-permute-start.11 = (bf16[4,64,256]{2,1,0:T(8,128)(2,1)S(1)}, bf16[4,64,256]{2,1,0:T(8,128)(2,1)S(1)}, u32[]{:S(2)}, u32[]{:S(2)}) collective-permute-start(bf16[4,64,256]{2,1,0:T(8,128)(2,1)S(1)} %get-tuple-element.85), channel_id=1, source_target_pairs={{0,4},{1,125},{2,6},{3,127},{4,8},{5,1},{6,10},{7,3},{8,12},{9,5},... | collective-permute-start | bytes 393224 | tf_op jit(solution)/shard_map/ppermute | solution.py:555
  43.8 1.2 %collective-permute-start.12 = (bf16[4,64,256]{2,1,0:T(8,128)(2,1)S(1)}, bf16[4,64,256]{2,1,0:T(8,128)(2,1)S(1)}, u32[]{:S(2)}, u32[]{:S(2)}) collective-permute-start(bf16[4,64,256]{2,1,0:T(8,128)(2,1)S(1)} %get-tuple-element.84), channel_id=1, source_target_pairs={{0,6},{1,123},{2,8},{3,125},{4,10},{5,127},{6,12},{7,1},{8,14},{9,... | collective-permute-start | bytes 393224 | tf_op jit(solution)/shard_map/ppermute | solution.py:555
  45.0 1.7 %collective-permute-start.13 = (bf16[4,64,256]{2,1,0:T(8,128)(2,1)S(1)}, bf16[4,64,256]{2,1,0:T(8,128)(2,1)S(1)}, u32[]{:S(2)}, u32[]{:S(2)}) collective-permute-start(bf16[4,64,256]{2,1,0:T(8,128)(2,1)S(1)} %get-tuple-element.86), channel_id=1, source_target_pairs={{0,2},{1,127},{2,4},{3,1},{4,6},{5,3},{6,8},{7,5},{8,10},{9,7},{10... | collective-permute-start | bytes 393224 | tf_op jit(solution)/shard_map/ppermute | solution.py:555
  46.7 4.9 %second_transposed_products.1 = (bf16[4,64,256]{2,1,0:T(8,128)(2,1)S(1)}, bf16[4,64,256]{2,1,0:T(8,128)(2,1)S(1)}, bf16[3,64,256]{2,1,0:T(8,128)(2,1)S(1)}, bf16[7,64,256]{2,1,0:T(8,128)(2,1)S(1)}) custom-call(s32[4,256]{1,0:T(4,128)S(1)} %get-tuple-element.40.draft, bf16[4,64,256]{2,1,0:T(8,128)(2,1)S(1)} %get-tuple-element.63.rounded.own, ...), custom_call_target="tpu_custom_call" | custom-call | flops 2000000000 | bytes 22000000 | tf_op jit(solution)/shard_map/second_transposed_products/pallas_call | solution.py:509
  51.6 0.1 collective-permute-start.15
  51.6 0.0 collective-permute-done.11.r2
  51.7 0.0 collective-permute-done.13.r1
  51.7 3.2 %collective-permute-start.14 = (bf16[5,64,256]{2,1,0:T(8,128)(2,1)S(1)}, bf16[5,64,256]{2,1,0:T(8,128)(2,1)S(1)}, u32[]{:S(2)}, u32[]{:S(2)}) collective-permute-start(bf16[5,64,256]{2,1,0:T(8,128)(2,1)S(1)} %pad_maximum_fusion.1), channel_id=1, source_target_pairs={{0,1},{1,0},{2,3},{3,2},{4,5},{5,4},{6,7},{7,6},{8,9},{9,8},{10,11... | collective-permute-start | bytes 491528 | tf_op jit(solution)/shard_map/ppermute | solution.py:552
  55.0 0.0 collective-permute-done.15.got
  55.0 1.4 %collective-permute-start.16 = (bf16[4,64,256]{2,1,0:T(8,128)(2,1)S(1)}, bf16[4,64,256]{2,1,0:T(8,128)(2,1)S(1)}, u32[]{:S(2)}, u32[]{:S(2)}) collective-permute-start(bf16[4,64,256]{2,1,0:T(8,128)(2,1)S(1)} %get-tuple-element.82), channel_id=1, source_target_pairs={{0,4},{1,125},{2,6},{3,127},{4,8},{5,1},{6,10},{7,3},{8,12},{9,5},... | collective-permute-start | bytes 393224 | tf_op jit(solution)/shard_map/ppermute | solution.py:555
  56.4 2.1 %collective-permute-start.18 = (bf16[4,64,256]{2,1,0:T(8,128)(2,1)S(1)}, bf16[4,64,256]{2,1,0:T(8,128)(2,1)S(1)}, u32[]{:S(2)}, u32[]{:S(2)}) collective-permute-start(bf16[4,64,256]{2,1,0:T(8,128)(2,1)S(1)} %get-tuple-element.83), channel_id=1, source_target_pairs={{0,2},{1,127},{2,4},{3,1},{4,6},{5,3},{6,8},{7,5},{8,10},{9,7},{10... | collective-permute-start | bytes 393224 | tf_op jit(solution)/shard_map/ppermute | solution.py:555
  58.5 0.0 collective-permute-start.17
  58.5 0.0 collective-permute-done.14.post
  58.5 6.4 %second_forward_products.1.partial = f32[4,64,256]{2,1,0:T(8,128)S(1)} custom-call(s32[4,256]{1,0:T(4,128)S(1)} %get-tuple-element.40.draft, bf16[4,64,256]{2,1,0:T(8,128)(2,1)S(1)} %get-tuple-element.63.rounded.own, bf16[4,64,256]{2,1,0:T(8,128)(2,1)S(1)} %collective-permute-done.13.r1, bf16[4,64,256]{2,1,0:T(8,128)(2,1)S(1)} %collective-permute-done.11.r2, ...), custom_call_target="tpu_custom_call" | custom-call | flops 2000000000 | bytes 22000000 | tf_op jit(solution)/shard_map/second_forward_products/pallas_call | solution.py:519
  64.9 0.0 collective-permute-done.17.r3
  64.9 0.0 collective-permute-done.16.r2
  65.0 2.1 %collective-permute-start.19 = (bf16[5,64,256]{2,1,0:T(8,128)(2,1)S(1)}, bf16[5,64,256]{2,1,0:T(8,128)(2,1)S(1)}, u32[]{:S(2)}, u32[]{:S(2)}) collective-permute-start(bf16[5,64,256]{2,1,0:T(8,128)(2,1)S(1)} %pad_maximum_fusion.2), channel_id=1, source_target_pairs={{0,1},{1,0},{2,3},{3,2},{4,5},{5,4},{6,7},{7,6},{8,9},{9,8},{10,11... | collective-permute-start | bytes 491528 | tf_op jit(solution)/shard_map/ppermute | solution.py:552
  67.2 0.7 %copy.22 = f32[64,1024]{1,0:T(8,128)} copy(f32[64,1024]{1,0:T(8,128)S(1)} %get-tuple-element.87) | data formatting | bytes 524288
  67.9 0.3 collective-permute-done.19.post
  68.2 1.0 %second_image.1 = f32[64,1024]{1,0:T(8,128)} custom-call(f32[4,64,256]{2,1,0:T(8,128)S(1)} %second_forward_products.1.partial, s32[16,256]{1,0:T(8,128)S(1)} %get-tuple-element.74.marked, bf16[4,64,256]{2,1,0:T(8,128)(2,1)S(1)} %collective-permute-done.18.r1, bf16[4,64,256]{2,1,0:T(8,128)(2,1)S(1)} %collective-permute-done.16.r2, ...), custom_call_target="tpu_custom_call" | custom-call | flops 2000000000 | bytes 22000000 | tf_op jit(solution)/shard_map/second_image/pallas_call | solution.py:528
  (20 shorter events, 0.2 us)
Async XLA Ops:
  0.6 2.7 %collective-permute-start = (bf16[64,1024]{1,0:T(8,128)(2,1)}, bf16[64,1024]{1,0:T(8,128)(2,1)S(1)}, u32[]{:S(2)}, u32[]{:S(2)}) collective-permute-start(bf16[64,1024]{1,0:T(8,128)(2,1)} %source.1), channel_id=1, source_target_pairs={{0,1},{1,0},{2,3},{3,2},{4,5},{5,4},{6,7},{7,6},{8,9},{9,8},{10,11... | collective-permute-start | bytes 393224 | tf_op jit(solution)/shard_map/ppermute | solution.py:552
  3.3 18.8 %collective-permute-start.1 = (bf16[2,64,1024]{2,1,0:T(8,128)(2,1)S(1)}, bf16[2,64,1024]{2,1,0:T(8,128)(2,1)S(1)}, u32[]{:S(2)}, u32[]{:S(2)}) collective-permute-start(bf16[2,64,1024]{2,1,0:T(8,128)(2,1)S(1)} %bitcast_dynamic-update-slice_fusion.both), channel_id=1, source_target_pairs={{0,4},{1,125},{2,6},{3,127},{4,8},{5,1},{6,10},{7,3},{8,12},{9,5},... | collective-permute-start | bytes 786440 | tf_op jit(solution)/shard_map/ppermute | solution.py:555
  11.7 10.4 %collective-permute-start.2 = (bf16[2,64,1024]{2,1,0:T(8,128)(2,1)S(1)}, bf16[2,64,1024]{2,1,0:T(8,128)(2,1)S(1)}, u32[]{:S(2)}, u32[]{:S(2)}) collective-permute-start(bf16[2,64,1024]{2,1,0:T(8,128)(2,1)S(1)} %bitcast_dynamic-update-slice_fusion.both), channel_id=1, source_target_pairs={{0,6},{1,123},{2,8},{3,125},{4,10},{5,127},{6,12},{7,1},{8,14},{9,... | collective-permute-start | bytes 786440 | tf_op jit(solution)/shard_map/ppermute | solution.py:555
  12.7 9.5 %collective-permute-start.3 = (bf16[2,64,1024]{2,1,0:T(8,128)(2,1)S(1)}, bf16[2,64,1024]{2,1,0:T(8,128)(2,1)S(1)}, u32[]{:S(2)}, u32[]{:S(2)}) collective-permute-start(bf16[2,64,1024]{2,1,0:T(8,128)(2,1)S(1)} %bitcast_dynamic-update-slice_fusion.both), channel_id=1, source_target_pairs={{0,2},{1,127},{2,4},{3,1},{4,6},{5,3},{6,8},{7,5},{8,10},{9,7},{10... | collective-permute-start | bytes 786440 | tf_op jit(solution)/shard_map/ppermute | solution.py:555
  22.0 8.3 %copy-start = (bf16[4,256,256]{2,1,0:T(8,128)(2,1)S(1)}, bf16[4,256,256]{2,1,0:T(8,128)(2,1)}, u32[]{:S(2)}) copy-start(bf16[4,256,256]{2,1,0:T(8,128)(2,1)} %diag.3) | copy-start | bytes 1572868
  22.0 1.9 %collective-permute-start.5 = (s16[11,80,256]{2,1,0:T(8,128)(2,1)S(1)}, s16[11,80,256]{2,1,0:T(8,128)(2,1)S(1)}, u32[]{:S(2)}, u32[]{:S(2)}) collective-permute-start(s16[11,80,256]{2,1,0:T(8,128)(2,1)S(1)} %get-tuple-element.46), channel_id=1, source_target_pairs={{0,1},{1,0},{2,3},{3,2},{4,5},{5,4},{6,7},{7,6},{8,9},{9,8},{10,11... | collective-permute-start | bytes 1351688 | tf_op jit(solution)/shard_map/ppermute | solution.py:552
  22.2 8.1 %collective-permute-start.4 = (bf16[5,64,1024]{2,1,0:T(8,128)(2,1)S(1)}, bf16[5,64,1024]{2,1,0:T(8,128)(2,1)S(1)}, u32[]{:S(2)}, u32[]{:S(2)}) collective-permute-start(bf16[5,64,1024]{2,1,0:T(8,128)(2,1)S(1)} %pad_maximum_fusion), channel_id=1, source_target_pairs={{0,1},{1,0},{2,3},{3,2},{4,5},{5,4},{6,7},{7,6},{8,9},{9,8},{10,11... | collective-permute-start | bytes 1966088 | tf_op jit(solution)/shard_map/ppermute | solution.py:552
  23.9 13.6 %collective-permute-start.6 = (s16[4,80,256]{2,1,0:T(8,128)(2,1)S(1)}, s16[4,80,256]{2,1,0:T(8,128)(2,1)S(1)}, u32[]{:S(2)}, u32[]{:S(2)}) collective-permute-start(s16[4,80,256]{2,1,0:T(8,128)(2,1)S(1)} %get-tuple-element.79), channel_id=1, source_target_pairs={{0,4},{1,125},{2,6},{3,127},{4,8},{5,1},{6,10},{7,3},{8,12},{9,5},... | collective-permute-start | bytes 491528 | tf_op jit(solution)/shard_map/ppermute | solution.py:555
  28.7 8.9 %collective-permute-start.8 = (s16[4,80,256]{2,1,0:T(8,128)(2,1)S(1)}, s16[4,80,256]{2,1,0:T(8,128)(2,1)S(1)}, u32[]{:S(2)}, u32[]{:S(2)}) collective-permute-start(s16[4,80,256]{2,1,0:T(8,128)(2,1)S(1)} %get-tuple-element.80), channel_id=1, source_target_pairs={{0,2},{1,127},{2,4},{3,1},{4,6},{5,3},{6,8},{7,5},{8,10},{9,7},{10... | collective-permute-start | bytes 491528 | tf_op jit(solution)/shard_map/ppermute | solution.py:555
  29.6 8.0 %collective-permute-start.7 = (s16[3,80,256]{2,1,0:T(8,128)(2,1)S(1)}, s16[3,80,256]{2,1,0:T(8,128)(2,1)S(1)}, u32[]{:S(2)}, u32[]{:S(2)}) collective-permute-start(s16[3,80,256]{2,1,0:T(8,128)(2,1)S(1)} %get-tuple-element.78), channel_id=1, source_target_pairs={{0,6},{1,123},{2,8},{3,125},{4,10},{5,127},{6,12},{7,1},{8,14},{9,... | collective-permute-start | bytes 368648 | tf_op jit(solution)/shard_map/ppermute | solution.py:555
  37.6 1.5 %collective-permute-start.9 = (s16[5,80,256]{2,1,0:T(8,128)(2,1)S(1)}, s16[5,80,256]{2,1,0:T(8,128)(2,1)S(1)}, u32[]{:S(2)}, u32[]{:S(2)}) collective-permute-start(s16[5,80,256]{2,1,0:T(8,128)(2,1)S(1)} %pad_add_fusion), channel_id=1, source_target_pairs={{0,1},{1,0},{2,3},{3,2},{4,5},{5,4},{6,7},{7,6},{8,9},{9,8},{10,11... | collective-permute-start | bytes 614408 | tf_op jit(solution)/shard_map/ppermute | solution.py:552
  39.7 1.6 %collective-permute-start.10 = (bf16[7,64,256]{2,1,0:T(8,128)(2,1)S(1)}, bf16[7,64,256]{2,1,0:T(8,128)(2,1)S(1)}, u32[]{:S(2)}, u32[]{:S(2)}) collective-permute-start(bf16[7,64,256]{2,1,0:T(8,128)(2,1)S(1)} %get-tuple-element.60), channel_id=1, source_target_pairs={{0,1},{1,0},{2,3},{3,2},{4,5},{5,4},{6,7},{7,6},{8,9},{9,8},{10,11... | collective-permute-start | bytes 688136 | tf_op jit(solution)/shard_map/ppermute | solution.py:552
  41.3 10.3 %collective-permute-start.11 = (bf16[4,64,256]{2,1,0:T(8,128)(2,1)S(1)}, bf16[4,64,256]{2,1,0:T(8,128)(2,1)S(1)}, u32[]{:S(2)}, u32[]{:S(2)}) collective-permute-start(bf16[4,64,256]{2,1,0:T(8,128)(2,1)S(1)} %get-tuple-element.85), channel_id=1, source_target_pairs={{0,4},{1,125},{2,6},{3,127},{4,8},{5,1},{6,10},{7,3},{8,12},{9,5},... | collective-permute-start | bytes 393224 | tf_op jit(solution)/shard_map/ppermute | solution.py:555
  43.8 7.9 %collective-permute-start.12 = (bf16[4,64,256]{2,1,0:T(8,128)(2,1)S(1)}, bf16[4,64,256]{2,1,0:T(8,128)(2,1)S(1)}, u32[]{:S(2)}, u32[]{:S(2)}) collective-permute-start(bf16[4,64,256]{2,1,0:T(8,128)(2,1)S(1)} %get-tuple-element.84), channel_id=1, source_target_pairs={{0,6},{1,123},{2,8},{3,125},{4,10},{5,127},{6,12},{7,1},{8,14},{9,... | collective-permute-start | bytes 393224 | tf_op jit(solution)/shard_map/ppermute | solution.py:555
  45.0 6.7 %collective-permute-start.13 = (bf16[4,64,256]{2,1,0:T(8,128)(2,1)S(1)}, bf16[4,64,256]{2,1,0:T(8,128)(2,1)S(1)}, u32[]{:S(2)}, u32[]{:S(2)}) collective-permute-start(bf16[4,64,256]{2,1,0:T(8,128)(2,1)S(1)} %get-tuple-element.86), channel_id=1, source_target_pairs={{0,2},{1,127},{2,4},{3,1},{4,6},{5,3},{6,8},{7,5},{8,10},{9,7},{10... | collective-permute-start | bytes 393224 | tf_op jit(solution)/shard_map/ppermute | solution.py:555
  51.6 3.4 %collective-permute-start.15 = (bf16[7,64,256]{2,1,0:T(8,128)(2,1)S(1)}, bf16[7,64,256]{2,1,0:T(8,128)(2,1)S(1)}, u32[]{:S(2)}, u32[]{:S(2)}) collective-permute-start(bf16[7,64,256]{2,1,0:T(8,128)(2,1)S(1)} %get-tuple-element.69), channel_id=1, source_target_pairs={{0,1},{1,0},{2,3},{3,2},{4,5},{5,4},{6,7},{7,6},{8,9},{9,8},{10,11... | collective-permute-start | bytes 688136 | tf_op jit(solution)/shard_map/ppermute | solution.py:552
  51.7 6.8 %collective-permute-start.14 = (bf16[5,64,256]{2,1,0:T(8,128)(2,1)S(1)}, bf16[5,64,256]{2,1,0:T(8,128)(2,1)S(1)}, u32[]{:S(2)}, u32[]{:S(2)}) collective-permute-start(bf16[5,64,256]{2,1,0:T(8,128)(2,1)S(1)} %pad_maximum_fusion.1), channel_id=1, source_target_pairs={{0,1},{1,0},{2,3},{3,2},{4,5},{5,4},{6,7},{7,6},{8,9},{9,8},{10,11... | collective-permute-start | bytes 491528 | tf_op jit(solution)/shard_map/ppermute | solution.py:552
  55.0 9.9 %collective-permute-start.16 = (bf16[4,64,256]{2,1,0:T(8,128)(2,1)S(1)}, bf16[4,64,256]{2,1,0:T(8,128)(2,1)S(1)}, u32[]{:S(2)}, u32[]{:S(2)}) collective-permute-start(bf16[4,64,256]{2,1,0:T(8,128)(2,1)S(1)} %get-tuple-element.82), channel_id=1, source_target_pairs={{0,4},{1,125},{2,6},{3,127},{4,8},{5,1},{6,10},{7,3},{8,12},{9,5},... | collective-permute-start | bytes 393224 | tf_op jit(solution)/shard_map/ppermute | solution.py:555
  56.4 8.6 %collective-permute-start.18 = (bf16[4,64,256]{2,1,0:T(8,128)(2,1)S(1)}, bf16[4,64,256]{2,1,0:T(8,128)(2,1)S(1)}, u32[]{:S(2)}, u32[]{:S(2)}) collective-permute-start(bf16[4,64,256]{2,1,0:T(8,128)(2,1)S(1)} %get-tuple-element.83), channel_id=1, source_target_pairs={{0,2},{1,127},{2,4},{3,1},{4,6},{5,3},{6,8},{7,5},{8,10},{9,7},{10... | collective-permute-start | bytes 393224 | tf_op jit(solution)/shard_map/ppermute | solution.py:555
  58.5 6.4 %collective-permute-start.17 = (bf16[3,64,256]{2,1,0:T(8,128)(2,1)S(1)}, bf16[3,64,256]{2,1,0:T(8,128)(2,1)S(1)}, u32[]{:S(2)}, u32[]{:S(2)}) collective-permute-start(bf16[3,64,256]{2,1,0:T(8,128)(2,1)S(1)} %get-tuple-element.81), channel_id=1, source_target_pairs={{0,6},{1,123},{2,8},{3,125},{4,10},{5,127},{6,12},{7,1},{8,14},{9,... | collective-permute-start | bytes 294920 | tf_op jit(solution)/shard_map/ppermute | solution.py:555
  65.0 3.1 %collective-permute-start.19 = (bf16[5,64,256]{2,1,0:T(8,128)(2,1)S(1)}, bf16[5,64,256]{2,1,0:T(8,128)(2,1)S(1)}, u32[]{:S(2)}, u32[]{:S(2)}) collective-permute-start(bf16[5,64,256]{2,1,0:T(8,128)(2,1)S(1)} %pad_maximum_fusion.2), channel_id=1, source_target_pairs={{0,1},{1,0},{2,3},{3,2},{4,5},{5,4},{6,7},{7,6},{8,9},{9,8},{10,11... | collective-permute-start | bytes 491528 | tf_op jit(solution)/shard_map/ppermute | solution.py:552
